TPU v7x, 32 devices: a whole 2x2x4 slice. The times are simulated.
32 devices in a mesh: dp: 2 (over x), wide: 16 (over z, y, core).
Axes of the slice: x: 2, y: 2, z: 4, core: 2. Of those that a mesh axis runs over, the one named last changes fastest.
Arguments:
- latents: bfloat16 [2, 32, 8, 16, 256], P('dp', 'wide'), may hold values from -36 to 36
- cotangent: bfloat16 [2, 32, 8, 16, 256], P('dp', 'wide'), may hold values from -41 to 41
- norm_gain: float32 [256], replicated, may hold values from 0.25 to 1.75
- norm_bias: float32 [256], replicated, may hold values from -3 to 3
- w_spatial: bfloat16 [2304, 256], P('dp'), may hold values from -0.125 to 0.125
- w_temporal: bfloat16 [768, 256], P('dp'), may hold values from -0.21875 to 0.21875
Outputs:
- block_out: bfloat16 [2, 32, 8, 16, 256], P('dp', 'wide')
- grad_latents: bfloat16 [2, 32, 8, 16, 256], P('dp', 'wide')
- grad_spatial: float32 [2304, 256], P('dp', 'wide')
- grad_temporal: float32 [768, 256], P('dp', 'wide')
- grad_norm: float32 [2, 256], P(None, 'wide')
All inputs are finite; a program needn't handle non-finite values.
Results may differ from a plain program's by a relative error of at most 0.012.
Values may be sent and summed in bfloat16 or wider, within the bound.
No kernel may reach another device: no remote copies, remote signals or barrier semaphores. Data moves between devices by JAX's collectives and lax.ppermute only.
A program may use at most 64 MiB of HBM per device.

v0:
```python
import math

import jax
import jax.numpy as jnp
from jax import lax
from jax.sharding import PartitionSpec as P

GROUPS = 32


epsilon = 1e-05


def contract(left, right):
    return lax.dot_general(
        left, right, (((0,), (0,)), ((), ())), preferred_element_type=jnp.float32
    )


def spatial_forward(activated, weights):
    frames, rows_here, cols_here, channels = activated.shape
    padded = jnp.pad(activated, ((0, 0), (1, 1), (1, 1), (0, 0)))
    running = jnp.zeros((frames * rows_here * cols_here, channels), jnp.float32)
    for tap_row in range(3):
        for tap_col in range(3):
            tap_index = 3 * tap_row + tap_col
            window = padded[
                :, tap_row : tap_row + rows_here, tap_col : tap_col + cols_here, :
            ].reshape(-1, channels)
            running = running + jnp.dot(
                window,
                weights[tap_index * channels : (tap_index + 1) * channels],
                preferred_element_type=jnp.float32,
            )
    return running.reshape(frames, rows_here, cols_here, channels)


def spatial_backward(activated, grad_out, weights):
    frames, rows_here, cols_here, channels = activated.shape
    pad_act = jnp.pad(activated, ((0, 0), (1, 1), (1, 1), (0, 0)))
    pad_grad = jnp.pad(grad_out, ((0, 0), (1, 1), (1, 1), (0, 0)))
    flat_grad = grad_out.reshape(-1, channels)
    running = jnp.zeros((frames * rows_here * cols_here, channels), jnp.float32)
    pieces = []
    for tap_row in range(3):
        for tap_col in range(3):
            tap_index = 3 * tap_row + tap_col
            block = weights[tap_index * channels : (tap_index + 1) * channels]
            window_grad = pad_grad[
                :, 2 - tap_row : 2 - tap_row + rows_here, 2 - tap_col : 2 - tap_col + cols_here, :
            ].reshape(-1, channels)
            running = running + jnp.dot(window_grad, block.T, preferred_element_type=jnp.float32)
            window_act = pad_act[
                :, tap_row : tap_row + rows_here, tap_col : tap_col + cols_here, :
            ].reshape(-1, channels)
            pieces.append(contract(window_act, flat_grad))
    return (
        running.reshape(frames, rows_here, cols_here, channels),
        jnp.concatenate(pieces, axis=0),
    )


def temporal_apply(extended, weights, frames):
    channels = extended.shape[-1]
    shape_out = (extended.shape[0], frames, extended.shape[2], channels)
    running = jnp.zeros((shape_out[0] * frames * shape_out[2], channels), jnp.float32)
    for time_delay in range(3):
        earlier = extended[:, 2 - time_delay : 2 - time_delay + frames].reshape(-1, channels)
        running = running + jnp.dot(
            earlier,
            weights[time_delay * channels : (time_delay + 1) * channels],
            preferred_element_type=jnp.float32,
        )
    return running.reshape(shape_out)


def temporal_adjoint(earlier_ext, later_ext, grad_rows, weights):
    frames = grad_rows.shape[1]
    channels = grad_rows.shape[-1]
    flat_grad = grad_rows.reshape(-1, channels)
    running = jnp.zeros(flat_grad.shape, jnp.float32)
    pieces = []
    for time_delay in range(3):
        block = weights[time_delay * channels : (time_delay + 1) * channels]
        later_rows = later_ext[:, time_delay : time_delay + frames].reshape(-1, channels)
        running = running + jnp.dot(later_rows, block.T, preferred_element_type=jnp.float32)
        earlier = earlier_ext[:, 2 - time_delay : 2 - time_delay + frames].reshape(-1, channels)
        pieces.append(contract(earlier, flat_grad))
    return (running.reshape(grad_rows.shape), jnp.concatenate(pieces, axis=0))


def local(latents, cotangent, norm_gain, norm_bias, w_spatial, w_temporal):
    clip_count, frames, rows_here, cols_here, channels = latents.shape
    per_group = channels // GROUPS
    cell_count = rows_here * cols_here
    spatial_full, temporal_full = (
        lax.all_gather(w_spatial, "dp", axis=0, tiled=True),
        lax.all_gather(w_temporal, "dp", axis=0, tiled=True),
    )
    widened = latents.astype(jnp.float32).reshape(
        clip_count, frames, rows_here, cols_here, GROUPS, per_group
    )
    group_sums = jnp.sum(widened, axis=(1, 2, 3, 5))
    squares = jnp.sum(widened * widened, axis=(1, 2, 3, 5))
    total_sums, total_squares = lax.psum((group_sums, squares), "wide")
    cells_count = lax.axis_size("wide") * frames * rows_here * cols_here * per_group
    group_mean = total_sums / cells_count
    variance = total_squares / cells_count - group_mean * group_mean
    inv_std = 1.0 / jnp.sqrt(variance + epsilon)
    mean_wide = group_mean[:, None, None, None, :, None]
    std_wide = inv_std[:, None, None, None, :, None]
    whitened = (widened - mean_wide) * std_wide
    flat_white = whitened.reshape(latents.shape)
    normed = flat_white * norm_gain + norm_bias
    sigmoid = jax.nn.sigmoid(normed)
    activated = (normed * sigmoid).astype(jnp.bfloat16)
    silu_slope = sigmoid * (1.0 + normed * (1.0 - sigmoid))
    stacked = activated.reshape(clip_count * frames, rows_here, cols_here, channels)
    spatial = (
        spatial_forward(stacked, spatial_full)
        .astype(jnp.bfloat16)
        .reshape(clip_count, frames, cell_count, channels)
    )
    grad_rows = cotangent.reshape(clip_count, frames, cell_count, channels)
    row_slab = lax.all_to_all(spatial, "wide", split_axis=2, concat_axis=1, tiled=True)
    extended = jnp.pad(row_slab, ((0, 0), (2, 0), (0, 0), (0, 0)))
    mixed_rows = temporal_apply(extended, temporal_full, row_slab.shape[1])
    returned = lax.all_to_all(
        mixed_rows.astype(jnp.bfloat16), "wide", split_axis=1, concat_axis=2, tiled=True
    ).astype(mixed_rows.dtype)
    grad_slab = lax.all_to_all(grad_rows, "wide", split_axis=2, concat_axis=1, tiled=True)
    earlier_ext = jnp.pad(row_slab, ((0, 0), (2, 0), (0, 0), (0, 0)))
    later_ext = jnp.pad(grad_slab, ((0, 0), (0, 2), (0, 0), (0, 0)))
    slab_wide, local_temporal = temporal_adjoint(earlier_ext, later_ext, grad_slab, temporal_full)
    grad_spatial_act = lax.all_to_all(
        slab_wide.astype(jnp.bfloat16), "wide", split_axis=1, concat_axis=2, tiled=True
    )
    block_out = (latents.astype(jnp.float32) + returned.reshape(latents.shape)).astype(jnp.bfloat16)
    grad_stack = grad_spatial_act.reshape(clip_count * frames, rows_here, cols_here, channels)
    grad_activated, local_spatial = spatial_backward(stacked, grad_stack, spatial_full)
    grad_normed = grad_activated.reshape(latents.shape) * silu_slope
    gain_term = jnp.sum(grad_normed * flat_white, axis=(0, 1, 2, 3))
    bias_term = jnp.sum(grad_normed, axis=(0, 1, 2, 3))
    local_norm = jnp.stack([gain_term, bias_term])
    grad_white = (grad_normed * norm_gain).reshape(widened.shape)
    mean_part = jnp.sum(grad_white, axis=(1, 2, 3, 5))
    cross_part = jnp.sum(grad_white * whitened, axis=(1, 2, 3, 5))
    mean_total, cross_total = lax.psum((mean_part, cross_part), "wide")
    grad_mean = mean_total / cells_count
    grad_cross = cross_total / cells_count
    inner = (
        grad_white
        - grad_mean[:, None, None, None, :, None]
        - whitened * grad_cross[:, None, None, None, :, None]
    ) * std_wide
    grad_latents = (cotangent.astype(jnp.float32) + inner.reshape(latents.shape)).astype(
        jnp.bfloat16
    )
    part_spatial, part_temporal, part_norm = (
        lax.psum_scatter(local_spatial, "wide", scatter_dimension=1, tiled=True),
        lax.psum_scatter(local_temporal, "wide", scatter_dimension=1, tiled=True),
        lax.psum_scatter(local_norm, "wide", scatter_dimension=1, tiled=True),
    )
    summed_spatial, summed_temporal = (
        lax.psum_scatter(
            part_spatial.astype(jnp.bfloat16), "dp", scatter_dimension=0, tiled=True
        ).astype(jnp.float32),
        lax.psum_scatter(
            part_temporal.astype(jnp.bfloat16), "dp", scatter_dimension=0, tiled=True
        ).astype(jnp.float32),
    )
    summed_norm = lax.psum(part_norm, "dp")
    all_cells = (
        clip_count * lax.axis_size("dp") * frames * lax.axis_size("wide") * rows_here * cols_here
    )
    grad_scale = 1.0 / math.sqrt(all_cells)
    return (
        block_out,
        grad_latents,
        summed_spatial * grad_scale,
        summed_temporal * grad_scale,
        summed_norm * grad_scale,
    )


def solution(mesh):
    return jax.shard_map(
        local,
        mesh=mesh,
        in_specs=(
            P("dp", "wide", None, None, None),
            P("dp", "wide", None, None, None),
            P(),
            P(),
            P("dp", None),
            P("dp", None),
        ),
        out_specs=(
            P("dp", "wide", None, None, None),
            P("dp", "wide", None, None, None),
            P("dp", "wide"),
            P("dp", "wide"),
            P(None, "wide"),
        ),
        check_vma=False,
    )
```

profile of v0, /device:TPU:0, one launch (start us, length us, event | category | flops | bytes accessed | tf_op | source)
XLA Modules:
  0.0 288.0 jit_solution(10324092278496474108)
XLA Ops:
  7.2 1.7 copy.35
  8.9 7.4 %all-to-all-start.2 = ((bf16[1,2,128,256]{3,1,0,2:T(2,128)(2,1)}), bf16[1,2,128,256]{3,1,0,2:T(2,128)(2,1)S(1)}, u32[]{:S(2)}, u32[]{:S(2)}) async-start(bf16[1,2,128,256]{3,1,0,2:T(2,128)(2,1)} %bitcast.26), calls=%async_computation.2 | async-start | bytes 262144 | tf_op jit(solution)/shard_map/all_to_all | solution.py:131
  17.1 7.9 %all_gather.7 = bf16[768,256]{1,0:T(8,128)(2,1)S(1)} all-gather(bf16[384,256]{1,0:T(8,128)(2,1)S(1)} %copy-done.3), channel_id=1, replica_groups=mesh['dp'=2,'wide'=16] {'dp'}, dimensions={0}, use_global_device_ids=true | all-gather | bytes 589824 | tf_op jit(solution)/shard_map/all_gather | solution.py:98
  26.3 5.7 %all-to-all-start.3 = ((bf16[1,32,8,256]{3,2,0,1:T(8,128)(2,1)}), bf16[1,32,8,256]{3,2,0,1:T(8,128)(2,1)S(1)}, u32[]{:S(2)}, u32[]{:S(2)}) async-start(bf16[1,32,8,256]{3,2,0,1:T(8,128)(2,1)} %fusion.3), calls=%async_computation.3 | async-start | bytes 262144 | tf_op jit(solution)/shard_map/all_to_all | solution.py:135
  32.6 33.9 %all-reduce.5 = (f32[1,32]{1,0:T(1,128)S(1)}, f32[1,32]{1,0:T(1,128)S(1)}) all-reduce(f32[1,32]{1,0:T(1,128)S(1)} %bitcast.208, f32[1,32]{1,0:T(1,128)S(1)} %bitcast.206), channel_id=1, replica_groups=mesh['dp'=2,'wide'=16] {'wide'}, use_global_device_ids=true, to_apply=%region_5.6 | all-reduce | flops 64 | bytes 512 | tf_op jit(solution)/shard_map/psum | solution.py:105
  67.0 1.2 fusion.67
  68.2 1.1 convolution_add_fusion.7
  72.1 0.9 convolution_dynamic-update-slice_fusion.8
  75.6 3.5 %all-to-all-start = ((bf16[1,2,128,256]{3,1,0,2:T(2,128)(2,1)}), bf16[1,2,128,256]{3,1,0,2:T(2,128)(2,1)S(1)}, u32[]{:S(2)}, u32[]{:S(2)}) async-start(bf16[1,2,128,256]{3,1,0,2:T(2,128)(2,1)} %copy.30), calls=%async_computation | async-start | bytes 262144 | tf_op jit(solution)/shard_map/all_to_all | solution.py:125
  79.2 0.9 convolution_dynamic-update-slice_fusion.7
  80.1 0.9 convolution_dynamic-update-slice_fusion.6
  81.1 0.9 convolution_dynamic-update-slice_fusion.5
  82.0 5.0 %all-to-all-done = bf16[1,2,128,256]{3,1,0,2:T(2,128)(2,1)S(1)} async-done(((bf16[1,2,128,256]{3,1,0,2:T(2,128)(2,1)}), bf16[1,2,128,256]{3,1,0,2:T(2,128)(2,1)S(1)}, u32[]{:S(2)}, u32[]{:S(2)}) %all-to-all-start) | async-done | bytes 131104 | tf_op jit(solution)/shard_map/all_to_all | solution.py:125
  87.8 1.2 copy.50
  89.0 0.9 convolution_dynamic-update-slice_fusion.4
  90.0 0.9 convolution_dynamic-update-slice_fusion.3
  90.9 0.9 convolution_dynamic-update-slice_fusion.2
  91.8 0.9 convolution_dynamic-update-slice_fusion.1
  92.7 0.9 convolution_dynamic-update-slice_fusion
  93.7 3.1 %copy.48 = f32[2304,256]{0,1:T(8,128)} copy(f32[2304,256]{1,0:T(8,128)} %convolution_dynamic-update-slice_fusion) | data formatting | bytes 4718592
  97.2 30.2 %all-reduce.4 = (f32[1,32]{1,0:T(1,128)S(1)}, f32[1,32]{1,0:T(1,128)S(1)}) all-reduce(f32[1,32]{1,0:T(1,128)S(1)} %bitcast.205, f32[1,32]{1,0:T(1,128)S(1)} %bitcast.207), channel_id=1, replica_groups=mesh['dp'=2,'wide'=16] {'wide'}, use_global_device_ids=true, to_apply=%region_11.12 | all-reduce | flops 64 | bytes 512 | tf_op jit(solution)/shard_map/psum | solution.py:148
  128.6 3.5 %all-to-all-start.1 = ((bf16[1,32,8,256]{3,2,0,1:T(8,128)(2,1)}), bf16[1,32,8,256]{3,2,0,1:T(8,128)(2,1)S(1)}, u32[]{:S(2)}, u32[]{:S(2)}) async-start(bf16[1,32,8,256]{3,2,0,1:T(8,128)(2,1)} %fusion.4), calls=%async_computation.1 | async-start | bytes 262144 | tf_op jit(solution)/shard_map/all_to_all | solution.py:128
  133.3 4.9 %psum.39 = f32[2,16]{1,0:T(2,128)S(1)} all-reduce(f32[2,16]{1,0:T(2,128)S(1)} %copy.53), channel_id=1, replica_groups=mesh['dp'=2,'wide'=16] {'dp'}, use_global_device_ids=true, to_apply=%region_19.20 | all-reduce | flops 32 | bytes 256 | tf_op jit(solution)/shard_map/psum | solution.py:172
  138.8 1.2 all-to-all-done.1
  140.1 43.6 %reduce-scatter.18.cloned.1.call-done = f32[16,768]{1,0:T(8,128)} async-done(((f32[256,768]{1,0:T(8,128)}), f32[16,768]{1,0:T(8,128)}) %reduce-scatter.18.cloned.1.call-update) | async-done | bytes 49168
  183.7 1.6 copy.51
  186.2 63.6 %reduce-scatter.16.cloned.1.call-done = f32[16,2304]{1,0:T(8,128)} async-done(((f32[256,2304]{1,0:T(8,128)}), f32[16,2304]{1,0:T(8,128)}) %reduce-scatter.16.cloned.1.call-update) | async-done | bytes 147472
  249.8 2.0 copy.49
  251.8 10.1 %reduce-scatter.14.cloned.1.call-done = bf16[384,16]{1,0:T(8,128)(2,1)} async-done(((bf16[768,16]{1,0:T(8,128)(2,1)}), bf16[384,16]{1,0:T(8,128)(2,1)}) %reduce-scatter.14.cloned.1.call-update) | async-done | bytes 12304 | tf_op jit(solution)/shard_map/reduce_scatter | solution.py:168
  261.9 0.9 convert_multiply_fusion.2
  263.5 15.8 %reduce-scatter.12.cloned.1.call-done = bf16[1152,16]{1,0:T(8,128)(2,1)} async-done(((bf16[2304,16]{1,0:T(8,128)(2,1)}), bf16[1152,16]{1,0:T(8,128)(2,1)}) %reduce-scatter.12.cloned.1.call-update) | async-done | bytes 36880 | tf_op jit(solution)/shard_map/reduce_scatter | solution.py:165
  279.3 1.0 convert_multiply_fusion
  (89 shorter events, 14.9 us)
Async XLA Ops:
  7.2 9.9 %copy-start.3 = (bf16[384,256]{1,0:T(8,128)(2,1)S(1)}, bf16[384,256]{1,0:T(8,128)(2,1)}, u32[]{:S(2)}) copy-start(bf16[384,256]{1,0:T(8,128)(2,1)} %param.11) | copy-start | bytes 589828
  8.9 16.1 %all-to-all-start.2 = ((bf16[1,2,128,256]{3,1,0,2:T(2,128)(2,1)}), bf16[1,2,128,256]{3,1,0,2:T(2,128)(2,1)S(1)}, u32[]{:S(2)}, u32[]{:S(2)}) async-start(bf16[1,2,128,256]{3,1,0,2:T(2,128)(2,1)} %bitcast.26), calls=%async_computation.2 | async-start | bytes 262144 | tf_op jit(solution)/shard_map/all_to_all | solution.py:131
  16.3 50.6 %all-gather.2.cloned.1.call-start = ((), (), s32[]{:S(2)}) async-start(), calls=%async_computation.9 | async-start | bytes 1769472 | tf_op jit(solution)/shard_map/all_gather | solution.py:97
  25.0 7.1 %copy-start.1 = (bf16[1,2,8,16,256]{4,3,2,1,0:T(8,128)(2,1)S(1)}, bf16[1,2,8,16,256]{4,3,2,1,0:T(8,128)(2,1)}, u32[]{:S(2)}) copy-start(bf16[1,2,8,16,256]{4,3,2,1,0:T(8,128)(2,1)} %param.6) | copy-start | bytes 393220
  26.3 40.5 %all-to-all-start.3 = ((bf16[1,32,8,256]{3,2,0,1:T(8,128)(2,1)}), bf16[1,32,8,256]{3,2,0,1:T(8,128)(2,1)S(1)}, u32[]{:S(2)}, u32[]{:S(2)}) async-start(bf16[1,32,8,256]{3,2,0,1:T(8,128)(2,1)} %fusion.3), calls=%async_computation.3 | async-start | bytes 262144 | tf_op jit(solution)/shard_map/all_to_all | solution.py:135
  32.1 100.5 %reduce-scatter.20.cloned.1.call-start = ((), (), s32[]{:S(2)}) async-start(), calls=%async_computation.14 | async-start | bytes 139264
  67.0 2.4 copy-start
  70.2 0.7 copy-start.4
  70.3 0.7 copy-start.5
  75.6 11.4 %all-to-all-start = ((bf16[1,2,128,256]{3,1,0,2:T(2,128)(2,1)}), bf16[1,2,128,256]{3,1,0,2:T(2,128)(2,1)S(1)}, u32[]{:S(2)}, u32[]{:S(2)}) async-start(bf16[1,2,128,256]{3,1,0,2:T(2,128)(2,1)} %copy.30), calls=%async_computation | async-start | bytes 262144 | tf_op jit(solution)/shard_map/all_to_all | solution.py:125
  79.1 104.6 %reduce-scatter.18.cloned.1.call-start = ((), (), s32[]{:S(2)}) async-start(), calls=%async_computation.13 | async-start | bytes 835584
  89.0 160.9 %reduce-scatter.16.cloned.1.call-start = ((), (), s32[]{:S(2)}) async-start(), calls=%async_computation.12 | async-start | bytes 2506752
  127.8 57.6 %copy-start.2 = (bf16[1,2,8,16,256]{4,3,2,1,0:T(8,128)(2,1)S(1)}, bf16[1,2,8,16,256]{4,3,2,1,0:T(8,128)(2,1)}, u32[]{:S(2)}) copy-start(bf16[1,2,8,16,256]{4,3,2,1,0:T(8,128)(2,1)} %param.7) | copy-start | bytes 393220
  128.6 11.4 %all-to-all-start.1 = ((bf16[1,32,8,256]{3,2,0,1:T(8,128)(2,1)}), bf16[1,32,8,256]{3,2,0,1:T(8,128)(2,1)S(1)}, u32[]{:S(2)}, u32[]{:S(2)}) async-start(bf16[1,32,8,256]{3,2,0,1:T(8,128)(2,1)} %fusion.4), calls=%async_computation.1 | async-start | bytes 262144 | tf_op jit(solution)/shard_map/all_to_all | solution.py:128
  132.1 129.8 %reduce-scatter.14.cloned.1.call-start = ((), (), s32[]{:S(2)}) async-start(), calls=%async_computation.11 | async-start | bytes 294912 | tf_op jit(solution)/shard_map/reduce_scatter | solution.py:168
  185.4 94.0 %reduce-scatter.12.cloned.1.call-start = ((), (), s32[]{:S(2)}) async-start(), calls=%async_computation.10 | async-start | bytes 884736 | tf_op jit(solution)/shard_map/reduce_scatter | solution.py:165
Sparse Core Ops, SparseCore 0:
  18.7 24.0 all-gather.1
  72.2 52.3 reduce-scatter.19
  128.1 55.5 reduce-scatter.17
  187.8 61.9 reduce-scatter.15
  251.9 9.9 reduce-scatter.13
  264.0 15.2 reduce-scatter.11
where the time goes:
time: 289 us; the launch traced here: 288 us
  waiting for transfers between devices  140 us (48%)
  blocking collectives  76.9 us (27%)
  starting transfers between devices  20.4 us (7%)
  matrix products  17.1 us (6%)
  local copies, waits for them, and re-layouts  14.7 us (5%)
  between operations  14.6 us (5%)
  other arithmetic  4.15 us (1%)
    unnamed x9, waiting for transfers between devices  108 us
    psum x1, blocking collectives, local(): total_sums, total_squares = lax.psum((group_sums, squares), 'wide')  33.9 us
    psum x1, blocking collectives, local(): mean_total, cross_total = lax.psum((mean_part, cross_part), 'wide')  30.2 us
    reduce_scatter x1, waiting for transfers between devices, local(): lax.psum_scatter(part_spatial.astype(jnp.bfloat16), 'dp', scatter_dimensi...  15.8 us
    unnamed x21, local copies, waits for them, and re-layouts  12.7 us
    reduce_scatter x1, waiting for transfers between devices, local(): lax.psum_scatter(part_temporal.astype(jnp.bfloat16), 'dp', scatter_dimens...  10.1 us
    dot_general x12, matrix products, contract(): lax.dot_general(left, right, (((0,), (0,)), ((), ())), preferred_element_...  9.04 us
    all_gather x1, blocking collectives, local(): lax.all_gather(w_temporal, 'dp', axis=0, tiled=True)  7.92 us
  transfers between devices with their start and end apart: 10, of which 6 were waited for; matrix products, arithmetic and copies ran while one was open for 10% of the time, Pallas kernels for 0%

commit v1 on v0

v1 whole, which is shorter than its diff:
```python
import functools
import math

import jax
import jax.numpy as jnp
from jax import lax
from jax.experimental import pallas as pl
from jax.experimental.pallas import tpu as pltpu
from jax.sharding import PartitionSpec as P

GROUPS = 32
EPSILON = 1e-05
F32 = jnp.float32
BF16 = jnp.bfloat16
VMEM = pl.BlockSpec(memory_space=pltpu.VMEM)
NT = (((1,), (1,)), ((), ()))
NN = (((1,), (0,)), ((), ()))


def call(body, out_shapes, scratch=(), flops=0, moved=0):
    many = isinstance(out_shapes, (tuple, list))

    def run(*operands):
        return pl.pallas_call(
            body,
            out_shape=out_shapes,
            in_specs=[VMEM] * len(operands),
            out_specs=[VMEM] * len(out_shapes) if many else VMEM,
            scratch_shapes=list(scratch),
            compiler_params=pltpu.CompilerParams(vmem_limit_bytes=40 * 1024 * 1024),
            cost_estimate=pl.CostEstimate(
                flops=flops, bytes_accessed=moved, transcendentals=0
            ),
        )(*operands)

    return run


def shape(dims, kind):
    return jax.ShapeDtypeStruct(dims, kind)


def mm(left, right, dims=NN):
    return lax.dot_general(left, right, dims, preferred_element_type=F32)


def group_total(rows, per_group):
    channels = rows.shape[-1]
    first = lax.broadcasted_iota(jnp.int32, (channels, channels), 0) // per_group
    second = lax.broadcasted_iota(jnp.int32, (channels, channels), 1) // per_group
    same = (first == second).astype(F32)
    return lax.dot_general(
        rows, same, NN, precision=lax.Precision.HIGHEST, preferred_element_type=F32
    )


def stats_body(lat_ref, out_ref):
    x = lat_ref[...].astype(F32)
    both = jnp.concatenate(
        [jnp.sum(x, axis=0, keepdims=True), jnp.sum(x * x, axis=0, keepdims=True)], axis=0
    )
    out_ref[...] = jnp.broadcast_to(both[None], out_ref.shape)


def whiten(lat, stats, count, per_group):
    total = group_total(jnp.sum(stats, axis=0), per_group) / count
    mean = total[0:1]
    inv_std = 1.0 / jnp.sqrt(total[1:2] - mean * mean + EPSILON)
    return (lat.astype(F32) - mean) * inv_std, inv_std


def store_shifted(pad_ref, values, frames, cells, cols):
    total = frames * cells
    column = lax.broadcasted_iota(jnp.int32, (total, 1), 0) % cols
    left = jnp.where(column == 0, 0.0, pltpu.roll(values, 1, 0))
    right = jnp.where(column == cols - 1, 0.0, pltpu.roll(values, total - 1, 0))
    edge = jnp.zeros((cols, values.shape[1]), BF16)
    for at, form in enumerate((left, values, right)):
        low = form.astype(BF16)
        for f in range(frames):
            pad_ref[at, f, 0:cols] = edge
            pad_ref[at, f, cols : cols + cells] = low[f * cells : (f + 1) * cells]
            pad_ref[at, f, cols + cells :] = edge


def window(pad_ref, dy, dx, frames, cells, cols):
    return jnp.concatenate(
        [pad_ref[dx, f, dy * cols : dy * cols + cells] for f in range(frames)], axis=0
    )


def main_body(
    sizes,
    lat_ref,
    cot_ref,
    halo_ref,
    stats_ref,
    gain_ref,
    bias_ref,
    ws_ref,
    wt_ref,
    *rest,
):
    D, W, frames, cells, cols, count, per_group, aligned = sizes
    pieces = rest[: 4 * (D - 1)]
    rest = rest[4 * (D - 1) :]
    spatial_ref, sums_ref, grad_ref, keep_ref, send_ref = rest[:5]
    full_ws, full_wt, act_pad, gsa_pad, gsa_t, cot_t = rest[5:]
    channels = lat_ref.shape[1]
    d = lax.axis_index("dp")
    core = lax.rem(lax.axis_index("wide"), 2)

    for shard_ref, full, offset in ((ws_ref, full_ws, 0), (wt_ref, full_wt, 1)):
        n = shard_ref.shape[0]
        full[pl.ds(pl.multiple_of(d * n, 16), n)] = shard_ref[...]
        for s in range(1, D):
            source = lax.rem(d + D - s, D)
            for which in range(2):
                piece = pieces[4 * (s - 1) + 2 * which + offset]
                half = n // 2
                holder = core if which == 0 else 1 - core
                start = pl.multiple_of(source * n + holder * half, 16)
                full[pl.ds(start, half)] = piece[...]

    cot = cot_ref[...]
    extended = jnp.concatenate([cot, halo_ref[...]], axis=0)
    rows = frames * cells
    gsa = jnp.zeros((rows, channels), F32)
    for k in range(3):
        gsa += mm(
            extended[k * cells : k * cells + rows],
            full_wt[k * channels : (k + 1) * channels],
            NT,
        )
    gsa = gsa.astype(BF16).astype(F32)
    store_shifted(gsa_pad, gsa, frames, cells, cols)

    white, _ = whiten(lat_ref[...], stats_ref[...], count, per_group)
    gain = gain_ref[...]
    normed = white * gain + bias_ref[...]
    sig = jax.nn.sigmoid(normed)
    act = (normed * sig).astype(BF16).astype(F32)
    store_shifted(act_pad, act, frames, cells, cols)

    gsa_t[...] = gsa.T.astype(BF16)
    for f in range(frames + 2):
        cot_t[:, f * cells : (f + 1) * cells] = (
            extended[f * cells : (f + 1) * cells].astype(F32).T.astype(BF16)
        )
    if aligned:
        step = channels // W
        order = [pl.ds(pl.multiple_of((2 * j + core) * step, 16), step) for j in range(W // 2)]
        order += [
            pl.ds(pl.multiple_of((2 * j + 1 - core) * step, 16), step) for j in range(W // 2)
        ]
        left_s = jnp.concatenate([gsa_t[at] for at in order], axis=0)
        left_t = jnp.concatenate([cot_t[at] for at in order], axis=0)
    else:
        left_s, left_t = gsa_t[...], cot_t[...]

    def put(block, column, shard, offset):
        if not aligned:
            keep_ref[:, offset + column : offset + column + channels] = block.astype(BF16)
            return
        low = block.astype(BF16)
        half = channels // 2
        for at in range(0, channels, 128):
            owner, place = (column + at) // shard, (column + at) % shard + offset
            keep_ref[owner, :, place : place + 128] = low[:half, at : at + 128]
            send_ref[owner, :, place : place + 128] = low[half:, at : at + 128]

    shard_s, shard_t = ws_ref.shape[0], wt_ref.shape[0]
    out = jnp.zeros((rows, channels), F32)
    for dy in range(3):
        for dx in range(3):
            tap = 3 * dy + dx
            seen = window(act_pad, dy, dx, frames, cells, cols)
            out += mm(seen, full_ws[tap * channels : (tap + 1) * channels])
            put(mm(left_s, seen), tap * channels, shard_s, 0)
    spatial = out.astype(BF16)
    spatial_ref[...] = spatial
    for k in range(3):
        put(
            mm(left_t[:, k * cells : k * cells + rows], spatial),
            k * channels,
            shard_t,
            shard_s if aligned else shard_s * D,
        )

    grad = jnp.zeros((rows, channels), F32)
    for dy in range(3):
        for dx in range(3):
            tap = 3 * dy + dx
            seen = window(gsa_pad, 2 - dy, 2 - dx, frames, cells, cols)
            grad += mm(seen, full_ws[tap * channels : (tap + 1) * channels], NT)
    grad = grad * (sig * (1.0 + normed * (1.0 - sig)))
    grad_ref[...] = grad
    both = jnp.concatenate(
        [
            jnp.sum(grad * white, axis=0, keepdims=True),
            jnp.sum(grad, axis=0, keepdims=True),
        ],
        axis=0,
    )
    sums_ref[...] = jnp.broadcast_to(both[None], sums_ref.shape)


def finish_body(
    sizes,
    lat_ref,
    cot_ref,
    stats_ref,
    gain_ref,
    grad_ref,
    sums_ref,
    spatial_ref,
    before_ref,
    wt_ref,
    *rest,
):
    D, W, frames, cells, cols, count, per_group, aligned = sizes
    pieces = rest[: 2 * (D - 1)]
    block_ref, glat_ref, norm_ref, full_wt = rest[2 * (D - 1) :]
    channels = lat_ref.shape[1]
    d = lax.axis_index("dp")
    core = lax.rem(lax.axis_index("wide"), 2)
    n = wt_ref.shape[0]
    full_wt[pl.ds(pl.multiple_of(d * n, 16), n)] = wt_ref[...]
    for s in range(1, D):
        source = lax.rem(d + D - s, D)
        for which in range(2):
            holder = core if which == 0 else 1 - core
            start = pl.multiple_of(source * n + holder * (n // 2), 16)
            full_wt[pl.ds(start, n // 2)] = pieces[2 * (s - 1) + which][...]
    extended = jnp.concatenate([before_ref[...], spatial_ref[...]], axis=0)
    rows = frames * cells
    temporal = jnp.zeros((rows, channels), F32)
    for k in range(3):
        start = (2 - k) * cells
        temporal += mm(
            extended[start : start + rows], full_wt[k * channels : (k + 1) * channels]
        )
    lat = lat_ref[...]
    block_ref[...] = (lat.astype(F32) + temporal).astype(BF16)

    white, inv_std = whiten(lat, stats_ref[...], count, per_group)
    gain = gain_ref[...]
    total = jnp.sum(sums_ref[...], axis=0)
    norm_ref[...] = total
    means = group_total(total * gain, per_group) / count
    inner = inv_std * (grad_ref[...] * gain - means[1:2] - white * means[0:1])
    glat_ref[...] = (cot_ref[...].astype(F32) + inner).astype(BF16)


def plane_body(sizes, keep_ref, got_ref, *outs):
    D = sizes[0]
    d = lax.axis_index("dp")
    y = lax.rem(lax.axis_index("wide") // 2, 2)
    at = 0
    for a in range(D):
        for b in range(2):
            owner, side = lax.rem(d + a, D), lax.rem(y + b, 2)
            outs[at][...] = (
                keep_ref[owner, :, side].astype(F32) + got_ref[owner, :, side].astype(F32)
            ).astype(BF16)
            at += 1


def line_body(depth, *refs):
    outs = refs[-depth:]
    z = lax.axis_index("wide") // 4
    for s in range(depth):
        owner = lax.rem(z + s, depth)
        total = refs[0][owner].astype(F32)
        for term in refs[1:-depth]:
            total += term[owner].astype(F32)
        outs[s][...] = total.astype(BF16)


def last_body(scale, split, terms, *refs):
    spatial_ref, temporal_ref, norm_ref = refs[-3:]
    total = refs[0][...].astype(F32)
    for term in refs[1:terms]:
        total += term[...].astype(F32)
    total = total * scale
    spatial_ref[...] = total[:, :split]
    temporal_ref[...] = total[:, split:]
    norm_columns(scale, refs[terms:-3], norm_ref)


def norm_columns(scale, terms, norm_ref):
    norm = terms[0][...]
    for term in terms[1:]:
        norm += term[...]
    channels, width = norm.shape[1], norm_ref.shape[1]
    row = lax.broadcasted_iota(jnp.int32, (channels, width), 0)
    column = lax.broadcasted_iota(jnp.int32, (channels, width), 1)
    pick = (row == column + lax.axis_index("wide") * width).astype(F32)
    norm_ref[...] = (
        lax.dot_general(
            norm, pick, NN, precision=lax.Precision.HIGHEST, preferred_element_type=F32
        )
        * scale
    )


def only_norm_body(scale, *refs):
    norm_columns(scale, refs[:-1], refs[-1])


def local(latents, cotangent, norm_gain, norm_bias, w_spatial, w_temporal):
    D, W = lax.axis_size("dp"), lax.axis_size("wide")
    _, frames, rows_here, cols, channels = latents.shape
    cells = rows_here * cols
    rows = frames * cells
    per_group = channels // GROUPS
    count = W * frames * cells * per_group
    shard_s, shard_t = w_spatial.shape[0], w_temporal.shape[0]
    aligned = (channels // W) % 16 == 0 and shard_s % 128 == 0 and shard_t % 128 == 0
    aligned = aligned and W % 4 == 0
    sizes = (D, W, frames, cells, cols, count, per_group, aligned)
    scale = 1.0 / math.sqrt(D * W * frames * cells)

    lat, cot = latents.reshape(rows, channels), cotangent.reshape(rows, channels)
    gain, bias = norm_gain.reshape(1, channels), norm_bias.reshape(1, channels)

    def over_all(moves):
        pairs = []
        for d in range(D):
            for w in range(W):
                to = moves(d, w)
                pairs.append((d * W + w, to[0] * W + to[1]))
        return pairs

    def send(value, moves):
        return lax.ppermute(value, ("dp", "wide"), over_all(moves))

    stats = call(stats_body, shape((W, 2, channels), F32))(lat)
    stats = lax.all_to_all(stats, "wide", split_axis=0, concat_axis=0, tiled=True)

    halo = lax.ppermute(cot, "wide", [(w + 1, w) for w in range(W - 1)])
    core = lax.rem(lax.axis_index("wide"), 2)
    half_s = lax.dynamic_slice_in_dim(w_spatial, core * (shard_s // 2), shard_s // 2, 0)
    half_t = lax.dynamic_slice_in_dim(w_temporal, core * (shard_t // 2), shard_t // 2, 0)
    pieces, pieces_t = [], []
    for s in range(1, D):
        here_t = send(half_t, lambda d, w: ((d + s) % D, w))
        here_s = send(half_s, lambda d, w: ((d + s) % D, w))
        there_t = send(here_t, lambda d, w: (d, w ^ 1))
        there_s = send(here_s, lambda d, w: (d, w ^ 1))
        pieces += [here_s, here_t, there_s, there_t]
        pieces_t += [here_t, there_t]

    R = shard_s + shard_t
    if aligned:
        grads = [shape((D, channels // 2, R), BF16)] * 2
    else:
        grads = [shape((channels, D * R), BF16), shape((8, 128), BF16)]
    spatial, sums, grad, keep, away = call(
        functools.partial(main_body, sizes),
        [
            shape((rows, channels), BF16),
            shape((W, 2, channels), F32),
            shape((rows, channels), F32),
        ]
        + grads,
        [
            pltpu.VMEM((D * shard_s, channels), BF16),
            pltpu.VMEM((D * shard_t, channels), BF16),
            pltpu.VMEM((3, frames, cells + 2 * cols, channels), BF16),
            pltpu.VMEM((3, frames, cells + 2 * cols, channels), BF16),
            pltpu.VMEM((channels, rows), BF16),
            pltpu.VMEM((channels, rows + 2 * cells), BF16),
        ],
        flops=2 * 33 * rows * channels * channels,
        moved=5_000_000,
    )(lat, cot, halo, stats, gain, bias, w_spatial, w_temporal, *pieces)

    sums = lax.all_to_all(sums, "wide", split_axis=0, concat_axis=0, tiled=True)
    before = lax.ppermute(spatial, "wide", [(w, w + 1) for w in range(W - 1)])

    def finish():
        return call(
            functools.partial(finish_body, sizes),
            [
                shape((rows, channels), BF16),
                shape((rows, channels), BF16),
                shape((2, channels), F32),
            ],
            [pltpu.VMEM((D * shard_t, channels), BF16)],
            flops=2 * 3 * rows * channels * channels,
            moved=2_000_000,
        )(lat, cot, stats, gain, grad, sums, spatial, before, w_temporal, *pieces_t)

    width = channels // W
    if aligned:
        Z = W // 4
        got = send(away, lambda d, w: (d, w ^ 1))
        view = (D, Z, 2, width, R)
        plane = call(
            functools.partial(plane_body, sizes),
            [shape((Z, width, R), BF16)] * (2 * D),
            moved=5_000_000,
        )(keep.reshape(view), got.reshape(view))
        terms, at = [plane[0]], 0
        for a in range(D):
            for b in range(2):
                if at > 0:
                    terms.append(
                        send(plane[at], lambda d, w: ((d + a) % D, w ^ (2 * b)))
                    )
                at += 1
        block_out, grad_latents, norm = finish()
        norms = [norm] + [send(norm, lambda d, w: ((d + s) % D, w)) for s in range(1, D)]
        line = call(
            functools.partial(line_body, Z),
            [shape((width, R), BF16)] * Z,
            moved=1_000_000,
        )(*terms)
        terms = [line[0]]
        for s in range(1, Z):
            terms.append(send(line[s], lambda d, w: (d, (w + 4 * s) % W)))
        grad_s, grad_t, norm = call(
            functools.partial(last_body, scale, shard_s, len(terms)),
            [
                shape((width, shard_s), F32),
                shape((width, shard_t), F32),
                shape((2, width), F32),
            ],
        )(*terms, *norms)
        grad_s, grad_t = grad_s.T, grad_t.T
    else:
        block_out, grad_latents, norm = finish()
        norms = [norm] + [send(norm, lambda d, w: ((d + s) % D, w)) for s in range(1, D)]
        norm = call(functools.partial(only_norm_body, scale), shape((2, width), F32))(*norms)
        part = lax.psum_scatter(keep.astype(F32), "wide", scatter_dimension=0, tiled=True)
        part = part.T.astype(BF16)
        grad_s, grad_t = (
            lax.psum_scatter(term, "dp", scatter_dimension=0, tiled=True).astype(F32) * scale
            for term in (part[: D * shard_s], part[D * shard_s :])
        )
    return (
        block_out.reshape(latents.shape),
        grad_latents.reshape(latents.shape),
        grad_s,
        grad_t,
        norm,
    )


def solution(mesh):
    return jax.shard_map(
        local,
        mesh=mesh,
        in_specs=(
            P("dp", "wide", None, None, None),
            P("dp", "wide", None, None, None),
            P(),
            P(),
            P("dp", None),
            P("dp", None),
        ),
        out_specs=(
            P("dp", "wide", None, None, None),
            P("dp", "wide", None, None, None),
            P("dp", "wide"),
            P("dp", "wide"),
            P(None, "wide"),
        ),
        check_vma=False,
    )
```

time: 289 us -> 60.2 us (0.21)
  waiting for transfers between devices: 140 us -> 17.5 us
  blocking collectives: 76.9 us -> 12.7 us
  matrix products: 17.1 us -> 0 us
  between operations: 14.6 us -> 0.77 us
  local copies, waits for them, and re-layouts: 14.7 us -> 2.79 us
  Pallas kernels: 0 us -> 5.24 us
  other arithmetic: 4.15 us -> 0 us
    unnamed x9 -> x0, waiting for transfers between devices: 108 us -> none
    psum x3 -> x0, blocking collectives: 69 us -> none  [the longest x1 33.9 us: local(): total_sums, total_squares = lax.psum((group_sums, squares), 'wide')]
    reduce_scatter x2 -> x0, waiting for transfers between devices: 25.9 us -> none  [the longest x1 15.8 us: local(): lax.psum_scatter(part_spatial.astype(jnp.bfloat16), 'dp', scatter_dimensi...]
    ppermute x0 -> x14, waiting for transfers between devices: none -> 17.5 us  [the longest x12 17.5 us: send(): return lax.ppermute(value, ('dp', 'wide'), over_all(moves))]
    ppermute x0 -> x14, starting transfers between devices: none -> 17.2 us  [the longest x12 14.6 us: send(): return lax.ppermute(value, ('dp', 'wide'), over_all(moves))]
    dot_general x36 -> x0, matrix products: 17.1 us -> none  [the longest x12 9.04 us: contract(): lax.dot_general(left, right, (((0,), (0,)), ((), ())), preferred_element_...]
    all_to_all x4 -> x1, starting transfers between devices: 20.1 us -> 3.66 us  [local(): sums = lax.all_to_all(sums, 'wide', split_axis=0, concat_axis=0, tiled=True)]
    all_to_all x0 -> x1, blocking collectives: none -> 12.7 us  [local(): lax.all_to_all(stats, 'wide', split_axis=0, concat_axis=0, tiled=True)]
  transfers between devices with their start and end apart: 10 -> 15, of which waited for: 6 -> 5; matrix products, arithmetic and copies ran while one was open for 10% -> 0% of each run, Pallas kernels for 0% -> 2%
where the time goes in v1:
time: 60.2 us; the launch traced here: 59.9 us
  starting transfers between devices  20.9 us (35%)
  waiting for transfers between devices  17.5 us (29%)
  blocking collectives  12.7 us (21%)
  Pallas kernels  5.24 us (9%)
  local copies, waits for them, and re-layouts  2.79 us (5%)
  between operations  0.77 us (1%)
    ppermute x12, waiting for transfers between devices, send(): return lax.ppermute(value, ('dp', 'wide'), over_all(moves))  17.5 us
    ppermute x12, starting transfers between devices, send(): return lax.ppermute(value, ('dp', 'wide'), over_all(moves))  14.6 us
    all_to_all x1, blocking collectives, local(): lax.all_to_all(stats, 'wide', split_axis=0, concat_axis=0, tiled=True)  12.7 us
    pallas_call x6, Pallas kernels, run(): pl.pallas_call(body, out_shape=out_shapes, in_specs=[VMEM] * len(operands...  5.24 us
    all_to_all x1, starting transfers between devices, local(): sums = lax.all_to_all(sums, 'wide', split_axis=0, concat_axis=0, tiled=True)  3.66 us
    unnamed x12, local copies, waits for them, and re-layouts  1.75 us
    ppermute x1, starting transfers between devices, local(): before = lax.ppermute(spatial, 'wide', [(w, w + 1) for w in range(W - 1)])  1.29 us
    ppermute x1, starting transfers between devices, local(): halo = lax.ppermute(cot, 'wide', [(w + 1, w) for w in range(W - 1)])  1.28 us
  transfers between devices with their start and end apart: 15, of which 5 were waited for; matrix products, arithmetic and copies ran while one was open for 0% of the time, Pallas kernels for 2%

profile of v1, /device:TPU:0, one launch (start us, length us, event | category | flops | bytes accessed | tf_op | source)
XLA Modules:
  0.0 59.9 jit_solution(17376727087492739452)
XLA Ops:
  0.7 1.0 %constant_dynamic-slice_fusion.1 = bf16[576,256]{1,0:T(8,128)(2,1)S(1)} fusion(bf16[1152,256]{1,0:T(8,128)(2,1)} %ws_ref.1, s32[]{:T(128)S(6)} %select_n.6), kind=kLoop, calls=%fused_computation.1 | loop fusion | bytes 589828 | tf_op jit(solution)/shard_map/dynamic_slice | solution.py:343
  1.7 0.0 copy-start
  1.7 3.0 %collective-permute-start.1 = (bf16[576,256]{1,0:T(8,128)(2,1)S(1)}, bf16[576,256]{1,0:T(8,128)(2,1)S(1)}, u32[]{:S(2)}, u32[]{:S(2)}) collective-permute-start(bf16[576,256]{1,0:T(8,128)(2,1)S(1)} %constant_dynamic-slice_fusion.1), channel_id=1, source_target_pairs={{0,16},{1,17},{2,18},{3,19},{4,20},{5,21},{6,22},{7,23},{8,24},{9,... | collective-permute-start | bytes 884744 | tf_op jit(solution)/shard_map/ppermute | solution.py:336
  4.7 7.0 %collective-permute-done.1.rest_0_ = bf16[576,256]{1,0:T(8,128)(2,1)S(1)} collective-permute-done((bf16[576,256]{1,0:T(8,128)(2,1)S(1)}, bf16[576,256]{1,0:T(8,128)(2,1)S(1)}, u32[]{:S(2)}, u32[]{:S(2)}) %collective-permute-start.1) | collective-permute-done | bytes 294944 | tf_op jit(solution)/shard_map/ppermute | solution.py:336
  11.7 0.0 collective-permute-start.3
  11.7 1.8 %collective-permute-start.2 = (bf16[192,256]{1,0:T(8,128)(2,1)S(1)}, bf16[192,256]{1,0:T(8,128)(2,1)S(1)}, u32[]{:S(2)}, u32[]{:S(2)}) collective-permute-start(bf16[192,256]{1,0:T(8,128)(2,1)S(1)} %constant_dynamic-slice_fusion), channel_id=1, source_target_pairs={{0,16},{1,17},{2,18},{3,19},{4,20},{5,21},{6,22},{7,23},{8,24},{9,... | collective-permute-start | bytes 294920 | tf_op jit(solution)/shard_map/ppermute | solution.py:336
  13.5 1.3 %collective-permute-start = (bf16[256,256]{1,0:T(8,128)(2,1)S(1)}, bf16[256,256]{1,0:T(8,128)(2,1)S(1)}, u32[]{:S(2)}, u32[]{:S(2)}) collective-permute-start(bf16[256,256]{1,0:T(8,128)(2,1)S(1)} %bitcast.15), channel_id=1, source_target_pairs={{1,0},{2,1},{3,2},{4,3},{5,4},{6,5},{7,6},{8,7},{9,8},{10,9},{11,1... | collective-permute-start | bytes 393224 | tf_op jit(solution)/shard_map/ppermute | solution.py:341
  14.8 2.2 %collective-permute-done.2.rest_1_.rest_0_ = bf16[192,256]{1,0:T(8,128)(2,1)S(1)} collective-permute-done((bf16[192,256]{1,0:T(8,128)(2,1)S(1)}, bf16[192,256]{1,0:T(8,128)(2,1)S(1)}, u32[]{:S(2)}, u32[]{:S(2)}) %collective-permute-start.2) | collective-permute-done | bytes 98336 | tf_op jit(solution)/shard_map/ppermute | solution.py:336
  17.0 0.0 collective-permute-start.4
  17.0 0.1 shard_map.101
  17.1 0.0 copy-start.5
  17.1 12.7 %all_to_all.10.stats_ref = f32[16,2,256]{2,1,0:T(2,128)S(1)} all-to-all(f32[16,2,256]{2,1,0:T(2,128)S(1)} %shard_map.101), channel_id=1, replica_groups=mesh['dp'=2,'wide'=16] {'wide'}, dimensions={0} | all-to-all | bytes 65536 | tf_op jit(solution)/shard_map/all_to_all | solution.py:339
  29.8 0.0 copy-start.4
  29.9 0.7 %copy-done.4 = f32[256]{0:T(256)S(1)} copy-done((f32[256]{0:T(256)S(1)}, f32[256]{0:T(256)}, u32[]{:S(2)}) %copy-start.4) | copy-done | bytes 1048
  30.5 1.1 %copy-done.2 = bf16[1152,256]{1,0:T(8,128)(2,1)S(1)} copy-done((bf16[1152,256]{1,0:T(8,128)(2,1)S(1)}, bf16[1152,256]{1,0:T(8,128)(2,1)}, u32[]{:S(2)}) %copy-start.2) | copy-done | bytes 589848
  31.6 2.9 %shard_map.102 = (bf16[256,256]{1,0:T(8,128)(2,1)S(1)}, f32[16,2,256]{2,1,0:T(2,128)}, f32[256,256]{1,0:T(8,128)S(1)}, bf16[2,128,1536]{2,1,0:T(8,128)(2,1)S(1)}, bf16[2,128,1536]{2,1,0:T(8,128)(2,1)S(1)}) custom-call(bf16[256,256]{1,0:T(8,128)(2,1)S(1)} %bitcast.13, bf16[256,256]{1,0:T(8,128)(2,1)S(1)} %bitcast.16, ...), custom_call_target="tpu_custom_call" | custom-call | flops 1107296256 | bytes 5000000 | tf_op jit(solution)/shard_map/pallas_call | solution.py:24
  34.5 2.3 %collective-permute-done.6 = bf16[2,128,1536]{2,1,0:T(8,128)(2,1)S(1)} collective-permute-done((bf16[2,128,1536]{2,1,0:T(8,128)(2,1)S(1)}, bf16[2,128,1536]{2,1,0:T(8,128)(2,1)S(1)}, u32[]{:S(2)}, u32[]{:S(2)}) %collective-permute-start.6) | collective-permute-done | bytes 786464 | tf_op jit(solution)/shard_map/ppermute | solution.py:336
  36.8 0.2 shard_map.104
  36.9 0.4 collective-permute-start.7
  37.3 1.5 %collective-permute-start.8 = (bf16[4,16,1536]{2,1,0:T(8,128)(2,1)S(1)}, bf16[4,16,1536]{2,1,0:T(8,128)(2,1)S(1)}, u32[]{:S(2)}, u32[]{:S(2)}) collective-permute-start(bf16[4,16,1536]{2,1,0:T(8,128)(2,1)S(1)} %get-tuple-element.33), channel_id=1, source_target_pairs={{0,16},{1,17},{2,18},{3,19},{4,20},{5,21},{6,22},{7,23},{8,24},{9,... | collective-permute-start | bytes 589832 | tf_op jit(solution)/shard_map/ppermute | solution.py:336
  38.8 1.7 %collective-permute-start.9 = (bf16[4,16,1536]{2,1,0:T(8,128)(2,1)S(1)}, bf16[4,16,1536]{2,1,0:T(8,128)(2,1)S(1)}, u32[]{:S(2)}, u32[]{:S(2)}) collective-permute-start(bf16[4,16,1536]{2,1,0:T(8,128)(2,1)S(1)} %get-tuple-element.34), channel_id=1, source_target_pairs={{0,18},{1,19},{2,16},{3,17},{4,22},{5,23},{6,20},{7,21},{8,26},{9,... | collective-permute-start | bytes 589832 | tf_op jit(solution)/shard_map/ppermute | solution.py:336
  40.5 1.3 %collective-permute-start.5 = (bf16[256,256]{1,0:T(8,128)(2,1)S(1)}, bf16[256,256]{1,0:T(8,128)(2,1)S(1)}, u32[]{:S(2)}, u32[]{:S(2)}) collective-permute-start(bf16[256,256]{1,0:T(8,128)(2,1)S(1)} %get-tuple-element.26.spatial_ref), channel_id=1, source_target_pairs={{0,1},{1,2},{2,3},{3,4},{4,5},{5,6},{6,7},{7,8},{8,9},{9,10},{10,1... | collective-permute-start | bytes 393224 | tf_op jit(solution)/shard_map/ppermute | solution.py:380
  41.8 3.7 %all-to-all-start.1 = ((f32[16,2,256]{2,1,0:T(2,128)}), f32[16,2,256]{2,1,0:T(2,128)S(1)}, u32[]{:S(2)}, u32[]{:S(2)}) async-start(f32[16,2,256]{2,1,0:T(2,128)} %get-tuple-element.25), calls=%async_computation.1 | async-start | bytes 65536 | tf_op jit(solution)/shard_map/all_to_all | solution.py:379
  45.5 3.9 %collective-permute-done.9.refs_3_ = bf16[4,16,1536]{2,1,0:T(8,128)(2,1)S(1)} collective-permute-done((bf16[4,16,1536]{2,1,0:T(8,128)(2,1)S(1)}, bf16[4,16,1536]{2,1,0:T(8,128)(2,1)S(1)}, u32[]{:S(2)}, u32[]{:S(2)}) %collective-permute-start.9) | collective-permute-done | bytes 196640 | tf_op jit(solution)/shard_map/ppermute | solution.py:336
  49.4 0.1 shard_map.105
  49.5 1.9 %collective-permute-start.10 = (bf16[16,1536]{1,0:T(8,128)(2,1)S(1)}, bf16[16,1536]{1,0:T(8,128)(2,1)S(1)}, u32[]{:S(2)}, u32[]{:S(2)}) collective-permute-start(bf16[16,1536]{1,0:T(8,128)(2,1)S(1)} %get-tuple-element.36), channel_id=1, source_target_pairs={{0,4},{1,5},{2,6},{3,7},{4,8},{5,9},{6,10},{7,11},{8,12},{9,13},{1... | collective-permute-start | bytes 147464 | tf_op jit(solution)/shard_map/ppermute | solution.py:336
  51.4 0.5 collective-permute-start.11
  51.9 2.3 %collective-permute-start.12 = (bf16[16,1536]{1,0:T(8,128)(2,1)S(1)}, bf16[16,1536]{1,0:T(8,128)(2,1)S(1)}, u32[]{:S(2)}, u32[]{:S(2)}) collective-permute-start(bf16[16,1536]{1,0:T(8,128)(2,1)S(1)} %get-tuple-element.38), channel_id=1, source_target_pairs={{0,12},{1,13},{2,14},{3,15},{4,0},{5,1},{6,2},{7,3},{8,4},{9,5},{1... | collective-permute-start | bytes 147464 | tf_op jit(solution)/shard_map/ppermute | solution.py:336
  54.3 1.3 %shard_map.103 = (bf16[256,256]{1,0:T(8,128)(2,1)}, bf16[256,256]{1,0:T(8,128)(2,1)}, f32[2,256]{1,0:T(2,128)S(1)}) custom-call(bf16[256,256]{1,0:T(8,128)(2,1)S(1)} %bitcast.14, bf16[256,256]{1,0:T(8,128)(2,1)S(1)} %bitcast.17, f32[16,2,256]{2,1,0:T(2,128)S(1)} %all_to_all.10.stats_ref, f32[1,256]{1,0:T(1,128)S(1)} %bitcast.19, ...), custom_call_target="tpu_custom_call" | custom-call | flops 100663296 | bytes 2000000 | tf_op jit(solution)/shard_map/pallas_call | solution.py:24
  55.5 1.5 %collective-permute-start.13 = (f32[2,256]{1,0:T(2,128)S(1)}, f32[2,256]{1,0:T(2,128)S(1)}, u32[]{:S(2)}, u32[]{:S(2)}) collective-permute-start(f32[2,256]{1,0:T(2,128)S(1)} %get-tuple-element.39.refs_4_), channel_id=1, source_target_pairs={{0,16},{1,17},{2,18},{3,19},{4,20},{5,21},{6,22},{7,23},{8,24},{9,... | collective-permute-start | bytes 6152 | tf_op jit(solution)/shard_map/ppermute | solution.py:336
  57.0 2.1 %collective-permute-done.13.refs_5_ = f32[2,256]{1,0:T(2,128)S(1)} collective-permute-done((f32[2,256]{1,0:T(2,128)S(1)}, f32[2,256]{1,0:T(2,128)S(1)}, u32[]{:S(2)}, u32[]{:S(2)}) %collective-permute-start.13) | collective-permute-done | bytes 2080 | tf_op jit(solution)/shard_map/ppermute | solution.py:336
  59.1 0.8 %shard_map.106 = (f32[16,1152]{1,0:T(8,128)}, f32[16,384]{1,0:T(8,128)}, f32[2,16]{1,0:T(2,128)}) custom-call(bf16[16,1536]{1,0:T(8,128)(2,1)S(1)} %get-tuple-element.35.refs_0_, bf16[16,1536]{1,0:T(8,128)(2,1)S(1)} %collective-permute-done.10.refs_1_, bf16[16,1536]{1,0:T(8,128)(2,1)S(1)} %collective-permute-done.11.refs_2_, ...), custom_call_target="tpu_custom_call" | custom-call | tf_op jit(solution)/shard_map/pallas_call | solution.py:24
  (19 shorter events, 0.1 us)
Async XLA Ops:
  0.6 11.1 %copy-start.1 = (bf16[384,256]{1,0:T(8,128)(2,1)S(1)}, bf16[384,256]{1,0:T(8,128)(2,1)}, u32[]{:S(2)}) copy-start(bf16[384,256]{1,0:T(8,128)(2,1)} %wt_ref.3) | copy-start | bytes 589828
  0.7 12.9 %copy-start.3 = (bf16[1,2,8,16,256]{4,3,2,1,0:T(8,128)(2,1)S(1)}, bf16[1,2,8,16,256]{4,3,2,1,0:T(8,128)(2,1)}, u32[]{:S(2)}) copy-start(bf16[1,2,8,16,256]{4,3,2,1,0:T(8,128)(2,1)} %param.7) | copy-start | bytes 393220
  1.7 15.3 %copy-start = (bf16[1,2,8,16,256]{4,3,2,1,0:T(8,128)(2,1)S(1)}, bf16[1,2,8,16,256]{4,3,2,1,0:T(8,128)(2,1)}, u32[]{:S(2)}) copy-start(bf16[1,2,8,16,256]{4,3,2,1,0:T(8,128)(2,1)} %param.6) | copy-start | bytes 393220
  1.7 10.0 %collective-permute-start.1 = (bf16[576,256]{1,0:T(8,128)(2,1)S(1)}, bf16[576,256]{1,0:T(8,128)(2,1)S(1)}, u32[]{:S(2)}, u32[]{:S(2)}) collective-permute-start(bf16[576,256]{1,0:T(8,128)(2,1)S(1)} %constant_dynamic-slice_fusion.1), channel_id=1, source_target_pairs={{0,16},{1,17},{2,18},{3,19},{4,20},{5,21},{6,22},{7,23},{8,24},{9,... | collective-permute-start | bytes 884744 | tf_op jit(solution)/shard_map/ppermute | solution.py:336
  11.7 18.1 %collective-permute-start.3 = (bf16[576,256]{1,0:T(8,128)(2,1)S(1)}, bf16[576,256]{1,0:T(8,128)(2,1)S(1)}, u32[]{:S(2)}, u32[]{:S(2)}) collective-permute-start(bf16[576,256]{1,0:T(8,128)(2,1)S(1)} %collective-permute-done.1.rest_0_), channel_id=1, source_target_pairs={{0,1},{1,0},{2,3},{3,2},{4,5},{5,4},{6,7},{7,6},{8,9},{9,8},{10,11... | collective-permute-start | bytes 884744 | tf_op jit(solution)/shard_map/ppermute | solution.py:336
  11.7 5.3 %collective-permute-start.2 = (bf16[192,256]{1,0:T(8,128)(2,1)S(1)}, bf16[192,256]{1,0:T(8,128)(2,1)S(1)}, u32[]{:S(2)}, u32[]{:S(2)}) collective-permute-start(bf16[192,256]{1,0:T(8,128)(2,1)S(1)} %constant_dynamic-slice_fusion), channel_id=1, source_target_pairs={{0,16},{1,17},{2,18},{3,19},{4,20},{5,21},{6,22},{7,23},{8,24},{9,... | collective-permute-start | bytes 294920 | tf_op jit(solution)/shard_map/ppermute | solution.py:336
  13.5 16.3 %collective-permute-start = (bf16[256,256]{1,0:T(8,128)(2,1)S(1)}, bf16[256,256]{1,0:T(8,128)(2,1)S(1)}, u32[]{:S(2)}, u32[]{:S(2)}) collective-permute-start(bf16[256,256]{1,0:T(8,128)(2,1)S(1)} %bitcast.15), channel_id=1, source_target_pairs={{1,0},{2,1},{3,2},{4,3},{5,4},{6,5},{7,6},{8,7},{9,8},{10,9},{11,1... | collective-permute-start | bytes 393224 | tf_op jit(solution)/shard_map/ppermute | solution.py:341
  17.0 12.8 %collective-permute-start.4 = (bf16[192,256]{1,0:T(8,128)(2,1)S(1)}, bf16[192,256]{1,0:T(8,128)(2,1)S(1)}, u32[]{:S(2)}, u32[]{:S(2)}) collective-permute-start(bf16[192,256]{1,0:T(8,128)(2,1)S(1)} %collective-permute-done.2.rest_1_.rest_0_), channel_id=1, source_target_pairs={{0,1},{1,0},{2,3},{3,2},{4,5},{5,4},{6,7},{7,6},{8,9},{9,8},{10,11... | collective-permute-start | bytes 294920 | tf_op jit(solution)/shard_map/ppermute | solution.py:336
  17.1 12.8 %copy-start.5 = (f32[256]{0:T(256)S(1)}, f32[256]{0:T(256)}, u32[]{:S(2)}) copy-start(f32[256]{0:T(256)} %param.9) | copy-start | bytes 3076
  29.8 0.7 %copy-start.4 = (f32[256]{0:T(256)S(1)}, f32[256]{0:T(256)}, u32[]{:S(2)}) copy-start(f32[256]{0:T(256)} %param.8) | copy-start | bytes 3076
  30.5 1.1 %copy-start.2 = (bf16[1152,256]{1,0:T(8,128)(2,1)S(1)}, bf16[1152,256]{1,0:T(8,128)(2,1)}, u32[]{:S(2)}) copy-start(bf16[1152,256]{1,0:T(8,128)(2,1)} %ws_ref.1) | copy-start | bytes 1769476
  34.5 2.3 %collective-permute-start.6 = (bf16[2,128,1536]{2,1,0:T(8,128)(2,1)S(1)}, bf16[2,128,1536]{2,1,0:T(8,128)(2,1)S(1)}, u32[]{:S(2)}, u32[]{:S(2)}) collective-permute-start(bf16[2,128,1536]{2,1,0:T(8,128)(2,1)S(1)} %get-tuple-element.30), channel_id=1, source_target_pairs={{0,1},{1,0},{2,3},{3,2},{4,5},{5,4},{6,7},{7,6},{8,9},{9,8},{10,11... | collective-permute-start | bytes 2359304 | tf_op jit(solution)/shard_map/ppermute | solution.py:336
  36.9 8.5 %collective-permute-start.7 = (bf16[4,16,1536]{2,1,0:T(8,128)(2,1)S(1)}, bf16[4,16,1536]{2,1,0:T(8,128)(2,1)S(1)}, u32[]{:S(2)}, u32[]{:S(2)}) collective-permute-start(bf16[4,16,1536]{2,1,0:T(8,128)(2,1)S(1)} %get-tuple-element.32), channel_id=1, source_target_pairs={{0,2},{1,3},{2,0},{3,1},{4,6},{5,7},{6,4},{7,5},{8,10},{9,11},{10,... | collective-permute-start | bytes 589832 | tf_op jit(solution)/shard_map/ppermute | solution.py:336
  37.3 8.1 %collective-permute-start.8 = (bf16[4,16,1536]{2,1,0:T(8,128)(2,1)S(1)}, bf16[4,16,1536]{2,1,0:T(8,128)(2,1)S(1)}, u32[]{:S(2)}, u32[]{:S(2)}) collective-permute-start(bf16[4,16,1536]{2,1,0:T(8,128)(2,1)S(1)} %get-tuple-element.33), channel_id=1, source_target_pairs={{0,16},{1,17},{2,18},{3,19},{4,20},{5,21},{6,22},{7,23},{8,24},{9,... | collective-permute-start | bytes 589832 | tf_op jit(solution)/shard_map/ppermute | solution.py:336
  38.8 10.6 %collective-permute-start.9 = (bf16[4,16,1536]{2,1,0:T(8,128)(2,1)S(1)}, bf16[4,16,1536]{2,1,0:T(8,128)(2,1)S(1)}, u32[]{:S(2)}, u32[]{:S(2)}) collective-permute-start(bf16[4,16,1536]{2,1,0:T(8,128)(2,1)S(1)} %get-tuple-element.34), channel_id=1, source_target_pairs={{0,18},{1,19},{2,16},{3,17},{4,22},{5,23},{6,20},{7,21},{8,26},{9,... | collective-permute-start | bytes 589832 | tf_op jit(solution)/shard_map/ppermute | solution.py:336
  40.5 13.8 %collective-permute-start.5 = (bf16[256,256]{1,0:T(8,128)(2,1)S(1)}, bf16[256,256]{1,0:T(8,128)(2,1)S(1)}, u32[]{:S(2)}, u32[]{:S(2)}) collective-permute-start(bf16[256,256]{1,0:T(8,128)(2,1)S(1)} %get-tuple-element.26.spatial_ref), channel_id=1, source_target_pairs={{0,1},{1,2},{2,3},{3,4},{4,5},{5,6},{6,7},{7,8},{8,9},{9,10},{10,1... | collective-permute-start | bytes 393224 | tf_op jit(solution)/shard_map/ppermute | solution.py:380
  41.8 12.5 %all-to-all-start.1 = ((f32[16,2,256]{2,1,0:T(2,128)}), f32[16,2,256]{2,1,0:T(2,128)S(1)}, u32[]{:S(2)}, u32[]{:S(2)}) async-start(f32[16,2,256]{2,1,0:T(2,128)} %get-tuple-element.25), calls=%async_computation.1 | async-start | bytes 65536 | tf_op jit(solution)/shard_map/all_to_all | solution.py:379
  49.5 9.6 %collective-permute-start.10 = (bf16[16,1536]{1,0:T(8,128)(2,1)S(1)}, bf16[16,1536]{1,0:T(8,128)(2,1)S(1)}, u32[]{:S(2)}, u32[]{:S(2)}) collective-permute-start(bf16[16,1536]{1,0:T(8,128)(2,1)S(1)} %get-tuple-element.36), channel_id=1, source_target_pairs={{0,4},{1,5},{2,6},{3,7},{4,8},{5,9},{6,10},{7,11},{8,12},{9,13},{1... | collective-permute-start | bytes 147464 | tf_op jit(solution)/shard_map/ppermute | solution.py:336
  51.4 7.7 %collective-permute-start.11 = (bf16[16,1536]{1,0:T(8,128)(2,1)S(1)}, bf16[16,1536]{1,0:T(8,128)(2,1)S(1)}, u32[]{:S(2)}, u32[]{:S(2)}) collective-permute-start(bf16[16,1536]{1,0:T(8,128)(2,1)S(1)} %get-tuple-element.37), channel_id=1, source_target_pairs={{0,8},{1,9},{2,10},{3,11},{4,12},{5,13},{6,14},{7,15},{8,0},{9,1},... | collective-permute-start | bytes 147464 | tf_op jit(solution)/shard_map/ppermute | solution.py:336
  51.9 7.2 %collective-permute-start.12 = (bf16[16,1536]{1,0:T(8,128)(2,1)S(1)}, bf16[16,1536]{1,0:T(8,128)(2,1)S(1)}, u32[]{:S(2)}, u32[]{:S(2)}) collective-permute-start(bf16[16,1536]{1,0:T(8,128)(2,1)S(1)} %get-tuple-element.38), channel_id=1, source_target_pairs={{0,12},{1,13},{2,14},{3,15},{4,0},{5,1},{6,2},{7,3},{8,4},{9,5},{1... | collective-permute-start | bytes 147464 | tf_op jit(solution)/shard_map/ppermute | solution.py:336
  55.5 3.6 %collective-permute-start.13 = (f32[2,256]{1,0:T(2,128)S(1)}, f32[2,256]{1,0:T(2,128)S(1)}, u32[]{:S(2)}, u32[]{:S(2)}) collective-permute-start(f32[2,256]{1,0:T(2,128)S(1)} %get-tuple-element.39.refs_4_), channel_id=1, source_target_pairs={{0,16},{1,17},{2,18},{3,19},{4,20},{5,21},{6,22},{7,23},{8,24},{9,... | collective-permute-start | bytes 6152 | tf_op jit(solution)/shard_map/ppermute | solution.py:336

commit v2 on v1

v2 whole, which is shorter than its diff:
```python
import functools
import math

import jax
import jax.numpy as jnp
from jax import lax
from jax.experimental import pallas as pl
from jax.experimental.pallas import tpu as pltpu
from jax.sharding import PartitionSpec as P

GROUPS = 32
EPSILON = 1e-05
F32 = jnp.float32
BF16 = jnp.bfloat16
VMEM = pl.BlockSpec(memory_space=pltpu.VMEM)
ANY = pl.BlockSpec(memory_space=pl.ANY)
NT = (((1,), (1,)), ((), ()))
NN = (((1,), (0,)), ((), ()))


def call(body, out_shapes, scratch=(), flops=0, moved=0, in_specs=None, out_specs=None):
    many = isinstance(out_shapes, (tuple, list))

    def run(*operands):
        return pl.pallas_call(
            body,
            out_shape=out_shapes,
            in_specs=in_specs or [VMEM] * len(operands),
            out_specs=out_specs or ([VMEM] * len(out_shapes) if many else VMEM),
            scratch_shapes=list(scratch),
            compiler_params=pltpu.CompilerParams(vmem_limit_bytes=40 * 1024 * 1024),
            cost_estimate=pl.CostEstimate(
                flops=flops, bytes_accessed=moved, transcendentals=0
            ),
        )(*operands)

    return run


def shape(dims, kind):
    return jax.ShapeDtypeStruct(dims, kind)


def mm(left, right, dims=NN):
    return lax.dot_general(left, right, dims, preferred_element_type=F32)


def group_total(rows, per_group):
    channels = rows.shape[-1]
    first = lax.broadcasted_iota(jnp.int32, (channels, channels), 0) // per_group
    second = lax.broadcasted_iota(jnp.int32, (channels, channels), 1) // per_group
    same = (first == second).astype(F32)
    return lax.dot_general(
        rows, same, NN, precision=lax.Precision.HIGHEST, preferred_element_type=F32
    )


def stats_body(lat_ref, ws_ref, wt_ref, out_ref, half_s_ref, half_t_ref, sem):
    core = lax.rem(lax.axis_index("wide"), 2)
    copies = []
    for at, (source, target) in enumerate(((wt_ref, half_t_ref), (ws_ref, half_s_ref))):
        half = target.shape[0]
        start = pl.multiple_of(core * half, 16)
        copies.append(
            pltpu.make_async_copy(source.at[pl.ds(start, half)], target, sem.at[at])
        )
        copies[-1].start()
    x = lat_ref[...].astype(F32)
    both = jnp.concatenate(
        [jnp.sum(x, axis=0, keepdims=True), jnp.sum(x * x, axis=0, keepdims=True)], axis=0
    )
    out_ref[...] = jnp.broadcast_to(both[None], out_ref.shape)
    for copy in copies:
        copy.wait()


def whiten(lat, stats, count, per_group):
    total = group_total(jnp.sum(stats, axis=0), per_group) / count
    mean = total[0:1]
    inv_std = 1.0 / jnp.sqrt(total[1:2] - mean * mean + EPSILON)
    return (lat.astype(F32) - mean) * inv_std, inv_std


def store_shifted(pad_ref, values, frames, cells, cols):
    total = frames * cells
    column = lax.broadcasted_iota(jnp.int32, (total, 1), 0) % cols
    left = jnp.where(column == 0, 0.0, pltpu.roll(values, 1, 0))
    right = jnp.where(column == cols - 1, 0.0, pltpu.roll(values, total - 1, 0))
    edge = jnp.zeros((cols, values.shape[1]), BF16)
    for at, form in enumerate((left, values, right)):
        low = form.astype(BF16)
        for f in range(frames):
            pad_ref[at, f, 0:cols] = edge
            pad_ref[at, f, cols : cols + cells] = low[f * cells : (f + 1) * cells]
            pad_ref[at, f, cols + cells :] = edge


def window(pad_ref, dy, dx, frames, cells, cols):
    return jnp.concatenate(
        [pad_ref[dx, f, dy * cols : dy * cols + cells] for f in range(frames)], axis=0
    )


def fill_weights(full, shard_ref, pieces, D, d, core):
    n = shard_ref.shape[0]
    full[pl.ds(pl.multiple_of(d * n, 16), n)] = shard_ref[...]
    for s in range(1, D):
        source = lax.rem(d + D - s, D)
        for which in range(2):
            holder = core if which == 0 else 1 - core
            start = pl.multiple_of(source * n + holder * (n // 2), 16)
            full[pl.ds(start, n // 2)] = pieces[2 * (s - 1) + which][...]


def core_order(transposed_ref, W, core):
    step = transposed_ref.shape[0] // W
    order = [(2 * j + core) * step for j in range(W // 2)]
    order += [(2 * j + 1 - core) * step for j in range(W // 2)]
    return jnp.concatenate(
        [transposed_ref[pl.ds(pl.multiple_of(at, 16), step)] for at in order], axis=0
    )


def put(block, column, shard, keep_ref, send_ref):
    low = block.astype(BF16)
    if send_ref is None:
        keep_ref[:, column : column + block.shape[1]] = low
        return
    half = block.shape[0] // 2
    for at in range(0, block.shape[1], 128):
        owner, place = (column + at) // shard, (column + at) % shard
        keep_ref[owner, :, place : place + 128] = low[:half, at : at + 128]
        send_ref[owner, :, place : place + 128] = low[half:, at : at + 128]


def normalise(lat_ref, stats_ref, gain_ref, bias_ref, count, per_group):
    white, inv_std = whiten(lat_ref[...], stats_ref[...], count, per_group)
    normed = white * gain_ref[...] + bias_ref[...]
    return white, normed, jax.nn.sigmoid(normed)


def first_body(sizes, lat_ref, cot_ref, halo_ref, stats_ref, gain_ref, bias_ref, wt_ref, *rest):
    D, W, frames, cells, cols, count, per_group, aligned = sizes
    pieces, rest = rest[: 2 * (D - 1)], rest[2 * (D - 1) :]
    full_wt, act_pad, gsa_t = rest[-3:]
    gsa_ref, keep_ref = rest[:2]
    send_ref = rest[2] if aligned else None
    channels = lat_ref.shape[1]
    d = lax.axis_index("dp")
    core = lax.rem(lax.axis_index("wide"), 2)
    fill_weights(full_wt, wt_ref, pieces, D, d, core)
    rows = frames * cells
    extended = jnp.concatenate([cot_ref[...], halo_ref[...]], axis=0)
    gsa = jnp.zeros((rows, channels), F32)
    for k in range(3):
        gsa += mm(
            extended[k * cells : k * cells + rows],
            full_wt[k * channels : (k + 1) * channels],
            NT,
        )
    gsa_ref[...] = gsa.astype(BF16)
    gsa_t[...] = gsa.astype(BF16).astype(F32).T.astype(BF16)
    _, normed, sig = normalise(lat_ref, stats_ref, gain_ref, bias_ref, count, per_group)
    act = (normed * sig).astype(BF16).astype(F32)
    store_shifted(act_pad, act, frames, cells, cols)
    left = core_order(gsa_t, W, core) if aligned else gsa_t[...]
    shard = wt_ref.shape[0] * 3
    for dy in range(3):
        for dx in range(3):
            seen = window(act_pad, dy, dx, frames, cells, cols)
            put(mm(left, seen), (3 * dy + dx) * channels, shard, keep_ref, send_ref)


def second_body(
    sizes, lat_ref, cot_ref, halo_ref, stats_ref, gain_ref, bias_ref, gsa_ref, ws_ref, *rest
):
    D, W, frames, cells, cols, count, per_group, aligned = sizes
    pieces, rest = rest[: 2 * (D - 1)], rest[2 * (D - 1) :]
    full_ws, act_pad, gsa_pad, cot_t = rest[-4:]
    spatial_ref, sums_ref, grad_ref, keep_ref = rest[:4]
    send_ref = rest[4] if aligned else None
    channels = lat_ref.shape[1]
    d = lax.axis_index("dp")
    core = lax.rem(lax.axis_index("wide"), 2)
    fill_weights(full_ws, ws_ref, pieces, D, d, core)
    rows = frames * cells
    white, normed, sig = normalise(lat_ref, stats_ref, gain_ref, bias_ref, count, per_group)
    act = (normed * sig).astype(BF16).astype(F32)
    store_shifted(act_pad, act, frames, cells, cols)
    store_shifted(gsa_pad, gsa_ref[...].astype(F32), frames, cells, cols)
    extended = jnp.concatenate([cot_ref[...], halo_ref[...]], axis=0)
    for f in range(frames + 2):
        cot_t[:, f * cells : (f + 1) * cells] = (
            extended[f * cells : (f + 1) * cells].astype(F32).T.astype(BF16)
        )
    left = core_order(cot_t, W, core) if aligned else cot_t[...]
    out = jnp.zeros((rows, channels), F32)
    for dy in range(3):
        for dx in range(3):
            tap = 3 * dy + dx
            seen = window(act_pad, dy, dx, frames, cells, cols)
            out += mm(seen, full_ws[tap * channels : (tap + 1) * channels])
    spatial = out.astype(BF16)
    spatial_ref[...] = spatial
    shard = ws_ref.shape[0] // 3
    for k in range(3):
        block = mm(left[:, k * cells : k * cells + rows], spatial)
        put(block, k * channels, shard, keep_ref, send_ref)

    grad = jnp.zeros((rows, channels), F32)
    for dy in range(3):
        for dx in range(3):
            tap = 3 * dy + dx
            seen = window(gsa_pad, 2 - dy, 2 - dx, frames, cells, cols)
            grad += mm(seen, full_ws[tap * channels : (tap + 1) * channels], NT)
    grad = grad * (sig * (1.0 + normed * (1.0 - sig)))
    grad_ref[...] = grad
    both = jnp.concatenate(
        [
            jnp.sum(grad * white, axis=0, keepdims=True),
            jnp.sum(grad, axis=0, keepdims=True),
        ],
        axis=0,
    )
    sums_ref[...] = jnp.broadcast_to(both[None], sums_ref.shape)


def finish_body(
    sizes,
    lat_ref,
    cot_ref,
    stats_ref,
    gain_ref,
    grad_ref,
    sums_ref,
    spatial_ref,
    before_ref,
    wt_ref,
    *rest,
):
    D, W, frames, cells, cols, count, per_group, aligned = sizes
    pieces = rest[: 2 * (D - 1)]
    block_ref, glat_ref, norm_ref, full_wt = rest[2 * (D - 1) :]
    channels = lat_ref.shape[1]
    d = lax.axis_index("dp")
    core = lax.rem(lax.axis_index("wide"), 2)
    fill_weights(full_wt, wt_ref, pieces, D, d, core)
    extended = jnp.concatenate([before_ref[...], spatial_ref[...]], axis=0)
    rows = frames * cells
    temporal = jnp.zeros((rows, channels), F32)
    for k in range(3):
        start = (2 - k) * cells
        temporal += mm(
            extended[start : start + rows], full_wt[k * channels : (k + 1) * channels]
        )
    lat = lat_ref[...]
    block_ref[...] = (lat.astype(F32) + temporal).astype(BF16)

    white, inv_std = whiten(lat, stats_ref[...], count, per_group)
    gain = gain_ref[...]
    total = jnp.sum(sums_ref[...], axis=0)
    norm_ref[...] = total
    means = group_total(total * gain, per_group) / count
    inner = inv_std * (grad_ref[...] * gain - means[1:2] - white * means[0:1])
    glat_ref[...] = (cot_ref[...].astype(F32) + inner).astype(BF16)


def plane_body(keep_ref, got_ref, out_ref):
    for a in range(keep_ref.shape[0]):
        for b in range(2):
            out_ref[2 * a + b] = (
                keep_ref[a, :, b].astype(F32) + got_ref[a, :, b].astype(F32)
            ).astype(BF16)


def sum_body(scale, terms_ref, out_ref):
    total = terms_ref[0].astype(F32)
    for at in range(1, terms_ref.shape[0]):
        total += terms_ref[at].astype(F32)
    if scale is not None:
        total = total * scale
    out_ref[...] = total.astype(out_ref.dtype)


def norm_columns(scale, terms, norm_ref):
    norm = terms[0][...]
    for term in terms[1:]:
        norm += term[...]
    channels, width = norm.shape[1], norm_ref.shape[1]
    row = lax.broadcasted_iota(jnp.int32, (channels, width), 0)
    column = lax.broadcasted_iota(jnp.int32, (channels, width), 1)
    pick = (row == column + lax.axis_index("wide") * width).astype(F32)
    norm_ref[...] = (
        lax.dot_general(
            norm, pick, NN, precision=lax.Precision.HIGHEST, preferred_element_type=F32
        )
        * scale
    )


def only_norm_body(scale, *refs):
    norm_columns(scale, refs[:-1], refs[-1])


def local(latents, cotangent, norm_gain, norm_bias, w_spatial, w_temporal):
    D, W = lax.axis_size("dp"), lax.axis_size("wide")
    _, frames, rows_here, cols, channels = latents.shape
    cells = rows_here * cols
    rows = frames * cells
    per_group = channels // GROUPS
    count = W * frames * cells * per_group
    shard_s, shard_t = w_spatial.shape[0], w_temporal.shape[0]
    aligned = (channels // W) % 16 == 0 and shard_s % 128 == 0 and shard_t % 128 == 0
    aligned = aligned and W % 4 == 0
    sizes = (D, W, frames, cells, cols, count, per_group, aligned)
    scale = 1.0 / math.sqrt(D * W * frames * cells)

    lat, cot = latents.reshape(rows, channels), cotangent.reshape(rows, channels)
    gain, bias = norm_gain.reshape(1, channels), norm_bias.reshape(1, channels)

    def over_all(moves):
        pairs = []
        for d in range(D):
            for w in range(W):
                to = moves(d, w)
                pairs.append((d * W + w, to[0] * W + to[1]))
        return pairs

    def send(value, moves):
        return lax.ppermute(value, ("dp", "wide"), over_all(moves))

    half_s, half_t = shard_s // 2, shard_t // 2
    stats, half_s, half_t = call(
        stats_body,
        [
            shape((W, 2, channels), F32),
            shape((half_s, channels), BF16),
            shape((half_t, channels), BF16),
        ],
        [pltpu.SemaphoreType.DMA((2,))],
        in_specs=[VMEM, ANY, ANY],
        out_specs=[VMEM, ANY, ANY],
    )(lat, w_spatial, w_temporal)
    stats = lax.all_to_all(stats, "wide", split_axis=0, concat_axis=0, tiled=True)

    halo = lax.ppermute(cot, "wide", [(w + 1, w) for w in range(W - 1)])
    pieces_s, pieces_t = [], []
    for s in range(1, D):
        here_t = send(half_t, lambda d, w: ((d + s) % D, w))
        here_s = send(half_s, lambda d, w: ((d + s) % D, w))
        there_t = send(here_t, lambda d, w: (d, w ^ 1))
        there_s = send(here_s, lambda d, w: (d, w ^ 1))
        pieces_s += [here_s, there_s]
        pieces_t += [here_t, there_t]

    def terms(shard):
        if aligned:
            return [shape((D, channels // 2, shard), BF16)] * 2
        return [shape((channels, D * shard), BF16)]

    pad = pltpu.VMEM((3, frames, cells + 2 * cols, channels), BF16)
    gsa, *grads_s = call(
        functools.partial(first_body, sizes),
        [shape((rows, channels), BF16)] + terms(shard_s),
        [pltpu.VMEM((D * shard_t, channels), BF16), pad, pltpu.VMEM((channels, rows), BF16)],
        flops=2 * 12 * rows * channels * channels,
        moved=3_000_000,
    )(lat, cot, halo, stats, gain, bias, w_temporal, *pieces_t)
    spatial, sums, grad, *grads_t = call(
        functools.partial(second_body, sizes),
        [
            shape((rows, channels), BF16),
            shape((W, 2, channels), F32),
            shape((rows, channels), F32),
        ]
        + terms(shard_t),
        [
            pltpu.VMEM((D * shard_s, channels), BF16),
            pad,
            pad,
            pltpu.VMEM((channels, rows + 2 * cells), BF16),
        ],
        flops=2 * 21 * rows * channels * channels,
        moved=3_000_000,
    )(lat, cot, halo, stats, gain, bias, gsa, w_spatial, *pieces_s)

    sums = lax.all_to_all(sums, "wide", split_axis=0, concat_axis=0, tiled=True)
    before = lax.ppermute(spatial, "wide", [(w, w + 1) for w in range(W - 1)])

    width = channels // W
    Z = W // 4

    def reduced(keep, away, shard):
        got = send(away, lambda d, w: (d, w ^ 1))
        view = (D, Z, 2, width, shard)
        plane = call(plane_body, shape((2 * D, Z, width, shard), BF16), moved=3_000_000)(
            keep.reshape(view), got.reshape(view)
        )
        groups = [
            [d * W + z * 4 + y * 2 + core for d in range(D) for y in range(2)]
            for z in range(Z)
            for core in range(2)
        ]
        plane = lax.all_to_all(
            plane,
            ("dp", "wide"),
            split_axis=0,
            concat_axis=0,
            axis_index_groups=groups,
            tiled=True,
        )
        line = call(
            functools.partial(sum_body, None), shape((Z, width, shard), BF16), moved=1_000_000
        )(plane)
        groups = [
            [d * W + z * 4 + at for z in range(Z)] for d in range(D) for at in range(4)
        ]
        line = lax.all_to_all(
            line,
            ("dp", "wide"),
            split_axis=0,
            concat_axis=0,
            axis_index_groups=groups,
            tiled=True,
        )
        return call(
            functools.partial(sum_body, scale), shape((width, shard), F32), moved=300_000
        )(line).T

    if aligned:
        grad_s = reduced(*grads_s, shard_s)
        grad_t = reduced(*grads_t, shard_t)
    else:
        outs = []
        for (full,) in (grads_s, grads_t):
            part = lax.psum_scatter(
                full.astype(F32), "wide", scatter_dimension=0, tiled=True
            ).T.astype(BF16)
            part = lax.psum_scatter(part, "dp", scatter_dimension=0, tiled=True)
            outs.append(part.astype(F32) * scale)
        grad_s, grad_t = outs

    block_out, grad_latents, norm = call(
        functools.partial(finish_body, sizes),
        [
            shape((rows, channels), BF16),
            shape((rows, channels), BF16),
            shape((2, channels), F32),
        ],
        [pltpu.VMEM((D * shard_t, channels), BF16)],
        flops=2 * 3 * rows * channels * channels,
        moved=2_000_000,
    )(lat, cot, stats, gain, grad, sums, spatial, before, w_temporal, *pieces_t)
    norms = [norm] + [send(norm, lambda d, w: ((d + s) % D, w)) for s in range(1, D)]
    norm = call(functools.partial(only_norm_body, scale), shape((2, width), F32))(*norms)
    return (
        block_out.reshape(latents.shape),
        grad_latents.reshape(latents.shape),
        grad_s,
        grad_t,
        norm,
    )


def solution(mesh):
    return jax.shard_map(
        local,
        mesh=mesh,
        in_specs=(
            P("dp", "wide", None, None, None),
            P("dp", "wide", None, None, None),
            P(),
            P(),
            P("dp", None),
            P("dp", None),
        ),
        out_specs=(
            P("dp", "wide", None, None, None),
            P("dp", "wide", None, None, None),
            P("dp", "wide"),
            P("dp", "wide"),
            P(None, "wide"),
        ),
        check_vma=False,
    )
```

time: 60.2 us -> 89.8 us (1.49)
  the two profiles are of different devices: /device:TPU:0 before, /device:TPU:8 now
where the time goes in v2:
time: 89.8 us; the launch traced here: 89.1 us
  waiting for transfers between devices  34.2 us (38%)
  starting transfers between devices  29.1 us (32%)
  blocking collectives  11.3 us (13%)
  Pallas kernels  10.2 us (11%)
  local copies, waits for them, and re-layouts  3.56 us (4%)
    all_to_all x2, waiting for transfers between devices, reduced(): lax.all_to_all(plane, ('dp', 'wide'), split_axis=0, concat_axis=0, axis_i...  12 us
    all_to_all x1, blocking collectives, local(): lax.all_to_all(stats, 'wide', split_axis=0, concat_axis=0, tiled=True)  11.3 us
    pallas_call x11, Pallas kernels, run(): pl.pallas_call(body, out_shape=out_shapes, in_specs=in_specs or [VMEM] *...  10.2 us
    ppermute x7, waiting for transfers between devices, send(): return lax.ppermute(value, ('dp', 'wide'), over_all(moves))  8.82 us
    all_to_all x2, starting transfers between devices, reduced(): lax.all_to_all(line, ('dp', 'wide'), split_axis=0, concat_axis=0, axis_in...  8.64 us
    all_to_all x2, starting transfers between devices, reduced(): lax.all_to_all(plane, ('dp', 'wide'), split_axis=0, concat_axis=0, axis_i...  6.84 us
    ppermute x1, waiting for transfers between devices, local(): before = lax.ppermute(spatial, 'wide', [(w, w + 1) for w in range(W - 1)])  5.26 us
    all_to_all x1, starting transfers between devices, local(): sums = lax.all_to_all(sums, 'wide', split_axis=0, concat_axis=0, tiled=True)  4.98 us
  transfers between devices with their start and end apart: 14, of which 7 were waited for; matrix products, arithmetic and copies ran while one was open for 0% of the time, Pallas kernels for 10%

profile of v2, /device:TPU:8, one launch (start us, length us, event | category | flops | bytes accessed | tf_op | source)
XLA Modules:
  0.0 89.1 jit_solution(16529291972368813013)
XLA Ops:
  0.6 0.9 %copy-done = bf16[384,256]{1,0:T(8,128)(2,1)S(1)} copy-done((bf16[384,256]{1,0:T(8,128)(2,1)S(1)}, bf16[384,256]{1,0:T(8,128)(2,1)}, u32[]{:S(2)}) %copy-start) | copy-done | bytes 196632
  1.6 1.1 %copy-done.2 = bf16[1152,256]{1,0:T(8,128)(2,1)S(1)} copy-done((bf16[1152,256]{1,0:T(8,128)(2,1)S(1)}, bf16[1152,256]{1,0:T(8,128)(2,1)}, u32[]{:S(2)}) %copy-start.2) | copy-done | bytes 589848
  2.6 0.9 %copy-done.4 = bf16[1,2,8,16,256]{4,3,2,1,0:T(8,128)(2,1)S(1)} copy-done((bf16[1,2,8,16,256]{4,3,2,1,0:T(8,128)(2,1)S(1)}, bf16[1,2,8,16,256]{4,3,2,1,0:T(8,128)(2,1)}, u32[]{:S(2)}) %copy-start.4) | copy-done | bytes 131096
  3.8 1.6 %collective-permute-start.3 = (bf16[576,256]{1,0:T(8,128)(2,1)S(1)}, bf16[576,256]{1,0:T(8,128)(2,1)S(1)}, u32[]{:S(2)}, u32[]{:S(2)}) collective-permute-start(bf16[576,256]{1,0:T(8,128)(2,1)S(1)} %get-tuple-element.22), channel_id=1, source_target_pairs={{0,16},{1,17},{2,18},{3,19},{4,20},{5,21},{6,22},{7,23},{8,24},{9,... | collective-permute-start | bytes 884744 | tf_op jit(solution)/shard_map/ppermute | solution.py:330
  5.3 0.5 collective-permute-start.1
  5.9 2.2 %collective-permute-start = (bf16[256,256]{1,0:T(8,128)(2,1)S(1)}, bf16[256,256]{1,0:T(8,128)(2,1)S(1)}, u32[]{:S(2)}, u32[]{:S(2)}) collective-permute-start(bf16[256,256]{1,0:T(8,128)(2,1)S(1)} %bitcast.20), channel_id=1, source_target_pairs={{1,0},{2,1},{3,2},{4,3},{5,4},{6,5},{7,6},{8,7},{9,8},{10,9},{11,1... | collective-permute-start | bytes 393224 | tf_op jit(solution)/shard_map/ppermute | solution.py:346
  8.1 6.6 %collective-permute-done.1.rest_0_ = bf16[192,256]{1,0:T(8,128)(2,1)S(1)} collective-permute-done((bf16[192,256]{1,0:T(8,128)(2,1)S(1)}, bf16[192,256]{1,0:T(8,128)(2,1)S(1)}, u32[]{:S(2)}, u32[]{:S(2)}) %collective-permute-start.1) | collective-permute-done | bytes 98336 | tf_op jit(solution)/shard_map/ppermute | solution.py:330
  15.2 11.3 %all_to_all.30.stats_ref = f32[16,2,256]{2,1,0:T(2,128)S(1)} all-to-all(f32[16,2,256]{2,1,0:T(2,128)S(1)} %get-tuple-element.19), channel_id=1, replica_groups=mesh['dp'=2,'wide'=16] {'wide'}, dimensions={0} | all-to-all | bytes 65536 | tf_op jit(solution)/shard_map/all_to_all | solution.py:344
  26.5 0.7 copy-done.7
  27.2 1.0 %shard_map.102 = (bf16[256,256]{1,0:T(8,128)(2,1)S(1)}, bf16[2,128,1152]{2,1,0:T(8,128)(2,1)S(1)}, bf16[2,128,1152]{2,1,0:T(8,128)(2,1)S(1)}) custom-call(bf16[256,256]{1,0:T(8,128)(2,1)S(1)} %bitcast.15, bf16[256,256]{1,0:T(8,128)(2,1)S(1)} %bitcast.21, bf16[256,256]{1,0:T(8,128)(2,1)S(1)} %collective-permute-done.halo_ref, ...), custom_call_target="tpu_custom_call" | custom-call | flops 402653184 | bytes 3000000 | tf_op jit(solution)/shard_map/pallas_call | solution.py:25
  28.4 2.5 %shard_map.103 = (bf16[256,256]{1,0:T(8,128)(2,1)S(1)}, f32[16,2,256]{2,1,0:T(2,128)}, f32[256,256]{1,0:T(8,128)S(1)}, bf16[2,128,384]{2,1,0:T(8,128)(2,1)S(1)}, bf16[2,128,384]{2,1,0:T(8,128)(2,1)S(1)}) custom-call(bf16[256,256]{1,0:T(8,128)(2,1)S(1)} %bitcast.16, bf16[256,256]{1,0:T(8,128)(2,1)S(1)} %bitcast.22, ...), custom_call_target="tpu_custom_call" | custom-call | flops 704643072 | bytes 3000000 | tf_op jit(solution)/shard_map/pallas_call | solution.py:25
  31.3 5.0 %all-to-all-start.1 = ((f32[16,2,256]{2,1,0:T(2,128)}), f32[16,2,256]{2,1,0:T(2,128)S(1)}, u32[]{:S(2)}, u32[]{:S(2)}) async-start(f32[16,2,256]{2,1,0:T(2,128)} %get-tuple-element.24), calls=%async_computation.1 | async-start | bytes 65536 | tf_op jit(solution)/shard_map/all_to_all | solution.py:387
  36.3 0.7 shard_map.108
  37.0 4.4 %all-to-all-done.1.sums_ref = f32[16,2,256]{2,1,0:T(2,128)S(1)} async-done(((f32[16,2,256]{2,1,0:T(2,128)}), f32[16,2,256]{2,1,0:T(2,128)S(1)}, u32[]{:S(2)}, u32[]{:S(2)}) %all-to-all-start.1) | async-done | bytes 32800 | tf_op jit(solution)/shard_map/all_to_all | solution.py:387
  41.4 3.4 %all-to-all-start.4 = ((bf16[4,4,16,384]{3,2,1,0:T(8,128)(2,1)}), bf16[4,4,16,384]{3,2,1,0:T(8,128)(2,1)S(1)}, u32[]{:S(2)}, u32[]{:S(2)}) async-start(bf16[4,4,16,384]{3,2,1,0:T(8,128)(2,1)} %shard_map.108), calls=%async_computation.4 | async-start | bytes 393216 | tf_op jit(solution)/shard_map/all_to_all | solution.py:404
  44.8 0.9 %shard_map.105 = bf16[4,4,16,1152]{3,2,1,0:T(8,128)(2,1)} custom-call(bf16[2,4,2,16,1152]{4,3,2,1,0:T(8,128)(2,1)S(1)} %bitcast.12, bf16[2,4,2,16,1152]{4,3,2,1,0:T(8,128)(2,1)S(1)} %bitcast.13), custom_call_target="tpu_custom_call" | custom-call | bytes 3000000 | tf_op jit(solution)/shard_map/pallas_call | solution.py:25
  45.8 4.4 %all-to-all-done.4.terms_ref = bf16[4,4,16,384]{3,2,1,0:T(8,128)(2,1)S(1)} async-done(((bf16[4,4,16,384]{3,2,1,0:T(8,128)(2,1)}), bf16[4,4,16,384]{3,2,1,0:T(8,128)(2,1)S(1)}, u32[]{:S(2)}, u32[]{:S(2)}) %all-to-all-start.4) | async-done | bytes 196640 | tf_op jit(solution)/shard_map/all_to_all | solution.py:404
  50.2 3.5 %all-to-all-start.2 = ((bf16[4,4,16,1152]{3,2,1,0:T(8,128)(2,1)}), bf16[4,4,16,1152]{3,2,1,0:T(8,128)(2,1)S(1)}, u32[]{:S(2)}, u32[]{:S(2)}) async-start(bf16[4,4,16,1152]{3,2,1,0:T(8,128)(2,1)} %shard_map.105), calls=%async_computation.2 | async-start | bytes 1179648 | tf_op jit(solution)/shard_map/all_to_all | solution.py:404
  53.6 0.6 shard_map.109
  54.3 7.6 %all-to-all-done.2.terms_ref = bf16[4,4,16,1152]{3,2,1,0:T(8,128)(2,1)S(1)} async-done(((bf16[4,4,16,1152]{3,2,1,0:T(8,128)(2,1)}), bf16[4,4,16,1152]{3,2,1,0:T(8,128)(2,1)S(1)}, u32[]{:S(2)}, u32[]{:S(2)}) %all-to-all-start.2) | async-done | bytes 589856 | tf_op jit(solution)/shard_map/all_to_all | solution.py:404
  61.9 4.1 %all-to-all-start.5 = ((bf16[4,16,384]{2,1,0:T(8,128)(2,1)}), bf16[4,16,384]{2,1,0:T(8,128)(2,1)S(1)}, u32[]{:S(2)}, u32[]{:S(2)}) async-start(bf16[4,16,384]{2,1,0:T(8,128)(2,1)} %shard_map.109), calls=%async_computation.5 | async-start | bytes 98304 | tf_op jit(solution)/shard_map/all_to_all | solution.py:418
  66.0 0.7 shard_map.106
  66.8 3.8 %all-to-all-done.5.terms_ref = bf16[4,16,384]{2,1,0:T(8,128)(2,1)S(1)} async-done(((bf16[4,16,384]{2,1,0:T(8,128)(2,1)}), bf16[4,16,384]{2,1,0:T(8,128)(2,1)S(1)}, u32[]{:S(2)}, u32[]{:S(2)}) %all-to-all-start.5) | async-done | bytes 49184 | tf_op jit(solution)/shard_map/all_to_all | solution.py:418
  70.5 4.5 %all-to-all-start.3 = ((bf16[4,16,1152]{2,1,0:T(8,128)(2,1)}), bf16[4,16,1152]{2,1,0:T(8,128)(2,1)S(1)}, u32[]{:S(2)}, u32[]{:S(2)}) async-start(bf16[4,16,1152]{2,1,0:T(8,128)(2,1)} %shard_map.106), calls=%async_computation.3 | async-start | bytes 294912 | tf_op jit(solution)/shard_map/all_to_all | solution.py:418
  75.1 1.9 %collective-permute-start.5 = (bf16[256,256]{1,0:T(8,128)(2,1)S(1)}, bf16[256,256]{1,0:T(8,128)(2,1)S(1)}, u32[]{:S(2)}, u32[]{:S(2)}) collective-permute-start(bf16[256,256]{1,0:T(8,128)(2,1)S(1)} %get-tuple-element.25.spatial_ref), channel_id=1, source_target_pairs={{0,1},{1,2},{2,3},{3,4},{4,5},{5,6},{6,7},{7,8},{8,9},{9,10},{10,1... | collective-permute-start | bytes 393224 | tf_op jit(solution)/shard_map/ppermute | solution.py:388
  77.0 5.3 %collective-permute-done.5.before_ref = bf16[256,256]{1,0:T(8,128)(2,1)S(1)} collective-permute-done((bf16[256,256]{1,0:T(8,128)(2,1)S(1)}, bf16[256,256]{1,0:T(8,128)(2,1)S(1)}, u32[]{:S(2)}, u32[]{:S(2)}) %collective-permute-start.5) | collective-permute-done | bytes 131104 | tf_op jit(solution)/shard_map/ppermute | solution.py:388
  82.2 1.3 %shard_map.104 = (bf16[256,256]{1,0:T(8,128)(2,1)}, bf16[256,256]{1,0:T(8,128)(2,1)}, f32[2,256]{1,0:T(2,128)S(1)}) custom-call(bf16[256,256]{1,0:T(8,128)(2,1)S(1)} %bitcast.17, bf16[256,256]{1,0:T(8,128)(2,1)S(1)} %bitcast.23, f32[16,2,256]{2,1,0:T(2,128)S(1)} %all_to_all.30.stats_ref, f32[1,256]{1,0:T(1,128)S(1)} %bitcast.26, ...), custom_call_target="tpu_custom_call" | custom-call | flops 100663296 | bytes 2000000 | tf_op jit(solution)/shard_map/pallas_call | solution.py:25
  83.5 1.4 %collective-permute-start.8 = (f32[2,256]{1,0:T(2,128)S(1)}, f32[2,256]{1,0:T(2,128)S(1)}, u32[]{:S(2)}, u32[]{:S(2)}) collective-permute-start(f32[2,256]{1,0:T(2,128)S(1)} %get-tuple-element.32.refs_0_), channel_id=1, source_target_pairs={{0,16},{1,17},{2,18},{3,19},{4,20},{5,21},{6,22},{7,23},{8,24},{9,... | collective-permute-start | bytes 6152 | tf_op jit(solution)/shard_map/ppermute | solution.py:330
  84.9 2.2 %collective-permute-done.8.refs_1_ = f32[2,256]{1,0:T(2,128)S(1)} collective-permute-done((f32[2,256]{1,0:T(2,128)S(1)}, f32[2,256]{1,0:T(2,128)S(1)}, u32[]{:S(2)}, u32[]{:S(2)}) %collective-permute-start.8) | collective-permute-done | bytes 2080 | tf_op jit(solution)/shard_map/ppermute | solution.py:330
  87.1 0.8 shard_map.111
  87.8 0.6 shard_map.110
  88.4 0.7 shard_map.107
  (26 shorter events, 1.4 us)
Async XLA Ops:
  0.6 0.9 %copy-start = (bf16[384,256]{1,0:T(8,128)(2,1)S(1)}, bf16[384,256]{1,0:T(8,128)(2,1)}, u32[]{:S(2)}) copy-start(bf16[384,256]{1,0:T(8,128)(2,1)} %wt_ref.5) | copy-start | bytes 589828
  1.6 1.1 %copy-start.2 = (bf16[1152,256]{1,0:T(8,128)(2,1)S(1)}, bf16[1152,256]{1,0:T(8,128)(2,1)}, u32[]{:S(2)}) copy-start(bf16[1152,256]{1,0:T(8,128)(2,1)} %ws_ref.3) | copy-start | bytes 1769476
  2.6 0.9 %copy-start.4 = (bf16[1,2,8,16,256]{4,3,2,1,0:T(8,128)(2,1)S(1)}, bf16[1,2,8,16,256]{4,3,2,1,0:T(8,128)(2,1)}, u32[]{:S(2)}) copy-start(bf16[1,2,8,16,256]{4,3,2,1,0:T(8,128)(2,1)} %param.6) | copy-start | bytes 393220
  3.5 2.3 %copy-start.6 = (bf16[1,2,8,16,256]{4,3,2,1,0:T(8,128)(2,1)S(1)}, bf16[1,2,8,16,256]{4,3,2,1,0:T(8,128)(2,1)}, u32[]{:S(2)}) copy-start(bf16[1,2,8,16,256]{4,3,2,1,0:T(8,128)(2,1)} %param.7) | copy-start | bytes 393220
  3.5 23.0 %copy-start.1 = (bf16[384,256]{1,0:T(8,128)(2,1)S(1)}, bf16[384,256]{1,0:T(8,128)(2,1)}, u32[]{:S(2)}) copy-start(bf16[384,256]{1,0:T(8,128)(2,1)} %wt_ref.5) | copy-start | bytes 589828
  3.8 10.9 %collective-permute-start.3 = (bf16[576,256]{1,0:T(8,128)(2,1)S(1)}, bf16[576,256]{1,0:T(8,128)(2,1)S(1)}, u32[]{:S(2)}, u32[]{:S(2)}) collective-permute-start(bf16[576,256]{1,0:T(8,128)(2,1)S(1)} %get-tuple-element.22), channel_id=1, source_target_pairs={{0,16},{1,17},{2,18},{3,19},{4,20},{5,21},{6,22},{7,23},{8,24},{9,... | collective-permute-start | bytes 884744 | tf_op jit(solution)/shard_map/ppermute | solution.py:330
  5.3 9.4 %collective-permute-start.1 = (bf16[192,256]{1,0:T(8,128)(2,1)S(1)}, bf16[192,256]{1,0:T(8,128)(2,1)S(1)}, u32[]{:S(2)}, u32[]{:S(2)}) collective-permute-start(bf16[192,256]{1,0:T(8,128)(2,1)S(1)} %get-tuple-element.20), channel_id=1, source_target_pairs={{0,16},{1,17},{2,18},{3,19},{4,20},{5,21},{6,22},{7,23},{8,24},{9,... | collective-permute-start | bytes 294920 | tf_op jit(solution)/shard_map/ppermute | solution.py:330
  5.9 20.6 %collective-permute-start = (bf16[256,256]{1,0:T(8,128)(2,1)S(1)}, bf16[256,256]{1,0:T(8,128)(2,1)S(1)}, u32[]{:S(2)}, u32[]{:S(2)}) collective-permute-start(bf16[256,256]{1,0:T(8,128)(2,1)S(1)} %bitcast.20), channel_id=1, source_target_pairs={{1,0},{2,1},{3,2},{4,3},{5,4},{6,5},{7,6},{8,7},{9,8},{10,9},{11,1... | collective-permute-start | bytes 393224 | tf_op jit(solution)/shard_map/ppermute | solution.py:346
  14.7 11.8 %collective-permute-start.2 = (bf16[192,256]{1,0:T(8,128)(2,1)S(1)}, bf16[192,256]{1,0:T(8,128)(2,1)S(1)}, u32[]{:S(2)}, u32[]{:S(2)}) collective-permute-start(bf16[192,256]{1,0:T(8,128)(2,1)S(1)} %collective-permute-done.1.rest_0_), channel_id=1, source_target_pairs={{0,1},{1,0},{2,3},{3,2},{4,5},{5,4},{6,7},{7,6},{8,9},{9,8},{10,11... | collective-permute-start | bytes 294920 | tf_op jit(solution)/shard_map/ppermute | solution.py:330
  14.7 13.7 %collective-permute-start.4 = (bf16[576,256]{1,0:T(8,128)(2,1)S(1)}, bf16[576,256]{1,0:T(8,128)(2,1)S(1)}, u32[]{:S(2)}, u32[]{:S(2)}) collective-permute-start(bf16[576,256]{1,0:T(8,128)(2,1)S(1)} %collective-permute-done.3.rest_0_), channel_id=1, source_target_pairs={{0,1},{1,0},{2,3},{3,2},{4,5},{5,4},{6,7},{7,6},{8,9},{9,8},{10,11... | collective-permute-start | bytes 884744 | tf_op jit(solution)/shard_map/ppermute | solution.py:330
  15.2 11.3 %copy-start.8 = (f32[256]{0:T(256)S(1)}, f32[256]{0:T(256)}, u32[]{:S(2)}) copy-start(f32[256]{0:T(256)} %param.9) | copy-start | bytes 3076
  26.5 0.7 copy-start.7
  27.2 1.2 %copy-start.3 = (bf16[1152,256]{1,0:T(8,128)(2,1)S(1)}, bf16[1152,256]{1,0:T(8,128)(2,1)}, u32[]{:S(2)}) copy-start(bf16[1152,256]{1,0:T(8,128)(2,1)} %ws_ref.3) | copy-start | bytes 1769476
  28.2 16.6 %collective-permute-start.6 = (bf16[2,128,1152]{2,1,0:T(8,128)(2,1)S(1)}, bf16[2,128,1152]{2,1,0:T(8,128)(2,1)S(1)}, u32[]{:S(2)}, u32[]{:S(2)}) collective-permute-start(bf16[2,128,1152]{2,1,0:T(8,128)(2,1)S(1)} %get-tuple-element.29), channel_id=1, source_target_pairs={{0,1},{1,0},{2,3},{3,2},{4,5},{5,4},{6,7},{7,6},{8,9},{9,8},{10,11... | collective-permute-start | bytes 1769480 | tf_op jit(solution)/shard_map/ppermute | solution.py:330
  30.9 5.4 %collective-permute-start.7 = (bf16[2,128,384]{2,1,0:T(8,128)(2,1)S(1)}, bf16[2,128,384]{2,1,0:T(8,128)(2,1)S(1)}, u32[]{:S(2)}, u32[]{:S(2)}) collective-permute-start(bf16[2,128,384]{2,1,0:T(8,128)(2,1)S(1)} %get-tuple-element.31), channel_id=1, source_target_pairs={{0,1},{1,0},{2,3},{3,2},{4,5},{5,4},{6,7},{7,6},{8,9},{9,8},{10,11... | collective-permute-start | bytes 589832 | tf_op jit(solution)/shard_map/ppermute | solution.py:330
  31.3 10.1 %all-to-all-start.1 = ((f32[16,2,256]{2,1,0:T(2,128)}), f32[16,2,256]{2,1,0:T(2,128)S(1)}, u32[]{:S(2)}, u32[]{:S(2)}) async-start(f32[16,2,256]{2,1,0:T(2,128)} %get-tuple-element.24), calls=%async_computation.1 | async-start | bytes 65536 | tf_op jit(solution)/shard_map/all_to_all | solution.py:387
  41.4 8.7 %all-to-all-start.4 = ((bf16[4,4,16,384]{3,2,1,0:T(8,128)(2,1)}), bf16[4,4,16,384]{3,2,1,0:T(8,128)(2,1)S(1)}, u32[]{:S(2)}, u32[]{:S(2)}) async-start(bf16[4,4,16,384]{3,2,1,0:T(8,128)(2,1)} %shard_map.108), calls=%async_computation.4 | async-start | bytes 393216 | tf_op jit(solution)/shard_map/all_to_all | solution.py:404
  50.2 11.8 %all-to-all-start.2 = ((bf16[4,4,16,1152]{3,2,1,0:T(8,128)(2,1)}), bf16[4,4,16,1152]{3,2,1,0:T(8,128)(2,1)S(1)}, u32[]{:S(2)}, u32[]{:S(2)}) async-start(bf16[4,4,16,1152]{3,2,1,0:T(8,128)(2,1)} %shard_map.105), calls=%async_computation.2 | async-start | bytes 1179648 | tf_op jit(solution)/shard_map/all_to_all | solution.py:404
  61.9 8.6 %all-to-all-start.5 = ((bf16[4,16,384]{2,1,0:T(8,128)(2,1)}), bf16[4,16,384]{2,1,0:T(8,128)(2,1)S(1)}, u32[]{:S(2)}, u32[]{:S(2)}) async-start(bf16[4,16,384]{2,1,0:T(8,128)(2,1)} %shard_map.109), calls=%async_computation.5 | async-start | bytes 98304 | tf_op jit(solution)/shard_map/all_to_all | solution.py:418
  66.8 15.4 %copy-start.5 = (bf16[1,2,8,16,256]{4,3,2,1,0:T(8,128)(2,1)S(1)}, bf16[1,2,8,16,256]{4,3,2,1,0:T(8,128)(2,1)}, u32[]{:S(2)}) copy-start(bf16[1,2,8,16,256]{4,3,2,1,0:T(8,128)(2,1)} %param.6) | copy-start | bytes 393220
  70.5 17.9 %all-to-all-start.3 = ((bf16[4,16,1152]{2,1,0:T(8,128)(2,1)}), bf16[4,16,1152]{2,1,0:T(8,128)(2,1)S(1)}, u32[]{:S(2)}, u32[]{:S(2)}) async-start(bf16[4,16,1152]{2,1,0:T(8,128)(2,1)} %shard_map.106), calls=%async_computation.3 | async-start | bytes 294912 | tf_op jit(solution)/shard_map/all_to_all | solution.py:418
  75.1 7.2 %collective-permute-start.5 = (bf16[256,256]{1,0:T(8,128)(2,1)S(1)}, bf16[256,256]{1,0:T(8,128)(2,1)S(1)}, u32[]{:S(2)}, u32[]{:S(2)}) collective-permute-start(bf16[256,256]{1,0:T(8,128)(2,1)S(1)} %get-tuple-element.25.spatial_ref), channel_id=1, source_target_pairs={{0,1},{1,2},{2,3},{3,4},{4,5},{5,6},{6,7},{7,8},{8,9},{9,10},{10,1... | collective-permute-start | bytes 393224 | tf_op jit(solution)/shard_map/ppermute | solution.py:388
  83.5 3.6 %collective-permute-start.8 = (f32[2,256]{1,0:T(2,128)S(1)}, f32[2,256]{1,0:T(2,128)S(1)}, u32[]{:S(2)}, u32[]{:S(2)}) collective-permute-start(f32[2,256]{1,0:T(2,128)S(1)} %get-tuple-element.32.refs_0_), channel_id=1, source_target_pairs={{0,16},{1,17},{2,18},{3,19},{4,20},{5,21},{6,22},{7,23},{8,24},{9,... | collective-permute-start | bytes 6152 | tf_op jit(solution)/shard_map/ppermute | solution.py:330

commit v3 on v1

--- a/solution.py
+++ b/solution.py
@@ -13,19 +13,20 @@
 F32 = jnp.float32
 BF16 = jnp.bfloat16
 VMEM = pl.BlockSpec(memory_space=pltpu.VMEM)
+HBM = pl.BlockSpec(memory_space=pltpu.HBM)
 NT = (((1,), (1,)), ((), ()))
 NN = (((1,), (0,)), ((), ()))
 
 
-def call(body, out_shapes, scratch=(), flops=0, moved=0):
+def call(body, out_shapes, scratch=(), flops=0, moved=0, in_specs=None, out_specs=None):
     many = isinstance(out_shapes, (tuple, list))
 
     def run(*operands):
         return pl.pallas_call(
             body,
             out_shape=out_shapes,
-            in_specs=[VMEM] * len(operands),
-            out_specs=[VMEM] * len(out_shapes) if many else VMEM,
+            in_specs=in_specs or [VMEM] * len(operands),
+            out_specs=out_specs or ([VMEM] * len(out_shapes) if many else VMEM),
             scratch_shapes=list(scratch),
             compiler_params=pltpu.CompilerParams(vmem_limit_bytes=40 * 1024 * 1024),
             cost_estimate=pl.CostEstimate(
@@ -54,12 +55,40 @@
     )
 
 
-def stats_body(lat_ref, out_ref):
+def stats_body(lat_ref, ws_ref, wt_ref, out_ref, half_ref, sem):
+    core = lax.rem(lax.axis_index("wide"), 2)
+    copies, place = [], 0
+    for at, source in enumerate((ws_ref, wt_ref)):
+        half = source.shape[0] // 2
+        start = pl.multiple_of(core * half, 16)
+        copies.append(
+            pltpu.make_async_copy(
+                source.at[pl.ds(start, half)], half_ref.at[pl.ds(place, half)], sem.at[at]
+            )
+        )
+        copies[-1].start()
+        place += half
     x = lat_ref[...].astype(F32)
     both = jnp.concatenate(
         [jnp.sum(x, axis=0, keepdims=True), jnp.sum(x * x, axis=0, keepdims=True)], axis=0
     )
     out_ref[...] = jnp.broadcast_to(both[None], out_ref.shape)
+    for copy in copies:
+        copy.wait()
+
+
+def fill_weights(full, shard_ref, pieces, offset, D):
+    d = lax.axis_index("dp")
+    core = lax.rem(lax.axis_index("wide"), 2)
+    n = shard_ref.shape[0]
+    half = n // 2
+    full[pl.ds(pl.multiple_of(d * n, 16), n)] = shard_ref[...]
+    for s in range(1, D):
+        source = lax.rem(d + D - s, D)
+        for which in range(2):
+            holder = core if which == 0 else 1 - core
+            start = pl.multiple_of(source * n + holder * half, 16)
+            full[pl.ds(start, half)] = pieces[2 * (s - 1) + which][offset : offset + half]
 
 
 def whiten(lat, stats, count, per_group):
@@ -102,25 +131,14 @@
     *rest,
 ):
     D, W, frames, cells, cols, count, per_group, aligned = sizes
-    pieces = rest[: 4 * (D - 1)]
-    rest = rest[4 * (D - 1) :]
+    pieces, rest = rest[: 2 * (D - 1)], rest[2 * (D - 1) :]
     spatial_ref, sums_ref, grad_ref, keep_ref, send_ref = rest[:5]
     full_ws, full_wt, act_pad, gsa_pad, gsa_t, cot_t = rest[5:]
     channels = lat_ref.shape[1]
-    d = lax.axis_index("dp")
     core = lax.rem(lax.axis_index("wide"), 2)
 
-    for shard_ref, full, offset in ((ws_ref, full_ws, 0), (wt_ref, full_wt, 1)):
-        n = shard_ref.shape[0]
-        full[pl.ds(pl.multiple_of(d * n, 16), n)] = shard_ref[...]
-        for s in range(1, D):
-            source = lax.rem(d + D - s, D)
-            for which in range(2):
-                piece = pieces[4 * (s - 1) + 2 * which + offset]
-                half = n // 2
-                holder = core if which == 0 else 1 - core
-                start = pl.multiple_of(source * n + holder * half, 16)
-                full[pl.ds(start, half)] = piece[...]
+    fill_weights(full_ws, ws_ref, pieces, 0, D)
+    fill_weights(full_wt, wt_ref, pieces, ws_ref.shape[0] // 2, D)
 
     cot = cot_ref[...]
     extended = jnp.concatenate([cot, halo_ref[...]], axis=0)
@@ -222,16 +240,7 @@
     pieces = rest[: 2 * (D - 1)]
     block_ref, glat_ref, norm_ref, full_wt = rest[2 * (D - 1) :]
     channels = lat_ref.shape[1]
-    d = lax.axis_index("dp")
-    core = lax.rem(lax.axis_index("wide"), 2)
-    n = wt_ref.shape[0]
-    full_wt[pl.ds(pl.multiple_of(d * n, 16), n)] = wt_ref[...]
-    for s in range(1, D):
-        source = lax.rem(d + D - s, D)
-        for which in range(2):
-            holder = core if which == 0 else 1 - core
-            start = pl.multiple_of(source * n + holder * (n // 2), 16)
-            full_wt[pl.ds(start, n // 2)] = pieces[2 * (s - 1) + which][...]
+    fill_weights(full_wt, wt_ref, pieces, pieces[0].shape[0] - wt_ref.shape[0] // 2, D)
     extended = jnp.concatenate([before_ref[...], spatial_ref[...]], axis=0)
     rows = frames * cells
     temporal = jnp.zeros((rows, channels), F32)
@@ -245,8 +254,9 @@
 
     white, inv_std = whiten(lat, stats_ref[...], count, per_group)
     gain = gain_ref[...]
-    total = jnp.sum(sums_ref[...], axis=0)
-    norm_ref[...] = total
+    d = lax.axis_index("dp")
+    total = jnp.sum(sums_ref[pl.ds(d * W, W)], axis=0)
+    norm_ref[...] = jnp.sum(sums_ref[...], axis=0)
     means = group_total(total * gain, per_group) / count
     inner = inv_std * (grad_ref[...] * gain - means[1:2] - white * means[0:1])
     glat_ref[...] = (cot_ref[...].astype(F32) + inner).astype(BF16)
@@ -285,13 +295,11 @@
     total = total * scale
     spatial_ref[...] = total[:, :split]
     temporal_ref[...] = total[:, split:]
-    norm_columns(scale, refs[terms:-3], norm_ref)
-
-
-def norm_columns(scale, terms, norm_ref):
-    norm = terms[0][...]
-    for term in terms[1:]:
-        norm += term[...]
+    norm_columns(scale, refs[terms], norm_ref)
+
+
+def norm_columns(scale, term_ref, norm_ref):
+    norm = term_ref[...]
     channels, width = norm.shape[1], norm_ref.shape[1]
     row = lax.broadcasted_iota(jnp.int32, (channels, width), 0)
     column = lax.broadcasted_iota(jnp.int32, (channels, width), 1)
@@ -304,8 +312,8 @@
     )
 
 
-def only_norm_body(scale, *refs):
-    norm_columns(scale, refs[:-1], refs[-1])
+def only_norm_body(scale, term_ref, norm_ref):
+    norm_columns(scale, term_ref, norm_ref)
 
 
 def local(latents, cotangent, norm_gain, norm_bias, w_spatial, w_temporal):
@@ -335,23 +343,22 @@
     def send(value, moves):
         return lax.ppermute(value, ("dp", "wide"), over_all(moves))
 
-    stats = call(stats_body, shape((W, 2, channels), F32))(lat)
+    R = shard_s + shard_t
+    stats, half = call(
+        stats_body,
+        [shape((W, 2, channels), F32), shape((R // 2, channels), BF16)],
+        [pltpu.SemaphoreType.DMA((2,))],
+        in_specs=[VMEM, HBM, HBM],
+    )(lat, w_spatial, w_temporal)
+    firsts = [send(half, lambda d, w: ((d + s) % D, w)) for s in range(1, D)]
+
+    halo = lax.ppermute(cot, "wide", [(w + 1, w) for w in range(W - 1)])
     stats = lax.all_to_all(stats, "wide", split_axis=0, concat_axis=0, tiled=True)
-
-    halo = lax.ppermute(cot, "wide", [(w + 1, w) for w in range(W - 1)])
-    core = lax.rem(lax.axis_index("wide"), 2)
-    half_s = lax.dynamic_slice_in_dim(w_spatial, core * (shard_s // 2), shard_s // 2, 0)
-    half_t = lax.dynamic_slice_in_dim(w_temporal, core * (shard_t // 2), shard_t // 2, 0)
-    pieces, pieces_t = [], []
-    for s in range(1, D):
-        here_t = send(half_t, lambda d, w: ((d + s) % D, w))
-        here_s = send(half_s, lambda d, w: ((d + s) % D, w))
-        there_t = send(here_t, lambda d, w: (d, w ^ 1))
-        there_s = send(here_s, lambda d, w: (d, w ^ 1))
-        pieces += [here_s, here_t, there_s, there_t]
-        pieces_t += [here_t, there_t]
-
-    R = shard_s + shard_t
+    firsts, stats = lax.optimization_barrier((firsts, stats))
+    pieces = []
+    for first in firsts:
+        pieces += [first, send(first, lambda d, w: (d, w ^ 1))]
+
     if aligned:
         grads = [shape((D, channels // 2, R), BF16)] * 2
     else:
@@ -360,7 +367,7 @@
         functools.partial(main_body, sizes),
         [
             shape((rows, channels), BF16),
-            shape((W, 2, channels), F32),
+            shape((D * W, 2, channels), F32),
             shape((rows, channels), F32),
         ]
         + grads,
@@ -376,7 +383,7 @@
         moved=5_000_000,
     )(lat, cot, halo, stats, gain, bias, w_spatial, w_temporal, *pieces)
 
-    sums = lax.all_to_all(sums, "wide", split_axis=0, concat_axis=0, tiled=True)
+    sums = lax.all_to_all(sums, ("dp", "wide"), split_axis=0, concat_axis=0, tiled=True)
     before = lax.ppermute(spatial, "wide", [(w, w + 1) for w in range(W - 1)])
 
     def finish():
@@ -390,7 +397,7 @@
             [pltpu.VMEM((D * shard_t, channels), BF16)],
             flops=2 * 3 * rows * channels * channels,
             moved=2_000_000,
-        )(lat, cot, stats, gain, grad, sums, spatial, before, w_temporal, *pieces_t)
+        )(lat, cot, stats, gain, grad, sums, spatial, before, w_temporal, *pieces)
 
     width = channels // W
     if aligned:
@@ -411,7 +418,6 @@
                     )
                 at += 1
         block_out, grad_latents, norm = finish()
-        norms = [norm] + [send(norm, lambda d, w: ((d + s) % D, w)) for s in range(1, D)]
         line = call(
             functools.partial(line_body, Z),
             [shape((width, R), BF16)] * Z,
@@ -427,12 +433,11 @@
                 shape((width, shard_t), F32),
                 shape((2, width), F32),
             ],
-        )(*terms, *norms)
+        )(*terms, norm)
         grad_s, grad_t = grad_s.T, grad_t.T
     else:
         block_out, grad_latents, norm = finish()
-        norms = [norm] + [send(norm, lambda d, w: ((d + s) % D, w)) for s in range(1, D)]
-        norm = call(functools.partial(only_norm_body, scale), shape((2, width), F32))(*norms)
+        norm = call(functools.partial(only_norm_body, scale), shape((2, width), F32))(norm)
         part = lax.psum_scatter(keep.astype(F32), "wide", scatter_dimension=0, tiled=True)
         part = part.T.astype(BF16)
         grad_s, grad_t = (

time: 60.2 us -> 53.2 us (0.88)
  waiting for transfers between devices: 17.5 us -> 9.53 us
  local copies, waits for them, and re-layouts: 2.79 us -> 3.58 us
    ppermute x12 -> x9, waiting for transfers between devices: 17.5 us -> 7.58 us  [send(): return lax.ppermute(value, ('dp', 'wide'), over_all(moves))]
    ppermute x1, waiting for transfers between devices: 0.01 us -> 1.94 us  [local(): halo = lax.ppermute(cot, 'wide', [(w + 1, w) for w in range(W - 1)])]
    unnamed x12 -> x16, local copies, waits for them, and re-layouts: 1.75 us -> 3.58 us
    dynamic_slice x2 -> x0, local copies, waits for them, and re-layouts: 1.04 us -> none  [the longest x1 1.03 us: local(): lax.dynamic_slice_in_dim(w_spatial, core * (shard_s // 2), shard_s // 2, 0)]
    ppermute x12 -> x9, starting transfers between devices: 14.6 us -> 14.9 us  [send(): return lax.ppermute(value, ('dp', 'wide'), over_all(moves))]
  transfers between devices with their start and end apart: 15 -> 12, of which waited for: 5 -> 6; matrix products, arithmetic and copies ran while one was open for 0% -> 0% of each run, Pallas kernels for 2% -> 3%
where the time goes in v3:
time: 53.2 us; the launch traced here: 52.8 us
  starting transfers between devices  21 us (39%)
  blocking collectives  12.5 us (23%)
  waiting for transfers between devices  9.53 us (18%)
  Pallas kernels  5.47 us (10%)
  local copies, waits for them, and re-layouts  3.58 us (7%)
  between operations  0.72 us (1%)
    ppermute x9, starting transfers between devices, send(): return lax.ppermute(value, ('dp', 'wide'), over_all(moves))  14.9 us
    all_to_all x1, blocking collectives, local(): lax.all_to_all(stats, 'wide', split_axis=0, concat_axis=0, tiled=True)  12.5 us
    ppermute x9, waiting for transfers between devices, send(): return lax.ppermute(value, ('dp', 'wide'), over_all(moves))  7.58 us
    pallas_call x6, Pallas kernels, run(): pl.pallas_call(body, out_shape=out_shapes, in_specs=in_specs or [VMEM] *...  5.47 us
    unnamed x16, local copies, waits for them, and re-layouts  3.58 us
    all_to_all x1, starting transfers between devices, local(): lax.all_to_all(sums, ('dp', 'wide'), split_axis=0, concat_axis=0, tiled=T...  3.44 us
    ppermute x1, waiting for transfers between devices, local(): halo = lax.ppermute(cot, 'wide', [(w + 1, w) for w in range(W - 1)])  1.94 us
    ppermute x1, starting transfers between devices, local(): before = lax.ppermute(spatial, 'wide', [(w, w + 1) for w in range(W - 1)])  1.42 us
  transfers between devices with their start and end apart: 12, of which 6 were waited for; matrix products, arithmetic and copies ran while one was open for 0% of the time, Pallas kernels for 3%

profile of v3, /device:TPU:0, one launch (start us, length us, event | category | flops | bytes accessed | tf_op | source)
XLA Modules:
  0.0 52.8 jit_solution(15919719458328921275)
XLA Ops:
  0.6 0.0 copy-start
  0.6 0.9 %copy-done = bf16[384,256]{1,0:T(8,128)(2,1)S(1)} copy-done((bf16[384,256]{1,0:T(8,128)(2,1)S(1)}, bf16[384,256]{1,0:T(8,128)(2,1)}, u32[]{:S(2)}) %copy-start) | copy-done | bytes 196632
  1.6 1.1 %copy-done.2 = bf16[1152,256]{1,0:T(8,128)(2,1)S(1)} copy-done((bf16[1152,256]{1,0:T(8,128)(2,1)S(1)}, bf16[1152,256]{1,0:T(8,128)(2,1)}, u32[]{:S(2)}) %copy-start.2) | copy-done | bytes 589848
  2.6 0.9 %copy-done.3 = bf16[1,2,8,16,256]{4,3,2,1,0:T(8,128)(2,1)S(1)} copy-done((bf16[1,2,8,16,256]{4,3,2,1,0:T(8,128)(2,1)S(1)}, bf16[1,2,8,16,256]{4,3,2,1,0:T(8,128)(2,1)}, u32[]{:S(2)}) %copy-start.3) | copy-done | bytes 131096
  3.5 0.3 shard_map.101
  3.8 3.0 %collective-permute-start = (bf16[768,256]{1,0:T(8,128)(2,1)S(1)}, bf16[768,256]{1,0:T(8,128)(2,1)S(1)}, u32[]{:S(2)}, u32[]{:S(2)}) collective-permute-start(bf16[768,256]{1,0:T(8,128)(2,1)S(1)} %get-tuple-element.28), channel_id=1, source_target_pairs={{0,16},{1,17},{2,18},{3,19},{4,20},{5,21},{6,22},{7,23},{8,24},{9,... | collective-permute-start | bytes 1179656 | tf_op jit(solution)/shard_map/ppermute | solution.py:344
  6.8 12.5 %all_to_all.10.stats_ref = f32[16,2,256]{2,1,0:T(2,128)S(1)} all-to-all(f32[16,2,256]{2,1,0:T(2,128)S(1)} %get-tuple-element.29), channel_id=1, replica_groups=mesh['dp'=2,'wide'=16] {'wide'}, dimensions={0} | all-to-all | bytes 65536 | tf_op jit(solution)/shard_map/all_to_all | solution.py:356
  19.3 0.0 collective-permute-done.rest_0_
  19.3 0.0 collective-permute-start.2
  19.3 1.3 %collective-permute-start.1 = (bf16[256,256]{1,0:T(8,128)(2,1)S(1)}, bf16[256,256]{1,0:T(8,128)(2,1)S(1)}, u32[]{:S(2)}, u32[]{:S(2)}) collective-permute-start(bf16[256,256]{1,0:T(8,128)(2,1)S(1)} %bitcast.15), channel_id=1, source_target_pairs={{1,0},{2,1},{3,2},{4,3},{5,4},{6,5},{7,6},{8,7},{9,8},{10,9},{11,1... | collective-permute-start | bytes 393224 | tf_op jit(solution)/shard_map/ppermute | solution.py:355
  20.6 1.9 %collective-permute-done.1.halo_ref = bf16[256,256]{1,0:T(8,128)(2,1)S(1)} collective-permute-done((bf16[256,256]{1,0:T(8,128)(2,1)S(1)}, bf16[256,256]{1,0:T(8,128)(2,1)S(1)}, u32[]{:S(2)}, u32[]{:S(2)}) %collective-permute-start.1) | collective-permute-done | bytes 131104 | tf_op jit(solution)/shard_map/ppermute | solution.py:355
  22.5 0.0 collective-permute-done.2.rest_1_
  22.6 0.7 %copy-done.6 = f32[256]{0:T(256)S(1)} copy-done((f32[256]{0:T(256)S(1)}, f32[256]{0:T(256)}, u32[]{:S(2)}) %copy-start.6) | copy-done | bytes 1048
  23.2 2.9 %shard_map.102 = (bf16[256,256]{1,0:T(8,128)(2,1)S(1)}, f32[32,2,256]{2,1,0:T(2,128)}, f32[256,256]{1,0:T(8,128)S(1)}, bf16[2,128,1536]{2,1,0:T(8,128)(2,1)S(1)}, bf16[2,128,1536]{2,1,0:T(8,128)(2,1)S(1)}) custom-call(bf16[256,256]{1,0:T(8,128)(2,1)S(1)} %bitcast.13, bf16[256,256]{1,0:T(8,128)(2,1)S(1)} %bitcast.16, ...), custom_call_target="tpu_custom_call" | custom-call | flops 1107296256 | bytes 5000000 | tf_op jit(solution)/shard_map/pallas_call | solution.py:25
  26.1 3.5 %collective-permute-start.4 = (bf16[2,128,1536]{2,1,0:T(8,128)(2,1)S(1)}, bf16[2,128,1536]{2,1,0:T(8,128)(2,1)S(1)}, u32[]{:S(2)}, u32[]{:S(2)}) collective-permute-start(bf16[2,128,1536]{2,1,0:T(8,128)(2,1)S(1)} %get-tuple-element.38), channel_id=1, source_target_pairs={{0,1},{1,0},{2,3},{3,2},{4,5},{5,4},{6,7},{7,6},{8,9},{9,8},{10,11... | collective-permute-start | bytes 2359304 | tf_op jit(solution)/shard_map/ppermute | solution.py:344
  29.7 1.9 %collective-permute-done.4 = bf16[2,128,1536]{2,1,0:T(8,128)(2,1)S(1)} collective-permute-done((bf16[2,128,1536]{2,1,0:T(8,128)(2,1)S(1)}, bf16[2,128,1536]{2,1,0:T(8,128)(2,1)S(1)}, u32[]{:S(2)}, u32[]{:S(2)}) %collective-permute-start.4) | collective-permute-done | bytes 786464 | tf_op jit(solution)/shard_map/ppermute | solution.py:344
  31.6 0.2 shard_map.104
  31.8 1.3 %collective-permute-start.5 = (bf16[4,16,1536]{2,1,0:T(8,128)(2,1)S(1)}, bf16[4,16,1536]{2,1,0:T(8,128)(2,1)S(1)}, u32[]{:S(2)}, u32[]{:S(2)}) collective-permute-start(bf16[4,16,1536]{2,1,0:T(8,128)(2,1)S(1)} %get-tuple-element.40), channel_id=1, source_target_pairs={{0,2},{1,3},{2,0},{3,1},{4,6},{5,7},{6,4},{7,5},{8,10},{9,11},{10,... | collective-permute-start | bytes 589832 | tf_op jit(solution)/shard_map/ppermute | solution.py:344
  33.1 0.5 %collective-permute-start.6 = (bf16[4,16,1536]{2,1,0:T(8,128)(2,1)S(1)}, bf16[4,16,1536]{2,1,0:T(8,128)(2,1)S(1)}, u32[]{:S(2)}, u32[]{:S(2)}) collective-permute-start(bf16[4,16,1536]{2,1,0:T(8,128)(2,1)S(1)} %get-tuple-element.41), channel_id=1, source_target_pairs={{0,16},{1,17},{2,18},{3,19},{4,20},{5,21},{6,22},{7,23},{8,24},{9,... | collective-permute-start | bytes 589832 | tf_op jit(solution)/shard_map/ppermute | solution.py:344
  33.6 1.7 %collective-permute-start.7 = (bf16[4,16,1536]{2,1,0:T(8,128)(2,1)S(1)}, bf16[4,16,1536]{2,1,0:T(8,128)(2,1)S(1)}, u32[]{:S(2)}, u32[]{:S(2)}) collective-permute-start(bf16[4,16,1536]{2,1,0:T(8,128)(2,1)S(1)} %get-tuple-element.42), channel_id=1, source_target_pairs={{0,18},{1,19},{2,16},{3,17},{4,22},{5,23},{6,20},{7,21},{8,26},{9,... | collective-permute-start | bytes 589832 | tf_op jit(solution)/shard_map/ppermute | solution.py:344
  35.3 1.4 %collective-permute-start.3 = (bf16[256,256]{1,0:T(8,128)(2,1)S(1)}, bf16[256,256]{1,0:T(8,128)(2,1)S(1)}, u32[]{:S(2)}, u32[]{:S(2)}) collective-permute-start(bf16[256,256]{1,0:T(8,128)(2,1)S(1)} %get-tuple-element.34.spatial_ref), channel_id=1, source_target_pairs={{0,1},{1,2},{2,3},{3,4},{4,5},{5,6},{6,7},{7,8},{8,9},{9,10},{10,1... | collective-permute-start | bytes 393224 | tf_op jit(solution)/shard_map/ppermute | solution.py:387
  36.8 3.4 %all-to-all-start.1 = ((f32[32,2,256]{2,1,0:T(2,128)}), f32[32,2,256]{2,1,0:T(2,128)S(1)}, u32[]{:S(2)}, u32[]{:S(2)}) async-start(f32[32,2,256]{2,1,0:T(2,128)} %get-tuple-element.33), calls=%async_computation.1 | async-start | bytes 131072 | tf_op jit(solution)/shard_map/all_to_all | solution.py:386
  40.2 0.6 %collective-permute-done.6.refs_2_ = bf16[4,16,1536]{2,1,0:T(8,128)(2,1)S(1)} collective-permute-done((bf16[4,16,1536]{2,1,0:T(8,128)(2,1)S(1)}, bf16[4,16,1536]{2,1,0:T(8,128)(2,1)S(1)}, u32[]{:S(2)}, u32[]{:S(2)}) %collective-permute-start.6) | collective-permute-done | bytes 196640 | tf_op jit(solution)/shard_map/ppermute | solution.py:344
  40.9 3.7 %collective-permute-done.7.refs_3_ = bf16[4,16,1536]{2,1,0:T(8,128)(2,1)S(1)} collective-permute-done((bf16[4,16,1536]{2,1,0:T(8,128)(2,1)S(1)}, bf16[4,16,1536]{2,1,0:T(8,128)(2,1)S(1)}, u32[]{:S(2)}, u32[]{:S(2)}) %collective-permute-start.7) | collective-permute-done | bytes 196640 | tf_op jit(solution)/shard_map/ppermute | solution.py:344
  44.6 0.1 shard_map.105
  44.7 2.0 %collective-permute-start.8 = (bf16[16,1536]{1,0:T(8,128)(2,1)S(1)}, bf16[16,1536]{1,0:T(8,128)(2,1)S(1)}, u32[]{:S(2)}, u32[]{:S(2)}) collective-permute-start(bf16[16,1536]{1,0:T(8,128)(2,1)S(1)} %get-tuple-element.44), channel_id=1, source_target_pairs={{0,4},{1,5},{2,6},{3,7},{4,8},{5,9},{6,10},{7,11},{8,12},{9,13},{1... | collective-permute-start | bytes 147464 | tf_op jit(solution)/shard_map/ppermute | solution.py:344
  46.7 0.3 collective-permute-start.9
  47.0 2.5 %collective-permute-start.10 = (bf16[16,1536]{1,0:T(8,128)(2,1)S(1)}, bf16[16,1536]{1,0:T(8,128)(2,1)S(1)}, u32[]{:S(2)}, u32[]{:S(2)}) collective-permute-start(bf16[16,1536]{1,0:T(8,128)(2,1)S(1)} %get-tuple-element.46), channel_id=1, source_target_pairs={{0,12},{1,13},{2,14},{3,15},{4,0},{5,1},{6,2},{7,3},{8,4},{9,5},{1... | collective-permute-start | bytes 147464 | tf_op jit(solution)/shard_map/ppermute | solution.py:344
  49.5 1.3 %shard_map.103 = (bf16[256,256]{1,0:T(8,128)(2,1)}, bf16[256,256]{1,0:T(8,128)(2,1)}, f32[2,256]{1,0:T(2,128)S(1)}) custom-call(bf16[256,256]{1,0:T(8,128)(2,1)S(1)} %bitcast.14, bf16[256,256]{1,0:T(8,128)(2,1)S(1)} %bitcast.17, f32[16,2,256]{2,1,0:T(2,128)S(1)} %all_to_all.10.stats_ref, f32[1,256]{1,0:T(1,128)S(1)} %bitcast.19, ...), custom_call_target="tpu_custom_call" | custom-call | flops 100663296 | bytes 2000000 | tf_op jit(solution)/shard_map/pallas_call | solution.py:25
  50.8 0.3 collective-permute-done.8.refs_1_
  51.1 1.0 %collective-permute-done.9.refs_2_ = bf16[16,1536]{1,0:T(8,128)(2,1)S(1)} collective-permute-done((bf16[16,1536]{1,0:T(8,128)(2,1)S(1)}, bf16[16,1536]{1,0:T(8,128)(2,1)S(1)}, u32[]{:S(2)}, u32[]{:S(2)}) %collective-permute-start.9) | collective-permute-done | bytes 49184 | tf_op jit(solution)/shard_map/ppermute | solution.py:344
  52.1 0.8 %shard_map.106 = (f32[16,1152]{1,0:T(8,128)}, f32[16,384]{1,0:T(8,128)}, f32[2,16]{1,0:T(2,128)}) custom-call(bf16[16,1536]{1,0:T(8,128)(2,1)S(1)} %get-tuple-element.43.refs_0_, bf16[16,1536]{1,0:T(8,128)(2,1)S(1)} %collective-permute-done.8.refs_1_, bf16[16,1536]{1,0:T(8,128)(2,1)S(1)} %collective-permute-done.9.refs_2_, ...), custom_call_target="tpu_custom_call" | custom-call | tf_op jit(solution)/shard_map/pallas_call | solution.py:25
  (15 shorter events, 0.0 us)
Async XLA Ops:
  0.6 0.9 %copy-start = (bf16[384,256]{1,0:T(8,128)(2,1)S(1)}, bf16[384,256]{1,0:T(8,128)(2,1)}, u32[]{:S(2)}) copy-start(bf16[384,256]{1,0:T(8,128)(2,1)} %wt_ref.5) | copy-start | bytes 589828
  1.6 1.1 %copy-start.2 = (bf16[1152,256]{1,0:T(8,128)(2,1)S(1)}, bf16[1152,256]{1,0:T(8,128)(2,1)}, u32[]{:S(2)}) copy-start(bf16[1152,256]{1,0:T(8,128)(2,1)} %ws_ref.3) | copy-start | bytes 1769476
  2.6 0.9 %copy-start.3 = (bf16[1,2,8,16,256]{4,3,2,1,0:T(8,128)(2,1)S(1)}, bf16[1,2,8,16,256]{4,3,2,1,0:T(8,128)(2,1)}, u32[]{:S(2)}) copy-start(bf16[1,2,8,16,256]{4,3,2,1,0:T(8,128)(2,1)} %param.6) | copy-start | bytes 393220
  3.5 15.8 %copy-start.5 = (bf16[1,2,8,16,256]{4,3,2,1,0:T(8,128)(2,1)S(1)}, bf16[1,2,8,16,256]{4,3,2,1,0:T(8,128)(2,1)}, u32[]{:S(2)}) copy-start(bf16[1,2,8,16,256]{4,3,2,1,0:T(8,128)(2,1)} %param.7) | copy-start | bytes 393220
  3.8 15.5 %collective-permute-start = (bf16[768,256]{1,0:T(8,128)(2,1)S(1)}, bf16[768,256]{1,0:T(8,128)(2,1)S(1)}, u32[]{:S(2)}, u32[]{:S(2)}) collective-permute-start(bf16[768,256]{1,0:T(8,128)(2,1)S(1)} %get-tuple-element.28), channel_id=1, source_target_pairs={{0,16},{1,17},{2,18},{3,19},{4,20},{5,21},{6,22},{7,23},{8,24},{9,... | collective-permute-start | bytes 1179656 | tf_op jit(solution)/shard_map/ppermute | solution.py:344
  6.8 15.8 %copy-start.7 = (f32[256]{0:T(256)S(1)}, f32[256]{0:T(256)}, u32[]{:S(2)}) copy-start(f32[256]{0:T(256)} %param.9) | copy-start | bytes 3076
  19.3 3.3 %collective-permute-start.2 = (bf16[768,256]{1,0:T(8,128)(2,1)S(1)}, bf16[768,256]{1,0:T(8,128)(2,1)S(1)}, u32[]{:S(2)}, u32[]{:S(2)}) collective-permute-start(bf16[768,256]{1,0:T(8,128)(2,1)S(1)} %collective-permute-done.rest_0_), channel_id=1, source_target_pairs={{0,1},{1,0},{2,3},{3,2},{4,5},{5,4},{6,7},{7,6},{8,9},{9,8},{10,11... | collective-permute-start | bytes 1179656 | tf_op jit(solution)/shard_map/ppermute | solution.py:344
  19.3 3.2 %collective-permute-start.1 = (bf16[256,256]{1,0:T(8,128)(2,1)S(1)}, bf16[256,256]{1,0:T(8,128)(2,1)S(1)}, u32[]{:S(2)}, u32[]{:S(2)}) collective-permute-start(bf16[256,256]{1,0:T(8,128)(2,1)S(1)} %bitcast.15), channel_id=1, source_target_pairs={{1,0},{2,1},{3,2},{4,3},{5,4},{6,5},{7,6},{8,7},{9,8},{10,9},{11,1... | collective-permute-start | bytes 393224 | tf_op jit(solution)/shard_map/ppermute | solution.py:355
  22.6 0.7 %copy-start.6 = (f32[256]{0:T(256)S(1)}, f32[256]{0:T(256)}, u32[]{:S(2)}) copy-start(f32[256]{0:T(256)} %param.8) | copy-start | bytes 3076
  26.1 5.4 %collective-permute-start.4 = (bf16[2,128,1536]{2,1,0:T(8,128)(2,1)S(1)}, bf16[2,128,1536]{2,1,0:T(8,128)(2,1)S(1)}, u32[]{:S(2)}, u32[]{:S(2)}) collective-permute-start(bf16[2,128,1536]{2,1,0:T(8,128)(2,1)S(1)} %get-tuple-element.38), channel_id=1, source_target_pairs={{0,1},{1,0},{2,3},{3,2},{4,5},{5,4},{6,7},{7,6},{8,9},{9,8},{10,11... | collective-permute-start | bytes 2359304 | tf_op jit(solution)/shard_map/ppermute | solution.py:344
  31.8 8.4 %collective-permute-start.5 = (bf16[4,16,1536]{2,1,0:T(8,128)(2,1)S(1)}, bf16[4,16,1536]{2,1,0:T(8,128)(2,1)S(1)}, u32[]{:S(2)}, u32[]{:S(2)}) collective-permute-start(bf16[4,16,1536]{2,1,0:T(8,128)(2,1)S(1)} %get-tuple-element.40), channel_id=1, source_target_pairs={{0,2},{1,3},{2,0},{3,1},{4,6},{5,7},{6,4},{7,5},{8,10},{9,11},{10,... | collective-permute-start | bytes 589832 | tf_op jit(solution)/shard_map/ppermute | solution.py:344
  33.1 7.8 %collective-permute-start.6 = (bf16[4,16,1536]{2,1,0:T(8,128)(2,1)S(1)}, bf16[4,16,1536]{2,1,0:T(8,128)(2,1)S(1)}, u32[]{:S(2)}, u32[]{:S(2)}) collective-permute-start(bf16[4,16,1536]{2,1,0:T(8,128)(2,1)S(1)} %get-tuple-element.41), channel_id=1, source_target_pairs={{0,16},{1,17},{2,18},{3,19},{4,20},{5,21},{6,22},{7,23},{8,24},{9,... | collective-permute-start | bytes 589832 | tf_op jit(solution)/shard_map/ppermute | solution.py:344
  33.6 11.0 %collective-permute-start.7 = (bf16[4,16,1536]{2,1,0:T(8,128)(2,1)S(1)}, bf16[4,16,1536]{2,1,0:T(8,128)(2,1)S(1)}, u32[]{:S(2)}, u32[]{:S(2)}) collective-permute-start(bf16[4,16,1536]{2,1,0:T(8,128)(2,1)S(1)} %get-tuple-element.42), channel_id=1, source_target_pairs={{0,18},{1,19},{2,16},{3,17},{4,22},{5,23},{6,20},{7,21},{8,26},{9,... | collective-permute-start | bytes 589832 | tf_op jit(solution)/shard_map/ppermute | solution.py:344
  35.3 14.1 %collective-permute-start.3 = (bf16[256,256]{1,0:T(8,128)(2,1)S(1)}, bf16[256,256]{1,0:T(8,128)(2,1)S(1)}, u32[]{:S(2)}, u32[]{:S(2)}) collective-permute-start(bf16[256,256]{1,0:T(8,128)(2,1)S(1)} %get-tuple-element.34.spatial_ref), channel_id=1, source_target_pairs={{0,1},{1,2},{2,3},{3,4},{4,5},{5,6},{6,7},{7,8},{8,9},{9,10},{10,1... | collective-permute-start | bytes 393224 | tf_op jit(solution)/shard_map/ppermute | solution.py:387
  36.8 12.7 %all-to-all-start.1 = ((f32[32,2,256]{2,1,0:T(2,128)}), f32[32,2,256]{2,1,0:T(2,128)S(1)}, u32[]{:S(2)}, u32[]{:S(2)}) async-start(f32[32,2,256]{2,1,0:T(2,128)} %get-tuple-element.33), calls=%async_computation.1 | async-start | bytes 131072 | tf_op jit(solution)/shard_map/all_to_all | solution.py:386
  44.6 4.9 %copy-start.1 = (bf16[384,256]{1,0:T(8,128)(2,1)S(1)}, bf16[384,256]{1,0:T(8,128)(2,1)}, u32[]{:S(2)}) copy-start(bf16[384,256]{1,0:T(8,128)(2,1)} %wt_ref.5) | copy-start | bytes 589828
  44.6 4.9 %copy-start.4 = (bf16[1,2,8,16,256]{4,3,2,1,0:T(8,128)(2,1)S(1)}, bf16[1,2,8,16,256]{4,3,2,1,0:T(8,128)(2,1)}, u32[]{:S(2)}) copy-start(bf16[1,2,8,16,256]{4,3,2,1,0:T(8,128)(2,1)} %param.6) | copy-start | bytes 393220
  44.7 6.4 %collective-permute-start.8 = (bf16[16,1536]{1,0:T(8,128)(2,1)S(1)}, bf16[16,1536]{1,0:T(8,128)(2,1)S(1)}, u32[]{:S(2)}, u32[]{:S(2)}) collective-permute-start(bf16[16,1536]{1,0:T(8,128)(2,1)S(1)} %get-tuple-element.44), channel_id=1, source_target_pairs={{0,4},{1,5},{2,6},{3,7},{4,8},{5,9},{6,10},{7,11},{8,12},{9,13},{1... | collective-permute-start | bytes 147464 | tf_op jit(solution)/shard_map/ppermute | solution.py:344
  46.7 5.4 %collective-permute-start.9 = (bf16[16,1536]{1,0:T(8,128)(2,1)S(1)}, bf16[16,1536]{1,0:T(8,128)(2,1)S(1)}, u32[]{:S(2)}, u32[]{:S(2)}) collective-permute-start(bf16[16,1536]{1,0:T(8,128)(2,1)S(1)} %get-tuple-element.45), channel_id=1, source_target_pairs={{0,8},{1,9},{2,10},{3,11},{4,12},{5,13},{6,14},{7,15},{8,0},{9,1},... | collective-permute-start | bytes 147464 | tf_op jit(solution)/shard_map/ppermute | solution.py:344
  47.0 5.0 %collective-permute-start.10 = (bf16[16,1536]{1,0:T(8,128)(2,1)S(1)}, bf16[16,1536]{1,0:T(8,128)(2,1)S(1)}, u32[]{:S(2)}, u32[]{:S(2)}) collective-permute-start(bf16[16,1536]{1,0:T(8,128)(2,1)S(1)} %get-tuple-element.46), channel_id=1, source_target_pairs={{0,12},{1,13},{2,14},{3,15},{4,0},{5,1},{6,2},{7,3},{8,4},{9,5},{1... | collective-permute-start | bytes 147464 | tf_op jit(solution)/shard_map/ppermute | solution.py:344

commit v4 on v2

v4 whole, which is shorter than its diff:
```python
import functools
import math

import jax
import jax.numpy as jnp
from jax import lax
from jax.experimental import pallas as pl
from jax.experimental.pallas import tpu as pltpu
from jax.sharding import PartitionSpec as P

GROUPS = 32
EPSILON = 1e-05
F32 = jnp.float32
BF16 = jnp.bfloat16
VMEM = pl.BlockSpec(memory_space=pltpu.VMEM)
HBM = pl.BlockSpec(memory_space=pltpu.HBM)
NT = (((1,), (1,)), ((), ()))
NN = (((1,), (0,)), ((), ()))


def call(body, out_shapes, scratch=(), flops=0, moved=0, in_specs=None, vmem=40):
    many = isinstance(out_shapes, (tuple, list))

    def run(*operands):
        return pl.pallas_call(
            body,
            out_shape=out_shapes,
            in_specs=in_specs or [VMEM] * len(operands),
            out_specs=[VMEM] * len(out_shapes) if many else VMEM,
            scratch_shapes=list(scratch),
            compiler_params=pltpu.CompilerParams(vmem_limit_bytes=vmem * 1024 * 1024),
            cost_estimate=pl.CostEstimate(
                flops=flops, bytes_accessed=moved, transcendentals=0
            ),
        )(*operands)

    return run


def shape(dims, kind):
    return jax.ShapeDtypeStruct(dims, kind)


def mm(left, right, dims=NN):
    return lax.dot_general(left, right, dims, preferred_element_type=F32)


def group_total(rows, per_group):
    channels = rows.shape[-1]
    first = lax.broadcasted_iota(jnp.int32, (channels, channels), 0) // per_group
    second = lax.broadcasted_iota(jnp.int32, (channels, channels), 1) // per_group
    same = (first == second).astype(F32)
    return lax.dot_general(
        rows, same, NN, precision=lax.Precision.HIGHEST, preferred_element_type=F32
    )


def stats_body(lat_ref, gain_ref, bias_ref, ws_ref, wt_ref, out_ref, affine_ref, half_ref, sem):
    core = lax.rem(lax.axis_index("wide"), 2)
    copies, place = [], 0
    for at, source in enumerate((ws_ref, wt_ref)):
        half = source.shape[0] // 2
        start = pl.multiple_of(core * half, 16)
        copies.append(
            pltpu.make_async_copy(
                source.at[pl.ds(start, half)], half_ref.at[pl.ds(place, half)], sem.at[at]
            )
        )
        copies[-1].start()
        place += half
    affine_ref[0:1] = gain_ref[...]
    affine_ref[1:2] = bias_ref[...]
    x = lat_ref[...].astype(F32)
    both = jnp.concatenate(
        [jnp.sum(x, axis=0, keepdims=True), jnp.sum(x * x, axis=0, keepdims=True)], axis=0
    )
    out_ref[...] = jnp.broadcast_to(both[None], out_ref.shape)
    for copy in copies:
        copy.wait()


def fill_weights(full, shard_ref, pieces, offset, D):
    d = lax.axis_index("dp")
    core = lax.rem(lax.axis_index("wide"), 2)
    n = shard_ref.shape[0]
    half = n // 2
    full[pl.ds(pl.multiple_of(d * n, 16), n)] = shard_ref[...]
    for s in range(1, D):
        source = lax.rem(d + D - s, D)
        for which in range(2):
            holder = core if which == 0 else 1 - core
            start = pl.multiple_of(source * n + holder * half, 16)
            full[pl.ds(start, half)] = pieces[2 * (s - 1) + which][offset : offset + half]


def whiten(lat, stats, count, per_group):
    total = group_total(jnp.sum(stats, axis=0), per_group) / count
    mean = total[0:1]
    inv_std = 1.0 / jnp.sqrt(total[1:2] - mean * mean + EPSILON)
    return (lat.astype(F32) - mean) * inv_std, inv_std


def store_shifted(pad_ref, values, frames, cells, cols):
    total = frames * cells
    column = lax.broadcasted_iota(jnp.int32, (total, 1), 0) % cols
    left = jnp.where(column == 0, 0.0, pltpu.roll(values, 1, 0))
    right = jnp.where(column == cols - 1, 0.0, pltpu.roll(values, total - 1, 0))
    edge = jnp.zeros((cols, values.shape[1]), BF16)
    for at, form in enumerate((left, values, right)):
        low = form.astype(BF16)
        for f in range(frames):
            pad_ref[at, f, 0:cols] = edge
            pad_ref[at, f, cols : cols + cells] = low[f * cells : (f + 1) * cells]
            pad_ref[at, f, cols + cells :] = edge


def window(pad_ref, dy, dx, frames, cells, cols):
    return jnp.concatenate(
        [pad_ref[dx, f, dy * cols : dy * cols + cells] for f in range(frames)], axis=0
    )


def in_parts(total):
    high = total.astype(BF16).astype(F32)
    return jnp.concatenate([high, total - high], axis=0).astype(BF16)


def from_parts(terms):
    total = 0.0
    for term in terms:
        wide = term.astype(F32)
        total = total + (wide[0:8] + wide[8:16])
    return total


def add(terms):
    total = terms[0].astype(F32)
    for term in terms[1:]:
        total += term.astype(F32)
    return total


def core_order(transposed_ref, W, core):
    step = transposed_ref.shape[0] // W
    order = [(2 * j + core) * step for j in range(W // 2)]
    order += [(2 * j + 1 - core) * step for j in range(W // 2)]
    return jnp.concatenate(
        [transposed_ref[pl.ds(pl.multiple_of(at, 16), step)] for at in order], axis=0
    )


def put(block, column, shard, keep_ref, send_ref):
    low = block.astype(BF16)
    if send_ref is None:
        keep_ref[:, column : column + block.shape[1]] = low
        return
    half = block.shape[0] // 2
    for at in range(0, block.shape[1], 128):
        owner, place = (column + at) // shard, (column + at) % shard
        keep_ref[owner, :, place : place + 128] = low[:half, at : at + 128]
        send_ref[owner, :, place : place + 128] = low[half:, at : at + 128]


def normalise(lat_ref, stats_ref, affine_ref, count, per_group):
    white, inv_std = whiten(lat_ref[...], stats_ref[...], count, per_group)
    normed = white * affine_ref[0:1] + affine_ref[1:2]
    return white, normed, jax.nn.sigmoid(normed)


def first_body(sizes, lat_ref, cot_ref, halo_ref, stats_ref, affine_ref, wt_ref, *rest):
    D, W, frames, cells, cols, count, per_group, aligned = sizes
    pieces, rest = rest[: 2 * (D - 1)], rest[2 * (D - 1) :]
    full_wt, act_pad, gsa_t = rest[-3:]
    gsa_ref, keep_ref = rest[:2]
    send_ref = rest[2] if aligned else None
    channels = lat_ref.shape[1]
    core = lax.rem(lax.axis_index("wide"), 2)
    fill_weights(full_wt, wt_ref, pieces, pieces[0].shape[0] - wt_ref.shape[0] // 2, D)
    rows = frames * cells
    extended = jnp.concatenate([cot_ref[...], halo_ref[...]], axis=0)
    gsa = jnp.zeros((rows, channels), F32)
    for k in range(3):
        gsa += mm(
            extended[k * cells : k * cells + rows],
            full_wt[k * channels : (k + 1) * channels],
            NT,
        )
    gsa_ref[...] = gsa.astype(BF16)
    gsa_t[...] = gsa.astype(BF16).astype(F32).T.astype(BF16)
    _, normed, sig = normalise(lat_ref, stats_ref, affine_ref, count, per_group)
    act = (normed * sig).astype(BF16).astype(F32)
    store_shifted(act_pad, act, frames, cells, cols)
    left = core_order(gsa_t, W, core) if aligned else gsa_t[...]
    shard = wt_ref.shape[0] * 3
    for dy in range(3):
        for dx in range(3):
            seen = window(act_pad, dy, dx, frames, cells, cols)
            put(mm(left, seen), (3 * dy + dx) * channels, shard, keep_ref, send_ref)


def second_body(
    sizes, lat_ref, cot_ref, halo_ref, stats_ref, affine_ref, gsa_ref, ws_ref, *rest
):
    D, W, frames, cells, cols, count, per_group, aligned = sizes
    pieces, rest = rest[: 2 * (D - 1)], rest[2 * (D - 1) :]
    full_ws, act_pad, gsa_pad, cot_t = rest[-4:]
    spatial_ref, grad_ref, keep_ref, other_ref = rest[:4]
    send_ref = other_ref if aligned else None
    channels = lat_ref.shape[1]
    core = lax.rem(lax.axis_index("wide"), 2)
    fill_weights(full_ws, ws_ref, pieces, 0, D)
    rows = frames * cells
    white, normed, sig = normalise(lat_ref, stats_ref, affine_ref, count, per_group)
    act = (normed * sig).astype(BF16).astype(F32)
    store_shifted(act_pad, act, frames, cells, cols)
    store_shifted(gsa_pad, gsa_ref[...].astype(F32), frames, cells, cols)
    extended = jnp.concatenate([cot_ref[...], halo_ref[...]], axis=0)
    for f in range(frames + 2):
        cot_t[:, f * cells : (f + 1) * cells] = (
            extended[f * cells : (f + 1) * cells].astype(F32).T.astype(BF16)
        )
    left = core_order(cot_t, W, core) if aligned else cot_t[...]
    out = jnp.zeros((rows, channels), F32)
    for dy in range(3):
        for dx in range(3):
            tap = 3 * dy + dx
            seen = window(act_pad, dy, dx, frames, cells, cols)
            out += mm(seen, full_ws[tap * channels : (tap + 1) * channels])
    spatial = out.astype(BF16)
    spatial_ref[...] = spatial
    shard = ws_ref.shape[0] // 3
    for k in range(3):
        block = mm(left[:, k * cells : k * cells + rows], spatial)
        put(block, k * channels, shard, keep_ref, send_ref)

    grad = jnp.zeros((rows, channels), F32)
    for dy in range(3):
        for dx in range(3):
            tap = 3 * dy + dx
            seen = window(gsa_pad, 2 - dy, 2 - dx, frames, cells, cols)
            grad += mm(seen, full_ws[tap * channels : (tap + 1) * channels], NT)
    grad = grad * (sig * (1.0 + normed * (1.0 - sig)))
    grad_ref[...] = grad
    gain_term = jnp.sum(grad * white, axis=0, keepdims=True)
    bias_term = jnp.sum(grad, axis=0, keepdims=True)
    if not aligned:
        both = jnp.concatenate([gain_term, bias_term], axis=0)
        other_ref[...] = jnp.broadcast_to(both[None], other_ref.shape)
        return
    d = lax.axis_index("dp")
    quarter = jnp.concatenate(
        [term[:, at : at + 128] for term in (gain_term, bias_term) for at in (0, 128)], axis=0
    )
    low = in_parts(
        jnp.concatenate([jnp.where(d == s, quarter, 0.0) for s in range(2)], axis=0)
    )
    for target in (keep_ref, send_ref):
        for owner in range(D):
            for at in range(0, channels // 2, 16):
                target[owner, at : at + 16, shard:] = low


def block_body(sizes, lat_ref, spatial_ref, before_ref, wt_ref, *rest):
    D, W, frames, cells, cols, count, per_group, aligned = sizes
    pieces = rest[: 2 * (D - 1)]
    block_ref, full_wt = rest[2 * (D - 1) :]
    channels = lat_ref.shape[1]
    fill_weights(full_wt, wt_ref, pieces, pieces[0].shape[0] - wt_ref.shape[0] // 2, D)
    extended = jnp.concatenate([before_ref[...], spatial_ref[...]], axis=0)
    rows = frames * cells
    temporal = jnp.zeros((rows, channels), F32)
    for k in range(3):
        start = (2 - k) * cells
        temporal += mm(
            extended[start : start + rows], full_wt[k * channels : (k + 1) * channels]
        )
    block_ref[...] = (lat_ref[...].astype(F32) + temporal).astype(BF16)


def latent_gradient(sizes, total, lat_ref, cot_ref, stats_ref, affine_ref, grad_ref):
    D, W, frames, cells, cols, count, per_group, aligned = sizes
    white, inv_std = whiten(lat_ref[...], stats_ref[...], count, per_group)
    gain = affine_ref[0:1]
    means = group_total(total * gain, per_group) / count
    inner = inv_std * (grad_ref[...] * gain - means[1:2] - white * means[0:1])
    return (cot_ref[...].astype(F32) + inner).astype(BF16)


def plane_body(keep_s, got_s, keep_t, got_t, *outs):
    d = lax.axis_index("dp")
    y = lax.rem(lax.axis_index("wide") // 2, 2)
    split = keep_s.shape[-1]
    ride = outs[0].shape[-1] - 128
    for a in range(2):
        for b in range(2):
            owner, side = lax.rem(d + a, 2), lax.rem(y + b, 2)
            out = outs[2 * a + b]
            for z in range(out.shape[0]):
                out[z, :, :split] = add([keep_s[owner, z, side], got_s[owner, z, side]]).astype(
                    BF16
                )
                both = [keep_t[owner, z, side], got_t[owner, z, side]]
                out[z, :, split:ride] = add([t[:, : ride - split] for t in both]).astype(BF16)
                out[z, :, ride:] = in_parts(from_parts([t[:, ride - split :] for t in both]))


def line_body(depth, *refs):
    terms, outs = refs[:4], refs[4:]
    z = lax.axis_index("wide") // 4
    ride = outs[0].shape[-1] - 128
    for s in range(depth):
        owner = lax.rem(z + s, depth)
        seen = [term[owner] for term in terms]
        outs[s][:, :ride] = add([t[:, :ride] for t in seen]).astype(BF16)
        outs[s][:, ride:] = in_parts(from_parts([t[:, ride:] for t in seen]))


def last_body(sizes, scale, depth, *refs):
    terms, operands, outs = refs[:depth], refs[depth:-4], refs[-4:]
    spatial_ref, temporal_ref, norm_ref, glat_ref = outs
    split = spatial_ref.shape[1]
    ride = terms[0].shape[1] - 128
    sums = from_parts([term[:, ride:] for term in terms])

    def rows_of(part):
        return jnp.concatenate(
            [jnp.concatenate([part[at : at + 1], part[at + 1 : at + 2]], axis=1) for at in (0, 2)],
            axis=0,
        )

    first, second = rows_of(sums[0:4]), rows_of(sums[4:8])
    own = jnp.where(lax.axis_index("dp") == 0, first, second)
    glat_ref[...] = latent_gradient(sizes, own, *operands)
    norm_columns(scale, first + second, norm_ref)
    total = add([term[:, :ride] for term in terms]) * scale
    spatial_ref[...] = total[:, :split]
    temporal_ref[...] = total[:, split:]


def apart_body(sizes, scale, sums_ref, *refs):
    norm_ref, glat_ref = refs[-2:]
    W = sizes[1]
    own = jnp.sum(sums_ref[pl.ds(lax.axis_index("dp") * W, W)], axis=0)
    norm_columns(scale, jnp.sum(sums_ref[...], axis=0), norm_ref)
    glat_ref[...] = latent_gradient(sizes, own, *refs[:-2])


def norm_columns(scale, norm, norm_ref):
    channels, width = norm.shape[1], norm_ref.shape[1]
    row = lax.broadcasted_iota(jnp.int32, (channels, width), 0)
    column = lax.broadcasted_iota(jnp.int32, (channels, width), 1)
    pick = (row == column + lax.axis_index("wide") * width).astype(F32)
    norm_ref[...] = (
        lax.dot_general(
            norm, pick, NN, precision=lax.Precision.HIGHEST, preferred_element_type=F32
        )
        * scale
    )


def local(latents, cotangent, norm_gain, norm_bias, w_spatial, w_temporal):
    D, W = lax.axis_size("dp"), lax.axis_size("wide")
    _, frames, rows_here, cols, channels = latents.shape
    cells = rows_here * cols
    rows = frames * cells
    per_group = channels // GROUPS
    count = W * frames * cells * per_group
    shard_s, shard_t = w_spatial.shape[0], w_temporal.shape[0]
    aligned = (channels // W) % 16 == 0 and shard_s % 128 == 0 and shard_t % 128 == 0
    aligned = aligned and W % 4 == 0 and D == 2 and channels == 256
    sizes = (D, W, frames, cells, cols, count, per_group, aligned)
    scale = 1.0 / math.sqrt(D * W * frames * cells)

    lat, cot = latents.reshape(rows, channels), cotangent.reshape(rows, channels)
    gain, bias = norm_gain.reshape(1, channels), norm_bias.reshape(1, channels)

    def over_all(moves):
        pairs = []
        for d in range(D):
            for w in range(W):
                to = moves(d, w)
                pairs.append((d * W + w, to[0] * W + to[1]))
        return pairs

    def send(value, moves):
        return lax.ppermute(value, ("dp", "wide"), over_all(moves))

    R = shard_s + shard_t
    stats, affine, half = call(
        stats_body,
        [
            shape((W, 2, channels), F32),
            shape((2, channels), F32),
            shape((R // 2, channels), BF16),
        ],
        [pltpu.SemaphoreType.DMA((2,))],
        in_specs=[VMEM, VMEM, VMEM, HBM, HBM],
        vmem=60,
    )(lat, gain, bias, w_spatial, w_temporal)
    firsts = [send(half, lambda d, w: ((d + s) % D, w)) for s in range(1, D)]

    halo = lax.ppermute(cot, "wide", [(w + 1, w) for w in range(W - 1)])
    stats = lax.all_to_all(stats, "wide", split_axis=0, concat_axis=0, tiled=True)
    firsts, stats, halo = lax.optimization_barrier((firsts, stats, halo))
    pieces = []
    for first in firsts:
        pieces += [first, send(first, lambda d, w: (d, w ^ 1))]

    ride = 128 if aligned else 0
    if aligned:
        terms_s = [shape((D, channels // 2, shard_s), BF16)] * 2
        terms_t = [shape((D, channels // 2, shard_t + ride), BF16)] * 2
    else:
        terms_s = [shape((channels, D * shard_s), BF16)]
        terms_t = [shape((channels, D * shard_t), BF16), shape((D * W, 2, channels), F32)]
    pad = pltpu.VMEM((3, frames, cells + 2 * cols, channels), BF16)
    gsa, *grads_s = call(
        functools.partial(first_body, sizes),
        [shape((rows, channels), BF16)] + terms_s,
        [pltpu.VMEM((D * shard_t, channels), BF16), pad, pltpu.VMEM((channels, rows), BF16)],
        flops=2 * 12 * rows * channels * channels,
        moved=3_000_000,
    )(lat, cot, halo, stats, affine, w_temporal, *pieces)
    spatial, grad, *grads_t = call(
        functools.partial(second_body, sizes),
        [shape((rows, channels), BF16), shape((rows, channels), F32)] + terms_t,
        [
            pltpu.VMEM((D * shard_s, channels), BF16),
            pad,
            pad,
            pltpu.VMEM((channels, rows + 2 * cells), BF16),
        ],
        flops=2 * 21 * rows * channels * channels,
        moved=3_000_000,
    )(lat, cot, halo, stats, affine, gsa, w_spatial, *pieces)
    before = lax.ppermute(spatial, "wide", [(w, w + 1) for w in range(W - 1)])
    block_out = call(
        functools.partial(block_body, sizes),
        shape((rows, channels), BF16),
        [pltpu.VMEM((D * shard_t, channels), BF16)],
        flops=2 * 3 * rows * channels * channels,
        moved=1_000_000,
    )(lat, spatial, before, w_temporal, *pieces)

    width = channels // W
    operands = (lat, cot, stats, affine, grad)
    if aligned:
        Z = W // 4

        def over_core(away):
            return send(away, lambda d, w: (d, w ^ 1))

        pairs = []
        for keep, away in (grads_s, grads_t):
            view = (D, Z, 2, width, keep.shape[-1])
            pairs += [keep.reshape(view), over_core(away).reshape(view)]
        plane = call(
            plane_body, [shape((Z, width, R + ride), BF16)] * (2 * D), moved=3_000_000
        )(*pairs)
        seen = [plane[0]] + [
            send(plane[2 * a + b], lambda d, w: ((d + a) % D, w ^ (2 * b)))
            for a, b in ((0, 1), (1, 0), (1, 1))
        ]
        line = call(
            functools.partial(line_body, Z),
            [shape((width, R + ride), BF16)] * Z,
            moved=1_000_000,
        )(*seen)
        terms = [line[0]]
        for s in range(1, Z):
            terms.append(send(line[s], lambda d, w: (d, (w + 4 * s) % W)))
        grad_s, grad_t, norm, grad_latents = call(
            functools.partial(last_body, sizes, scale, Z),
            [
                shape((width, shard_s), F32),
                shape((width, shard_t), F32),
                shape((2, width), F32),
                shape((rows, channels), BF16),
            ],
            moved=1_000_000,
        )(*terms, *operands)
        grad_s, grad_t = grad_s.T, grad_t.T
    else:
        sums = lax.all_to_all(
            grads_t[1], ("dp", "wide"), split_axis=0, concat_axis=0, tiled=True
        )
        norm, grad_latents = call(
            functools.partial(apart_body, sizes, scale),
            [shape((2, width), F32), shape((rows, channels), BF16)],
        )(sums, *operands)
        outs = []
        for full in (grads_s[0], grads_t[0]):
            part = lax.psum_scatter(
                full.astype(F32), "wide", scatter_dimension=0, tiled=True
            ).T.astype(BF16)
            part = lax.psum_scatter(part, "dp", scatter_dimension=0, tiled=True)
            outs.append(part.astype(F32) * scale)
        grad_s, grad_t = outs
    return (
        block_out.reshape(latents.shape),
        grad_latents.reshape(latents.shape),
        grad_s,
        grad_t,
        norm,
    )


def solution(mesh):
    return jax.shard_map(
        local,
        mesh=mesh,
        in_specs=(
            P("dp", "wide", None, None, None),
            P("dp", "wide", None, None, None),
            P(),
            P(),
            P("dp", None),
            P("dp", None),
        ),
        out_specs=(
            P("dp", "wide", None, None, None),
            P("dp", "wide", None, None, None),
            P("dp", "wide"),
            P("dp", "wide"),
            P(None, "wide"),
        ),
        check_vma=False,
    )
```

time: 89.8 us -> 50.4 us (0.56)
  the two profiles are of different devices: /device:TPU:8 before, /device:TPU:0 now
where the time goes in v4:
time: 50.4 us; the launch traced here: 50.1 us
  starting transfers between devices  14.5 us (29%)
  blocking collectives  13.3 us (26%)
  waiting for transfers between devices  13.3 us (26%)
  Pallas kernels  8.16 us (16%)
  between operations  0.74 us (1%)
    ppermute x10, waiting for transfers between devices, send(): return lax.ppermute(value, ('dp', 'wide'), over_all(moves))  13.3 us
    all_to_all x1, blocking collectives, local(): lax.all_to_all(stats, 'wide', split_axis=0, concat_axis=0, tiled=True)  13.3 us
    ppermute x10, starting transfers between devices, send(): return lax.ppermute(value, ('dp', 'wide'), over_all(moves))  11.8 us
    pallas_call x7, Pallas kernels, run(): pl.pallas_call(body, out_shape=out_shapes, in_specs=in_specs or [VMEM] *...  8.16 us
    ppermute x1, starting transfers between devices, local(): before = lax.ppermute(spatial, 'wide', [(w, w + 1) for w in range(W - 1)])  1.42 us
    ppermute x1, starting transfers between devices, local(): halo = lax.ppermute(cot, 'wide', [(w + 1, w) for w in range(W - 1)])  1.28 us
  transfers between devices with their start and end apart: 12, of which 7 were waited for; matrix products, arithmetic and copies ran while one was open for 0% of the time, Pallas kernels for 6%

profile of v4, /device:TPU:0, one launch (start us, length us, event | category | flops | bytes accessed | tf_op | source)
XLA Modules:
  0.0 50.1 jit_solution(4281649098535754978)
XLA Ops:
  0.7 2.8 %shard_map.101 = (f32[16,2,256]{2,1,0:T(2,128)}, f32[2,256]{1,0:T(2,128)}, bf16[768,256]{1,0:T(8,128)(2,1)}) custom-call(bf16[256,256]{1,0:T(8,128)(2,1)} %bitcast.12, f32[1,256]{1,0:T(1,128)} %bitcast.26, f32[1,256]{1,0:T(1,128)} %bitcast.27, bf16[1152,256]{1,0:T(8,128)(2,1)} %ws_ref.3, bf16[384,256]{1,0:T(8,128)(2,1)} %wt_ref.5), custom_call_target="tpu_custom_call" | custom-call | tf_op jit(solution)/shard_map/pallas_call | solution.py:25
  3.4 3.0 %collective-permute-start = (bf16[768,256]{1,0:T(8,128)(2,1)}, bf16[768,256]{1,0:T(8,128)(2,1)S(1)}, u32[]{:S(2)}, u32[]{:S(2)}) collective-permute-start(bf16[768,256]{1,0:T(8,128)(2,1)} %get-tuple-element.30), channel_id=1, source_target_pairs={{0,16},{1,17},{2,18},{3,19},{4,20},{5,21},{6,22},{7,23},{8,24},{9,... | collective-permute-start | bytes 1179656 | tf_op jit(solution)/shard_map/ppermute | solution.py:386
  6.4 1.3 %collective-permute-start.1 = (bf16[256,256]{1,0:T(8,128)(2,1)S(1)}, bf16[256,256]{1,0:T(8,128)(2,1)S(1)}, u32[]{:S(2)}, u32[]{:S(2)}) collective-permute-start(bf16[256,256]{1,0:T(8,128)(2,1)S(1)} %bitcast.21), channel_id=1, source_target_pairs={{1,0},{2,1},{3,2},{4,3},{5,4},{6,5},{7,6},{8,7},{9,8},{10,9},{11,1... | collective-permute-start | bytes 393224 | tf_op jit(solution)/shard_map/ppermute | solution.py:402
  7.7 0.0 copy-start.4
  7.7 13.3 %all_to_all.5.stats_ref.refs_6_ = f32[16,2,256]{2,1,0:T(2,128)S(1)} all-to-all(f32[16,2,256]{2,1,0:T(2,128)} %get-tuple-element.31), channel_id=1, replica_groups=mesh['dp'=2,'wide'=16] {'wide'}, dimensions={0} | all-to-all | bytes 65536 | tf_op jit(solution)/shard_map/all_to_all | solution.py:403
  21.0 0.0 collective-permute-done.1.halo_ref
  21.0 0.0 collective-permute-done.rest_0_
  21.1 1.7 %collective-permute-done.2.rest_1_ = bf16[768,256]{1,0:T(8,128)(2,1)S(1)} collective-permute-done((bf16[768,256]{1,0:T(8,128)(2,1)S(1)}, bf16[768,256]{1,0:T(8,128)(2,1)S(1)}, u32[]{:S(2)}, u32[]{:S(2)}) %collective-permute-start.2) | collective-permute-done | bytes 393248 | tf_op jit(solution)/shard_map/ppermute | solution.py:386
  22.8 0.0 copy-start.2
  22.8 1.0 %shard_map.102 = (bf16[256,256]{1,0:T(8,128)(2,1)S(1)}, bf16[2,128,1152]{2,1,0:T(8,128)(2,1)S(1)}, bf16[2,128,1152]{2,1,0:T(8,128)(2,1)S(1)}) custom-call(bf16[256,256]{1,0:T(8,128)(2,1)S(1)} %bitcast.13, bf16[256,256]{1,0:T(8,128)(2,1)S(1)} %bitcast.22, bf16[256,256]{1,0:T(8,128)(2,1)S(1)} %collective-permute-done.1.halo_ref, ...), custom_call_target="tpu_custom_call" | custom-call | flops 402653184 | bytes 3000000 | tf_op jit(solution)/shard_map/pallas_call | solution.py:25
  23.8 0.2 collective-permute-start.4
  24.0 1.9 %shard_map.103 = (bf16[256,256]{1,0:T(8,128)(2,1)S(1)}, f32[256,256]{1,0:T(8,128)S(1)}, bf16[2,128,512]{2,1,0:T(8,128)(2,1)S(1)}, bf16[2,128,512]{2,1,0:T(8,128)(2,1)S(1)}) custom-call(bf16[256,256]{1,0:T(8,128)(2,1)S(1)} %bitcast.14, bf16[256,256]{1,0:T(8,128)(2,1)S(1)} %bitcast.23, bf16[256,256]{1,0:T(8,128)(2,1)S(1)} %collective-permute-done.1.halo_ref, ...), custom_call_target="tpu_custom_call" | custom-call | flops 704643072 | bytes 3000000 | tf_op jit(solution)/shard_map/pallas_call | solution.py:25
  26.0 0.4 collective-permute-start.5
  26.4 1.2 %collective-permute-done.5 = bf16[2,128,512]{2,1,0:T(8,128)(2,1)S(1)} collective-permute-done((bf16[2,128,512]{2,1,0:T(8,128)(2,1)S(1)}, bf16[2,128,512]{2,1,0:T(8,128)(2,1)S(1)}, u32[]{:S(2)}, u32[]{:S(2)}) %collective-permute-start.5) | collective-permute-done | bytes 262176 | tf_op jit(solution)/shard_map/ppermute | solution.py:386
  27.6 0.0 collective-permute-done.4
  27.6 0.2 shard_map.105
  27.8 0.4 collective-permute-start.6
  28.2 0.5 %collective-permute-start.7 = (bf16[4,16,1664]{2,1,0:T(8,128)(2,1)S(1)}, bf16[4,16,1664]{2,1,0:T(8,128)(2,1)S(1)}, u32[]{:S(2)}, u32[]{:S(2)}) collective-permute-start(bf16[4,16,1664]{2,1,0:T(8,128)(2,1)S(1)} %get-tuple-element.44), channel_id=1, source_target_pairs={{0,16},{1,17},{2,18},{3,19},{4,20},{5,21},{6,22},{7,23},{8,24},{9,... | collective-permute-start | bytes 638984 | tf_op jit(solution)/shard_map/ppermute | solution.py:386
  28.8 2.6 %collective-permute-start.8 = (bf16[4,16,1664]{2,1,0:T(8,128)(2,1)S(1)}, bf16[4,16,1664]{2,1,0:T(8,128)(2,1)S(1)}, u32[]{:S(2)}, u32[]{:S(2)}) collective-permute-start(bf16[4,16,1664]{2,1,0:T(8,128)(2,1)S(1)} %get-tuple-element.45), channel_id=1, source_target_pairs={{0,18},{1,19},{2,16},{3,17},{4,22},{5,23},{6,20},{7,21},{8,26},{9,... | collective-permute-start | bytes 638984 | tf_op jit(solution)/shard_map/ppermute | solution.py:386
  31.4 1.4 %collective-permute-start.3 = (bf16[256,256]{1,0:T(8,128)(2,1)S(1)}, bf16[256,256]{1,0:T(8,128)(2,1)S(1)}, u32[]{:S(2)}, u32[]{:S(2)}) collective-permute-start(bf16[256,256]{1,0:T(8,128)(2,1)S(1)} %get-tuple-element.37.spatial_ref), channel_id=1, source_target_pairs={{0,1},{1,2},{2,3},{3,4},{4,5},{5,6},{6,7},{7,8},{8,9},{9,10},{10,1... | collective-permute-start | bytes 393224 | tf_op jit(solution)/shard_map/ppermute | solution.py:436
  32.8 2.6 %collective-permute-done.6.refs_1_ = bf16[4,16,1664]{2,1,0:T(8,128)(2,1)S(1)} collective-permute-done((bf16[4,16,1664]{2,1,0:T(8,128)(2,1)S(1)}, bf16[4,16,1664]{2,1,0:T(8,128)(2,1)S(1)}, u32[]{:S(2)}, u32[]{:S(2)}) %collective-permute-start.6) | collective-permute-done | bytes 213024 | tf_op jit(solution)/shard_map/ppermute | solution.py:386
  35.4 0.9 %collective-permute-done.7.refs_2_ = bf16[4,16,1664]{2,1,0:T(8,128)(2,1)S(1)} collective-permute-done((bf16[4,16,1664]{2,1,0:T(8,128)(2,1)S(1)}, bf16[4,16,1664]{2,1,0:T(8,128)(2,1)S(1)}, u32[]{:S(2)}, u32[]{:S(2)}) %collective-permute-start.7) | collective-permute-done | bytes 213024 | tf_op jit(solution)/shard_map/ppermute | solution.py:386
  36.3 4.8 %collective-permute-done.8.refs_3_ = bf16[4,16,1664]{2,1,0:T(8,128)(2,1)S(1)} collective-permute-done((bf16[4,16,1664]{2,1,0:T(8,128)(2,1)S(1)}, bf16[4,16,1664]{2,1,0:T(8,128)(2,1)S(1)}, u32[]{:S(2)}, u32[]{:S(2)}) %collective-permute-start.8) | collective-permute-done | bytes 213024 | tf_op jit(solution)/shard_map/ppermute | solution.py:386
  41.2 0.1 shard_map.106
  41.3 1.6 %collective-permute-start.9 = (bf16[16,1664]{1,0:T(8,128)(2,1)S(1)}, bf16[16,1664]{1,0:T(8,128)(2,1)S(1)}, u32[]{:S(2)}, u32[]{:S(2)}) collective-permute-start(bf16[16,1664]{1,0:T(8,128)(2,1)S(1)} %get-tuple-element.47), channel_id=1, source_target_pairs={{0,4},{1,5},{2,6},{3,7},{4,8},{5,9},{6,10},{7,11},{8,12},{9,13},{1... | collective-permute-start | bytes 159752 | tf_op jit(solution)/shard_map/ppermute | solution.py:386
  42.9 0.7 %collective-permute-start.10 = (bf16[16,1664]{1,0:T(8,128)(2,1)S(1)}, bf16[16,1664]{1,0:T(8,128)(2,1)S(1)}, u32[]{:S(2)}, u32[]{:S(2)}) collective-permute-start(bf16[16,1664]{1,0:T(8,128)(2,1)S(1)} %get-tuple-element.48), channel_id=1, source_target_pairs={{0,8},{1,9},{2,10},{3,11},{4,12},{5,13},{6,14},{7,15},{8,0},{9,1},... | collective-permute-start | bytes 159752 | tf_op jit(solution)/shard_map/ppermute | solution.py:386
  43.6 2.3 %collective-permute-start.11 = (bf16[16,1664]{1,0:T(8,128)(2,1)S(1)}, bf16[16,1664]{1,0:T(8,128)(2,1)S(1)}, u32[]{:S(2)}, u32[]{:S(2)}) collective-permute-start(bf16[16,1664]{1,0:T(8,128)(2,1)S(1)} %get-tuple-element.49), channel_id=1, source_target_pairs={{0,12},{1,13},{2,14},{3,15},{4,0},{5,1},{6,2},{7,3},{8,4},{9,5},{1... | collective-permute-start | bytes 159752 | tf_op jit(solution)/shard_map/ppermute | solution.py:386
  45.9 1.0 %shard_map.104 = bf16[256,256]{1,0:T(8,128)(2,1)} custom-call(bf16[256,256]{1,0:T(8,128)(2,1)S(1)} %bitcast.15, bf16[256,256]{1,0:T(8,128)(2,1)S(1)} %get-tuple-element.37.spatial_ref, bf16[256,256]{1,0:T(8,128)(2,1)S(1)} %collective-permute-done.3.before_ref, bf16[384,256]{1,0:T(8,128)(2,1)S(1)} %copy-done.1, ...), custom_call_target="tpu_custom_call" | custom-call | flops 100663296 | bytes 1000000 | tf_op jit(solution)/shard_map/pallas_call | solution.py:25
  46.9 0.9 %collective-permute-done.9.refs_1_ = bf16[16,1664]{1,0:T(8,128)(2,1)S(1)} collective-permute-done((bf16[16,1664]{1,0:T(8,128)(2,1)S(1)}, bf16[16,1664]{1,0:T(8,128)(2,1)S(1)}, u32[]{:S(2)}, u32[]{:S(2)}) %collective-permute-start.9) | collective-permute-done | bytes 53280 | tf_op jit(solution)/shard_map/ppermute | solution.py:386
  47.8 1.2 %collective-permute-done.10.refs_2_ = bf16[16,1664]{1,0:T(8,128)(2,1)S(1)} collective-permute-done((bf16[16,1664]{1,0:T(8,128)(2,1)S(1)}, bf16[16,1664]{1,0:T(8,128)(2,1)S(1)}, u32[]{:S(2)}, u32[]{:S(2)}) %collective-permute-start.10) | collective-permute-done | bytes 53280 | tf_op jit(solution)/shard_map/ppermute | solution.py:386
  48.9 0.0 collective-permute-done.11.refs_3_
  48.9 1.1 %shard_map.107 = (f32[16,1152]{1,0:T(8,128)}, f32[16,384]{1,0:T(8,128)}, f32[2,16]{1,0:T(2,128)}, bf16[256,256]{1,0:T(8,128)(2,1)}) custom-call(bf16[16,1664]{1,0:T(8,128)(2,1)S(1)} %get-tuple-element.46.refs_0_, bf16[16,1664]{1,0:T(8,128)(2,1)S(1)} %collective-permute-done.9.refs_1_, bf16[16,1664]{1,0:T(8,128)(2,1)S(1)} %collective-permute-done.10.refs_2_, ...), custom_call_target="tpu_custom_call" | custom-call | bytes 1000000 | tf_op jit(solution)/shard_map/pallas_call | solution.py:25
  (10 shorter events, 0.0 us)
Async XLA Ops:
  0.6 5.8 %copy-start.3 = (bf16[1,2,8,16,256]{4,3,2,1,0:T(8,128)(2,1)S(1)}, bf16[1,2,8,16,256]{4,3,2,1,0:T(8,128)(2,1)}, u32[]{:S(2)}) copy-start(bf16[1,2,8,16,256]{4,3,2,1,0:T(8,128)(2,1)} %param.7) | copy-start | bytes 393220
  0.6 22.1 %copy-start = (bf16[1,2,8,16,256]{4,3,2,1,0:T(8,128)(2,1)S(1)}, bf16[1,2,8,16,256]{4,3,2,1,0:T(8,128)(2,1)}, u32[]{:S(2)}) copy-start(bf16[1,2,8,16,256]{4,3,2,1,0:T(8,128)(2,1)} %param.6) | copy-start | bytes 393220
  0.7 22.1 %copy-start.1 = (bf16[384,256]{1,0:T(8,128)(2,1)S(1)}, bf16[384,256]{1,0:T(8,128)(2,1)}, u32[]{:S(2)}) copy-start(bf16[384,256]{1,0:T(8,128)(2,1)} %wt_ref.5) | copy-start | bytes 589828
  3.4 17.6 %collective-permute-start = (bf16[768,256]{1,0:T(8,128)(2,1)}, bf16[768,256]{1,0:T(8,128)(2,1)S(1)}, u32[]{:S(2)}, u32[]{:S(2)}) collective-permute-start(bf16[768,256]{1,0:T(8,128)(2,1)} %get-tuple-element.30), channel_id=1, source_target_pairs={{0,16},{1,17},{2,18},{3,19},{4,20},{5,21},{6,22},{7,23},{8,24},{9,... | collective-permute-start | bytes 1179656 | tf_op jit(solution)/shard_map/ppermute | solution.py:386
  6.4 14.6 %collective-permute-start.1 = (bf16[256,256]{1,0:T(8,128)(2,1)S(1)}, bf16[256,256]{1,0:T(8,128)(2,1)S(1)}, u32[]{:S(2)}, u32[]{:S(2)}) collective-permute-start(bf16[256,256]{1,0:T(8,128)(2,1)S(1)} %bitcast.21), channel_id=1, source_target_pairs={{1,0},{2,1},{3,2},{4,3},{5,4},{6,5},{7,6},{8,7},{9,8},{10,9},{11,1... | collective-permute-start | bytes 393224 | tf_op jit(solution)/shard_map/ppermute | solution.py:402
  7.7 15.1 %copy-start.4 = (f32[2,256]{1,0:T(2,128)S(1)}, f32[2,256]{1,0:T(2,128)}, u32[]{:S(2)}) copy-start(f32[2,256]{1,0:T(2,128)} %get-tuple-element.34.affine_ref.refs_7_) | copy-start | bytes 6148
  21.1 1.7 %collective-permute-start.2 = (bf16[768,256]{1,0:T(8,128)(2,1)S(1)}, bf16[768,256]{1,0:T(8,128)(2,1)S(1)}, u32[]{:S(2)}, u32[]{:S(2)}) collective-permute-start(bf16[768,256]{1,0:T(8,128)(2,1)S(1)} %collective-permute-done.rest_0_), channel_id=1, source_target_pairs={{0,1},{1,0},{2,3},{3,2},{4,5},{5,4},{6,7},{7,6},{8,9},{9,8},{10,11... | collective-permute-start | bytes 1179656 | tf_op jit(solution)/shard_map/ppermute | solution.py:386
  22.8 1.2 %copy-start.2 = (bf16[1152,256]{1,0:T(8,128)(2,1)S(1)}, bf16[1152,256]{1,0:T(8,128)(2,1)}, u32[]{:S(2)}) copy-start(bf16[1152,256]{1,0:T(8,128)(2,1)} %ws_ref.3) | copy-start | bytes 1769476
  23.8 3.8 %collective-permute-start.4 = (bf16[2,128,1152]{2,1,0:T(8,128)(2,1)S(1)}, bf16[2,128,1152]{2,1,0:T(8,128)(2,1)S(1)}, u32[]{:S(2)}, u32[]{:S(2)}) collective-permute-start(bf16[2,128,1152]{2,1,0:T(8,128)(2,1)S(1)} %get-tuple-element.39), channel_id=1, source_target_pairs={{0,1},{1,0},{2,3},{3,2},{4,5},{5,4},{6,7},{7,6},{8,9},{9,8},{10,11... | collective-permute-start | bytes 1769480 | tf_op jit(solution)/shard_map/ppermute | solution.py:386
  26.0 1.6 %collective-permute-start.5 = (bf16[2,128,512]{2,1,0:T(8,128)(2,1)S(1)}, bf16[2,128,512]{2,1,0:T(8,128)(2,1)S(1)}, u32[]{:S(2)}, u32[]{:S(2)}) collective-permute-start(bf16[2,128,512]{2,1,0:T(8,128)(2,1)S(1)} %get-tuple-element.41), channel_id=1, source_target_pairs={{0,1},{1,0},{2,3},{3,2},{4,5},{5,4},{6,7},{7,6},{8,9},{9,8},{10,11... | collective-permute-start | bytes 786440 | tf_op jit(solution)/shard_map/ppermute | solution.py:386
  27.8 7.6 %collective-permute-start.6 = (bf16[4,16,1664]{2,1,0:T(8,128)(2,1)S(1)}, bf16[4,16,1664]{2,1,0:T(8,128)(2,1)S(1)}, u32[]{:S(2)}, u32[]{:S(2)}) collective-permute-start(bf16[4,16,1664]{2,1,0:T(8,128)(2,1)S(1)} %get-tuple-element.43), channel_id=1, source_target_pairs={{0,2},{1,3},{2,0},{3,1},{4,6},{5,7},{6,4},{7,5},{8,10},{9,11},{10,... | collective-permute-start | bytes 638984 | tf_op jit(solution)/shard_map/ppermute | solution.py:386
  28.2 8.1 %collective-permute-start.7 = (bf16[4,16,1664]{2,1,0:T(8,128)(2,1)S(1)}, bf16[4,16,1664]{2,1,0:T(8,128)(2,1)S(1)}, u32[]{:S(2)}, u32[]{:S(2)}) collective-permute-start(bf16[4,16,1664]{2,1,0:T(8,128)(2,1)S(1)} %get-tuple-element.44), channel_id=1, source_target_pairs={{0,16},{1,17},{2,18},{3,19},{4,20},{5,21},{6,22},{7,23},{8,24},{9,... | collective-permute-start | bytes 638984 | tf_op jit(solution)/shard_map/ppermute | solution.py:386
  28.8 12.4 %collective-permute-start.8 = (bf16[4,16,1664]{2,1,0:T(8,128)(2,1)S(1)}, bf16[4,16,1664]{2,1,0:T(8,128)(2,1)S(1)}, u32[]{:S(2)}, u32[]{:S(2)}) collective-permute-start(bf16[4,16,1664]{2,1,0:T(8,128)(2,1)S(1)} %get-tuple-element.45), channel_id=1, source_target_pairs={{0,18},{1,19},{2,16},{3,17},{4,22},{5,23},{6,20},{7,21},{8,26},{9,... | collective-permute-start | bytes 638984 | tf_op jit(solution)/shard_map/ppermute | solution.py:386
  31.4 14.5 %collective-permute-start.3 = (bf16[256,256]{1,0:T(8,128)(2,1)S(1)}, bf16[256,256]{1,0:T(8,128)(2,1)S(1)}, u32[]{:S(2)}, u32[]{:S(2)}) collective-permute-start(bf16[256,256]{1,0:T(8,128)(2,1)S(1)} %get-tuple-element.37.spatial_ref), channel_id=1, source_target_pairs={{0,1},{1,2},{2,3},{3,4},{4,5},{5,6},{6,7},{7,8},{8,9},{9,10},{10,1... | collective-permute-start | bytes 393224 | tf_op jit(solution)/shard_map/ppermute | solution.py:436
  41.3 6.5 %collective-permute-start.9 = (bf16[16,1664]{1,0:T(8,128)(2,1)S(1)}, bf16[16,1664]{1,0:T(8,128)(2,1)S(1)}, u32[]{:S(2)}, u32[]{:S(2)}) collective-permute-start(bf16[16,1664]{1,0:T(8,128)(2,1)S(1)} %get-tuple-element.47), channel_id=1, source_target_pairs={{0,4},{1,5},{2,6},{3,7},{4,8},{5,9},{6,10},{7,11},{8,12},{9,13},{1... | collective-permute-start | bytes 159752 | tf_op jit(solution)/shard_map/ppermute | solution.py:386
  42.9 6.0 %collective-permute-start.10 = (bf16[16,1664]{1,0:T(8,128)(2,1)S(1)}, bf16[16,1664]{1,0:T(8,128)(2,1)S(1)}, u32[]{:S(2)}, u32[]{:S(2)}) collective-permute-start(bf16[16,1664]{1,0:T(8,128)(2,1)S(1)} %get-tuple-element.48), channel_id=1, source_target_pairs={{0,8},{1,9},{2,10},{3,11},{4,12},{5,13},{6,14},{7,15},{8,0},{9,1},... | collective-permute-start | bytes 159752 | tf_op jit(solution)/shard_map/ppermute | solution.py:386
  43.6 5.3 %collective-permute-start.11 = (bf16[16,1664]{1,0:T(8,128)(2,1)S(1)}, bf16[16,1664]{1,0:T(8,128)(2,1)S(1)}, u32[]{:S(2)}, u32[]{:S(2)}) collective-permute-start(bf16[16,1664]{1,0:T(8,128)(2,1)S(1)} %get-tuple-element.49), channel_id=1, source_target_pairs={{0,12},{1,13},{2,14},{3,15},{4,0},{5,1},{6,2},{7,3},{8,4},{9,5},{1... | collective-permute-start | bytes 159752 | tf_op jit(solution)/shard_map/ppermute | solution.py:386

commit v5 on v4

--- a/solution.py
+++ b/solution.py
@@ -14,11 +14,12 @@
 BF16 = jnp.bfloat16
 VMEM = pl.BlockSpec(memory_space=pltpu.VMEM)
 HBM = pl.BlockSpec(memory_space=pltpu.HBM)
+OTHERS = ((0, 0, 0), (1, 1, 1), (1, 1, 0), (0, 1, 1), (1, 0, 1), (1, 0, 0), (0, 1, 0), (0, 0, 1))
 NT = (((1,), (1,)), ((), ()))
 NN = (((1,), (0,)), ((), ()))
 
 
-def call(body, out_shapes, scratch=(), flops=0, moved=0, in_specs=None, vmem=40):
+def call(body, out_shapes, scratch=(), flops=0, moved=0, in_specs=None, out_specs=None, vmem=40):
     many = isinstance(out_shapes, (tuple, list))
 
     def run(*operands):
@@ -26,7 +27,7 @@
             body,
             out_shape=out_shapes,
             in_specs=in_specs or [VMEM] * len(operands),
-            out_specs=[VMEM] * len(out_shapes) if many else VMEM,
+            out_specs=out_specs or ([VMEM] * len(out_shapes) if many else VMEM),
             scratch_shapes=list(scratch),
             compiler_params=pltpu.CompilerParams(vmem_limit_bytes=vmem * 1024 * 1024),
             cost_estimate=pl.CostEstimate(
@@ -55,27 +56,28 @@
     )
 
 
-def stats_body(lat_ref, gain_ref, bias_ref, ws_ref, wt_ref, out_ref, affine_ref, half_ref, sem):
+def stats_body(lat_ref, gain_ref, bias_ref, ws_ref, wt_ref, out_ref, affine_ref, half_ref, *scratch):
+    lat_here, gain_here, bias_here, sems = scratch
     core = lax.rem(lax.axis_index("wide"), 2)
-    copies, place = [], 0
-    for at, source in enumerate((ws_ref, wt_ref)):
+    moves, place = [(lat_ref, lat_here), (gain_ref, gain_here), (bias_ref, bias_here)], 0
+    for source in (ws_ref, wt_ref):
         half = source.shape[0] // 2
         start = pl.multiple_of(core * half, 16)
-        copies.append(
-            pltpu.make_async_copy(
-                source.at[pl.ds(start, half)], half_ref.at[pl.ds(place, half)], sem.at[at]
-            )
-        )
-        copies[-1].start()
+        moves.append((source.at[pl.ds(start, half)], half_ref.at[pl.ds(place, half)]))
         place += half
-    affine_ref[0:1] = gain_ref[...]
-    affine_ref[1:2] = bias_ref[...]
-    x = lat_ref[...].astype(F32)
+    copies = [pltpu.make_async_copy(*move, sems.at[at]) for at, move in enumerate(moves)]
+    for copy in copies:
+        copy.start()
+    for copy in copies[:3]:
+        copy.wait()
+    affine_ref[0:1] = gain_here[...]
+    affine_ref[1:2] = bias_here[...]
+    x = lat_here[...].astype(F32)
     both = jnp.concatenate(
         [jnp.sum(x, axis=0, keepdims=True), jnp.sum(x * x, axis=0, keepdims=True)], axis=0
     )
     out_ref[...] = jnp.broadcast_to(both[None], out_ref.shape)
-    for copy in copies:
+    for copy in copies[3:]:
         copy.wait()
 
 
@@ -286,30 +288,29 @@
     return (cot_ref[...].astype(F32) + inner).astype(BF16)
 
 
-def plane_body(keep_s, got_s, keep_t, got_t, *outs):
+def block_terms_body(keep_s, got_s, keep_t, got_t, *outs):
     d = lax.axis_index("dp")
-    y = lax.rem(lax.axis_index("wide") // 2, 2)
+    w = lax.axis_index("wide")
+    y, pair = lax.rem(w // 2, 2), lax.rem(w // 4, 2)
     split = keep_s.shape[-1]
     ride = outs[0].shape[-1] - 128
-    for a in range(2):
-        for b in range(2):
-            owner, side = lax.rem(d + a, 2), lax.rem(y + b, 2)
-            out = outs[2 * a + b]
-            for z in range(out.shape[0]):
-                out[z, :, :split] = add([keep_s[owner, z, side], got_s[owner, z, side]]).astype(
-                    BF16
-                )
-                both = [keep_t[owner, z, side], got_t[owner, z, side]]
-                out[z, :, split:ride] = add([t[:, : ride - split] for t in both]).astype(BF16)
-                out[z, :, ride:] = in_parts(from_parts([t[:, ride - split :] for t in both]))
+    for at, (a, b, c) in enumerate(OTHERS):
+        owner, side, near = lax.rem(d + a, 2), lax.rem(y + b, 2), lax.rem(pair + c, 2)
+        out = outs[at]
+        for far in range(out.shape[0]):
+            z = 2 * far + near
+            out[far, :, :split] = add([keep_s[owner, z, side], got_s[owner, z, side]]).astype(BF16)
+            both = [keep_t[owner, z, side], got_t[owner, z, side]]
+            out[far, :, split:ride] = add([t[:, : ride - split] for t in both]).astype(BF16)
+            out[far, :, ride:] = in_parts(from_parts([t[:, ride - split :] for t in both]))
 
 
 def line_body(depth, *refs):
-    terms, outs = refs[:4], refs[4:]
-    z = lax.axis_index("wide") // 4
+    terms, outs = refs[:-depth], refs[-depth:]
+    far = lax.axis_index("wide") // 8
     ride = outs[0].shape[-1] - 128
     for s in range(depth):
-        owner = lax.rem(z + s, depth)
+        owner = lax.rem(far + s, depth)
         seen = [term[owner] for term in terms]
         outs[s][:, :ride] = add([t[:, :ride] for t in seen]).astype(BF16)
         outs[s][:, ride:] = in_parts(from_parts([t[:, ride:] for t in seen]))
@@ -367,7 +368,7 @@
     count = W * frames * cells * per_group
     shard_s, shard_t = w_spatial.shape[0], w_temporal.shape[0]
     aligned = (channels // W) % 16 == 0 and shard_s % 128 == 0 and shard_t % 128 == 0
-    aligned = aligned and W % 4 == 0 and D == 2 and channels == 256
+    aligned = aligned and W % 8 == 0 and D == 2 and channels == 256
     sizes = (D, W, frames, cells, cols, count, per_group, aligned)
     scale = 1.0 / math.sqrt(D * W * frames * cells)
 
@@ -393,8 +394,14 @@
             shape((2, channels), F32),
             shape((R // 2, channels), BF16),
         ],
-        [pltpu.SemaphoreType.DMA((2,))],
-        in_specs=[VMEM, VMEM, VMEM, HBM, HBM],
+        [
+            pltpu.VMEM((rows, channels), BF16),
+            pltpu.VMEM((1, channels), F32),
+            pltpu.VMEM((1, channels), F32),
+            pltpu.SemaphoreType.DMA((5,)),
+        ],
+        in_specs=[HBM] * 5,
+        out_specs=[VMEM, VMEM, HBM],
         vmem=60,
     )(lat, gain, bias, w_spatial, w_temporal)
     firsts = [send(half, lambda d, w: ((d + s) % D, w)) for s in range(1, D)]
@@ -445,7 +452,7 @@
     width = channels // W
     operands = (lat, cot, stats, affine, grad)
     if aligned:
-        Z = W // 4
+        Z, far = W // 4, W // 8
 
         def over_core(away):
             return send(away, lambda d, w: (d, w ^ 1))
@@ -454,23 +461,24 @@
         for keep, away in (grads_s, grads_t):
             view = (D, Z, 2, width, keep.shape[-1])
             pairs += [keep.reshape(view), over_core(away).reshape(view)]
-        plane = call(
-            plane_body, [shape((Z, width, R + ride), BF16)] * (2 * D), moved=3_000_000
+        sums = call(
+            block_terms_body,
+            [shape((far, width, R + ride), BF16)] * len(OTHERS),
+            moved=3_000_000,
         )(*pairs)
-        seen = [plane[0]] + [
-            send(plane[2 * a + b], lambda d, w: ((d + a) % D, w ^ (2 * b)))
-            for a, b in ((0, 1), (1, 0), (1, 1))
-        ]
+        seen = [sums[0]]
+        for value, (a, b, c) in zip(sums[1:], OTHERS[1:]):
+            seen.append(send(value, lambda d, w: (d ^ a, w ^ (2 * b + 4 * c))))
         line = call(
-            functools.partial(line_body, Z),
-            [shape((width, R + ride), BF16)] * Z,
+            functools.partial(line_body, far),
+            [shape((width, R + ride), BF16)] * far,
             moved=1_000_000,
         )(*seen)
         terms = [line[0]]
-        for s in range(1, Z):
-            terms.append(send(line[s], lambda d, w: (d, (w + 4 * s) % W)))
+        for s in range(1, far):
+            terms.append(send(line[s], lambda d, w: (d, (w + 8 * s) % W)))
         grad_s, grad_t, norm, grad_latents = call(
-            functools.partial(last_body, sizes, scale, Z),
+            functools.partial(last_body, sizes, scale, far),
             [
                 shape((width, shard_s), F32),
                 shape((width, shard_t), F32),

time: 50.4 us -> 62.2 us (1.23)
  Pallas kernels: 8.16 us -> 19.1 us
  starting transfers between devices: 14.5 us -> 15.8 us
    pallas_call x7, Pallas kernels: 8.16 us -> 19.1 us  [run(): pl.pallas_call(body, out_shape=out_shapes, in_specs=in_specs or [VMEM] *...]
    ppermute x10 -> x12, starting transfers between devices: 11.8 us -> 13.2 us  [send(): return lax.ppermute(value, ('dp', 'wide'), over_all(moves))]
    ppermute x10 -> x12, waiting for transfers between devices: 13.3 us -> 13 us  [send(): return lax.ppermute(value, ('dp', 'wide'), over_all(moves))]
  transfers between devices with their start and end apart: 12 -> 14, of which waited for: 7 -> 7; matrix products, arithmetic and copies ran while one was open for 0% -> 0% of each run, Pallas kernels for 6% -> 5%
where the time goes in v5:
time: 62.2 us; the launch traced here: 61.9 us
  Pallas kernels  19.1 us (31%)
  starting transfers between devices  15.8 us (25%)
  blocking collectives  13.3 us (21%)
  waiting for transfers between devices  13 us (21%)
  between operations  0.75 us (1%)
    pallas_call x7, Pallas kernels, run(): pl.pallas_call(body, out_shape=out_shapes, in_specs=in_specs or [VMEM] *...  19.1 us
    all_to_all x1, blocking collectives, local(): lax.all_to_all(stats, 'wide', split_axis=0, concat_axis=0, tiled=True)  13.3 us
    ppermute x12, starting transfers between devices, send(): return lax.ppermute(value, ('dp', 'wide'), over_all(moves))  13.2 us
    ppermute x12, waiting for transfers between devices, send(): return lax.ppermute(value, ('dp', 'wide'), over_all(moves))  13 us
    ppermute x1, starting transfers between devices, local(): before = lax.ppermute(spatial, 'wide', [(w, w + 1) for w in range(W - 1)])  1.29 us
    ppermute x1, starting transfers between devices, local(): halo = lax.ppermute(cot, 'wide', [(w + 1, w) for w in range(W - 1)])  1.28 us
  transfers between devices with their start and end apart: 14, of which 7 were waited for; matrix products, arithmetic and copies ran while one was open for 0% of the time, Pallas kernels for 5%

profile of v5, /device:TPU:0, one launch (start us, length us, event | category | flops | bytes accessed | tf_op | source)
XLA Modules:
  0.0 61.9 jit_solution(16853834518757475018)
XLA Ops:
  0.7 13.7 %shard_map.101 = (f32[16,2,256]{2,1,0:T(2,128)}, f32[2,256]{1,0:T(2,128)}, bf16[768,256]{1,0:T(8,128)(2,1)}) custom-call(bf16[256,256]{1,0:T(8,128)(2,1)} %bitcast.12, f32[1,256]{1,0:T(1,128)} %bitcast.26, f32[1,256]{1,0:T(1,128)} %bitcast.27, bf16[1152,256]{1,0:T(8,128)(2,1)} %ws_ref.3, bf16[384,256]{1,0:T(8,128)(2,1)} %wt_ref.5), custom_call_target="tpu_custom_call" | custom-call | tf_op jit(solution)/shard_map/pallas_call | solution.py:26
  14.4 3.0 %collective-permute-start = (bf16[768,256]{1,0:T(8,128)(2,1)}, bf16[768,256]{1,0:T(8,128)(2,1)S(1)}, u32[]{:S(2)}, u32[]{:S(2)}) collective-permute-start(bf16[768,256]{1,0:T(8,128)(2,1)} %get-tuple-element.32), channel_id=1, source_target_pairs={{0,16},{1,17},{2,18},{3,19},{4,20},{5,21},{6,22},{7,23},{8,24},{9,... | collective-permute-start | bytes 1179656 | tf_op jit(solution)/shard_map/ppermute | solution.py:387
  17.4 1.3 %collective-permute-start.1 = (bf16[256,256]{1,0:T(8,128)(2,1)S(1)}, bf16[256,256]{1,0:T(8,128)(2,1)S(1)}, u32[]{:S(2)}, u32[]{:S(2)}) collective-permute-start(bf16[256,256]{1,0:T(8,128)(2,1)S(1)} %bitcast.21), channel_id=1, source_target_pairs={{1,0},{2,1},{3,2},{4,3},{5,4},{6,5},{7,6},{8,7},{9,8},{10,9},{11,1... | collective-permute-start | bytes 393224 | tf_op jit(solution)/shard_map/ppermute | solution.py:409
  18.7 0.0 copy-start.4
  18.7 13.3 %all_to_all.5.stats_ref.refs_4_ = f32[16,2,256]{2,1,0:T(2,128)S(1)} all-to-all(f32[16,2,256]{2,1,0:T(2,128)} %get-tuple-element.33), channel_id=1, replica_groups=mesh['dp'=2,'wide'=16] {'wide'}, dimensions={0} | all-to-all | bytes 65536 | tf_op jit(solution)/shard_map/all_to_all | solution.py:410
  32.0 1.7 %collective-permute-done.2.rest_1_ = bf16[768,256]{1,0:T(8,128)(2,1)S(1)} collective-permute-done((bf16[768,256]{1,0:T(8,128)(2,1)S(1)}, bf16[768,256]{1,0:T(8,128)(2,1)S(1)}, u32[]{:S(2)}, u32[]{:S(2)}) %collective-permute-start.2) | collective-permute-done | bytes 393248 | tf_op jit(solution)/shard_map/ppermute | solution.py:387
  33.7 0.0 copy-start.2
  33.7 1.0 %shard_map.102 = (bf16[256,256]{1,0:T(8,128)(2,1)S(1)}, bf16[2,128,1152]{2,1,0:T(8,128)(2,1)S(1)}, bf16[2,128,1152]{2,1,0:T(8,128)(2,1)S(1)}) custom-call(bf16[256,256]{1,0:T(8,128)(2,1)S(1)} %bitcast.13, bf16[256,256]{1,0:T(8,128)(2,1)S(1)} %bitcast.22, bf16[256,256]{1,0:T(8,128)(2,1)S(1)} %collective-permute-done.1.halo_ref, ...), custom_call_target="tpu_custom_call" | custom-call | flops 402653184 | bytes 3000000 | tf_op jit(solution)/shard_map/pallas_call | solution.py:26
  34.8 0.2 collective-permute-start.4
  35.0 1.9 %shard_map.103 = (bf16[256,256]{1,0:T(8,128)(2,1)S(1)}, f32[256,256]{1,0:T(8,128)S(1)}, bf16[2,128,512]{2,1,0:T(8,128)(2,1)S(1)}, bf16[2,128,512]{2,1,0:T(8,128)(2,1)S(1)}) custom-call(bf16[256,256]{1,0:T(8,128)(2,1)S(1)} %bitcast.14, bf16[256,256]{1,0:T(8,128)(2,1)S(1)} %bitcast.23, bf16[256,256]{1,0:T(8,128)(2,1)S(1)} %collective-permute-done.1.halo_ref, ...), custom_call_target="tpu_custom_call" | custom-call | flops 704643072 | bytes 3000000 | tf_op jit(solution)/shard_map/pallas_call | solution.py:26
  36.9 0.4 collective-permute-start.5
  37.4 1.2 %collective-permute-done.5 = bf16[2,128,512]{2,1,0:T(8,128)(2,1)S(1)} collective-permute-done((bf16[2,128,512]{2,1,0:T(8,128)(2,1)S(1)}, bf16[2,128,512]{2,1,0:T(8,128)(2,1)S(1)}, u32[]{:S(2)}, u32[]{:S(2)}) %collective-permute-start.5) | collective-permute-done | bytes 262176 | tf_op jit(solution)/shard_map/ppermute | solution.py:387
  38.5 0.2 shard_map.105
  38.7 0.4 collective-permute-start.6
  39.2 2.3 %collective-permute-start.7 = (bf16[2,16,1664]{2,1,0:T(8,128)(2,1)S(1)}, bf16[2,16,1664]{2,1,0:T(8,128)(2,1)S(1)}, u32[]{:S(2)}, u32[]{:S(2)}) collective-permute-start(bf16[2,16,1664]{2,1,0:T(8,128)(2,1)S(1)} %get-tuple-element.46), channel_id=1, source_target_pairs={{0,18},{1,19},{2,16},{3,17},{4,22},{5,23},{6,20},{7,21},{8,26},{9,... | collective-permute-start | bytes 319496 | tf_op jit(solution)/shard_map/ppermute | solution.py:387
  41.5 1.5 %collective-permute-start.8 = (bf16[2,16,1664]{2,1,0:T(8,128)(2,1)S(1)}, bf16[2,16,1664]{2,1,0:T(8,128)(2,1)S(1)}, u32[]{:S(2)}, u32[]{:S(2)}) collective-permute-start(bf16[2,16,1664]{2,1,0:T(8,128)(2,1)S(1)} %get-tuple-element.47), channel_id=1, source_target_pairs={{0,6},{1,7},{2,4},{3,5},{4,2},{5,3},{6,0},{7,1},{8,14},{9,15},{10,... | collective-permute-start | bytes 319496 | tf_op jit(solution)/shard_map/ppermute | solution.py:387
  43.0 0.6 collective-permute-start.9
  43.6 1.5 %collective-permute-start.10 = (bf16[2,16,1664]{2,1,0:T(8,128)(2,1)S(1)}, bf16[2,16,1664]{2,1,0:T(8,128)(2,1)S(1)}, u32[]{:S(2)}, u32[]{:S(2)}) collective-permute-start(bf16[2,16,1664]{2,1,0:T(8,128)(2,1)S(1)} %get-tuple-element.49), channel_id=1, source_target_pairs={{0,16},{1,17},{2,18},{3,19},{4,20},{5,21},{6,22},{7,23},{8,24},{9,... | collective-permute-start | bytes 319496 | tf_op jit(solution)/shard_map/ppermute | solution.py:387
  45.1 2.4 %collective-permute-done.6.refs_1_ = bf16[2,16,1664]{2,1,0:T(8,128)(2,1)S(1)} collective-permute-done((bf16[2,16,1664]{2,1,0:T(8,128)(2,1)S(1)}, bf16[2,16,1664]{2,1,0:T(8,128)(2,1)S(1)}, u32[]{:S(2)}, u32[]{:S(2)}) %collective-permute-start.6) | collective-permute-done | bytes 106528 | tf_op jit(solution)/shard_map/ppermute | solution.py:387
  47.5 0.3 collective-permute-start.11
  47.8 2.0 %collective-permute-done.7.refs_2_ = bf16[2,16,1664]{2,1,0:T(8,128)(2,1)S(1)} collective-permute-done((bf16[2,16,1664]{2,1,0:T(8,128)(2,1)S(1)}, bf16[2,16,1664]{2,1,0:T(8,128)(2,1)S(1)}, u32[]{:S(2)}, u32[]{:S(2)}) %collective-permute-start.7) | collective-permute-done | bytes 106528 | tf_op jit(solution)/shard_map/ppermute | solution.py:387
  49.7 0.9 %collective-permute-start.12 = (bf16[2,16,1664]{2,1,0:T(8,128)(2,1)S(1)}, bf16[2,16,1664]{2,1,0:T(8,128)(2,1)S(1)}, u32[]{:S(2)}, u32[]{:S(2)}) collective-permute-start(bf16[2,16,1664]{2,1,0:T(8,128)(2,1)S(1)} %get-tuple-element.51), channel_id=1, source_target_pairs={{0,4},{1,5},{2,6},{3,7},{4,0},{5,1},{6,2},{7,3},{8,12},{9,13},{10,... | collective-permute-start | bytes 319496 | tf_op jit(solution)/shard_map/ppermute | solution.py:387
  50.6 0.0 collective-permute-done.8.refs_3_
  50.6 1.3 %collective-permute-start.3 = (bf16[256,256]{1,0:T(8,128)(2,1)S(1)}, bf16[256,256]{1,0:T(8,128)(2,1)S(1)}, u32[]{:S(2)}, u32[]{:S(2)}) collective-permute-start(bf16[256,256]{1,0:T(8,128)(2,1)S(1)} %get-tuple-element.39.spatial_ref), channel_id=1, source_target_pairs={{0,1},{1,2},{2,3},{3,4},{4,5},{5,6},{6,7},{7,8},{8,9},{9,10},{10,1... | collective-permute-start | bytes 393224 | tf_op jit(solution)/shard_map/ppermute | solution.py:443
  51.9 0.7 %collective-permute-done.10.refs_5_ = bf16[2,16,1664]{2,1,0:T(8,128)(2,1)S(1)} collective-permute-done((bf16[2,16,1664]{2,1,0:T(8,128)(2,1)S(1)}, bf16[2,16,1664]{2,1,0:T(8,128)(2,1)S(1)}, u32[]{:S(2)}, u32[]{:S(2)}) %collective-permute-start.10) | collective-permute-done | bytes 106528 | tf_op jit(solution)/shard_map/ppermute | solution.py:387
  52.6 1.8 %collective-permute-done.12.refs_7_ = bf16[2,16,1664]{2,1,0:T(8,128)(2,1)S(1)} collective-permute-done((bf16[2,16,1664]{2,1,0:T(8,128)(2,1)S(1)}, bf16[2,16,1664]{2,1,0:T(8,128)(2,1)S(1)}, u32[]{:S(2)}, u32[]{:S(2)}) %collective-permute-start.12) | collective-permute-done | bytes 106528 | tf_op jit(solution)/shard_map/ppermute | solution.py:387
  54.4 0.1 shard_map.106
  54.5 2.0 %collective-permute-start.13 = (bf16[16,1664]{1,0:T(8,128)(2,1)S(1)}, bf16[16,1664]{1,0:T(8,128)(2,1)S(1)}, u32[]{:S(2)}, u32[]{:S(2)}) collective-permute-start(bf16[16,1664]{1,0:T(8,128)(2,1)S(1)} %get-tuple-element.53), channel_id=1, source_target_pairs={{0,8},{1,9},{2,10},{3,11},{4,12},{5,13},{6,14},{7,15},{8,0},{9,1},... | collective-permute-start | bytes 159752 | tf_op jit(solution)/shard_map/ppermute | solution.py:387
  56.6 0.0 collective-permute-done.3.before_ref
  56.6 1.0 %shard_map.104 = bf16[256,256]{1,0:T(8,128)(2,1)} custom-call(bf16[256,256]{1,0:T(8,128)(2,1)S(1)} %bitcast.15, bf16[256,256]{1,0:T(8,128)(2,1)S(1)} %get-tuple-element.39.spatial_ref, bf16[256,256]{1,0:T(8,128)(2,1)S(1)} %collective-permute-done.3.before_ref, bf16[384,256]{1,0:T(8,128)(2,1)S(1)} %copy-done.1, ...), custom_call_target="tpu_custom_call" | custom-call | flops 100663296 | bytes 1000000 | tf_op jit(solution)/shard_map/pallas_call | solution.py:26
  57.6 3.2 %collective-permute-done.13.refs_1_ = bf16[16,1664]{1,0:T(8,128)(2,1)S(1)} collective-permute-done((bf16[16,1664]{1,0:T(8,128)(2,1)S(1)}, bf16[16,1664]{1,0:T(8,128)(2,1)S(1)}, u32[]{:S(2)}, u32[]{:S(2)}) %collective-permute-start.13) | collective-permute-done | bytes 53280 | tf_op jit(solution)/shard_map/ppermute | solution.py:387
  60.8 1.1 %shard_map.107 = (f32[16,1152]{1,0:T(8,128)}, f32[16,384]{1,0:T(8,128)}, f32[2,16]{1,0:T(2,128)}, bf16[256,256]{1,0:T(8,128)(2,1)}) custom-call(bf16[16,1664]{1,0:T(8,128)(2,1)S(1)} %get-tuple-element.52.refs_0_, bf16[16,1664]{1,0:T(8,128)(2,1)S(1)} %collective-permute-done.13.refs_1_, bf16[256,256]{1,0:T(8,128)(2,1)S(1)} %bitcast.16, ...), custom_call_target="tpu_custom_call" | custom-call | bytes 1000000 | tf_op jit(solution)/shard_map/pallas_call | solution.py:26
  (14 shorter events, 0.0 us)
Async XLA Ops:
  0.6 16.7 %copy-start.3 = (bf16[1,2,8,16,256]{4,3,2,1,0:T(8,128)(2,1)S(1)}, bf16[1,2,8,16,256]{4,3,2,1,0:T(8,128)(2,1)}, u32[]{:S(2)}) copy-start(bf16[1,2,8,16,256]{4,3,2,1,0:T(8,128)(2,1)} %param.7) | copy-start | bytes 393220
  0.6 33.1 %copy-start = (bf16[1,2,8,16,256]{4,3,2,1,0:T(8,128)(2,1)S(1)}, bf16[1,2,8,16,256]{4,3,2,1,0:T(8,128)(2,1)}, u32[]{:S(2)}) copy-start(bf16[1,2,8,16,256]{4,3,2,1,0:T(8,128)(2,1)} %param.6) | copy-start | bytes 393220
  0.7 33.1 %copy-start.1 = (bf16[384,256]{1,0:T(8,128)(2,1)S(1)}, bf16[384,256]{1,0:T(8,128)(2,1)}, u32[]{:S(2)}) copy-start(bf16[384,256]{1,0:T(8,128)(2,1)} %wt_ref.5) | copy-start | bytes 589828
  14.4 17.6 %collective-permute-start = (bf16[768,256]{1,0:T(8,128)(2,1)}, bf16[768,256]{1,0:T(8,128)(2,1)S(1)}, u32[]{:S(2)}, u32[]{:S(2)}) collective-permute-start(bf16[768,256]{1,0:T(8,128)(2,1)} %get-tuple-element.32), channel_id=1, source_target_pairs={{0,16},{1,17},{2,18},{3,19},{4,20},{5,21},{6,22},{7,23},{8,24},{9,... | collective-permute-start | bytes 1179656 | tf_op jit(solution)/shard_map/ppermute | solution.py:387
  17.4 14.6 %collective-permute-start.1 = (bf16[256,256]{1,0:T(8,128)(2,1)S(1)}, bf16[256,256]{1,0:T(8,128)(2,1)S(1)}, u32[]{:S(2)}, u32[]{:S(2)}) collective-permute-start(bf16[256,256]{1,0:T(8,128)(2,1)S(1)} %bitcast.21), channel_id=1, source_target_pairs={{1,0},{2,1},{3,2},{4,3},{5,4},{6,5},{7,6},{8,7},{9,8},{10,9},{11,1... | collective-permute-start | bytes 393224 | tf_op jit(solution)/shard_map/ppermute | solution.py:409
  18.7 15.1 %copy-start.4 = (f32[2,256]{1,0:T(2,128)S(1)}, f32[2,256]{1,0:T(2,128)}, u32[]{:S(2)}) copy-start(f32[2,256]{1,0:T(2,128)} %get-tuple-element.36.affine_ref.refs_5_) | copy-start | bytes 6148
  32.0 1.7 %collective-permute-start.2 = (bf16[768,256]{1,0:T(8,128)(2,1)S(1)}, bf16[768,256]{1,0:T(8,128)(2,1)S(1)}, u32[]{:S(2)}, u32[]{:S(2)}) collective-permute-start(bf16[768,256]{1,0:T(8,128)(2,1)S(1)} %collective-permute-done.rest_0_), channel_id=1, source_target_pairs={{0,1},{1,0},{2,3},{3,2},{4,5},{5,4},{6,7},{7,6},{8,9},{9,8},{10,11... | collective-permute-start | bytes 1179656 | tf_op jit(solution)/shard_map/ppermute | solution.py:387
  33.7 1.2 %copy-start.2 = (bf16[1152,256]{1,0:T(8,128)(2,1)S(1)}, bf16[1152,256]{1,0:T(8,128)(2,1)}, u32[]{:S(2)}) copy-start(bf16[1152,256]{1,0:T(8,128)(2,1)} %ws_ref.3) | copy-start | bytes 1769476
  34.8 3.8 %collective-permute-start.4 = (bf16[2,128,1152]{2,1,0:T(8,128)(2,1)S(1)}, bf16[2,128,1152]{2,1,0:T(8,128)(2,1)S(1)}, u32[]{:S(2)}, u32[]{:S(2)}) collective-permute-start(bf16[2,128,1152]{2,1,0:T(8,128)(2,1)S(1)} %get-tuple-element.41), channel_id=1, source_target_pairs={{0,1},{1,0},{2,3},{3,2},{4,5},{5,4},{6,7},{7,6},{8,9},{9,8},{10,11... | collective-permute-start | bytes 1769480 | tf_op jit(solution)/shard_map/ppermute | solution.py:387
  36.9 1.6 %collective-permute-start.5 = (bf16[2,128,512]{2,1,0:T(8,128)(2,1)S(1)}, bf16[2,128,512]{2,1,0:T(8,128)(2,1)S(1)}, u32[]{:S(2)}, u32[]{:S(2)}) collective-permute-start(bf16[2,128,512]{2,1,0:T(8,128)(2,1)S(1)} %get-tuple-element.43), channel_id=1, source_target_pairs={{0,1},{1,0},{2,3},{3,2},{4,5},{5,4},{6,7},{7,6},{8,9},{9,8},{10,11... | collective-permute-start | bytes 786440 | tf_op jit(solution)/shard_map/ppermute | solution.py:387
  38.7 8.7 %collective-permute-start.6 = (bf16[2,16,1664]{2,1,0:T(8,128)(2,1)S(1)}, bf16[2,16,1664]{2,1,0:T(8,128)(2,1)S(1)}, u32[]{:S(2)}, u32[]{:S(2)}) collective-permute-start(bf16[2,16,1664]{2,1,0:T(8,128)(2,1)S(1)} %get-tuple-element.45), channel_id=1, source_target_pairs={{0,22},{1,23},{2,20},{3,21},{4,18},{5,19},{6,16},{7,17},{8,30},{9,... | collective-permute-start | bytes 319496 | tf_op jit(solution)/shard_map/ppermute | solution.py:387
  39.2 10.5 %collective-permute-start.7 = (bf16[2,16,1664]{2,1,0:T(8,128)(2,1)S(1)}, bf16[2,16,1664]{2,1,0:T(8,128)(2,1)S(1)}, u32[]{:S(2)}, u32[]{:S(2)}) collective-permute-start(bf16[2,16,1664]{2,1,0:T(8,128)(2,1)S(1)} %get-tuple-element.46), channel_id=1, source_target_pairs={{0,18},{1,19},{2,16},{3,17},{4,22},{5,23},{6,20},{7,21},{8,26},{9,... | collective-permute-start | bytes 319496 | tf_op jit(solution)/shard_map/ppermute | solution.py:387
  41.5 9.1 %collective-permute-start.8 = (bf16[2,16,1664]{2,1,0:T(8,128)(2,1)S(1)}, bf16[2,16,1664]{2,1,0:T(8,128)(2,1)S(1)}, u32[]{:S(2)}, u32[]{:S(2)}) collective-permute-start(bf16[2,16,1664]{2,1,0:T(8,128)(2,1)S(1)} %get-tuple-element.47), channel_id=1, source_target_pairs={{0,6},{1,7},{2,4},{3,5},{4,2},{5,3},{6,0},{7,1},{8,14},{9,15},{10,... | collective-permute-start | bytes 319496 | tf_op jit(solution)/shard_map/ppermute | solution.py:387
  43.0 8.9 %collective-permute-start.9 = (bf16[2,16,1664]{2,1,0:T(8,128)(2,1)S(1)}, bf16[2,16,1664]{2,1,0:T(8,128)(2,1)S(1)}, u32[]{:S(2)}, u32[]{:S(2)}) collective-permute-start(bf16[2,16,1664]{2,1,0:T(8,128)(2,1)S(1)} %get-tuple-element.48), channel_id=1, source_target_pairs={{0,20},{1,21},{2,22},{3,23},{4,16},{5,17},{6,18},{7,19},{8,28},{9,... | collective-permute-start | bytes 319496 | tf_op jit(solution)/shard_map/ppermute | solution.py:387
  43.6 9.0 %collective-permute-start.10 = (bf16[2,16,1664]{2,1,0:T(8,128)(2,1)S(1)}, bf16[2,16,1664]{2,1,0:T(8,128)(2,1)S(1)}, u32[]{:S(2)}, u32[]{:S(2)}) collective-permute-start(bf16[2,16,1664]{2,1,0:T(8,128)(2,1)S(1)} %get-tuple-element.49), channel_id=1, source_target_pairs={{0,16},{1,17},{2,18},{3,19},{4,20},{5,21},{6,22},{7,23},{8,24},{9,... | collective-permute-start | bytes 319496 | tf_op jit(solution)/shard_map/ppermute | solution.py:387
  47.5 5.2 %collective-permute-start.11 = (bf16[2,16,1664]{2,1,0:T(8,128)(2,1)S(1)}, bf16[2,16,1664]{2,1,0:T(8,128)(2,1)S(1)}, u32[]{:S(2)}, u32[]{:S(2)}) collective-permute-start(bf16[2,16,1664]{2,1,0:T(8,128)(2,1)S(1)} %get-tuple-element.50), channel_id=1, source_target_pairs={{0,2},{1,3},{2,0},{3,1},{4,6},{5,7},{6,4},{7,5},{8,10},{9,11},{10,... | collective-permute-start | bytes 319496 | tf_op jit(solution)/shard_map/ppermute | solution.py:387
  49.7 4.7 %collective-permute-start.12 = (bf16[2,16,1664]{2,1,0:T(8,128)(2,1)S(1)}, bf16[2,16,1664]{2,1,0:T(8,128)(2,1)S(1)}, u32[]{:S(2)}, u32[]{:S(2)}) collective-permute-start(bf16[2,16,1664]{2,1,0:T(8,128)(2,1)S(1)} %get-tuple-element.51), channel_id=1, source_target_pairs={{0,4},{1,5},{2,6},{3,7},{4,0},{5,1},{6,2},{7,3},{8,12},{9,13},{10,... | collective-permute-start | bytes 319496 | tf_op jit(solution)/shard_map/ppermute | solution.py:387
  50.6 6.0 %collective-permute-start.3 = (bf16[256,256]{1,0:T(8,128)(2,1)S(1)}, bf16[256,256]{1,0:T(8,128)(2,1)S(1)}, u32[]{:S(2)}, u32[]{:S(2)}) collective-permute-start(bf16[256,256]{1,0:T(8,128)(2,1)S(1)} %get-tuple-element.39.spatial_ref), channel_id=1, source_target_pairs={{0,1},{1,2},{2,3},{3,4},{4,5},{5,6},{6,7},{7,8},{8,9},{9,10},{10,1... | collective-permute-start | bytes 393224 | tf_op jit(solution)/shard_map/ppermute | solution.py:443
  54.5 6.2 %collective-permute-start.13 = (bf16[16,1664]{1,0:T(8,128)(2,1)S(1)}, bf16[16,1664]{1,0:T(8,128)(2,1)S(1)}, u32[]{:S(2)}, u32[]{:S(2)}) collective-permute-start(bf16[16,1664]{1,0:T(8,128)(2,1)S(1)} %get-tuple-element.53), channel_id=1, source_target_pairs={{0,8},{1,9},{2,10},{3,11},{4,12},{5,13},{6,14},{7,15},{8,0},{9,1},... | collective-permute-start | bytes 159752 | tf_op jit(solution)/shard_map/ppermute | solution.py:387

commit v6 on v4

--- a/solution.py
+++ b/solution.py
@@ -14,11 +14,12 @@
 BF16 = jnp.bfloat16
 VMEM = pl.BlockSpec(memory_space=pltpu.VMEM)
 HBM = pl.BlockSpec(memory_space=pltpu.HBM)
+FIRST_VMEM = 60 << 20
 NT = (((1,), (1,)), ((), ()))
 NN = (((1,), (0,)), ((), ()))
 
 
-def call(body, out_shapes, scratch=(), flops=0, moved=0, in_specs=None, vmem=40):
+def call(body, out_shapes, scratch=(), flops=0, moved=0, in_specs=None, vmem=40 << 20):
     many = isinstance(out_shapes, (tuple, list))
 
     def run(*operands):
@@ -28,7 +29,7 @@
             in_specs=in_specs or [VMEM] * len(operands),
             out_specs=[VMEM] * len(out_shapes) if many else VMEM,
             scratch_shapes=list(scratch),
-            compiler_params=pltpu.CompilerParams(vmem_limit_bytes=vmem * 1024 * 1024),
+            compiler_params=pltpu.CompilerParams(vmem_limit_bytes=vmem),
             cost_estimate=pl.CostEstimate(
                 flops=flops, bytes_accessed=moved, transcendentals=0
             ),
@@ -55,28 +56,33 @@
     )
 
 
-def stats_body(lat_ref, gain_ref, bias_ref, ws_ref, wt_ref, out_ref, affine_ref, half_ref, sem):
+def stats_body(lat_ref, gain_ref, bias_ref, ws_ref, wt_ref, out_ref, affine_ref, half_ref, *scratch):
+    lat_here, gain_here, bias_here, sems = scratch
     core = lax.rem(lax.axis_index("wide"), 2)
-    copies, place = [], 0
-    for at, source in enumerate((ws_ref, wt_ref)):
+    moves, place = [(lat_ref, lat_here), (gain_ref, gain_here), (bias_ref, bias_here)], 0
+    for source in (ws_ref, wt_ref):
         half = source.shape[0] // 2
         start = pl.multiple_of(core * half, 16)
-        copies.append(
-            pltpu.make_async_copy(
-                source.at[pl.ds(start, half)], half_ref.at[pl.ds(place, half)], sem.at[at]
-            )
-        )
-        copies[-1].start()
+        moves.append((source.at[pl.ds(start, half)], half_ref.at[pl.ds(place, half)]))
         place += half
-    affine_ref[0:1] = gain_ref[...]
-    affine_ref[1:2] = bias_ref[...]
-    x = lat_ref[...].astype(F32)
+    copies = [pltpu.make_async_copy(*move, sems.at[at]) for at, move in enumerate(moves)]
+    for copy in copies:
+        copy.start()
+    for copy in copies[:3]:
+        copy.wait()
+    affine_ref[0:1] = gain_here[...]
+    affine_ref[1:2] = bias_here[...]
+    x = lat_here[...].astype(F32)
     both = jnp.concatenate(
         [jnp.sum(x, axis=0, keepdims=True), jnp.sum(x * x, axis=0, keepdims=True)], axis=0
     )
     out_ref[...] = jnp.broadcast_to(both[None], out_ref.shape)
-    for copy in copies:
+    for copy in copies[3:]:
         copy.wait()
+
+
+def transpose_body(cot_ref, out_ref):
+    out_ref[...] = cot_ref[...].astype(F32).T.astype(BF16)
 
 
 def fill_weights(full, shard_ref, pieces, offset, D):
@@ -199,7 +205,7 @@
 
 
 def second_body(
-    sizes, lat_ref, cot_ref, halo_ref, stats_ref, affine_ref, gsa_ref, ws_ref, *rest
+    sizes, lat_ref, cot_t_ref, halo_ref, stats_ref, affine_ref, gsa_ref, ws_ref, *rest
 ):
     D, W, frames, cells, cols, count, per_group, aligned = sizes
     pieces, rest = rest[: 2 * (D - 1)], rest[2 * (D - 1) :]
@@ -214,10 +220,10 @@
     act = (normed * sig).astype(BF16).astype(F32)
     store_shifted(act_pad, act, frames, cells, cols)
     store_shifted(gsa_pad, gsa_ref[...].astype(F32), frames, cells, cols)
-    extended = jnp.concatenate([cot_ref[...], halo_ref[...]], axis=0)
-    for f in range(frames + 2):
-        cot_t[:, f * cells : (f + 1) * cells] = (
-            extended[f * cells : (f + 1) * cells].astype(F32).T.astype(BF16)
+    cot_t[:, :rows] = cot_t_ref[...]
+    for f in range(2):
+        cot_t[:, rows + f * cells : rows + (f + 1) * cells] = (
+            halo_ref[f * cells : (f + 1) * cells].astype(F32).T.astype(BF16)
         )
     left = core_order(cot_t, W, core) if aligned else cot_t[...]
     out = jnp.zeros((rows, channels), F32)
@@ -393,15 +399,21 @@
             shape((2, channels), F32),
             shape((R // 2, channels), BF16),
         ],
-        [pltpu.SemaphoreType.DMA((2,))],
-        in_specs=[VMEM, VMEM, VMEM, HBM, HBM],
-        vmem=60,
+        [
+            pltpu.VMEM((rows, channels), BF16),
+            pltpu.VMEM((1, channels), F32),
+            pltpu.VMEM((1, channels), F32),
+            pltpu.SemaphoreType.DMA((5,)),
+        ],
+        in_specs=[HBM] * 5,
+        vmem=FIRST_VMEM,
     )(lat, gain, bias, w_spatial, w_temporal)
+    cot_t = call(transpose_body, shape((channels, rows), BF16), moved=300_000)(cot)
     firsts = [send(half, lambda d, w: ((d + s) % D, w)) for s in range(1, D)]
 
     halo = lax.ppermute(cot, "wide", [(w + 1, w) for w in range(W - 1)])
     stats = lax.all_to_all(stats, "wide", split_axis=0, concat_axis=0, tiled=True)
-    firsts, stats, halo = lax.optimization_barrier((firsts, stats, halo))
+    firsts, stats, halo, cot_t = lax.optimization_barrier((firsts, stats, halo, cot_t))
     pieces = []
     for first in firsts:
         pieces += [first, send(first, lambda d, w: (d, w ^ 1))]
@@ -432,7 +444,7 @@
         ],
         flops=2 * 21 * rows * channels * channels,
         moved=3_000_000,
-    )(lat, cot, halo, stats, affine, gsa, w_spatial, *pieces)
+    )(lat, cot_t, halo, stats, affine, gsa, w_spatial, *pieces)
     before = lax.ppermute(spatial, "wide", [(w, w + 1) for w in range(W - 1)])
     block_out = call(
         functools.partial(block_body, sizes),

time: 50.4 us -> 49.5 us (0.982)
  blocking collectives: 13.3 us -> 0 us
  starting transfers between devices: 14.5 us -> 21.2 us
  waiting for transfers between devices: 13.3 us -> 19.8 us
  Pallas kernels: 8.16 us -> 7.42 us
    all_to_all x1 -> x0, blocking collectives: 13.3 us -> none  [local(): lax.all_to_all(stats, 'wide', split_axis=0, concat_axis=0, tiled=True)]
    all_to_all x0 -> x1, starting transfers between devices: none -> 6.68 us  [local(): lax.all_to_all(stats, 'wide', split_axis=0, concat_axis=0, tiled=True)]
    all_to_all x0 -> x1, waiting for transfers between devices: none -> 6.5 us  [local(): lax.all_to_all(stats, 'wide', split_axis=0, concat_axis=0, tiled=True)]
    pallas_call x7 -> x8, Pallas kernels: 8.16 us -> 7.42 us  [run(): pl.pallas_call(body, out_shape=out_shapes, in_specs=in_specs or [VMEM] *...]
  transfers between devices with their start and end apart: 12 -> 13, of which waited for: 7 -> 8; matrix products, arithmetic and copies ran while one was open for 0% -> 0% of each run, Pallas kernels for 6% -> 6%
where the time goes in v6:
time: 49.5 us; the launch traced here: 49.2 us
  starting transfers between devices  21.2 us (43%)
  waiting for transfers between devices  19.8 us (40%)
  Pallas kernels  7.42 us (15%)
  between operations  0.75 us (2%)
    ppermute x10, waiting for transfers between devices, send(): return lax.ppermute(value, ('dp', 'wide'), over_all(moves))  13.3 us
    ppermute x10, starting transfers between devices, send(): return lax.ppermute(value, ('dp', 'wide'), over_all(moves))  11.8 us
    pallas_call x8, Pallas kernels, run(): pl.pallas_call(body, out_shape=out_shapes, in_specs=in_specs or [VMEM] *...  7.42 us
    all_to_all x1, starting transfers between devices, local(): lax.all_to_all(stats, 'wide', split_axis=0, concat_axis=0, tiled=True)  6.68 us
    all_to_all x1, waiting for transfers between devices, local(): lax.all_to_all(stats, 'wide', split_axis=0, concat_axis=0, tiled=True)  6.5 us
    ppermute x1, starting transfers between devices, local(): before = lax.ppermute(spatial, 'wide', [(w, w + 1) for w in range(W - 1)])  1.42 us
    ppermute x1, starting transfers between devices, local(): halo = lax.ppermute(cot, 'wide', [(w + 1, w) for w in range(W - 1)])  1.28 us
  transfers between devices with their start and end apart: 13, of which 8 were waited for; matrix products, arithmetic and copies ran while one was open for 0% of the time, Pallas kernels for 6%

profile of v6, /device:TPU:0, one launch (start us, length us, event | category | flops | bytes accessed | tf_op | source)
XLA Modules:
  0.0 49.2 jit_solution(559666348680829633)
XLA Ops:
  0.6 1.9 %shard_map.101 = (f32[16,2,256]{2,1,0:T(2,128)}, f32[2,256]{1,0:T(2,128)}, bf16[768,256]{1,0:T(8,128)(2,1)}) custom-call(bf16[256,256]{1,0:T(8,128)(2,1)} %bitcast.12, f32[1,256]{1,0:T(1,128)} %bitcast.26, f32[1,256]{1,0:T(1,128)} %bitcast.27, bf16[1152,256]{1,0:T(8,128)(2,1)} %ws_ref.3, bf16[384,256]{1,0:T(8,128)(2,1)} %wt_ref.5), custom_call_target="tpu_custom_call" | custom-call | tf_op jit(solution)/shard_map/pallas_call | solution.py:26
  2.6 0.0 copy-start.1
  2.6 3.0 %collective-permute-start = (bf16[768,256]{1,0:T(8,128)(2,1)}, bf16[768,256]{1,0:T(8,128)(2,1)S(1)}, u32[]{:S(2)}, u32[]{:S(2)}) collective-permute-start(bf16[768,256]{1,0:T(8,128)(2,1)} %get-tuple-element.31), channel_id=1, source_target_pairs={{0,16},{1,17},{2,18},{3,19},{4,20},{5,21},{6,22},{7,23},{8,24},{9,... | collective-permute-start | bytes 1179656 | tf_op jit(solution)/shard_map/ppermute | solution.py:392
  5.6 1.3 %collective-permute-start.1 = (bf16[256,256]{1,0:T(8,128)(2,1)S(1)}, bf16[256,256]{1,0:T(8,128)(2,1)S(1)}, u32[]{:S(2)}, u32[]{:S(2)}) collective-permute-start(bf16[256,256]{1,0:T(8,128)(2,1)S(1)} %bitcast.19), channel_id=1, source_target_pairs={{1,0},{2,1},{3,2},{4,3},{5,4},{6,5},{7,6},{8,7},{9,8},{10,9},{11,1... | collective-permute-start | bytes 393224 | tf_op jit(solution)/shard_map/ppermute | solution.py:414
  6.9 6.7 %all-to-all-start = ((f32[16,2,256]{2,1,0:T(2,128)}), f32[16,2,256]{2,1,0:T(2,128)S(1)}, u32[]{:S(2)}, u32[]{:S(2)}) async-start(f32[16,2,256]{2,1,0:T(2,128)} %get-tuple-element.32), calls=%async_computation | async-start | bytes 65536 | tf_op jit(solution)/shard_map/all_to_all | solution.py:415
  13.6 0.0 copy-start
  13.6 0.0 copy-start.4
  13.6 0.1 shard_map.102.cot_t_ref
  13.7 6.5 %all-to-all-done.stats_ref.refs_6_ = f32[16,2,256]{2,1,0:T(2,128)S(1)} async-done(((f32[16,2,256]{2,1,0:T(2,128)}), f32[16,2,256]{2,1,0:T(2,128)S(1)}, u32[]{:S(2)}, u32[]{:S(2)}) %all-to-all-start) | async-done | bytes 32800 | tf_op jit(solution)/shard_map/all_to_all | solution.py:415
  20.2 1.7 %collective-permute-done.2.rest_1_ = bf16[768,256]{1,0:T(8,128)(2,1)S(1)} collective-permute-done((bf16[768,256]{1,0:T(8,128)(2,1)S(1)}, bf16[768,256]{1,0:T(8,128)(2,1)S(1)}, u32[]{:S(2)}, u32[]{:S(2)}) %collective-permute-start.2) | collective-permute-done | bytes 393248 | tf_op jit(solution)/shard_map/ppermute | solution.py:392
  21.9 0.0 copy-start.2
  22.0 1.0 %shard_map.103 = (bf16[256,256]{1,0:T(8,128)(2,1)S(1)}, bf16[2,128,1152]{2,1,0:T(8,128)(2,1)S(1)}, bf16[2,128,1152]{2,1,0:T(8,128)(2,1)S(1)}) custom-call(bf16[256,256]{1,0:T(8,128)(2,1)S(1)} %bitcast.13, bf16[256,256]{1,0:T(8,128)(2,1)S(1)} %bitcast.21, bf16[256,256]{1,0:T(8,128)(2,1)S(1)} %collective-permute-done.1.halo_ref, ...), custom_call_target="tpu_custom_call" | custom-call | flops 402653184 | bytes 3000000 | tf_op jit(solution)/shard_map/pallas_call | solution.py:26
  23.0 0.2 collective-permute-start.4
  23.2 1.9 %shard_map.104 = (bf16[256,256]{1,0:T(8,128)(2,1)S(1)}, f32[256,256]{1,0:T(8,128)S(1)}, bf16[2,128,512]{2,1,0:T(8,128)(2,1)S(1)}, bf16[2,128,512]{2,1,0:T(8,128)(2,1)S(1)}) custom-call(bf16[256,256]{1,0:T(8,128)(2,1)S(1)} %bitcast.14, bf16[256,256]{1,0:T(8,128)(2,1)S(1)} %shard_map.102.cot_t_ref, bf16[256,256]{1,0:T(8,128)(2,1)S(1)} %collective-permute-done.1.halo_ref, ...), custom_call_target="tpu_custom_call" | custom-call | flops 704643072 | bytes 3000000 | tf_op jit(solution)/shard_map/pallas_call | solution.py:26
  25.1 0.4 collective-permute-start.5
  25.6 1.2 %collective-permute-done.5 = bf16[2,128,512]{2,1,0:T(8,128)(2,1)S(1)} collective-permute-done((bf16[2,128,512]{2,1,0:T(8,128)(2,1)S(1)}, bf16[2,128,512]{2,1,0:T(8,128)(2,1)S(1)}, u32[]{:S(2)}, u32[]{:S(2)}) %collective-permute-start.5) | collective-permute-done | bytes 262176 | tf_op jit(solution)/shard_map/ppermute | solution.py:392
  26.7 0.2 shard_map.106
  27.0 0.4 collective-permute-start.6
  27.4 0.5 %collective-permute-start.7 = (bf16[4,16,1664]{2,1,0:T(8,128)(2,1)S(1)}, bf16[4,16,1664]{2,1,0:T(8,128)(2,1)S(1)}, u32[]{:S(2)}, u32[]{:S(2)}) collective-permute-start(bf16[4,16,1664]{2,1,0:T(8,128)(2,1)S(1)} %get-tuple-element.46), channel_id=1, source_target_pairs={{0,16},{1,17},{2,18},{3,19},{4,20},{5,21},{6,22},{7,23},{8,24},{9,... | collective-permute-start | bytes 638984 | tf_op jit(solution)/shard_map/ppermute | solution.py:392
  27.9 2.6 %collective-permute-start.8 = (bf16[4,16,1664]{2,1,0:T(8,128)(2,1)S(1)}, bf16[4,16,1664]{2,1,0:T(8,128)(2,1)S(1)}, u32[]{:S(2)}, u32[]{:S(2)}) collective-permute-start(bf16[4,16,1664]{2,1,0:T(8,128)(2,1)S(1)} %get-tuple-element.47), channel_id=1, source_target_pairs={{0,18},{1,19},{2,16},{3,17},{4,22},{5,23},{6,20},{7,21},{8,26},{9,... | collective-permute-start | bytes 638984 | tf_op jit(solution)/shard_map/ppermute | solution.py:392
  30.5 1.4 %collective-permute-start.3 = (bf16[256,256]{1,0:T(8,128)(2,1)S(1)}, bf16[256,256]{1,0:T(8,128)(2,1)S(1)}, u32[]{:S(2)}, u32[]{:S(2)}) collective-permute-start(bf16[256,256]{1,0:T(8,128)(2,1)S(1)} %get-tuple-element.39.spatial_ref), channel_id=1, source_target_pairs={{0,1},{1,2},{2,3},{3,4},{4,5},{5,6},{6,7},{7,8},{8,9},{9,10},{10,1... | collective-permute-start | bytes 393224 | tf_op jit(solution)/shard_map/ppermute | solution.py:448
  32.0 2.6 %collective-permute-done.6.refs_1_ = bf16[4,16,1664]{2,1,0:T(8,128)(2,1)S(1)} collective-permute-done((bf16[4,16,1664]{2,1,0:T(8,128)(2,1)S(1)}, bf16[4,16,1664]{2,1,0:T(8,128)(2,1)S(1)}, u32[]{:S(2)}, u32[]{:S(2)}) %collective-permute-start.6) | collective-permute-done | bytes 213024 | tf_op jit(solution)/shard_map/ppermute | solution.py:392
  34.6 0.9 %collective-permute-done.7.refs_2_ = bf16[4,16,1664]{2,1,0:T(8,128)(2,1)S(1)} collective-permute-done((bf16[4,16,1664]{2,1,0:T(8,128)(2,1)S(1)}, bf16[4,16,1664]{2,1,0:T(8,128)(2,1)S(1)}, u32[]{:S(2)}, u32[]{:S(2)}) %collective-permute-start.7) | collective-permute-done | bytes 213024 | tf_op jit(solution)/shard_map/ppermute | solution.py:392
  35.5 4.8 %collective-permute-done.8.refs_3_ = bf16[4,16,1664]{2,1,0:T(8,128)(2,1)S(1)} collective-permute-done((bf16[4,16,1664]{2,1,0:T(8,128)(2,1)S(1)}, bf16[4,16,1664]{2,1,0:T(8,128)(2,1)S(1)}, u32[]{:S(2)}, u32[]{:S(2)}) %collective-permute-start.8) | collective-permute-done | bytes 213024 | tf_op jit(solution)/shard_map/ppermute | solution.py:392
  40.3 0.1 shard_map.107
  40.4 1.6 %collective-permute-start.9 = (bf16[16,1664]{1,0:T(8,128)(2,1)S(1)}, bf16[16,1664]{1,0:T(8,128)(2,1)S(1)}, u32[]{:S(2)}, u32[]{:S(2)}) collective-permute-start(bf16[16,1664]{1,0:T(8,128)(2,1)S(1)} %get-tuple-element.49), channel_id=1, source_target_pairs={{0,4},{1,5},{2,6},{3,7},{4,8},{5,9},{6,10},{7,11},{8,12},{9,13},{1... | collective-permute-start | bytes 159752 | tf_op jit(solution)/shard_map/ppermute | solution.py:392
  42.1 0.7 %collective-permute-start.10 = (bf16[16,1664]{1,0:T(8,128)(2,1)S(1)}, bf16[16,1664]{1,0:T(8,128)(2,1)S(1)}, u32[]{:S(2)}, u32[]{:S(2)}) collective-permute-start(bf16[16,1664]{1,0:T(8,128)(2,1)S(1)} %get-tuple-element.50), channel_id=1, source_target_pairs={{0,8},{1,9},{2,10},{3,11},{4,12},{5,13},{6,14},{7,15},{8,0},{9,1},... | collective-permute-start | bytes 159752 | tf_op jit(solution)/shard_map/ppermute | solution.py:392
  42.8 2.3 %collective-permute-start.11 = (bf16[16,1664]{1,0:T(8,128)(2,1)S(1)}, bf16[16,1664]{1,0:T(8,128)(2,1)S(1)}, u32[]{:S(2)}, u32[]{:S(2)}) collective-permute-start(bf16[16,1664]{1,0:T(8,128)(2,1)S(1)} %get-tuple-element.51), channel_id=1, source_target_pairs={{0,12},{1,13},{2,14},{3,15},{4,0},{5,1},{6,2},{7,3},{8,4},{9,5},{1... | collective-permute-start | bytes 159752 | tf_op jit(solution)/shard_map/ppermute | solution.py:392
  45.0 1.0 %shard_map.105 = bf16[256,256]{1,0:T(8,128)(2,1)} custom-call(bf16[256,256]{1,0:T(8,128)(2,1)S(1)} %bitcast.15, bf16[256,256]{1,0:T(8,128)(2,1)S(1)} %get-tuple-element.39.spatial_ref, bf16[256,256]{1,0:T(8,128)(2,1)S(1)} %collective-permute-done.3.before_ref, bf16[384,256]{1,0:T(8,128)(2,1)S(1)} %copy-done.1, ...), custom_call_target="tpu_custom_call" | custom-call | flops 100663296 | bytes 1000000 | tf_op jit(solution)/shard_map/pallas_call | solution.py:26
  46.0 0.9 %collective-permute-done.9.refs_1_ = bf16[16,1664]{1,0:T(8,128)(2,1)S(1)} collective-permute-done((bf16[16,1664]{1,0:T(8,128)(2,1)S(1)}, bf16[16,1664]{1,0:T(8,128)(2,1)S(1)}, u32[]{:S(2)}, u32[]{:S(2)}) %collective-permute-start.9) | collective-permute-done | bytes 53280 | tf_op jit(solution)/shard_map/ppermute | solution.py:392
  46.9 1.2 %collective-permute-done.10.refs_2_ = bf16[16,1664]{1,0:T(8,128)(2,1)S(1)} collective-permute-done((bf16[16,1664]{1,0:T(8,128)(2,1)S(1)}, bf16[16,1664]{1,0:T(8,128)(2,1)S(1)}, u32[]{:S(2)}, u32[]{:S(2)}) %collective-permute-start.10) | collective-permute-done | bytes 53280 | tf_op jit(solution)/shard_map/ppermute | solution.py:392
  48.1 1.1 %shard_map.108 = (f32[16,1152]{1,0:T(8,128)}, f32[16,384]{1,0:T(8,128)}, f32[2,16]{1,0:T(2,128)}, bf16[256,256]{1,0:T(8,128)(2,1)}) custom-call(bf16[16,1664]{1,0:T(8,128)(2,1)S(1)} %get-tuple-element.48.refs_0_, bf16[16,1664]{1,0:T(8,128)(2,1)S(1)} %collective-permute-done.9.refs_1_, bf16[16,1664]{1,0:T(8,128)(2,1)S(1)} %collective-permute-done.10.refs_2_, ...), custom_call_target="tpu_custom_call" | custom-call | bytes 1000000 | tf_op jit(solution)/shard_map/pallas_call | solution.py:26
  (12 shorter events, 0.0 us)
Async XLA Ops:
  0.6 5.0 %copy-start.3 = (bf16[1,2,8,16,256]{4,3,2,1,0:T(8,128)(2,1)S(1)}, bf16[1,2,8,16,256]{4,3,2,1,0:T(8,128)(2,1)}, u32[]{:S(2)}) copy-start(bf16[1,2,8,16,256]{4,3,2,1,0:T(8,128)(2,1)} %param.7) | copy-start | bytes 393220
  2.6 19.4 %copy-start.1 = (bf16[384,256]{1,0:T(8,128)(2,1)S(1)}, bf16[384,256]{1,0:T(8,128)(2,1)}, u32[]{:S(2)}) copy-start(bf16[384,256]{1,0:T(8,128)(2,1)} %wt_ref.5) | copy-start | bytes 589828
  2.6 17.6 %collective-permute-start = (bf16[768,256]{1,0:T(8,128)(2,1)}, bf16[768,256]{1,0:T(8,128)(2,1)S(1)}, u32[]{:S(2)}, u32[]{:S(2)}) collective-permute-start(bf16[768,256]{1,0:T(8,128)(2,1)} %get-tuple-element.31), channel_id=1, source_target_pairs={{0,16},{1,17},{2,18},{3,19},{4,20},{5,21},{6,22},{7,23},{8,24},{9,... | collective-permute-start | bytes 1179656 | tf_op jit(solution)/shard_map/ppermute | solution.py:392
  5.6 14.6 %collective-permute-start.1 = (bf16[256,256]{1,0:T(8,128)(2,1)S(1)}, bf16[256,256]{1,0:T(8,128)(2,1)S(1)}, u32[]{:S(2)}, u32[]{:S(2)}) collective-permute-start(bf16[256,256]{1,0:T(8,128)(2,1)S(1)} %bitcast.19), channel_id=1, source_target_pairs={{1,0},{2,1},{3,2},{4,3},{5,4},{6,5},{7,6},{8,7},{9,8},{10,9},{11,1... | collective-permute-start | bytes 393224 | tf_op jit(solution)/shard_map/ppermute | solution.py:414
  6.9 13.3 %all-to-all-start = ((f32[16,2,256]{2,1,0:T(2,128)}), f32[16,2,256]{2,1,0:T(2,128)S(1)}, u32[]{:S(2)}, u32[]{:S(2)}) async-start(f32[16,2,256]{2,1,0:T(2,128)} %get-tuple-element.32), calls=%async_computation | async-start | bytes 65536 | tf_op jit(solution)/shard_map/all_to_all | solution.py:415
  13.6 8.4 %copy-start = (bf16[1,2,8,16,256]{4,3,2,1,0:T(8,128)(2,1)S(1)}, bf16[1,2,8,16,256]{4,3,2,1,0:T(8,128)(2,1)}, u32[]{:S(2)}) copy-start(bf16[1,2,8,16,256]{4,3,2,1,0:T(8,128)(2,1)} %param.6) | copy-start | bytes 393220
  13.6 8.4 %copy-start.4 = (f32[2,256]{1,0:T(2,128)S(1)}, f32[2,256]{1,0:T(2,128)}, u32[]{:S(2)}) copy-start(f32[2,256]{1,0:T(2,128)} %get-tuple-element.36.affine_ref.refs_7_) | copy-start | bytes 6148
  20.2 1.7 %collective-permute-start.2 = (bf16[768,256]{1,0:T(8,128)(2,1)S(1)}, bf16[768,256]{1,0:T(8,128)(2,1)S(1)}, u32[]{:S(2)}, u32[]{:S(2)}) collective-permute-start(bf16[768,256]{1,0:T(8,128)(2,1)S(1)} %collective-permute-done.rest_0_), channel_id=1, source_target_pairs={{0,1},{1,0},{2,3},{3,2},{4,5},{5,4},{6,7},{7,6},{8,9},{9,8},{10,11... | collective-permute-start | bytes 1179656 | tf_op jit(solution)/shard_map/ppermute | solution.py:392
  21.9 1.2 %copy-start.2 = (bf16[1152,256]{1,0:T(8,128)(2,1)S(1)}, bf16[1152,256]{1,0:T(8,128)(2,1)}, u32[]{:S(2)}) copy-start(bf16[1152,256]{1,0:T(8,128)(2,1)} %ws_ref.3) | copy-start | bytes 1769476
  23.0 3.8 %collective-permute-start.4 = (bf16[2,128,1152]{2,1,0:T(8,128)(2,1)S(1)}, bf16[2,128,1152]{2,1,0:T(8,128)(2,1)S(1)}, u32[]{:S(2)}, u32[]{:S(2)}) collective-permute-start(bf16[2,128,1152]{2,1,0:T(8,128)(2,1)S(1)} %get-tuple-element.41), channel_id=1, source_target_pairs={{0,1},{1,0},{2,3},{3,2},{4,5},{5,4},{6,7},{7,6},{8,9},{9,8},{10,11... | collective-permute-start | bytes 1769480 | tf_op jit(solution)/shard_map/ppermute | solution.py:392
  25.1 1.6 %collective-permute-start.5 = (bf16[2,128,512]{2,1,0:T(8,128)(2,1)S(1)}, bf16[2,128,512]{2,1,0:T(8,128)(2,1)S(1)}, u32[]{:S(2)}, u32[]{:S(2)}) collective-permute-start(bf16[2,128,512]{2,1,0:T(8,128)(2,1)S(1)} %get-tuple-element.43), channel_id=1, source_target_pairs={{0,1},{1,0},{2,3},{3,2},{4,5},{5,4},{6,7},{7,6},{8,9},{9,8},{10,11... | collective-permute-start | bytes 786440 | tf_op jit(solution)/shard_map/ppermute | solution.py:392
  27.0 7.6 %collective-permute-start.6 = (bf16[4,16,1664]{2,1,0:T(8,128)(2,1)S(1)}, bf16[4,16,1664]{2,1,0:T(8,128)(2,1)S(1)}, u32[]{:S(2)}, u32[]{:S(2)}) collective-permute-start(bf16[4,16,1664]{2,1,0:T(8,128)(2,1)S(1)} %get-tuple-element.45), channel_id=1, source_target_pairs={{0,2},{1,3},{2,0},{3,1},{4,6},{5,7},{6,4},{7,5},{8,10},{9,11},{10,... | collective-permute-start | bytes 638984 | tf_op jit(solution)/shard_map/ppermute | solution.py:392
  27.4 8.1 %collective-permute-start.7 = (bf16[4,16,1664]{2,1,0:T(8,128)(2,1)S(1)}, bf16[4,16,1664]{2,1,0:T(8,128)(2,1)S(1)}, u32[]{:S(2)}, u32[]{:S(2)}) collective-permute-start(bf16[4,16,1664]{2,1,0:T(8,128)(2,1)S(1)} %get-tuple-element.46), channel_id=1, source_target_pairs={{0,16},{1,17},{2,18},{3,19},{4,20},{5,21},{6,22},{7,23},{8,24},{9,... | collective-permute-start | bytes 638984 | tf_op jit(solution)/shard_map/ppermute | solution.py:392
  27.9 12.4 %collective-permute-start.8 = (bf16[4,16,1664]{2,1,0:T(8,128)(2,1)S(1)}, bf16[4,16,1664]{2,1,0:T(8,128)(2,1)S(1)}, u32[]{:S(2)}, u32[]{:S(2)}) collective-permute-start(bf16[4,16,1664]{2,1,0:T(8,128)(2,1)S(1)} %get-tuple-element.47), channel_id=1, source_target_pairs={{0,18},{1,19},{2,16},{3,17},{4,22},{5,23},{6,20},{7,21},{8,26},{9,... | collective-permute-start | bytes 638984 | tf_op jit(solution)/shard_map/ppermute | solution.py:392
  30.5 14.5 %collective-permute-start.3 = (bf16[256,256]{1,0:T(8,128)(2,1)S(1)}, bf16[256,256]{1,0:T(8,128)(2,1)S(1)}, u32[]{:S(2)}, u32[]{:S(2)}) collective-permute-start(bf16[256,256]{1,0:T(8,128)(2,1)S(1)} %get-tuple-element.39.spatial_ref), channel_id=1, source_target_pairs={{0,1},{1,2},{2,3},{3,4},{4,5},{5,6},{6,7},{7,8},{8,9},{9,10},{10,1... | collective-permute-start | bytes 393224 | tf_op jit(solution)/shard_map/ppermute | solution.py:448
  40.4 6.5 %collective-permute-start.9 = (bf16[16,1664]{1,0:T(8,128)(2,1)S(1)}, bf16[16,1664]{1,0:T(8,128)(2,1)S(1)}, u32[]{:S(2)}, u32[]{:S(2)}) collective-permute-start(bf16[16,1664]{1,0:T(8,128)(2,1)S(1)} %get-tuple-element.49), channel_id=1, source_target_pairs={{0,4},{1,5},{2,6},{3,7},{4,8},{5,9},{6,10},{7,11},{8,12},{9,13},{1... | collective-permute-start | bytes 159752 | tf_op jit(solution)/shard_map/ppermute | solution.py:392
  42.1 6.0 %collective-permute-start.10 = (bf16[16,1664]{1,0:T(8,128)(2,1)S(1)}, bf16[16,1664]{1,0:T(8,128)(2,1)S(1)}, u32[]{:S(2)}, u32[]{:S(2)}) collective-permute-start(bf16[16,1664]{1,0:T(8,128)(2,1)S(1)} %get-tuple-element.50), channel_id=1, source_target_pairs={{0,8},{1,9},{2,10},{3,11},{4,12},{5,13},{6,14},{7,15},{8,0},{9,1},... | collective-permute-start | bytes 159752 | tf_op jit(solution)/shard_map/ppermute | solution.py:392
  42.8 5.3 %collective-permute-start.11 = (bf16[16,1664]{1,0:T(8,128)(2,1)S(1)}, bf16[16,1664]{1,0:T(8,128)(2,1)S(1)}, u32[]{:S(2)}, u32[]{:S(2)}) collective-permute-start(bf16[16,1664]{1,0:T(8,128)(2,1)S(1)} %get-tuple-element.51), channel_id=1, source_target_pairs={{0,12},{1,13},{2,14},{3,15},{4,0},{5,1},{6,2},{7,3},{8,4},{9,5},{1... | collective-permute-start | bytes 159752 | tf_op jit(solution)/shard_map/ppermute | solution.py:392

commit v7 on v6

--- a/solution.py
+++ b/solution.py
@@ -295,38 +295,36 @@
 def plane_body(keep_s, got_s, keep_t, got_t, *outs):
     d = lax.axis_index("dp")
     y = lax.rem(lax.axis_index("wide") // 2, 2)
-    split = keep_s.shape[-1]
-    ride = outs[0].shape[-1] - 128
     for a in range(2):
         for b in range(2):
             owner, side = lax.rem(d + a, 2), lax.rem(y + b, 2)
-            out = outs[2 * a + b]
-            for z in range(out.shape[0]):
-                out[z, :, :split] = add([keep_s[owner, z, side], got_s[owner, z, side]]).astype(
-                    BF16
-                )
+            out_s, out_t = outs[2 * a + b], outs[4 + 2 * a + b]
+            ride = out_t.shape[-1] - 128
+            for z in range(out_s.shape[0]):
+                out_s[z] = add([keep_s[owner, z, side], got_s[owner, z, side]]).astype(BF16)
                 both = [keep_t[owner, z, side], got_t[owner, z, side]]
-                out[z, :, split:ride] = add([t[:, : ride - split] for t in both]).astype(BF16)
-                out[z, :, ride:] = in_parts(from_parts([t[:, ride - split :] for t in both]))
-
-
-def line_body(depth, *refs):
+                out_t[z, :, :ride] = add([t[:, :ride] for t in both]).astype(BF16)
+                out_t[z, :, ride:] = in_parts(from_parts([t[:, ride:] for t in both]))
+
+
+def line_body(depth, ride, *refs):
     terms, outs = refs[:4], refs[4:]
     z = lax.axis_index("wide") // 4
-    ride = outs[0].shape[-1] - 128
+    width = outs[0].shape[-1] - ride
     for s in range(depth):
         owner = lax.rem(z + s, depth)
         seen = [term[owner] for term in terms]
-        outs[s][:, :ride] = add([t[:, :ride] for t in seen]).astype(BF16)
-        outs[s][:, ride:] = in_parts(from_parts([t[:, ride:] for t in seen]))
+        outs[s][:, :width] = add([t[:, :width] for t in seen]).astype(BF16)
+        if ride:
+            outs[s][:, width:] = in_parts(from_parts([t[:, width:] for t in seen]))
 
 
 def last_body(sizes, scale, depth, *refs):
-    terms, operands, outs = refs[:depth], refs[depth:-4], refs[-4:]
+    terms_s, terms_t = refs[:depth], refs[depth : 2 * depth]
+    operands, outs = refs[2 * depth : -4], refs[-4:]
     spatial_ref, temporal_ref, norm_ref, glat_ref = outs
-    split = spatial_ref.shape[1]
-    ride = terms[0].shape[1] - 128
-    sums = from_parts([term[:, ride:] for term in terms])
+    ride = temporal_ref.shape[1]
+    sums = from_parts([term[:, ride:] for term in terms_t])
 
     def rows_of(part):
         return jnp.concatenate(
@@ -338,9 +336,8 @@
     own = jnp.where(lax.axis_index("dp") == 0, first, second)
     glat_ref[...] = latent_gradient(sizes, own, *operands)
     norm_columns(scale, first + second, norm_ref)
-    total = add([term[:, :ride] for term in terms]) * scale
-    spatial_ref[...] = total[:, :split]
-    temporal_ref[...] = total[:, split:]
+    spatial_ref[...] = add([term[...] for term in terms_s]) * scale
+    temporal_ref[...] = add([term[:, :ride] for term in terms_t]) * scale
 
 
 def apart_body(sizes, scale, sums_ref, *refs):
@@ -467,20 +464,25 @@
             view = (D, Z, 2, width, keep.shape[-1])
             pairs += [keep.reshape(view), over_core(away).reshape(view)]
         plane = call(
-            plane_body, [shape((Z, width, R + ride), BF16)] * (2 * D), moved=3_000_000
+            plane_body,
+            [shape((Z, width, shard_s), BF16)] * 4 + [shape((Z, width, shard_t + ride), BF16)] * 4,
+            moved=3_000_000,
         )(*pairs)
-        seen = [plane[0]] + [
-            send(plane[2 * a + b], lambda d, w: ((d + a) % D, w ^ (2 * b)))
-            for a, b in ((0, 1), (1, 0), (1, 1))
-        ]
-        line = call(
-            functools.partial(line_body, Z),
-            [shape((width, R + ride), BF16)] * Z,
-            moved=1_000_000,
-        )(*seen)
-        terms = [line[0]]
-        for s in range(1, Z):
-            terms.append(send(line[s], lambda d, w: (d, (w + 4 * s) % W)))
+        parts = []
+        for sums, extra in ((plane[:4], 0), (plane[4:], ride)):
+            seen = [sums[0]] + [
+                send(sums[2 * a + b], lambda d, w: ((d + a) % D, w ^ (2 * b)))
+                for a, b in ((0, 1), (1, 0), (1, 1))
+            ]
+            line = call(
+                functools.partial(line_body, Z, extra),
+                [shape((width, sums[0].shape[-1]), BF16)] * Z,
+                moved=1_000_000,
+            )(*seen)
+            parts.append([line[0]])
+            for s in range(1, Z):
+                parts[-1].append(send(line[s], lambda d, w: (d, (w + 4 * s) % W)))
+        terms = parts[0] + parts[1]
         grad_s, grad_t, norm, grad_latents = call(
             functools.partial(last_body, sizes, scale, Z),
             [

time: 49.5 us -> 55.2 us (1.12)
  starting transfers between devices: 21.2 us -> 26.2 us
  waiting for transfers between devices: 19.8 us -> 20.5 us
    ppermute x10 -> x16, starting transfers between devices: 11.8 us -> 16.8 us  [send(): return lax.ppermute(value, ('dp', 'wide'), over_all(moves))]
    ppermute x10 -> x16, waiting for transfers between devices: 13.3 us -> 14 us  [send(): return lax.ppermute(value, ('dp', 'wide'), over_all(moves))]
    pallas_call x8 -> x9, Pallas kernels: 7.42 us -> 7.44 us  [run(): pl.pallas_call(body, out_shape=out_shapes, in_specs=in_specs or [VMEM] *...]
  transfers between devices with their start and end apart: 13 -> 19, of which waited for: 8 -> 9; matrix products, arithmetic and copies ran while one was open for 0% -> 0% of each run, Pallas kernels for 6% -> 6%
where the time goes in v7:
time: 55.2 us; the launch traced here: 55 us
  starting transfers between devices  26.2 us (47%)
  waiting for transfers between devices  20.5 us (37%)
  Pallas kernels  7.44 us (13%)
  between operations  0.78 us (1%)
    ppermute x16, starting transfers between devices, send(): return lax.ppermute(value, ('dp', 'wide'), over_all(moves))  16.8 us
    ppermute x16, waiting for transfers between devices, send(): return lax.ppermute(value, ('dp', 'wide'), over_all(moves))  14 us
    pallas_call x9, Pallas kernels, run(): pl.pallas_call(body, out_shape=out_shapes, in_specs=in_specs or [VMEM] *...  7.44 us
    all_to_all x1, starting transfers between devices, local(): lax.all_to_all(stats, 'wide', split_axis=0, concat_axis=0, tiled=True)  6.68 us
    all_to_all x1, waiting for transfers between devices, local(): lax.all_to_all(stats, 'wide', split_axis=0, concat_axis=0, tiled=True)  6.5 us
    ppermute x1, starting transfers between devices, local(): before = lax.ppermute(spatial, 'wide', [(w, w + 1) for w in range(W - 1)])  1.42 us
    ppermute x1, starting transfers between devices, local(): halo = lax.ppermute(cot, 'wide', [(w + 1, w) for w in range(W - 1)])  1.28 us
  transfers between devices with their start and end apart: 19, of which 9 were waited for; matrix products, arithmetic and copies ran while one was open for 0% of the time, Pallas kernels for 6%

profile of v7, /device:TPU:0, one launch (start us, length us, event | category | flops | bytes accessed | tf_op | source)
XLA Modules:
  0.0 55.0 jit_solution(10451056307183460502)
XLA Ops:
  0.6 1.9 %shard_map.101 = (f32[16,2,256]{2,1,0:T(2,128)}, f32[2,256]{1,0:T(2,128)}, bf16[768,256]{1,0:T(8,128)(2,1)}) custom-call(bf16[256,256]{1,0:T(8,128)(2,1)} %bitcast.12, f32[1,256]{1,0:T(1,128)} %bitcast.26, f32[1,256]{1,0:T(1,128)} %bitcast.27, bf16[1152,256]{1,0:T(8,128)(2,1)} %ws_ref.3, bf16[384,256]{1,0:T(8,128)(2,1)} %wt_ref.5), custom_call_target="tpu_custom_call" | custom-call | tf_op jit(solution)/shard_map/pallas_call | solution.py:26
  2.6 3.0 %collective-permute-start = (bf16[768,256]{1,0:T(8,128)(2,1)}, bf16[768,256]{1,0:T(8,128)(2,1)S(1)}, u32[]{:S(2)}, u32[]{:S(2)}) collective-permute-start(bf16[768,256]{1,0:T(8,128)(2,1)} %get-tuple-element.39), channel_id=1, source_target_pairs={{0,16},{1,17},{2,18},{3,19},{4,20},{5,21},{6,22},{7,23},{8,24},{9,... | collective-permute-start | bytes 1179656 | tf_op jit(solution)/shard_map/ppermute | solution.py:389
  5.6 1.3 %collective-permute-start.1 = (bf16[256,256]{1,0:T(8,128)(2,1)S(1)}, bf16[256,256]{1,0:T(8,128)(2,1)S(1)}, u32[]{:S(2)}, u32[]{:S(2)}) collective-permute-start(bf16[256,256]{1,0:T(8,128)(2,1)S(1)} %bitcast.19), channel_id=1, source_target_pairs={{1,0},{2,1},{3,2},{4,3},{5,4},{6,5},{7,6},{8,7},{9,8},{10,9},{11,1... | collective-permute-start | bytes 393224 | tf_op jit(solution)/shard_map/ppermute | solution.py:411
  6.9 6.7 %all-to-all-start = ((f32[16,2,256]{2,1,0:T(2,128)}), f32[16,2,256]{2,1,0:T(2,128)S(1)}, u32[]{:S(2)}, u32[]{:S(2)}) async-start(f32[16,2,256]{2,1,0:T(2,128)} %get-tuple-element.40), calls=%async_computation | async-start | bytes 65536 | tf_op jit(solution)/shard_map/all_to_all | solution.py:412
  13.6 0.1 shard_map.102.cot_t_ref
  13.7 6.5 %all-to-all-done.stats_ref.refs_10_ = f32[16,2,256]{2,1,0:T(2,128)S(1)} async-done(((f32[16,2,256]{2,1,0:T(2,128)}), f32[16,2,256]{2,1,0:T(2,128)S(1)}, u32[]{:S(2)}, u32[]{:S(2)}) %all-to-all-start) | async-done | bytes 32800 | tf_op jit(solution)/shard_map/all_to_all | solution.py:412
  20.2 1.7 %collective-permute-done.2.rest_1_ = bf16[768,256]{1,0:T(8,128)(2,1)S(1)} collective-permute-done((bf16[768,256]{1,0:T(8,128)(2,1)S(1)}, bf16[768,256]{1,0:T(8,128)(2,1)S(1)}, u32[]{:S(2)}, u32[]{:S(2)}) %collective-permute-start.2) | collective-permute-done | bytes 393248 | tf_op jit(solution)/shard_map/ppermute | solution.py:389
  22.0 1.0 %shard_map.103 = (bf16[256,256]{1,0:T(8,128)(2,1)S(1)}, bf16[2,128,1152]{2,1,0:T(8,128)(2,1)S(1)}, bf16[2,128,1152]{2,1,0:T(8,128)(2,1)S(1)}) custom-call(bf16[256,256]{1,0:T(8,128)(2,1)S(1)} %bitcast.13, bf16[256,256]{1,0:T(8,128)(2,1)S(1)} %bitcast.21, bf16[256,256]{1,0:T(8,128)(2,1)S(1)} %collective-permute-done.1.halo_ref, ...), custom_call_target="tpu_custom_call" | custom-call | flops 402653184 | bytes 3000000 | tf_op jit(solution)/shard_map/pallas_call | solution.py:26
  23.0 0.2 collective-permute-start.4
  23.2 1.9 %shard_map.104 = (bf16[256,256]{1,0:T(8,128)(2,1)S(1)}, f32[256,256]{1,0:T(8,128)S(1)}, bf16[2,128,512]{2,1,0:T(8,128)(2,1)S(1)}, bf16[2,128,512]{2,1,0:T(8,128)(2,1)S(1)}) custom-call(bf16[256,256]{1,0:T(8,128)(2,1)S(1)} %bitcast.14, bf16[256,256]{1,0:T(8,128)(2,1)S(1)} %shard_map.102.cot_t_ref, bf16[256,256]{1,0:T(8,128)(2,1)S(1)} %collective-permute-done.1.halo_ref, ...), custom_call_target="tpu_custom_call" | custom-call | flops 704643072 | bytes 3000000 | tf_op jit(solution)/shard_map/pallas_call | solution.py:26
  25.1 0.4 collective-permute-start.5
  25.6 1.2 %collective-permute-done.5 = bf16[2,128,512]{2,1,0:T(8,128)(2,1)S(1)} collective-permute-done((bf16[2,128,512]{2,1,0:T(8,128)(2,1)S(1)}, bf16[2,128,512]{2,1,0:T(8,128)(2,1)S(1)}, u32[]{:S(2)}, u32[]{:S(2)}) %collective-permute-start.5) | collective-permute-done | bytes 262176 | tf_op jit(solution)/shard_map/ppermute | solution.py:389
  26.8 0.2 shard_map.106
  27.0 0.4 collective-permute-start.6
  27.4 0.5 collective-permute-start.7
  27.9 2.6 %collective-permute-start.8 = (bf16[4,16,1152]{2,1,0:T(8,128)(2,1)S(1)}, bf16[4,16,1152]{2,1,0:T(8,128)(2,1)S(1)}, u32[]{:S(2)}, u32[]{:S(2)}) collective-permute-start(bf16[4,16,1152]{2,1,0:T(8,128)(2,1)S(1)} %get-tuple-element.55), channel_id=1, source_target_pairs={{0,18},{1,19},{2,16},{3,17},{4,22},{5,23},{6,20},{7,21},{8,26},{9,... | collective-permute-start | bytes 442376 | tf_op jit(solution)/shard_map/ppermute | solution.py:389
  30.5 1.4 %collective-permute-start.3 = (bf16[256,256]{1,0:T(8,128)(2,1)S(1)}, bf16[256,256]{1,0:T(8,128)(2,1)S(1)}, u32[]{:S(2)}, u32[]{:S(2)}) collective-permute-start(bf16[256,256]{1,0:T(8,128)(2,1)S(1)} %get-tuple-element.47.spatial_ref), channel_id=1, source_target_pairs={{0,1},{1,2},{2,3},{3,4},{4,5},{5,6},{6,7},{7,8},{8,9},{9,10},{10,1... | collective-permute-start | bytes 393224 | tf_op jit(solution)/shard_map/ppermute | solution.py:445
  32.0 0.9 %collective-permute-start.12 = (bf16[4,16,512]{2,1,0:T(8,128)(2,1)S(1)}, bf16[4,16,512]{2,1,0:T(8,128)(2,1)S(1)}, u32[]{:S(2)}, u32[]{:S(2)}) collective-permute-start(bf16[4,16,512]{2,1,0:T(8,128)(2,1)S(1)} %get-tuple-element.61), channel_id=1, source_target_pairs={{0,2},{1,3},{2,0},{3,1},{4,6},{5,7},{6,4},{7,5},{8,10},{9,11},{10,... | collective-permute-start | bytes 196616 | tf_op jit(solution)/shard_map/ppermute | solution.py:389
  32.9 0.3 collective-permute-done.6.refs_1_
  33.2 0.5 collective-permute-start.13
  33.7 0.4 collective-permute-done.7.refs_2_
  34.1 1.7 %collective-permute-start.14 = (bf16[4,16,512]{2,1,0:T(8,128)(2,1)S(1)}, bf16[4,16,512]{2,1,0:T(8,128)(2,1)S(1)}, u32[]{:S(2)}, u32[]{:S(2)}) collective-permute-start(bf16[4,16,512]{2,1,0:T(8,128)(2,1)S(1)} %get-tuple-element.63), channel_id=1, source_target_pairs={{0,18},{1,19},{2,16},{3,17},{4,22},{5,23},{6,20},{7,21},{8,26},{9,... | collective-permute-start | bytes 196616 | tf_op jit(solution)/shard_map/ppermute | solution.py:389
  35.8 2.4 %collective-permute-done.8.refs_3_ = bf16[4,16,1152]{2,1,0:T(8,128)(2,1)S(1)} collective-permute-done((bf16[4,16,1152]{2,1,0:T(8,128)(2,1)S(1)}, bf16[4,16,1152]{2,1,0:T(8,128)(2,1)S(1)}, u32[]{:S(2)}, u32[]{:S(2)}) %collective-permute-start.8) | collective-permute-done | bytes 147488 | tf_op jit(solution)/shard_map/ppermute | solution.py:389
  38.3 1.1 %collective-permute-start.9 = (bf16[16,1152]{1,0:T(8,128)(2,1)S(1)}, bf16[16,1152]{1,0:T(8,128)(2,1)S(1)}, u32[]{:S(2)}, u32[]{:S(2)}) collective-permute-start(bf16[16,1152]{1,0:T(8,128)(2,1)S(1)} %get-tuple-element.57), channel_id=1, source_target_pairs={{0,4},{1,5},{2,6},{3,7},{4,8},{5,9},{6,10},{7,11},{8,12},{9,13},{1... | collective-permute-start | bytes 110600 | tf_op jit(solution)/shard_map/ppermute | solution.py:389
  39.3 0.3 collective-permute-done.12.refs_1_
  39.6 2.5 %collective-permute-start.10 = (bf16[16,1152]{1,0:T(8,128)(2,1)S(1)}, bf16[16,1152]{1,0:T(8,128)(2,1)S(1)}, u32[]{:S(2)}, u32[]{:S(2)}) collective-permute-start(bf16[16,1152]{1,0:T(8,128)(2,1)S(1)} %get-tuple-element.58), channel_id=1, source_target_pairs={{0,8},{1,9},{2,10},{3,11},{4,12},{5,13},{6,14},{7,15},{8,0},{9,1},... | collective-permute-start | bytes 110600 | tf_op jit(solution)/shard_map/ppermute | solution.py:389
  42.1 2.3 %collective-permute-start.11 = (bf16[16,1152]{1,0:T(8,128)(2,1)S(1)}, bf16[16,1152]{1,0:T(8,128)(2,1)S(1)}, u32[]{:S(2)}, u32[]{:S(2)}) collective-permute-start(bf16[16,1152]{1,0:T(8,128)(2,1)S(1)} %get-tuple-element.59), channel_id=1, source_target_pairs={{0,12},{1,13},{2,14},{3,15},{4,0},{5,1},{6,2},{7,3},{8,4},{9,5},{1... | collective-permute-start | bytes 110600 | tf_op jit(solution)/shard_map/ppermute | solution.py:389
  44.6 0.6 %collective-permute-start.16 = (bf16[16,512]{1,0:T(8,128)(2,1)S(1)}, bf16[16,512]{1,0:T(8,128)(2,1)S(1)}, u32[]{:S(2)}, u32[]{:S(2)}) collective-permute-start(bf16[16,512]{1,0:T(8,128)(2,1)S(1)} %get-tuple-element.66), channel_id=1, source_target_pairs={{0,8},{1,9},{2,10},{3,11},{4,12},{5,13},{6,14},{7,15},{8,0},{9,1},... | collective-permute-start | bytes 49160 | tf_op jit(solution)/shard_map/ppermute | solution.py:389
  45.1 5.0 %collective-permute-done.15.refs_5_ = bf16[16,512]{1,0:T(8,128)(2,1)S(1)} collective-permute-done((bf16[16,512]{1,0:T(8,128)(2,1)S(1)}, bf16[16,512]{1,0:T(8,128)(2,1)S(1)}, u32[]{:S(2)}, u32[]{:S(2)}) %collective-permute-start.15) | collective-permute-done | bytes 16416 | tf_op jit(solution)/shard_map/ppermute | solution.py:389
  50.1 1.0 %shard_map.105 = bf16[256,256]{1,0:T(8,128)(2,1)} custom-call(bf16[256,256]{1,0:T(8,128)(2,1)S(1)} %bitcast.15, bf16[256,256]{1,0:T(8,128)(2,1)S(1)} %get-tuple-element.47.spatial_ref, bf16[256,256]{1,0:T(8,128)(2,1)S(1)} %collective-permute-done.3.before_ref, bf16[384,256]{1,0:T(8,128)(2,1)S(1)} %copy-done.1, ...), custom_call_target="tpu_custom_call" | custom-call | flops 100663296 | bytes 1000000 | tf_op jit(solution)/shard_map/pallas_call | solution.py:26
  51.1 2.8 %collective-permute-done.17.refs_7_ = bf16[16,512]{1,0:T(8,128)(2,1)S(1)} collective-permute-done((bf16[16,512]{1,0:T(8,128)(2,1)S(1)}, bf16[16,512]{1,0:T(8,128)(2,1)S(1)}, u32[]{:S(2)}, u32[]{:S(2)}) %collective-permute-start.17) | collective-permute-done | bytes 16416 | tf_op jit(solution)/shard_map/ppermute | solution.py:389
  53.8 1.1 %shard_map.109 = (f32[16,1152]{1,0:T(8,128)}, f32[16,384]{1,0:T(8,128)}, f32[2,16]{1,0:T(2,128)}, bf16[256,256]{1,0:T(8,128)(2,1)}) custom-call(bf16[16,1152]{1,0:T(8,128)(2,1)S(1)} %get-tuple-element.56.refs_0_, bf16[16,1152]{1,0:T(8,128)(2,1)S(1)} %collective-permute-done.9.refs_1_, bf16[16,1152]{1,0:T(8,128)(2,1)S(1)} %collective-permute-done.10.refs_2_, ...), custom_call_target="tpu_custom_call" | custom-call | bytes 1000000 | tf_op jit(solution)/shard_map/pallas_call | solution.py:26
  (25 shorter events, 0.2 us)
Async XLA Ops:
  0.6 5.0 %copy-start.3 = (bf16[1,2,8,16,256]{4,3,2,1,0:T(8,128)(2,1)S(1)}, bf16[1,2,8,16,256]{4,3,2,1,0:T(8,128)(2,1)}, u32[]{:S(2)}) copy-start(bf16[1,2,8,16,256]{4,3,2,1,0:T(8,128)(2,1)} %param.7) | copy-start | bytes 393220
  2.6 19.4 %copy-start.1 = (bf16[384,256]{1,0:T(8,128)(2,1)S(1)}, bf16[384,256]{1,0:T(8,128)(2,1)}, u32[]{:S(2)}) copy-start(bf16[384,256]{1,0:T(8,128)(2,1)} %wt_ref.5) | copy-start | bytes 589828
  2.6 17.6 %collective-permute-start = (bf16[768,256]{1,0:T(8,128)(2,1)}, bf16[768,256]{1,0:T(8,128)(2,1)S(1)}, u32[]{:S(2)}, u32[]{:S(2)}) collective-permute-start(bf16[768,256]{1,0:T(8,128)(2,1)} %get-tuple-element.39), channel_id=1, source_target_pairs={{0,16},{1,17},{2,18},{3,19},{4,20},{5,21},{6,22},{7,23},{8,24},{9,... | collective-permute-start | bytes 1179656 | tf_op jit(solution)/shard_map/ppermute | solution.py:389
  5.6 14.6 %collective-permute-start.1 = (bf16[256,256]{1,0:T(8,128)(2,1)S(1)}, bf16[256,256]{1,0:T(8,128)(2,1)S(1)}, u32[]{:S(2)}, u32[]{:S(2)}) collective-permute-start(bf16[256,256]{1,0:T(8,128)(2,1)S(1)} %bitcast.19), channel_id=1, source_target_pairs={{1,0},{2,1},{3,2},{4,3},{5,4},{6,5},{7,6},{8,7},{9,8},{10,9},{11,1... | collective-permute-start | bytes 393224 | tf_op jit(solution)/shard_map/ppermute | solution.py:411
  6.9 13.3 %all-to-all-start = ((f32[16,2,256]{2,1,0:T(2,128)}), f32[16,2,256]{2,1,0:T(2,128)S(1)}, u32[]{:S(2)}, u32[]{:S(2)}) async-start(f32[16,2,256]{2,1,0:T(2,128)} %get-tuple-element.40), calls=%async_computation | async-start | bytes 65536 | tf_op jit(solution)/shard_map/all_to_all | solution.py:412
  13.6 8.4 %copy-start = (bf16[1,2,8,16,256]{4,3,2,1,0:T(8,128)(2,1)S(1)}, bf16[1,2,8,16,256]{4,3,2,1,0:T(8,128)(2,1)}, u32[]{:S(2)}) copy-start(bf16[1,2,8,16,256]{4,3,2,1,0:T(8,128)(2,1)} %param.6) | copy-start | bytes 393220
  13.6 8.4 %copy-start.4 = (f32[2,256]{1,0:T(2,128)S(1)}, f32[2,256]{1,0:T(2,128)}, u32[]{:S(2)}) copy-start(f32[2,256]{1,0:T(2,128)} %get-tuple-element.44.affine_ref.refs_11_) | copy-start | bytes 6148
  20.2 1.7 %collective-permute-start.2 = (bf16[768,256]{1,0:T(8,128)(2,1)S(1)}, bf16[768,256]{1,0:T(8,128)(2,1)S(1)}, u32[]{:S(2)}, u32[]{:S(2)}) collective-permute-start(bf16[768,256]{1,0:T(8,128)(2,1)S(1)} %collective-permute-done.rest_0_), channel_id=1, source_target_pairs={{0,1},{1,0},{2,3},{3,2},{4,5},{5,4},{6,7},{7,6},{8,9},{9,8},{10,11... | collective-permute-start | bytes 1179656 | tf_op jit(solution)/shard_map/ppermute | solution.py:389
  22.0 1.2 %copy-start.2 = (bf16[1152,256]{1,0:T(8,128)(2,1)S(1)}, bf16[1152,256]{1,0:T(8,128)(2,1)}, u32[]{:S(2)}) copy-start(bf16[1152,256]{1,0:T(8,128)(2,1)} %ws_ref.3) | copy-start | bytes 1769476
  23.0 3.8 %collective-permute-start.4 = (bf16[2,128,1152]{2,1,0:T(8,128)(2,1)S(1)}, bf16[2,128,1152]{2,1,0:T(8,128)(2,1)S(1)}, u32[]{:S(2)}, u32[]{:S(2)}) collective-permute-start(bf16[2,128,1152]{2,1,0:T(8,128)(2,1)S(1)} %get-tuple-element.49), channel_id=1, source_target_pairs={{0,1},{1,0},{2,3},{3,2},{4,5},{5,4},{6,7},{7,6},{8,9},{9,8},{10,11... | collective-permute-start | bytes 1769480 | tf_op jit(solution)/shard_map/ppermute | solution.py:389
  25.1 1.6 %collective-permute-start.5 = (bf16[2,128,512]{2,1,0:T(8,128)(2,1)S(1)}, bf16[2,128,512]{2,1,0:T(8,128)(2,1)S(1)}, u32[]{:S(2)}, u32[]{:S(2)}) collective-permute-start(bf16[2,128,512]{2,1,0:T(8,128)(2,1)S(1)} %get-tuple-element.51), channel_id=1, source_target_pairs={{0,1},{1,0},{2,3},{3,2},{4,5},{5,4},{6,7},{7,6},{8,9},{9,8},{10,11... | collective-permute-start | bytes 786440 | tf_op jit(solution)/shard_map/ppermute | solution.py:389
  27.0 6.2 %collective-permute-start.6 = (bf16[4,16,1152]{2,1,0:T(8,128)(2,1)S(1)}, bf16[4,16,1152]{2,1,0:T(8,128)(2,1)S(1)}, u32[]{:S(2)}, u32[]{:S(2)}) collective-permute-start(bf16[4,16,1152]{2,1,0:T(8,128)(2,1)S(1)} %get-tuple-element.53), channel_id=1, source_target_pairs={{0,2},{1,3},{2,0},{3,1},{4,6},{5,7},{6,4},{7,5},{8,10},{9,11},{10,... | collective-permute-start | bytes 442376 | tf_op jit(solution)/shard_map/ppermute | solution.py:389
  27.4 6.7 %collective-permute-start.7 = (bf16[4,16,1152]{2,1,0:T(8,128)(2,1)S(1)}, bf16[4,16,1152]{2,1,0:T(8,128)(2,1)S(1)}, u32[]{:S(2)}, u32[]{:S(2)}) collective-permute-start(bf16[4,16,1152]{2,1,0:T(8,128)(2,1)S(1)} %get-tuple-element.54), channel_id=1, source_target_pairs={{0,16},{1,17},{2,18},{3,19},{4,20},{5,21},{6,22},{7,23},{8,24},{9,... | collective-permute-start | bytes 442376 | tf_op jit(solution)/shard_map/ppermute | solution.py:389
  27.9 10.3 %collective-permute-start.8 = (bf16[4,16,1152]{2,1,0:T(8,128)(2,1)S(1)}, bf16[4,16,1152]{2,1,0:T(8,128)(2,1)S(1)}, u32[]{:S(2)}, u32[]{:S(2)}) collective-permute-start(bf16[4,16,1152]{2,1,0:T(8,128)(2,1)S(1)} %get-tuple-element.55), channel_id=1, source_target_pairs={{0,18},{1,19},{2,16},{3,17},{4,22},{5,23},{6,20},{7,21},{8,26},{9,... | collective-permute-start | bytes 442376 | tf_op jit(solution)/shard_map/ppermute | solution.py:389
  30.5 14.0 %collective-permute-start.3 = (bf16[256,256]{1,0:T(8,128)(2,1)S(1)}, bf16[256,256]{1,0:T(8,128)(2,1)S(1)}, u32[]{:S(2)}, u32[]{:S(2)}) collective-permute-start(bf16[256,256]{1,0:T(8,128)(2,1)S(1)} %get-tuple-element.47.spatial_ref), channel_id=1, source_target_pairs={{0,1},{1,2},{2,3},{3,4},{4,5},{5,6},{6,7},{7,8},{8,9},{9,10},{10,1... | collective-permute-start | bytes 393224 | tf_op jit(solution)/shard_map/ppermute | solution.py:445
  32.0 7.6 %collective-permute-start.12 = (bf16[4,16,512]{2,1,0:T(8,128)(2,1)S(1)}, bf16[4,16,512]{2,1,0:T(8,128)(2,1)S(1)}, u32[]{:S(2)}, u32[]{:S(2)}) collective-permute-start(bf16[4,16,512]{2,1,0:T(8,128)(2,1)S(1)} %get-tuple-element.61), channel_id=1, source_target_pairs={{0,2},{1,3},{2,0},{3,1},{4,6},{5,7},{6,4},{7,5},{8,10},{9,11},{10,... | collective-permute-start | bytes 196616 | tf_op jit(solution)/shard_map/ppermute | solution.py:389
  33.2 8.9 %collective-permute-start.13 = (bf16[4,16,512]{2,1,0:T(8,128)(2,1)S(1)}, bf16[4,16,512]{2,1,0:T(8,128)(2,1)S(1)}, u32[]{:S(2)}, u32[]{:S(2)}) collective-permute-start(bf16[4,16,512]{2,1,0:T(8,128)(2,1)S(1)} %get-tuple-element.62), channel_id=1, source_target_pairs={{0,16},{1,17},{2,18},{3,19},{4,20},{5,21},{6,22},{7,23},{8,24},{9,... | collective-permute-start | bytes 196616 | tf_op jit(solution)/shard_map/ppermute | solution.py:389
  34.1 10.3 %collective-permute-start.14 = (bf16[4,16,512]{2,1,0:T(8,128)(2,1)S(1)}, bf16[4,16,512]{2,1,0:T(8,128)(2,1)S(1)}, u32[]{:S(2)}, u32[]{:S(2)}) collective-permute-start(bf16[4,16,512]{2,1,0:T(8,128)(2,1)S(1)} %get-tuple-element.63), channel_id=1, source_target_pairs={{0,18},{1,19},{2,16},{3,17},{4,22},{5,23},{6,20},{7,21},{8,26},{9,... | collective-permute-start | bytes 196616 | tf_op jit(solution)/shard_map/ppermute | solution.py:389
  38.3 15.5 %collective-permute-start.9 = (bf16[16,1152]{1,0:T(8,128)(2,1)S(1)}, bf16[16,1152]{1,0:T(8,128)(2,1)S(1)}, u32[]{:S(2)}, u32[]{:S(2)}) collective-permute-start(bf16[16,1152]{1,0:T(8,128)(2,1)S(1)} %get-tuple-element.57), channel_id=1, source_target_pairs={{0,4},{1,5},{2,6},{3,7},{4,8},{5,9},{6,10},{7,11},{8,12},{9,13},{1... | collective-permute-start | bytes 110600 | tf_op jit(solution)/shard_map/ppermute | solution.py:389
  39.6 14.2 %collective-permute-start.10 = (bf16[16,1152]{1,0:T(8,128)(2,1)S(1)}, bf16[16,1152]{1,0:T(8,128)(2,1)S(1)}, u32[]{:S(2)}, u32[]{:S(2)}) collective-permute-start(bf16[16,1152]{1,0:T(8,128)(2,1)S(1)} %get-tuple-element.58), channel_id=1, source_target_pairs={{0,8},{1,9},{2,10},{3,11},{4,12},{5,13},{6,14},{7,15},{8,0},{9,1},... | collective-permute-start | bytes 110600 | tf_op jit(solution)/shard_map/ppermute | solution.py:389
  42.1 11.7 %collective-permute-start.11 = (bf16[16,1152]{1,0:T(8,128)(2,1)S(1)}, bf16[16,1152]{1,0:T(8,128)(2,1)S(1)}, u32[]{:S(2)}, u32[]{:S(2)}) collective-permute-start(bf16[16,1152]{1,0:T(8,128)(2,1)S(1)} %get-tuple-element.59), channel_id=1, source_target_pairs={{0,12},{1,13},{2,14},{3,15},{4,0},{5,1},{6,2},{7,3},{8,4},{9,5},{1... | collective-permute-start | bytes 110600 | tf_op jit(solution)/shard_map/ppermute | solution.py:389
  44.5 5.6 %collective-permute-start.15 = (bf16[16,512]{1,0:T(8,128)(2,1)S(1)}, bf16[16,512]{1,0:T(8,128)(2,1)S(1)}, u32[]{:S(2)}, u32[]{:S(2)}) collective-permute-start(bf16[16,512]{1,0:T(8,128)(2,1)S(1)} %get-tuple-element.65), channel_id=1, source_target_pairs={{0,4},{1,5},{2,6},{3,7},{4,8},{5,9},{6,10},{7,11},{8,12},{9,13},{1... | collective-permute-start | bytes 49160 | tf_op jit(solution)/shard_map/ppermute | solution.py:389
  44.6 6.5 %collective-permute-start.16 = (bf16[16,512]{1,0:T(8,128)(2,1)S(1)}, bf16[16,512]{1,0:T(8,128)(2,1)S(1)}, u32[]{:S(2)}, u32[]{:S(2)}) collective-permute-start(bf16[16,512]{1,0:T(8,128)(2,1)S(1)} %get-tuple-element.66), channel_id=1, source_target_pairs={{0,8},{1,9},{2,10},{3,11},{4,12},{5,13},{6,14},{7,15},{8,0},{9,1},... | collective-permute-start | bytes 49160 | tf_op jit(solution)/shard_map/ppermute | solution.py:389
  50.1 3.7 %collective-permute-start.17 = (bf16[16,512]{1,0:T(8,128)(2,1)S(1)}, bf16[16,512]{1,0:T(8,128)(2,1)S(1)}, u32[]{:S(2)}, u32[]{:S(2)}) collective-permute-start(bf16[16,512]{1,0:T(8,128)(2,1)S(1)} %get-tuple-element.67), channel_id=1, source_target_pairs={{0,12},{1,13},{2,14},{3,15},{4,0},{5,1},{6,2},{7,3},{8,4},{9,5},{1... | collective-permute-start | bytes 49160 | tf_op jit(solution)/shard_map/ppermute | solution.py:389

commit v8 on v6

--- a/solution.py
+++ b/solution.py
@@ -99,11 +99,16 @@
             full[pl.ds(start, half)] = pieces[2 * (s - 1) + which][offset : offset + half]
 
 
-def whiten(lat, stats, count, per_group):
+def group_params(stats, count, per_group):
     total = group_total(jnp.sum(stats, axis=0), per_group) / count
     mean = total[0:1]
-    inv_std = 1.0 / jnp.sqrt(total[1:2] - mean * mean + EPSILON)
-    return (lat.astype(F32) - mean) * inv_std, inv_std
+    return jnp.concatenate(
+        [mean, 1.0 / jnp.sqrt(total[1:2] - mean * mean + EPSILON)], axis=0
+    )
+
+
+def whiten(lat, params):
+    return (lat.astype(F32) - params[0:1]) * params[1:2]
 
 
 def store_shifted(pad_ref, values, frames, cells, cols):
@@ -167,23 +172,29 @@
         send_ref[owner, :, place : place + 128] = low[half:, at : at + 128]
 
 
-def normalise(lat_ref, stats_ref, affine_ref, count, per_group):
-    white, inv_std = whiten(lat_ref[...], stats_ref[...], count, per_group)
+def normalise(lat_ref, params, affine_ref):
+    white = whiten(lat_ref[...], params)
     normed = white * affine_ref[0:1] + affine_ref[1:2]
     return white, normed, jax.nn.sigmoid(normed)
 
 
-def first_body(sizes, lat_ref, cot_ref, halo_ref, stats_ref, affine_ref, wt_ref, *rest):
+def pick_halo(near_ref, next_ref):
+    core = lax.rem(lax.axis_index("wide"), 2)
+    return jnp.where(core == 0, near_ref[...].astype(F32), next_ref[...].astype(F32))
+
+
+def first_body(sizes, lat_ref, cot_ref, near_ref, next_ref, stats_ref, affine_ref, wt_ref, *rest):
     D, W, frames, cells, cols, count, per_group, aligned = sizes
     pieces, rest = rest[: 2 * (D - 1)], rest[2 * (D - 1) :]
     full_wt, act_pad, gsa_t = rest[-3:]
-    gsa_ref, keep_ref = rest[:2]
-    send_ref = rest[2] if aligned else None
+    gsa_ref, params_ref, seen_ref, keep_ref = rest[:4]
+    send_ref = rest[4] if aligned else None
     channels = lat_ref.shape[1]
     core = lax.rem(lax.axis_index("wide"), 2)
     fill_weights(full_wt, wt_ref, pieces, pieces[0].shape[0] - wt_ref.shape[0] // 2, D)
     rows = frames * cells
-    extended = jnp.concatenate([cot_ref[...], halo_ref[...]], axis=0)
+    halo = pick_halo(near_ref, next_ref).astype(BF16)
+    extended = jnp.concatenate([cot_ref[...], halo], axis=0)
     gsa = jnp.zeros((rows, channels), F32)
     for k in range(3):
         gsa += mm(
@@ -193,58 +204,65 @@
         )
     gsa_ref[...] = gsa.astype(BF16)
     gsa_t[...] = gsa.astype(BF16).astype(F32).T.astype(BF16)
-    _, normed, sig = normalise(lat_ref, stats_ref, affine_ref, count, per_group)
+    params = group_params(stats_ref[...], count, per_group)
+    params_ref[...] = params
+    _, normed, sig = normalise(lat_ref, params, affine_ref)
     act = (normed * sig).astype(BF16).astype(F32)
     store_shifted(act_pad, act, frames, cells, cols)
     left = core_order(gsa_t, W, core) if aligned else gsa_t[...]
     shard = wt_ref.shape[0] * 3
     for dy in range(3):
         for dx in range(3):
+            at = (3 * dy + dx) * channels
             seen = window(act_pad, dy, dx, frames, cells, cols)
-            put(mm(left, seen), (3 * dy + dx) * channels, shard, keep_ref, send_ref)
+            seen_ref[:, at : at + channels] = seen
+            put(mm(left, seen), at, shard, keep_ref, send_ref)
 
 
 def second_body(
-    sizes, lat_ref, cot_t_ref, halo_ref, stats_ref, affine_ref, gsa_ref, ws_ref, *rest
+    sizes,
+    lat_ref,
+    cot_t_ref,
+    near_ref,
+    next_ref,
+    params_ref,
+    affine_ref,
+    gsa_ref,
+    seen_ref,
+    ws_ref,
+    *rest,
 ):
     D, W, frames, cells, cols, count, per_group, aligned = sizes
     pieces, rest = rest[: 2 * (D - 1)], rest[2 * (D - 1) :]
-    full_ws, act_pad, gsa_pad, cot_t = rest[-4:]
+    full_ws, side_ws, gsa_pad, gsa_seen, cot_t = rest[-5:]
     spatial_ref, grad_ref, keep_ref, other_ref = rest[:4]
     send_ref = other_ref if aligned else None
     channels = lat_ref.shape[1]
     core = lax.rem(lax.axis_index("wide"), 2)
     fill_weights(full_ws, ws_ref, pieces, 0, D)
     rows = frames * cells
-    white, normed, sig = normalise(lat_ref, stats_ref, affine_ref, count, per_group)
-    act = (normed * sig).astype(BF16).astype(F32)
-    store_shifted(act_pad, act, frames, cells, cols)
     store_shifted(gsa_pad, gsa_ref[...].astype(F32), frames, cells, cols)
     cot_t[:, :rows] = cot_t_ref[...]
-    for f in range(2):
-        cot_t[:, rows + f * cells : rows + (f + 1) * cells] = (
-            halo_ref[f * cells : (f + 1) * cells].astype(F32).T.astype(BF16)
-        )
+    cot_t[:, rows : rows + 2 * cells] = (
+        pick_halo(near_ref, next_ref)[: 2 * cells].T.astype(BF16)
+    )
     left = core_order(cot_t, W, core) if aligned else cot_t[...]
-    out = jnp.zeros((rows, channels), F32)
-    for dy in range(3):
-        for dx in range(3):
-            tap = 3 * dy + dx
-            seen = window(act_pad, dy, dx, frames, cells, cols)
-            out += mm(seen, full_ws[tap * channels : (tap + 1) * channels])
-    spatial = out.astype(BF16)
+    spatial = mm(seen_ref[...], full_ws[...]).astype(BF16)
     spatial_ref[...] = spatial
     shard = ws_ref.shape[0] // 3
     for k in range(3):
         block = mm(left[:, k * cells : k * cells + rows], spatial)
         put(block, k * channels, shard, keep_ref, send_ref)
 
-    grad = jnp.zeros((rows, channels), F32)
     for dy in range(3):
         for dx in range(3):
-            tap = 3 * dy + dx
-            seen = window(gsa_pad, 2 - dy, 2 - dx, frames, cells, cols)
-            grad += mm(seen, full_ws[tap * channels : (tap + 1) * channels], NT)
+            at = (3 * dy + dx) * channels
+            gsa_seen[:, at : at + channels] = window(
+                gsa_pad, 2 - dy, 2 - dx, frames, cells, cols
+            )
+            side_ws[:, at : at + channels] = full_ws[at : at + channels]
+    grad = mm(gsa_seen[...], side_ws[...], NT)
+    white, normed, sig = normalise(lat_ref, params_ref[...], affine_ref)
     grad = grad * (sig * (1.0 + normed * (1.0 - sig)))
     grad_ref[...] = grad
     gain_term = jnp.sum(grad * white, axis=0, keepdims=True)
@@ -283,9 +301,9 @@
     block_ref[...] = (lat_ref[...].astype(F32) + temporal).astype(BF16)
 
 
-def latent_gradient(sizes, total, lat_ref, cot_ref, stats_ref, affine_ref, grad_ref):
-    D, W, frames, cells, cols, count, per_group, aligned = sizes
-    white, inv_std = whiten(lat_ref[...], stats_ref[...], count, per_group)
+def latent_gradient(sizes, total, lat_ref, cot_ref, params_ref, affine_ref, grad_ref):
+    count, per_group = sizes[5:7]
+    white, inv_std = whiten(lat_ref[...], params_ref[...]), params_ref[1:2]
     gain = affine_ref[0:1]
     means = group_total(total * gain, per_group) / count
     inner = inv_std * (grad_ref[...] * gain - means[1:2] - white * means[0:1])
@@ -411,9 +429,10 @@
     cot_t = call(transpose_body, shape((channels, rows), BF16), moved=300_000)(cot)
     firsts = [send(half, lambda d, w: ((d + s) % D, w)) for s in range(1, D)]
 
-    halo = lax.ppermute(cot, "wide", [(w + 1, w) for w in range(W - 1)])
+    next_cot = lax.ppermute(cot, "wide", [(w + 1, w) for w in range(1, W - 1, 2)])
+    near_cot = send(cot, lambda d, w: (d, w ^ 1))
     stats = lax.all_to_all(stats, "wide", split_axis=0, concat_axis=0, tiled=True)
-    firsts, stats, halo, cot_t = lax.optimization_barrier((firsts, stats, halo, cot_t))
+    firsts, stats, next_cot, cot_t = lax.optimization_barrier((firsts, stats, next_cot, cot_t))
     pieces = []
     for first in firsts:
         pieces += [first, send(first, lambda d, w: (d, w ^ 1))]
@@ -426,25 +445,32 @@
         terms_s = [shape((channels, D * shard_s), BF16)]
         terms_t = [shape((channels, D * shard_t), BF16), shape((D * W, 2, channels), F32)]
     pad = pltpu.VMEM((3, frames, cells + 2 * cols, channels), BF16)
-    gsa, *grads_s = call(
+    taps = D * shard_s
+    gsa, params, seen, *grads_s = call(
         functools.partial(first_body, sizes),
-        [shape((rows, channels), BF16)] + terms_s,
+        [
+            shape((rows, channels), BF16),
+            shape((2, channels), F32),
+            shape((rows, taps), BF16),
+        ]
+        + terms_s,
         [pltpu.VMEM((D * shard_t, channels), BF16), pad, pltpu.VMEM((channels, rows), BF16)],
         flops=2 * 12 * rows * channels * channels,
         moved=3_000_000,
-    )(lat, cot, halo, stats, affine, w_temporal, *pieces)
+    )(lat, cot, near_cot, next_cot, stats, affine, w_temporal, *pieces)
     spatial, grad, *grads_t = call(
         functools.partial(second_body, sizes),
         [shape((rows, channels), BF16), shape((rows, channels), F32)] + terms_t,
         [
-            pltpu.VMEM((D * shard_s, channels), BF16),
+            pltpu.VMEM((taps, channels), BF16),
+            pltpu.VMEM((channels, taps), BF16),
             pad,
-            pad,
+            pltpu.VMEM((rows, taps), BF16),
             pltpu.VMEM((channels, rows + 2 * cells), BF16),
         ],
         flops=2 * 21 * rows * channels * channels,
         moved=3_000_000,
-    )(lat, cot_t, halo, stats, affine, gsa, w_spatial, *pieces)
+    )(lat, cot_t, near_cot, next_cot, params, affine, gsa, seen, w_spatial, *pieces)
     before = lax.ppermute(spatial, "wide", [(w, w + 1) for w in range(W - 1)])
     block_out = call(
         functools.partial(block_body, sizes),
@@ -455,7 +481,7 @@
     )(lat, spatial, before, w_temporal, *pieces)
 
     width = channels // W
-    operands = (lat, cot, stats, affine, grad)
+    operands = (lat, cot, params, affine, grad)
     if aligned:
         Z = W // 4
 

time: 49.5 us -> 50.9 us (1.028)
  local copies, waits for them, and re-layouts: 0.03 us -> 2.49 us
  waiting for transfers between devices: 19.8 us -> 18.8 us
    unnamed x10 -> x12, local copies, waits for them, and re-layouts: 0.03 us -> 2.49 us
    all_to_all x1, waiting for transfers between devices: 6.5 us -> 5.62 us  [local(): lax.all_to_all(stats, 'wide', split_axis=0, concat_axis=0, tiled=True)]
    ppermute x1, starting transfers between devices: 1.28 us -> 0.66 us  [local(): lax.ppermute(cot, 'wide', [(w + 1, w) for w in range(1, W - 1, 2)])]
    ppermute x10 -> x11, starting transfers between devices: 11.8 us -> 12.3 us  [send(): return lax.ppermute(value, ('dp', 'wide'), over_all(moves))]
    ppermute x10 -> x11, waiting for transfers between devices: 13.3 us -> 13.2 us  [send(): return lax.ppermute(value, ('dp', 'wide'), over_all(moves))]
  transfers between devices with their start and end apart: 13 -> 14, of which waited for: 8 -> 8; matrix products, arithmetic and copies ran while one was open for 0% -> 0% of each run, Pallas kernels for 6% -> 6%
where the time goes in v8:
time: 50.9 us; the launch traced here: 50.6 us
  starting transfers between devices  21.3 us (42%)
  waiting for transfers between devices  18.8 us (37%)
  Pallas kernels  7.22 us (14%)
  local copies, waits for them, and re-layouts  2.49 us (5%)
  between operations  0.76 us (1%)
    ppermute x11, waiting for transfers between devices, send(): return lax.ppermute(value, ('dp', 'wide'), over_all(moves))  13.2 us
    ppermute x11, starting transfers between devices, send(): return lax.ppermute(value, ('dp', 'wide'), over_all(moves))  12.3 us
    pallas_call x8, Pallas kernels, run(): pl.pallas_call(body, out_shape=out_shapes, in_specs=in_specs or [VMEM] *...  7.22 us
    all_to_all x1, starting transfers between devices, local(): lax.all_to_all(stats, 'wide', split_axis=0, concat_axis=0, tiled=True)  6.86 us
    all_to_all x1, waiting for transfers between devices, local(): lax.all_to_all(stats, 'wide', split_axis=0, concat_axis=0, tiled=True)  5.62 us
    unnamed x12, local copies, waits for them, and re-layouts  2.49 us
    ppermute x1, starting transfers between devices, local(): before = lax.ppermute(spatial, 'wide', [(w, w + 1) for w in range(W - 1)])  1.42 us
  transfers between devices with their start and end apart: 14, of which 8 were waited for; matrix products, arithmetic and copies ran while one was open for 0% of the time, Pallas kernels for 6%

profile of v8, /device:TPU:0, one launch (start us, length us, event | category | flops | bytes accessed | tf_op | source)
XLA Modules:
  0.0 50.6 jit_solution(16703505573823449996)
XLA Ops:
  0.7 2.0 %shard_map.101 = (f32[16,2,256]{2,1,0:T(2,128)}, f32[2,256]{1,0:T(2,128)}, bf16[768,256]{1,0:T(8,128)(2,1)}) custom-call(bf16[256,256]{1,0:T(8,128)(2,1)} %bitcast.12, f32[1,256]{1,0:T(1,128)} %bitcast.27, f32[1,256]{1,0:T(1,128)} %bitcast.28, bf16[1152,256]{1,0:T(8,128)(2,1)} %ws_ref.3, bf16[384,256]{1,0:T(8,128)(2,1)} %wt_ref.5), custom_call_target="tpu_custom_call" | custom-call | tf_op jit(solution)/shard_map/pallas_call | solution.py:26
  2.6 3.0 %collective-permute-start = (bf16[768,256]{1,0:T(8,128)(2,1)}, bf16[768,256]{1,0:T(8,128)(2,1)S(1)}, u32[]{:S(2)}, u32[]{:S(2)}) collective-permute-start(bf16[768,256]{1,0:T(8,128)(2,1)} %get-tuple-element.33), channel_id=1, source_target_pairs={{0,16},{1,17},{2,18},{3,19},{4,20},{5,21},{6,22},{7,23},{8,24},{9,... | collective-permute-start | bytes 1179656 | tf_op jit(solution)/shard_map/ppermute | solution.py:410
  5.6 0.7 %collective-permute-start.1 = (bf16[256,256]{1,0:T(8,128)(2,1)}, bf16[256,256]{1,0:T(8,128)(2,1)S(1)}, u32[]{:S(2)}, u32[]{:S(2)}) collective-permute-start(bf16[256,256]{1,0:T(8,128)(2,1)} %bitcast.17), channel_id=1, source_target_pairs={{2,1},{4,3},{6,5},{8,7},{10,9},{12,11},{14,13},{18,17},{20,19},{22... | collective-permute-start | bytes 393224 | tf_op jit(solution)/shard_map/ppermute | solution.py:432
  6.3 6.9 %all-to-all-start = ((f32[16,2,256]{2,1,0:T(2,128)}), f32[16,2,256]{2,1,0:T(2,128)S(1)}, u32[]{:S(2)}, u32[]{:S(2)}) async-start(f32[16,2,256]{2,1,0:T(2,128)} %get-tuple-element.34), calls=%async_computation | async-start | bytes 65536 | tf_op jit(solution)/shard_map/all_to_all | solution.py:434
  13.2 0.9 %copy-done.3 = bf16[1,2,8,16,256]{4,3,2,1,0:T(8,128)(2,1)S(1)} copy-done((bf16[1,2,8,16,256]{4,3,2,1,0:T(8,128)(2,1)S(1)}, bf16[1,2,8,16,256]{4,3,2,1,0:T(8,128)(2,1)}, u32[]{:S(2)}) %copy-start.3) | copy-done | bytes 131096
  14.1 0.1 shard_map.102.cot_t_ref
  14.2 5.6 %all-to-all-done.stats_ref = f32[16,2,256]{2,1,0:T(2,128)S(1)} async-done(((f32[16,2,256]{2,1,0:T(2,128)}), f32[16,2,256]{2,1,0:T(2,128)S(1)}, u32[]{:S(2)}, u32[]{:S(2)}) %all-to-all-start) | async-done | bytes 32800 | tf_op jit(solution)/shard_map/all_to_all | solution.py:434
  19.8 0.5 collective-permute-start.2
  20.3 1.6 %collective-permute-done.2.near_ref = bf16[256,256]{1,0:T(8,128)(2,1)S(1)} collective-permute-done((bf16[256,256]{1,0:T(8,128)(2,1)}, bf16[256,256]{1,0:T(8,128)(2,1)S(1)}, u32[]{:S(2)}, u32[]{:S(2)}) %collective-permute-start.2) | collective-permute-done | bytes 131104 | tf_op jit(solution)/shard_map/ppermute | solution.py:410
  22.0 0.9 %copy-done.4 = bf16[1,2,8,16,256]{4,3,2,1,0:T(8,128)(2,1)S(1)} copy-done((bf16[1,2,8,16,256]{4,3,2,1,0:T(8,128)(2,1)S(1)}, bf16[1,2,8,16,256]{4,3,2,1,0:T(8,128)(2,1)}, u32[]{:S(2)}) %copy-start.4) | copy-done | bytes 131096
  22.9 0.7 %copy-done.5 = f32[2,256]{1,0:T(2,128)S(1)} copy-done((f32[2,256]{1,0:T(2,128)S(1)}, f32[2,256]{1,0:T(2,128)}, u32[]{:S(2)}) %copy-start.5) | copy-done | bytes 2072
  23.5 1.0 %shard_map.103 = (bf16[256,256]{1,0:T(8,128)(2,1)S(1)}, f32[2,256]{1,0:T(2,128)S(1)}, bf16[256,2304]{1,0:T(8,128)(2,1)S(1)}, bf16[2,128,1152]{2,1,0:T(8,128)(2,1)S(1)}, bf16[2,128,1152]{2,1,0:T(8,128)(2,1)S(1)}) custom-call(bf16[256,256]{1,0:T(8,128)(2,1)S(1)} %bitcast.13, bf16[256,256]{1,0:T(8,128)(2,1)S(1)} %bitcast.20, ...), custom_call_target="tpu_custom_call" | custom-call | flops 402653184 | bytes 3000000 | tf_op jit(solution)/shard_map/pallas_call | solution.py:26
  24.6 0.2 collective-permute-start.5
  24.8 1.7 %shard_map.104 = (bf16[256,256]{1,0:T(8,128)(2,1)S(1)}, f32[256,256]{1,0:T(8,128)S(1)}, bf16[2,128,512]{2,1,0:T(8,128)(2,1)S(1)}, bf16[2,128,512]{2,1,0:T(8,128)(2,1)S(1)}) custom-call(bf16[256,256]{1,0:T(8,128)(2,1)S(1)} %bitcast.14, bf16[256,256]{1,0:T(8,128)(2,1)S(1)} %shard_map.102.cot_t_ref, bf16[256,256]{1,0:T(8,128)(2,1)S(1)} %collective-permute-done.2.near_ref, ...), custom_call_target="tpu_custom_call" | custom-call | flops 704643072 | bytes 3000000 | tf_op jit(solution)/shard_map/pallas_call | solution.py:26
  26.5 0.4 collective-permute-start.6
  27.0 1.2 %collective-permute-done.6 = bf16[2,128,512]{2,1,0:T(8,128)(2,1)S(1)} collective-permute-done((bf16[2,128,512]{2,1,0:T(8,128)(2,1)S(1)}, bf16[2,128,512]{2,1,0:T(8,128)(2,1)S(1)}, u32[]{:S(2)}, u32[]{:S(2)}) %collective-permute-start.6) | collective-permute-done | bytes 262176 | tf_op jit(solution)/shard_map/ppermute | solution.py:410
  28.1 0.2 shard_map.106
  28.3 0.4 collective-permute-start.7
  28.8 0.5 %collective-permute-start.8 = (bf16[4,16,1664]{2,1,0:T(8,128)(2,1)S(1)}, bf16[4,16,1664]{2,1,0:T(8,128)(2,1)S(1)}, u32[]{:S(2)}, u32[]{:S(2)}) collective-permute-start(bf16[4,16,1664]{2,1,0:T(8,128)(2,1)S(1)} %get-tuple-element.50), channel_id=1, source_target_pairs={{0,16},{1,17},{2,18},{3,19},{4,20},{5,21},{6,22},{7,23},{8,24},{9,... | collective-permute-start | bytes 638984 | tf_op jit(solution)/shard_map/ppermute | solution.py:410
  29.3 2.6 %collective-permute-start.9 = (bf16[4,16,1664]{2,1,0:T(8,128)(2,1)S(1)}, bf16[4,16,1664]{2,1,0:T(8,128)(2,1)S(1)}, u32[]{:S(2)}, u32[]{:S(2)}) collective-permute-start(bf16[4,16,1664]{2,1,0:T(8,128)(2,1)S(1)} %get-tuple-element.51), channel_id=1, source_target_pairs={{0,18},{1,19},{2,16},{3,17},{4,22},{5,23},{6,20},{7,21},{8,26},{9,... | collective-permute-start | bytes 638984 | tf_op jit(solution)/shard_map/ppermute | solution.py:410
  31.9 1.4 %collective-permute-start.4 = (bf16[256,256]{1,0:T(8,128)(2,1)S(1)}, bf16[256,256]{1,0:T(8,128)(2,1)S(1)}, u32[]{:S(2)}, u32[]{:S(2)}) collective-permute-start(bf16[256,256]{1,0:T(8,128)(2,1)S(1)} %get-tuple-element.43.spatial_ref), channel_id=1, source_target_pairs={{0,1},{1,2},{2,3},{3,4},{4,5},{5,6},{6,7},{7,8},{8,9},{9,10},{10,1... | collective-permute-start | bytes 393224 | tf_op jit(solution)/shard_map/ppermute | solution.py:474
  33.3 2.6 %collective-permute-done.7.refs_1_ = bf16[4,16,1664]{2,1,0:T(8,128)(2,1)S(1)} collective-permute-done((bf16[4,16,1664]{2,1,0:T(8,128)(2,1)S(1)}, bf16[4,16,1664]{2,1,0:T(8,128)(2,1)S(1)}, u32[]{:S(2)}, u32[]{:S(2)}) %collective-permute-start.7) | collective-permute-done | bytes 213024 | tf_op jit(solution)/shard_map/ppermute | solution.py:410
  35.9 0.9 %collective-permute-done.8.refs_2_ = bf16[4,16,1664]{2,1,0:T(8,128)(2,1)S(1)} collective-permute-done((bf16[4,16,1664]{2,1,0:T(8,128)(2,1)S(1)}, bf16[4,16,1664]{2,1,0:T(8,128)(2,1)S(1)}, u32[]{:S(2)}, u32[]{:S(2)}) %collective-permute-start.8) | collective-permute-done | bytes 213024 | tf_op jit(solution)/shard_map/ppermute | solution.py:410
  36.9 4.8 %collective-permute-done.9.refs_3_ = bf16[4,16,1664]{2,1,0:T(8,128)(2,1)S(1)} collective-permute-done((bf16[4,16,1664]{2,1,0:T(8,128)(2,1)S(1)}, bf16[4,16,1664]{2,1,0:T(8,128)(2,1)S(1)}, u32[]{:S(2)}, u32[]{:S(2)}) %collective-permute-start.9) | collective-permute-done | bytes 213024 | tf_op jit(solution)/shard_map/ppermute | solution.py:410
  41.7 0.1 shard_map.107
  41.8 1.6 %collective-permute-start.10 = (bf16[16,1664]{1,0:T(8,128)(2,1)S(1)}, bf16[16,1664]{1,0:T(8,128)(2,1)S(1)}, u32[]{:S(2)}, u32[]{:S(2)}) collective-permute-start(bf16[16,1664]{1,0:T(8,128)(2,1)S(1)} %get-tuple-element.53), channel_id=1, source_target_pairs={{0,4},{1,5},{2,6},{3,7},{4,8},{5,9},{6,10},{7,11},{8,12},{9,13},{1... | collective-permute-start | bytes 159752 | tf_op jit(solution)/shard_map/ppermute | solution.py:410
  43.4 0.7 %collective-permute-start.11 = (bf16[16,1664]{1,0:T(8,128)(2,1)S(1)}, bf16[16,1664]{1,0:T(8,128)(2,1)S(1)}, u32[]{:S(2)}, u32[]{:S(2)}) collective-permute-start(bf16[16,1664]{1,0:T(8,128)(2,1)S(1)} %get-tuple-element.54), channel_id=1, source_target_pairs={{0,8},{1,9},{2,10},{3,11},{4,12},{5,13},{6,14},{7,15},{8,0},{9,1},... | collective-permute-start | bytes 159752 | tf_op jit(solution)/shard_map/ppermute | solution.py:410
  44.1 2.3 %collective-permute-start.12 = (bf16[16,1664]{1,0:T(8,128)(2,1)S(1)}, bf16[16,1664]{1,0:T(8,128)(2,1)S(1)}, u32[]{:S(2)}, u32[]{:S(2)}) collective-permute-start(bf16[16,1664]{1,0:T(8,128)(2,1)S(1)} %get-tuple-element.55), channel_id=1, source_target_pairs={{0,12},{1,13},{2,14},{3,15},{4,0},{5,1},{6,2},{7,3},{8,4},{9,5},{1... | collective-permute-start | bytes 159752 | tf_op jit(solution)/shard_map/ppermute | solution.py:410
  46.4 1.0 %shard_map.105 = bf16[256,256]{1,0:T(8,128)(2,1)} custom-call(bf16[256,256]{1,0:T(8,128)(2,1)S(1)} %bitcast.15, bf16[256,256]{1,0:T(8,128)(2,1)S(1)} %get-tuple-element.43.spatial_ref, bf16[256,256]{1,0:T(8,128)(2,1)S(1)} %collective-permute-done.4.before_ref, bf16[384,256]{1,0:T(8,128)(2,1)S(1)} %copy-done.2, ...), custom_call_target="tpu_custom_call" | custom-call | flops 100663296 | bytes 1000000 | tf_op jit(solution)/shard_map/pallas_call | solution.py:26
  47.4 0.9 %collective-permute-done.10.refs_1_ = bf16[16,1664]{1,0:T(8,128)(2,1)S(1)} collective-permute-done((bf16[16,1664]{1,0:T(8,128)(2,1)S(1)}, bf16[16,1664]{1,0:T(8,128)(2,1)S(1)}, u32[]{:S(2)}, u32[]{:S(2)}) %collective-permute-start.10) | collective-permute-done | bytes 53280 | tf_op jit(solution)/shard_map/ppermute | solution.py:410
  48.3 1.2 %collective-permute-done.11.refs_2_ = bf16[16,1664]{1,0:T(8,128)(2,1)S(1)} collective-permute-done((bf16[16,1664]{1,0:T(8,128)(2,1)S(1)}, bf16[16,1664]{1,0:T(8,128)(2,1)S(1)}, u32[]{:S(2)}, u32[]{:S(2)}) %collective-permute-start.11) | collective-permute-done | bytes 53280 | tf_op jit(solution)/shard_map/ppermute | solution.py:410
  49.5 1.1 %shard_map.108 = (f32[16,1152]{1,0:T(8,128)}, f32[16,384]{1,0:T(8,128)}, f32[2,16]{1,0:T(2,128)}, bf16[256,256]{1,0:T(8,128)(2,1)}) custom-call(bf16[16,1664]{1,0:T(8,128)(2,1)S(1)} %get-tuple-element.52.refs_0_, bf16[16,1664]{1,0:T(8,128)(2,1)S(1)} %collective-permute-done.10.refs_1_, bf16[16,1664]{1,0:T(8,128)(2,1)S(1)} %collective-permute-done.11.refs_2_, ...), custom_call_target="tpu_custom_call" | custom-call | bytes 1000000 | tf_op jit(solution)/shard_map/pallas_call | solution.py:26
  (16 shorter events, 0.0 us)
Async XLA Ops:
  0.6 21.3 %copy-start.2 = (bf16[384,256]{1,0:T(8,128)(2,1)S(1)}, bf16[384,256]{1,0:T(8,128)(2,1)}, u32[]{:S(2)}) copy-start(bf16[384,256]{1,0:T(8,128)(2,1)} %wt_ref.5) | copy-start | bytes 589828
  0.6 21.3 %copy-start = (bf16[1,2,8,16,256]{4,3,2,1,0:T(8,128)(2,1)S(1)}, bf16[1,2,8,16,256]{4,3,2,1,0:T(8,128)(2,1)}, u32[]{:S(2)}) copy-start(bf16[1,2,8,16,256]{4,3,2,1,0:T(8,128)(2,1)} %param.6) | copy-start | bytes 393220
  0.7 24.1 %copy-start.1 = (bf16[1152,256]{1,0:T(8,128)(2,1)S(1)}, bf16[1152,256]{1,0:T(8,128)(2,1)}, u32[]{:S(2)}) copy-start(bf16[1152,256]{1,0:T(8,128)(2,1)} %ws_ref.3) | copy-start | bytes 1769476
  2.6 17.2 %collective-permute-start = (bf16[768,256]{1,0:T(8,128)(2,1)}, bf16[768,256]{1,0:T(8,128)(2,1)S(1)}, u32[]{:S(2)}, u32[]{:S(2)}) collective-permute-start(bf16[768,256]{1,0:T(8,128)(2,1)} %get-tuple-element.33), channel_id=1, source_target_pairs={{0,16},{1,17},{2,18},{3,19},{4,20},{5,21},{6,22},{7,23},{8,24},{9,... | collective-permute-start | bytes 1179656 | tf_op jit(solution)/shard_map/ppermute | solution.py:410
  5.6 14.2 %collective-permute-start.1 = (bf16[256,256]{1,0:T(8,128)(2,1)}, bf16[256,256]{1,0:T(8,128)(2,1)S(1)}, u32[]{:S(2)}, u32[]{:S(2)}) collective-permute-start(bf16[256,256]{1,0:T(8,128)(2,1)} %bitcast.17), channel_id=1, source_target_pairs={{2,1},{4,3},{6,5},{8,7},{10,9},{12,11},{14,13},{18,17},{20,19},{22... | collective-permute-start | bytes 393224 | tf_op jit(solution)/shard_map/ppermute | solution.py:432
  6.3 13.5 %all-to-all-start = ((f32[16,2,256]{2,1,0:T(2,128)}), f32[16,2,256]{2,1,0:T(2,128)S(1)}, u32[]{:S(2)}, u32[]{:S(2)}) async-start(f32[16,2,256]{2,1,0:T(2,128)} %get-tuple-element.34), calls=%async_computation | async-start | bytes 65536 | tf_op jit(solution)/shard_map/all_to_all | solution.py:434
  13.2 0.9 %copy-start.3 = (bf16[1,2,8,16,256]{4,3,2,1,0:T(8,128)(2,1)S(1)}, bf16[1,2,8,16,256]{4,3,2,1,0:T(8,128)(2,1)}, u32[]{:S(2)}) copy-start(bf16[1,2,8,16,256]{4,3,2,1,0:T(8,128)(2,1)} %param.7) | copy-start | bytes 393220
  19.8 2.1 %collective-permute-start.3 = (bf16[768,256]{1,0:T(8,128)(2,1)S(1)}, bf16[768,256]{1,0:T(8,128)(2,1)S(1)}, u32[]{:S(2)}, u32[]{:S(2)}) collective-permute-start(bf16[768,256]{1,0:T(8,128)(2,1)S(1)} %collective-permute-done.rest_0_), channel_id=1, source_target_pairs={{0,1},{1,0},{2,3},{3,2},{4,5},{5,4},{6,7},{7,6},{8,9},{9,8},{10,11... | collective-permute-start | bytes 1179656 | tf_op jit(solution)/shard_map/ppermute | solution.py:410
  19.8 2.1 %collective-permute-start.2 = (bf16[256,256]{1,0:T(8,128)(2,1)}, bf16[256,256]{1,0:T(8,128)(2,1)S(1)}, u32[]{:S(2)}, u32[]{:S(2)}) collective-permute-start(bf16[256,256]{1,0:T(8,128)(2,1)} %bitcast.18), channel_id=1, source_target_pairs={{0,1},{1,0},{2,3},{3,2},{4,5},{5,4},{6,7},{7,6},{8,9},{9,8},{10,11... | collective-permute-start | bytes 393224 | tf_op jit(solution)/shard_map/ppermute | solution.py:410
  21.9 0.9 %copy-start.4 = (bf16[1,2,8,16,256]{4,3,2,1,0:T(8,128)(2,1)S(1)}, bf16[1,2,8,16,256]{4,3,2,1,0:T(8,128)(2,1)}, u32[]{:S(2)}) copy-start(bf16[1,2,8,16,256]{4,3,2,1,0:T(8,128)(2,1)} %param.7) | copy-start | bytes 393220
  22.8 0.7 %copy-start.5 = (f32[2,256]{1,0:T(2,128)S(1)}, f32[2,256]{1,0:T(2,128)}, u32[]{:S(2)}) copy-start(f32[2,256]{1,0:T(2,128)} %get-tuple-element.38.affine_ref.refs_7_) | copy-start | bytes 6148
  24.6 3.5 %collective-permute-start.5 = (bf16[2,128,1152]{2,1,0:T(8,128)(2,1)S(1)}, bf16[2,128,1152]{2,1,0:T(8,128)(2,1)S(1)}, u32[]{:S(2)}, u32[]{:S(2)}) collective-permute-start(bf16[2,128,1152]{2,1,0:T(8,128)(2,1)S(1)} %get-tuple-element.45), channel_id=1, source_target_pairs={{0,1},{1,0},{2,3},{3,2},{4,5},{5,4},{6,7},{7,6},{8,9},{9,8},{10,11... | collective-permute-start | bytes 1769480 | tf_op jit(solution)/shard_map/ppermute | solution.py:410
  26.5 1.6 %collective-permute-start.6 = (bf16[2,128,512]{2,1,0:T(8,128)(2,1)S(1)}, bf16[2,128,512]{2,1,0:T(8,128)(2,1)S(1)}, u32[]{:S(2)}, u32[]{:S(2)}) collective-permute-start(bf16[2,128,512]{2,1,0:T(8,128)(2,1)S(1)} %get-tuple-element.47), channel_id=1, source_target_pairs={{0,1},{1,0},{2,3},{3,2},{4,5},{5,4},{6,7},{7,6},{8,9},{9,8},{10,11... | collective-permute-start | bytes 786440 | tf_op jit(solution)/shard_map/ppermute | solution.py:410
  28.3 7.6 %collective-permute-start.7 = (bf16[4,16,1664]{2,1,0:T(8,128)(2,1)S(1)}, bf16[4,16,1664]{2,1,0:T(8,128)(2,1)S(1)}, u32[]{:S(2)}, u32[]{:S(2)}) collective-permute-start(bf16[4,16,1664]{2,1,0:T(8,128)(2,1)S(1)} %get-tuple-element.49), channel_id=1, source_target_pairs={{0,2},{1,3},{2,0},{3,1},{4,6},{5,7},{6,4},{7,5},{8,10},{9,11},{10,... | collective-permute-start | bytes 638984 | tf_op jit(solution)/shard_map/ppermute | solution.py:410
  28.8 8.1 %collective-permute-start.8 = (bf16[4,16,1664]{2,1,0:T(8,128)(2,1)S(1)}, bf16[4,16,1664]{2,1,0:T(8,128)(2,1)S(1)}, u32[]{:S(2)}, u32[]{:S(2)}) collective-permute-start(bf16[4,16,1664]{2,1,0:T(8,128)(2,1)S(1)} %get-tuple-element.50), channel_id=1, source_target_pairs={{0,16},{1,17},{2,18},{3,19},{4,20},{5,21},{6,22},{7,23},{8,24},{9,... | collective-permute-start | bytes 638984 | tf_op jit(solution)/shard_map/ppermute | solution.py:410
  29.3 12.4 %collective-permute-start.9 = (bf16[4,16,1664]{2,1,0:T(8,128)(2,1)S(1)}, bf16[4,16,1664]{2,1,0:T(8,128)(2,1)S(1)}, u32[]{:S(2)}, u32[]{:S(2)}) collective-permute-start(bf16[4,16,1664]{2,1,0:T(8,128)(2,1)S(1)} %get-tuple-element.51), channel_id=1, source_target_pairs={{0,18},{1,19},{2,16},{3,17},{4,22},{5,23},{6,20},{7,21},{8,26},{9,... | collective-permute-start | bytes 638984 | tf_op jit(solution)/shard_map/ppermute | solution.py:410
  31.9 14.5 %collective-permute-start.4 = (bf16[256,256]{1,0:T(8,128)(2,1)S(1)}, bf16[256,256]{1,0:T(8,128)(2,1)S(1)}, u32[]{:S(2)}, u32[]{:S(2)}) collective-permute-start(bf16[256,256]{1,0:T(8,128)(2,1)S(1)} %get-tuple-element.43.spatial_ref), channel_id=1, source_target_pairs={{0,1},{1,2},{2,3},{3,4},{4,5},{5,6},{6,7},{7,8},{8,9},{9,10},{10,1... | collective-permute-start | bytes 393224 | tf_op jit(solution)/shard_map/ppermute | solution.py:474
  41.8 6.5 %collective-permute-start.10 = (bf16[16,1664]{1,0:T(8,128)(2,1)S(1)}, bf16[16,1664]{1,0:T(8,128)(2,1)S(1)}, u32[]{:S(2)}, u32[]{:S(2)}) collective-permute-start(bf16[16,1664]{1,0:T(8,128)(2,1)S(1)} %get-tuple-element.53), channel_id=1, source_target_pairs={{0,4},{1,5},{2,6},{3,7},{4,8},{5,9},{6,10},{7,11},{8,12},{9,13},{1... | collective-permute-start | bytes 159752 | tf_op jit(solution)/shard_map/ppermute | solution.py:410
  43.4 6.0 %collective-permute-start.11 = (bf16[16,1664]{1,0:T(8,128)(2,1)S(1)}, bf16[16,1664]{1,0:T(8,128)(2,1)S(1)}, u32[]{:S(2)}, u32[]{:S(2)}) collective-permute-start(bf16[16,1664]{1,0:T(8,128)(2,1)S(1)} %get-tuple-element.54), channel_id=1, source_target_pairs={{0,8},{1,9},{2,10},{3,11},{4,12},{5,13},{6,14},{7,15},{8,0},{9,1},... | collective-permute-start | bytes 159752 | tf_op jit(solution)/shard_map/ppermute | solution.py:410
  44.1 5.3 %collective-permute-start.12 = (bf16[16,1664]{1,0:T(8,128)(2,1)S(1)}, bf16[16,1664]{1,0:T(8,128)(2,1)S(1)}, u32[]{:S(2)}, u32[]{:S(2)}) collective-permute-start(bf16[16,1664]{1,0:T(8,128)(2,1)S(1)} %get-tuple-element.55), channel_id=1, source_target_pairs={{0,12},{1,13},{2,14},{3,15},{4,0},{5,1},{6,2},{7,3},{8,4},{9,5},{1... | collective-permute-start | bytes 159752 | tf_op jit(solution)/shard_map/ppermute | solution.py:410

commit v9 on v8

--- a/solution.py
+++ b/solution.py
@@ -56,36 +56,35 @@
     )
 
 
-def stats_body(lat_ref, gain_ref, bias_ref, ws_ref, wt_ref, out_ref, affine_ref, half_ref, *scratch):
+def stats_body(lat_ref, gain_ref, bias_ref, ws_ref, wt_ref, out_ref, half_s_ref, half_t_ref, *scratch):
     lat_here, gain_here, bias_here, sems = scratch
     core = lax.rem(lax.axis_index("wide"), 2)
-    moves, place = [(lat_ref, lat_here), (gain_ref, gain_here), (bias_ref, bias_here)], 0
-    for source in (ws_ref, wt_ref):
-        half = source.shape[0] // 2
+    moves = [(lat_ref, lat_here), (gain_ref, gain_here), (bias_ref, bias_here)]
+    for source, target in ((wt_ref, half_t_ref), (ws_ref, half_s_ref)):
+        half = target.shape[0]
         start = pl.multiple_of(core * half, 16)
-        moves.append((source.at[pl.ds(start, half)], half_ref.at[pl.ds(place, half)]))
-        place += half
+        moves.append((source.at[pl.ds(start, half)], target))
     copies = [pltpu.make_async_copy(*move, sems.at[at]) for at, move in enumerate(moves)]
     for copy in copies:
         copy.start()
     for copy in copies[:3]:
         copy.wait()
-    affine_ref[0:1] = gain_here[...]
-    affine_ref[1:2] = bias_here[...]
     x = lat_here[...].astype(F32)
     both = jnp.concatenate(
-        [jnp.sum(x, axis=0, keepdims=True), jnp.sum(x * x, axis=0, keepdims=True)], axis=0
+        [
+            jnp.sum(x, axis=0, keepdims=True),
+            jnp.sum(x * x, axis=0, keepdims=True),
+            gain_here[...],
+            bias_here[...],
+        ],
+        axis=0,
     )
     out_ref[...] = jnp.broadcast_to(both[None], out_ref.shape)
     for copy in copies[3:]:
         copy.wait()
 
 
-def transpose_body(cot_ref, out_ref):
-    out_ref[...] = cot_ref[...].astype(F32).T.astype(BF16)
-
-
-def fill_weights(full, shard_ref, pieces, offset, D):
+def fill_weights(full, shard_ref, pieces, D):
     d = lax.axis_index("dp")
     core = lax.rem(lax.axis_index("wide"), 2)
     n = shard_ref.shape[0]
@@ -96,7 +95,7 @@
         for which in range(2):
             holder = core if which == 0 else 1 - core
             start = pl.multiple_of(source * n + holder * half, 16)
-            full[pl.ds(start, half)] = pieces[2 * (s - 1) + which][offset : offset + half]
+            full[pl.ds(start, half)] = pieces[2 * (s - 1) + which][...]
 
 
 def group_params(stats, count, per_group):
@@ -172,9 +171,9 @@
         send_ref[owner, :, place : place + 128] = low[half:, at : at + 128]
 
 
-def normalise(lat_ref, params, affine_ref):
+def normalise(lat_ref, params):
     white = whiten(lat_ref[...], params)
-    normed = white * affine_ref[0:1] + affine_ref[1:2]
+    normed = white * params[2:3] + params[3:4]
     return white, normed, jax.nn.sigmoid(normed)
 
 
@@ -183,18 +182,20 @@
     return jnp.where(core == 0, near_ref[...].astype(F32), next_ref[...].astype(F32))
 
 
-def first_body(sizes, lat_ref, cot_ref, near_ref, next_ref, stats_ref, affine_ref, wt_ref, *rest):
+def ready_body(sizes, lat_ref, cot_ref, near_ref, next_ref, wt_ref, *rest):
     D, W, frames, cells, cols, count, per_group, aligned = sizes
     pieces, rest = rest[: 2 * (D - 1)], rest[2 * (D - 1) :]
-    full_wt, act_pad, gsa_t = rest[-3:]
-    gsa_ref, params_ref, seen_ref, keep_ref = rest[:4]
-    send_ref = rest[4] if aligned else None
+    lat_copy, cot_copy, left_t_ref, left_s_ref, gsa_seen, full_wt = rest[:6]
+    gsa_pad, gsa_t, cot_t = rest[6:]
     channels = lat_ref.shape[1]
     core = lax.rem(lax.axis_index("wide"), 2)
-    fill_weights(full_wt, wt_ref, pieces, pieces[0].shape[0] - wt_ref.shape[0] // 2, D)
     rows = frames * cells
-    halo = pick_halo(near_ref, next_ref).astype(BF16)
-    extended = jnp.concatenate([cot_ref[...], halo], axis=0)
+    fill_weights(full_wt, wt_ref, pieces, D)
+    lat_copy[...] = lat_ref[...]
+    cot = cot_ref[...]
+    cot_copy[...] = cot
+    halo = pick_halo(near_ref, next_ref)
+    extended = jnp.concatenate([cot, halo.astype(BF16)], axis=0)
     gsa = jnp.zeros((rows, channels), F32)
     for k in range(3):
         gsa += mm(
@@ -202,51 +203,55 @@
             full_wt[k * channels : (k + 1) * channels],
             NT,
         )
-    gsa_ref[...] = gsa.astype(BF16)
-    gsa_t[...] = gsa.astype(BF16).astype(F32).T.astype(BF16)
-    params = group_params(stats_ref[...], count, per_group)
+    gsa = gsa.astype(BF16).astype(F32)
+    store_shifted(gsa_pad, gsa, frames, cells, cols)
+    for dy in range(3):
+        for dx in range(3):
+            at = (3 * dy + dx) * channels
+            gsa_seen[:, at : at + channels] = window(
+                gsa_pad, 2 - dy, 2 - dx, frames, cells, cols
+            )
+    gsa_t[...] = gsa.T.astype(BF16)
+    cot_t[:, :rows] = cot.astype(F32).T.astype(BF16)
+    cot_t[:, rows : rows + 2 * cells] = halo[: 2 * cells].T.astype(BF16)
+    left_s_ref[...] = core_order(gsa_t, W, core) if aligned else gsa_t[...]
+    left_t_ref[...] = core_order(cot_t, W, core) if aligned else cot_t[...]
+
+
+def first_body(sizes, lat_ref, stats_ref, left_s_ref, *rest):
+    D, W, frames, cells, cols, count, per_group, aligned = sizes
+    params_ref, seen_ref, keep_ref = rest[:3]
+    send_ref = rest[3] if aligned else None
+    act_pad = rest[-1]
+    channels = lat_ref.shape[1]
+    params = jnp.concatenate(
+        [group_params(stats_ref[:, 0:2], count, per_group), stats_ref[0, 2:4]], axis=0
+    )
     params_ref[...] = params
-    _, normed, sig = normalise(lat_ref, params, affine_ref)
+    _, normed, sig = normalise(lat_ref, params)
     act = (normed * sig).astype(BF16).astype(F32)
     store_shifted(act_pad, act, frames, cells, cols)
-    left = core_order(gsa_t, W, core) if aligned else gsa_t[...]
-    shard = wt_ref.shape[0] * 3
+    left = left_s_ref[...]
     for dy in range(3):
         for dx in range(3):
             at = (3 * dy + dx) * channels
             seen = window(act_pad, dy, dx, frames, cells, cols)
             seen_ref[:, at : at + channels] = seen
-            put(mm(left, seen), at, shard, keep_ref, send_ref)
+            put(mm(left, seen), at, keep_ref.shape[-1], keep_ref, send_ref)
 
 
 def second_body(
-    sizes,
-    lat_ref,
-    cot_t_ref,
-    near_ref,
-    next_ref,
-    params_ref,
-    affine_ref,
-    gsa_ref,
-    seen_ref,
-    ws_ref,
-    *rest,
+    sizes, lat_ref, left_t_ref, params_ref, gsa_seen_ref, seen_ref, ws_ref, *rest
 ):
     D, W, frames, cells, cols, count, per_group, aligned = sizes
     pieces, rest = rest[: 2 * (D - 1)], rest[2 * (D - 1) :]
-    full_ws, side_ws, gsa_pad, gsa_seen, cot_t = rest[-5:]
+    full_ws, side_ws = rest[-2:]
     spatial_ref, grad_ref, keep_ref, other_ref = rest[:4]
     send_ref = other_ref if aligned else None
     channels = lat_ref.shape[1]
-    core = lax.rem(lax.axis_index("wide"), 2)
-    fill_weights(full_ws, ws_ref, pieces, 0, D)
+    fill_weights(full_ws, ws_ref, pieces, D)
     rows = frames * cells
-    store_shifted(gsa_pad, gsa_ref[...].astype(F32), frames, cells, cols)
-    cot_t[:, :rows] = cot_t_ref[...]
-    cot_t[:, rows : rows + 2 * cells] = (
-        pick_halo(near_ref, next_ref)[: 2 * cells].T.astype(BF16)
-    )
-    left = core_order(cot_t, W, core) if aligned else cot_t[...]
+    left = left_t_ref[...]
     spatial = mm(seen_ref[...], full_ws[...]).astype(BF16)
     spatial_ref[...] = spatial
     shard = ws_ref.shape[0] // 3
@@ -254,15 +259,11 @@
         block = mm(left[:, k * cells : k * cells + rows], spatial)
         put(block, k * channels, shard, keep_ref, send_ref)
 
-    for dy in range(3):
-        for dx in range(3):
-            at = (3 * dy + dx) * channels
-            gsa_seen[:, at : at + channels] = window(
-                gsa_pad, 2 - dy, 2 - dx, frames, cells, cols
-            )
-            side_ws[:, at : at + channels] = full_ws[at : at + channels]
-    grad = mm(gsa_seen[...], side_ws[...], NT)
-    white, normed, sig = normalise(lat_ref, params_ref[...], affine_ref)
+    for tap in range(9):
+        at = tap * channels
+        side_ws[:, at : at + channels] = full_ws[at : at + channels]
+    grad = mm(gsa_seen_ref[...], side_ws[...], NT)
+    white, normed, sig = normalise(lat_ref, params_ref[...])
     grad = grad * (sig * (1.0 + normed * (1.0 - sig)))
     grad_ref[...] = grad
     gain_term = jnp.sum(grad * white, axis=0, keepdims=True)
@@ -284,12 +285,9 @@
                 target[owner, at : at + 16, shard:] = low
 
 
-def block_body(sizes, lat_ref, spatial_ref, before_ref, wt_ref, *rest):
+def block_body(sizes, lat_ref, spatial_ref, before_ref, full_wt, block_ref):
     D, W, frames, cells, cols, count, per_group, aligned = sizes
-    pieces = rest[: 2 * (D - 1)]
-    block_ref, full_wt = rest[2 * (D - 1) :]
     channels = lat_ref.shape[1]
-    fill_weights(full_wt, wt_ref, pieces, pieces[0].shape[0] - wt_ref.shape[0] // 2, D)
     extended = jnp.concatenate([before_ref[...], spatial_ref[...]], axis=0)
     rows = frames * cells
     temporal = jnp.zeros((rows, channels), F32)
@@ -301,10 +299,10 @@
     block_ref[...] = (lat_ref[...].astype(F32) + temporal).astype(BF16)
 
 
-def latent_gradient(sizes, total, lat_ref, cot_ref, params_ref, affine_ref, grad_ref):
+def latent_gradient(sizes, total, lat_ref, cot_ref, params_ref, grad_ref):
     count, per_group = sizes[5:7]
     white, inv_std = whiten(lat_ref[...], params_ref[...]), params_ref[1:2]
-    gain = affine_ref[0:1]
+    gain = params_ref[2:3]
     means = group_total(total * gain, per_group) / count
     inner = inv_std * (grad_ref[...] * gain - means[1:2] - white * means[0:1])
     return (cot_ref[...].astype(F32) + inner).astype(BF16)
@@ -410,12 +408,12 @@
         return lax.ppermute(value, ("dp", "wide"), over_all(moves))
 
     R = shard_s + shard_t
-    stats, affine, half = call(
+    stats, half_s, half_t = call(
         stats_body,
         [
-            shape((W, 2, channels), F32),
-            shape((2, channels), F32),
-            shape((R // 2, channels), BF16),
+            shape((W, 4, channels), F32),
+            shape((shard_s // 2, channels), BF16),
+            shape((shard_t // 2, channels), BF16),
         ],
         [
             pltpu.VMEM((rows, channels), BF16),
@@ -426,16 +424,43 @@
         in_specs=[HBM] * 5,
         vmem=FIRST_VMEM,
     )(lat, gain, bias, w_spatial, w_temporal)
-    cot_t = call(transpose_body, shape((channels, rows), BF16), moved=300_000)(cot)
-    firsts = [send(half, lambda d, w: ((d + s) % D, w)) for s in range(1, D)]
+    firsts_t = [send(half_t, lambda d, w: ((d + s) % D, w)) for s in range(1, D)]
+    half_s, firsts_t = lax.optimization_barrier((half_s, firsts_t))
+    firsts_s = [send(half_s, lambda d, w: ((d + s) % D, w)) for s in range(1, D)]
 
     next_cot = lax.ppermute(cot, "wide", [(w + 1, w) for w in range(1, W - 1, 2)])
     near_cot = send(cot, lambda d, w: (d, w ^ 1))
+    pieces_t, pieces_s = [], []
+    for first in firsts_t:
+        pieces_t += [first, send(first, lambda d, w: (d, w ^ 1))]
+    stats, pieces_t, near_cot, cot = lax.optimization_barrier(
+        (stats, pieces_t, near_cot, cot)
+    )
     stats = lax.all_to_all(stats, "wide", split_axis=0, concat_axis=0, tiled=True)
-    firsts, stats, next_cot, cot_t = lax.optimization_barrier((firsts, stats, next_cot, cot_t))
-    pieces = []
-    for first in firsts:
-        pieces += [first, send(first, lambda d, w: (d, w ^ 1))]
+    taps = D * shard_s
+    pad = pltpu.VMEM((3, frames, cells + 2 * cols, channels), BF16)
+    ready = call(
+        functools.partial(ready_body, sizes),
+        [
+            shape((rows, channels), BF16),
+            shape((rows, channels), BF16),
+            shape((channels, rows + 2 * cells), BF16),
+            shape((channels, rows), BF16),
+            shape((rows, taps), BF16),
+            shape((D * shard_t, channels), BF16),
+        ],
+        [
+            pad,
+            pltpu.VMEM((channels, rows), BF16),
+            pltpu.VMEM((channels, rows + 2 * cells), BF16),
+        ],
+        flops=2 * 3 * rows * channels * channels,
+        moved=2_000_000,
+    )(lat, cot, near_cot, next_cot, w_temporal, *pieces_t)
+    firsts_s, stats, ready = lax.optimization_barrier((firsts_s, stats, ready))
+    lat, cot, left_t, left_s, gsa_seen, full_wt = ready
+    for first in firsts_s:
+        pieces_s += [first, send(first, lambda d, w: (d, w ^ 1))]
 
     ride = 128 if aligned else 0
     if aligned:
@@ -444,44 +469,31 @@
     else:
         terms_s = [shape((channels, D * shard_s), BF16)]
         terms_t = [shape((channels, D * shard_t), BF16), shape((D * W, 2, channels), F32)]
-    pad = pltpu.VMEM((3, frames, cells + 2 * cols, channels), BF16)
-    taps = D * shard_s
-    gsa, params, seen, *grads_s = call(
+    params, seen, *grads_s = call(
         functools.partial(first_body, sizes),
-        [
-            shape((rows, channels), BF16),
-            shape((2, channels), F32),
-            shape((rows, taps), BF16),
-        ]
-        + terms_s,
-        [pltpu.VMEM((D * shard_t, channels), BF16), pad, pltpu.VMEM((channels, rows), BF16)],
-        flops=2 * 12 * rows * channels * channels,
+        [shape((4, channels), F32), shape((rows, taps), BF16)] + terms_s,
+        [pad],
+        flops=2 * 9 * rows * channels * channels,
         moved=3_000_000,
-    )(lat, cot, near_cot, next_cot, stats, affine, w_temporal, *pieces)
+    )(lat, stats, left_s)
     spatial, grad, *grads_t = call(
         functools.partial(second_body, sizes),
         [shape((rows, channels), BF16), shape((rows, channels), F32)] + terms_t,
-        [
-            pltpu.VMEM((taps, channels), BF16),
-            pltpu.VMEM((channels, taps), BF16),
-            pad,
-            pltpu.VMEM((rows, taps), BF16),
-            pltpu.VMEM((channels, rows + 2 * cells), BF16),
-        ],
+        [pltpu.VMEM((taps, channels), BF16), pltpu.VMEM((channels, taps), BF16)],
         flops=2 * 21 * rows * channels * channels,
         moved=3_000_000,
-    )(lat, cot_t, near_cot, next_cot, params, affine, gsa, seen, w_spatial, *pieces)
+    )(lat, left_t, params, gsa_seen, seen, w_spatial, *pieces_s)
     before = lax.ppermute(spatial, "wide", [(w, w + 1) for w in range(W - 1)])
     block_out = call(
         functools.partial(block_body, sizes),
         shape((rows, channels), BF16),
-        [pltpu.VMEM((D * shard_t, channels), BF16)],
         flops=2 * 3 * rows * channels * channels,
         moved=1_000_000,
-    )(lat, spatial, before, w_temporal, *pieces)
+    )(lat, spatial, before, full_wt)
 
     width = channels // W
-    operands = (lat, cot, params, affine, grad)
+
+    operands = (lat, cot, params, grad)
     if aligned:
         Z = W // 4
 

time: 50.9 us -> 55 us (1.081)
  local copies, waits for them, and re-layouts: 2.49 us -> 4.26 us
  starting transfers between devices: 21.3 us -> 22.8 us
  Pallas kernels: 7.22 us -> 8.44 us
    all_to_all x1, waiting for transfers between devices: 5.62 us -> 2.99 us  [local(): lax.all_to_all(stats, 'wide', split_axis=0, concat_axis=0, tiled=True)]
    ppermute x11 -> x13, waiting for transfers between devices: 13.2 us -> 15.4 us  [send(): return lax.ppermute(value, ('dp', 'wide'), over_all(moves))]
    unnamed x12 -> x16, local copies, waits for them, and re-layouts: 2.49 us -> 4.26 us
    ppermute x11 -> x13, starting transfers between devices: 12.3 us -> 14 us  [send(): return lax.ppermute(value, ('dp', 'wide'), over_all(moves))]
    pallas_call x8, Pallas kernels: 7.22 us -> 8.44 us  [run(): pl.pallas_call(body, out_shape=out_shapes, in_specs=in_specs or [VMEM] *...]
  transfers between devices with their start and end apart: 14 -> 16, of which waited for: 8 -> 9; matrix products, arithmetic and copies ran while one was open for 0% -> 0% of each run, Pallas kernels for 6% -> 10%
where the time goes in v9:
time: 55 us; the launch traced here: 54.6 us
  starting transfers between devices  22.8 us (41%)
  waiting for transfers between devices  18.4 us (33%)
  Pallas kernels  8.44 us (15%)
  local copies, waits for them, and re-layouts  4.26 us (8%)
  between operations  0.77 us (1%)
    ppermute x13, waiting for transfers between devices, send(): return lax.ppermute(value, ('dp', 'wide'), over_all(moves))  15.4 us
    ppermute x13, starting transfers between devices, send(): return lax.ppermute(value, ('dp', 'wide'), over_all(moves))  14 us
    pallas_call x8, Pallas kernels, run(): pl.pallas_call(body, out_shape=out_shapes, in_specs=in_specs or [VMEM] *...  8.44 us
    all_to_all x1, starting transfers between devices, local(): lax.all_to_all(stats, 'wide', split_axis=0, concat_axis=0, tiled=True)  6.86 us
    unnamed x16, local copies, waits for them, and re-layouts  4.26 us
    all_to_all x1, waiting for transfers between devices, local(): lax.all_to_all(stats, 'wide', split_axis=0, concat_axis=0, tiled=True)  2.99 us
    ppermute x1, starting transfers between devices, local(): before = lax.ppermute(spatial, 'wide', [(w, w + 1) for w in range(W - 1)])  1.29 us
  transfers between devices with their start and end apart: 16, of which 9 were waited for; matrix products, arithmetic and copies ran while one was open for 0% of the time, Pallas kernels for 10%

profile of v9, /device:TPU:0, one launch (start us, length us, event | category | flops | bytes accessed | tf_op | source)
XLA Modules:
  0.0 54.6 jit_solution(10891619043568484033)
XLA Ops:
  0.6 1.9 %shard_map.101 = (f32[16,4,256]{2,1,0:T(4,128)}, bf16[576,256]{1,0:T(8,128)(2,1)}, bf16[192,256]{1,0:T(8,128)(2,1)}) custom-call(bf16[256,256]{1,0:T(8,128)(2,1)} %bitcast.14, f32[1,256]{1,0:T(1,128)} %bitcast.22, f32[1,256]{1,0:T(1,128)} %bitcast.23, bf16[1152,256]{1,0:T(8,128)(2,1)} %ws_ref.3, bf16[384,256]{1,0:T(8,128)(2,1)} %wt_ref.3), custom_call_target="tpu_custom_call" | custom-call | tf_op jit(solution)/shard_map/pallas_call | solution.py:26
  2.6 3.0 %collective-permute-start = (bf16[192,256]{1,0:T(8,128)(2,1)}, bf16[192,256]{1,0:T(8,128)(2,1)S(1)}, u32[]{:S(2)}, u32[]{:S(2)}) collective-permute-start(bf16[192,256]{1,0:T(8,128)(2,1)} %get-tuple-element.50), channel_id=1, source_target_pairs={{0,16},{1,17},{2,18},{3,19},{4,20},{5,21},{6,22},{7,23},{8,24},{9,... | collective-permute-start | bytes 294920 | tf_op jit(solution)/shard_map/ppermute | solution.py:408
  5.6 3.0 %collective-permute-done.rest_0_ = bf16[192,256]{1,0:T(8,128)(2,1)S(1)} collective-permute-done((bf16[192,256]{1,0:T(8,128)(2,1)}, bf16[192,256]{1,0:T(8,128)(2,1)S(1)}, u32[]{:S(2)}, u32[]{:S(2)}) %collective-permute-start) | collective-permute-done | bytes 98336 | tf_op jit(solution)/shard_map/ppermute | solution.py:408
  8.6 1.8 %collective-permute-start.1 = (bf16[576,256]{1,0:T(8,128)(2,1)}, bf16[576,256]{1,0:T(8,128)(2,1)S(1)}, u32[]{:S(2)}, u32[]{:S(2)}) collective-permute-start(bf16[576,256]{1,0:T(8,128)(2,1)} %get-tuple-element.51), channel_id=1, source_target_pairs={{0,16},{1,17},{2,18},{3,19},{4,20},{5,21},{6,22},{7,23},{8,24},{9,... | collective-permute-start | bytes 884744 | tf_op jit(solution)/shard_map/ppermute | solution.py:408
  10.4 0.5 collective-permute-start.2
  11.0 0.7 %collective-permute-start.4 = (bf16[256,256]{1,0:T(8,128)(2,1)}, bf16[256,256]{1,0:T(8,128)(2,1)S(1)}, u32[]{:S(2)}, u32[]{:S(2)}) collective-permute-start(bf16[256,256]{1,0:T(8,128)(2,1)} %bitcast.19), channel_id=1, source_target_pairs={{2,1},{4,3},{6,5},{8,7},{10,9},{12,11},{14,13},{18,17},{20,19},{22... | collective-permute-start | bytes 393224 | tf_op jit(solution)/shard_map/ppermute | solution.py:431
  11.6 0.5 collective-permute-done.3.near_ref
  12.1 6.9 %all-to-all-start = ((f32[16,4,256]{2,1,0:T(4,128)}), f32[16,4,256]{2,1,0:T(4,128)}, u32[]{:S(2)}, u32[]{:S(2)}) async-start(f32[16,4,256]{2,1,0:T(4,128)} %get-tuple-element.54), calls=%async_computation | async-start | bytes 131072 | tf_op jit(solution)/shard_map/all_to_all | solution.py:439
  19.1 0.9 %copy-done.2 = bf16[1,2,8,16,256]{4,3,2,1,0:T(8,128)(2,1)S(1)} copy-done((bf16[1,2,8,16,256]{4,3,2,1,0:T(8,128)(2,1)S(1)}, bf16[1,2,8,16,256]{4,3,2,1,0:T(8,128)(2,1)}, u32[]{:S(2)}) %copy-start.2) | copy-done | bytes 131096
  20.0 0.9 %copy-done.3 = bf16[1,2,8,16,256]{4,3,2,1,0:T(8,128)(2,1)S(1)} copy-done((bf16[1,2,8,16,256]{4,3,2,1,0:T(8,128)(2,1)S(1)}, bf16[1,2,8,16,256]{4,3,2,1,0:T(8,128)(2,1)}, u32[]{:S(2)}) %copy-start.3) | copy-done | bytes 131096
  20.9 0.9 %copy-done.5 = bf16[192,256]{1,0:T(8,128)(2,1)S(1)} copy-done((bf16[192,256]{1,0:T(8,128)(2,1)S(1)}, bf16[192,256]{1,0:T(8,128)(2,1)}, u32[]{:S(2)}) %copy-start.5) | copy-done | bytes 98328
  21.8 0.6 %shard_map.102 = (bf16[256,256]{1,0:T(8,128)(2,1)S(1)}, bf16[256,256]{1,0:T(8,128)(2,1)S(1)}, bf16[256,512]{1,0:T(8,128)(2,1)S(1)}, bf16[256,256]{1,0:T(8,128)(2...) custom-call(bf16[256,256]{1,0:T(8,128)(2,1)S(1)} %bitcast.15, bf16[256,256]{1,0:T(8,128)(2,1)S(1)} %bitcast.20, ...), custom_call_target="tpu_custom_call" | custom-call | flops 100663296 | bytes 2000000 | tf_op jit(solution)/shard_map/pallas_call | solution.py:26
  22.3 0.6 %copy-done.6 = bf16[256,256]{1,0:T(8,128)(2,1)} copy-done((bf16[256,256]{1,0:T(8,128)(2,1)}, bf16[256,256]{1,0:T(8,128)(2,1)S(1)}, u32[]{:S(2)}) %copy-start.6) | copy-done | bytes 131096
  23.0 3.0 %all-to-all-done.stats_ref = f32[16,4,256]{2,1,0:T(4,128)} async-done(((f32[16,4,256]{2,1,0:T(4,128)}), f32[16,4,256]{2,1,0:T(4,128)}, u32[]{:S(2)}, u32[]{:S(2)}) %all-to-all-start) | async-done | bytes 65568 | tf_op jit(solution)/shard_map/all_to_all | solution.py:439
  26.0 0.9 %copy-done.7 = bf16[256,256]{1,0:T(8,128)(2,1)S(1)} copy-done((bf16[256,256]{1,0:T(8,128)(2,1)S(1)}, bf16[256,256]{1,0:T(8,128)(2,1)}, u32[]{:S(2)}) %copy-start.7) | copy-done | bytes 131096
  26.9 1.9 %shard_map.103 = (f32[4,256]{1,0:T(4,128)S(1)}, bf16[256,2304]{1,0:T(8,128)(2,1)S(1)}, bf16[2,128,1152]{2,1,0:T(8,128)(2,1)S(1)}, bf16[2,128,1152]{2,1,0:T(8,128)(2,1)S(1)}) custom-call(bf16[256,256]{1,0:T(8,128)(2,1)S(1)} %get-tuple-element.65.lat_ref.refs_4_, f32[16,4,256]{2,1,0:T(4,128)} %all-to-all-done.stats_ref, bf16[256,256]{1,0:T(8,128)(2,1)S(1)} %copy-done.7), custom_call_target="tpu_custom_call" | custom-call | flops 301989888 | bytes 3000000 | tf_op jit(solution)/shard_map/pallas_call | solution.py:26
  28.8 0.6 %collective-permute-start.7 = (bf16[2,128,1152]{2,1,0:T(8,128)(2,1)S(1)}, bf16[2,128,1152]{2,1,0:T(8,128)(2,1)S(1)}, u32[]{:S(2)}, u32[]{:S(2)}) collective-permute-start(bf16[2,128,1152]{2,1,0:T(8,128)(2,1)S(1)} %get-tuple-element.76), channel_id=1, source_target_pairs={{0,1},{1,0},{2,3},{3,2},{4,5},{5,4},{6,7},{7,6},{8,9},{9,8},{10,11... | collective-permute-start | bytes 1769480 | tf_op jit(solution)/shard_map/ppermute | solution.py:408
  29.4 1.7 %shard_map.104 = (bf16[256,256]{1,0:T(8,128)(2,1)S(1)}, f32[256,256]{1,0:T(8,128)S(1)}, bf16[2,128,512]{2,1,0:T(8,128)(2,1)S(1)}, bf16[2,128,512]{2,1,0:T(8,128)(2,1)S(1)}) custom-call(bf16[256,256]{1,0:T(8,128)(2,1)S(1)} %get-tuple-element.65.lat_ref.refs_4_, bf16[256,512]{1,0:T(8,128)(2,1)S(1)} %get-tuple-element.66.left_t_ref, ...), custom_call_target="tpu_custom_call" | custom-call | flops 704643072 | bytes 3000000 | tf_op jit(solution)/shard_map/pallas_call | solution.py:26
  31.2 1.5 %collective-permute-done.8 = bf16[2,128,512]{2,1,0:T(8,128)(2,1)S(1)} collective-permute-done((bf16[2,128,512]{2,1,0:T(8,128)(2,1)S(1)}, bf16[2,128,512]{2,1,0:T(8,128)(2,1)S(1)}, u32[]{:S(2)}, u32[]{:S(2)}) %collective-permute-start.8) | collective-permute-done | bytes 262176 | tf_op jit(solution)/shard_map/ppermute | solution.py:408
  33.1 0.5 collective-permute-start.10
  33.6 2.8 %collective-permute-start.11 = (bf16[4,16,1664]{2,1,0:T(8,128)(2,1)S(1)}, bf16[4,16,1664]{2,1,0:T(8,128)(2,1)S(1)}, u32[]{:S(2)}, u32[]{:S(2)}) collective-permute-start(bf16[4,16,1664]{2,1,0:T(8,128)(2,1)S(1)} %get-tuple-element.82), channel_id=1, source_target_pairs={{0,18},{1,19},{2,16},{3,17},{4,22},{5,23},{6,20},{7,21},{8,26},{9,... | collective-permute-start | bytes 638984 | tf_op jit(solution)/shard_map/ppermute | solution.py:408
  36.4 1.3 %collective-permute-start.6 = (bf16[256,256]{1,0:T(8,128)(2,1)S(1)}, bf16[256,256]{1,0:T(8,128)(2,1)S(1)}, u32[]{:S(2)}, u32[]{:S(2)}) collective-permute-start(bf16[256,256]{1,0:T(8,128)(2,1)S(1)} %get-tuple-element.73.spatial_ref), channel_id=1, source_target_pairs={{0,1},{1,2},{2,3},{3,4},{4,5},{5,6},{6,7},{7,8},{8,9},{9,10},{10,1... | collective-permute-start | bytes 393224 | tf_op jit(solution)/shard_map/ppermute | solution.py:486
  37.7 2.5 %collective-permute-done.9.refs_1_ = bf16[4,16,1664]{2,1,0:T(8,128)(2,1)S(1)} collective-permute-done((bf16[4,16,1664]{2,1,0:T(8,128)(2,1)S(1)}, bf16[4,16,1664]{2,1,0:T(8,128)(2,1)S(1)}, u32[]{:S(2)}, u32[]{:S(2)}) %collective-permute-start.9) | collective-permute-done | bytes 213024 | tf_op jit(solution)/shard_map/ppermute | solution.py:408
  40.2 1.0 %collective-permute-done.10.refs_2_ = bf16[4,16,1664]{2,1,0:T(8,128)(2,1)S(1)} collective-permute-done((bf16[4,16,1664]{2,1,0:T(8,128)(2,1)S(1)}, bf16[4,16,1664]{2,1,0:T(8,128)(2,1)S(1)}, u32[]{:S(2)}, u32[]{:S(2)}) %collective-permute-start.10) | collective-permute-done | bytes 213024 | tf_op jit(solution)/shard_map/ppermute | solution.py:408
  41.2 4.8 %collective-permute-done.11.refs_3_ = bf16[4,16,1664]{2,1,0:T(8,128)(2,1)S(1)} collective-permute-done((bf16[4,16,1664]{2,1,0:T(8,128)(2,1)S(1)}, bf16[4,16,1664]{2,1,0:T(8,128)(2,1)S(1)}, u32[]{:S(2)}, u32[]{:S(2)}) %collective-permute-start.11) | collective-permute-done | bytes 213024 | tf_op jit(solution)/shard_map/ppermute | solution.py:408
  46.1 1.4 %collective-permute-start.12 = (bf16[16,1664]{1,0:T(8,128)(2,1)S(1)}, bf16[16,1664]{1,0:T(8,128)(2,1)S(1)}, u32[]{:S(2)}, u32[]{:S(2)}) collective-permute-start(bf16[16,1664]{1,0:T(8,128)(2,1)S(1)} %get-tuple-element.84), channel_id=1, source_target_pairs={{0,4},{1,5},{2,6},{3,7},{4,8},{5,9},{6,10},{7,11},{8,12},{9,13},{1... | collective-permute-start | bytes 159752 | tf_op jit(solution)/shard_map/ppermute | solution.py:408
  47.5 1.1 %collective-permute-start.13 = (bf16[16,1664]{1,0:T(8,128)(2,1)S(1)}, bf16[16,1664]{1,0:T(8,128)(2,1)S(1)}, u32[]{:S(2)}, u32[]{:S(2)}) collective-permute-start(bf16[16,1664]{1,0:T(8,128)(2,1)S(1)} %get-tuple-element.85), channel_id=1, source_target_pairs={{0,8},{1,9},{2,10},{3,11},{4,12},{5,13},{6,14},{7,15},{8,0},{9,1},... | collective-permute-start | bytes 159752 | tf_op jit(solution)/shard_map/ppermute | solution.py:408
  48.7 1.9 %collective-permute-start.14 = (bf16[16,1664]{1,0:T(8,128)(2,1)S(1)}, bf16[16,1664]{1,0:T(8,128)(2,1)S(1)}, u32[]{:S(2)}, u32[]{:S(2)}) collective-permute-start(bf16[16,1664]{1,0:T(8,128)(2,1)S(1)} %get-tuple-element.86), channel_id=1, source_target_pairs={{0,12},{1,13},{2,14},{3,15},{4,0},{5,1},{6,2},{7,3},{8,4},{9,5},{1... | collective-permute-start | bytes 159752 | tf_op jit(solution)/shard_map/ppermute | solution.py:408
  50.5 0.9 %shard_map.105 = bf16[256,256]{1,0:T(8,128)(2,1)} custom-call(bf16[256,256]{1,0:T(8,128)(2,1)S(1)} %get-tuple-element.65.lat_ref.refs_4_, bf16[256,256]{1,0:T(8,128)(2,1)S(1)} %get-tuple-element.73.spatial_ref, bf16[256,256]{1,0:T(8,128)(2,1)S(1)} %collective-permute-done.6.before_ref, bf16[768,256]{1,0:T(8,128)(2,1)S(1)} %get-tuple-element.74.full_wt), custom_call_target="tpu_custom_call" | custom-call | flops 100663296 | bytes 1000000 | tf_op jit(solution)/shard_map/pallas_call | solution.py:26
  51.5 0.7 %collective-permute-done.12.refs_1_ = bf16[16,1664]{1,0:T(8,128)(2,1)S(1)} collective-permute-done((bf16[16,1664]{1,0:T(8,128)(2,1)S(1)}, bf16[16,1664]{1,0:T(8,128)(2,1)S(1)}, u32[]{:S(2)}, u32[]{:S(2)}) %collective-permute-start.12) | collective-permute-done | bytes 53280 | tf_op jit(solution)/shard_map/ppermute | solution.py:408
  52.2 1.3 %collective-permute-done.13.refs_2_ = bf16[16,1664]{1,0:T(8,128)(2,1)S(1)} collective-permute-done((bf16[16,1664]{1,0:T(8,128)(2,1)S(1)}, bf16[16,1664]{1,0:T(8,128)(2,1)S(1)}, u32[]{:S(2)}, u32[]{:S(2)}) %collective-permute-start.13) | collective-permute-done | bytes 53280 | tf_op jit(solution)/shard_map/ppermute | solution.py:408
  53.5 1.1 %shard_map.108 = (f32[16,1152]{1,0:T(8,128)}, f32[16,384]{1,0:T(8,128)}, f32[2,16]{1,0:T(2,128)}, bf16[256,256]{1,0:T(8,128)(2,1)}) custom-call(bf16[16,1664]{1,0:T(8,128)(2,1)S(1)} %get-tuple-element.83.refs_0_, bf16[16,1664]{1,0:T(8,128)(2,1)S(1)} %collective-permute-done.12.refs_1_, bf16[16,1664]{1,0:T(8,128)(2,1)S(1)} %collective-permute-done.13.refs_2_, ...), custom_call_target="tpu_custom_call" | custom-call | bytes 1000000 | tf_op jit(solution)/shard_map/pallas_call | solution.py:26
  (24 shorter events, 0.7 us)
Async XLA Ops:
  0.6 18.4 %copy-start.1 = (bf16[384,256]{1,0:T(8,128)(2,1)S(1)}, bf16[384,256]{1,0:T(8,128)(2,1)}, u32[]{:S(2)}) copy-start(bf16[384,256]{1,0:T(8,128)(2,1)} %wt_ref.3) | copy-start | bytes 589828
  2.6 26.8 %copy-start = (bf16[1152,256]{1,0:T(8,128)(2,1)S(1)}, bf16[1152,256]{1,0:T(8,128)(2,1)}, u32[]{:S(2)}) copy-start(bf16[1152,256]{1,0:T(8,128)(2,1)} %ws_ref.3) | copy-start | bytes 1769476
  2.6 6.0 %collective-permute-start = (bf16[192,256]{1,0:T(8,128)(2,1)}, bf16[192,256]{1,0:T(8,128)(2,1)S(1)}, u32[]{:S(2)}, u32[]{:S(2)}) collective-permute-start(bf16[192,256]{1,0:T(8,128)(2,1)} %get-tuple-element.50), channel_id=1, source_target_pairs={{0,16},{1,17},{2,18},{3,19},{4,20},{5,21},{6,22},{7,23},{8,24},{9,... | collective-permute-start | bytes 294920 | tf_op jit(solution)/shard_map/ppermute | solution.py:408
  8.6 17.4 %collective-permute-start.1 = (bf16[576,256]{1,0:T(8,128)(2,1)}, bf16[576,256]{1,0:T(8,128)(2,1)S(1)}, u32[]{:S(2)}, u32[]{:S(2)}) collective-permute-start(bf16[576,256]{1,0:T(8,128)(2,1)} %get-tuple-element.51), channel_id=1, source_target_pairs={{0,16},{1,17},{2,18},{3,19},{4,20},{5,21},{6,22},{7,23},{8,24},{9,... | collective-permute-start | bytes 884744 | tf_op jit(solution)/shard_map/ppermute | solution.py:408
  10.4 1.7 %collective-permute-start.3 = (bf16[256,256]{1,0:T(8,128)(2,1)}, bf16[256,256]{1,0:T(8,128)(2,1)S(1)}, u32[]{:S(2)}, u32[]{:S(2)}) collective-permute-start(bf16[256,256]{1,0:T(8,128)(2,1)} %bitcast.18), channel_id=1, source_target_pairs={{0,1},{1,0},{2,3},{3,2},{4,5},{5,4},{6,7},{7,6},{8,9},{9,8},{10,11... | collective-permute-start | bytes 393224 | tf_op jit(solution)/shard_map/ppermute | solution.py:408
  10.4 1.7 %collective-permute-start.2 = (bf16[192,256]{1,0:T(8,128)(2,1)S(1)}, bf16[192,256]{1,0:T(8,128)(2,1)S(1)}, u32[]{:S(2)}, u32[]{:S(2)}) collective-permute-start(bf16[192,256]{1,0:T(8,128)(2,1)S(1)} %collective-permute-done.rest_0_), channel_id=1, source_target_pairs={{0,1},{1,0},{2,3},{3,2},{4,5},{5,4},{6,7},{7,6},{8,9},{9,8},{10,11... | collective-permute-start | bytes 294920 | tf_op jit(solution)/shard_map/ppermute | solution.py:408
  11.0 8.1 %collective-permute-start.4 = (bf16[256,256]{1,0:T(8,128)(2,1)}, bf16[256,256]{1,0:T(8,128)(2,1)S(1)}, u32[]{:S(2)}, u32[]{:S(2)}) collective-permute-start(bf16[256,256]{1,0:T(8,128)(2,1)} %bitcast.19), channel_id=1, source_target_pairs={{2,1},{4,3},{6,5},{8,7},{10,9},{12,11},{14,13},{18,17},{20,19},{22... | collective-permute-start | bytes 393224 | tf_op jit(solution)/shard_map/ppermute | solution.py:431
  12.1 6.9 %copy-start.4 = (bf16[192,256]{1,0:T(8,128)(2,1)}, bf16[192,256]{1,0:T(8,128)(2,1)S(1)}, u32[]{:S(2)}) copy-start(bf16[192,256]{1,0:T(8,128)(2,1)S(1)} %collective-permute-done.2.rest_1_) | copy-start | bytes 294916
  12.1 13.8 %all-to-all-start = ((f32[16,4,256]{2,1,0:T(4,128)}), f32[16,4,256]{2,1,0:T(4,128)}, u32[]{:S(2)}, u32[]{:S(2)}) async-start(f32[16,4,256]{2,1,0:T(4,128)} %get-tuple-element.54), calls=%async_computation | async-start | bytes 131072 | tf_op jit(solution)/shard_map/all_to_all | solution.py:439
  19.0 0.9 %copy-start.2 = (bf16[1,2,8,16,256]{4,3,2,1,0:T(8,128)(2,1)S(1)}, bf16[1,2,8,16,256]{4,3,2,1,0:T(8,128)(2,1)}, u32[]{:S(2)}) copy-start(bf16[1,2,8,16,256]{4,3,2,1,0:T(8,128)(2,1)} %param.6) | copy-start | bytes 393220
  20.0 0.9 %copy-start.3 = (bf16[1,2,8,16,256]{4,3,2,1,0:T(8,128)(2,1)S(1)}, bf16[1,2,8,16,256]{4,3,2,1,0:T(8,128)(2,1)}, u32[]{:S(2)}) copy-start(bf16[1,2,8,16,256]{4,3,2,1,0:T(8,128)(2,1)} %param.7) | copy-start | bytes 393220
  20.9 0.9 %copy-start.5 = (bf16[192,256]{1,0:T(8,128)(2,1)S(1)}, bf16[192,256]{1,0:T(8,128)(2,1)}, u32[]{:S(2)}) copy-start(bf16[192,256]{1,0:T(8,128)(2,1)} %copy-done.4) | copy-start | bytes 294916
  22.3 0.7 %copy-start.6 = (bf16[256,256]{1,0:T(8,128)(2,1)}, bf16[256,256]{1,0:T(8,128)(2,1)S(1)}, u32[]{:S(2)}) copy-start(bf16[256,256]{1,0:T(8,128)(2,1)S(1)} %get-tuple-element.68.left_s_ref) | copy-start | bytes 393220
  26.0 3.4 %collective-permute-start.5 = (bf16[576,256]{1,0:T(8,128)(2,1)S(1)}, bf16[576,256]{1,0:T(8,128)(2,1)S(1)}, u32[]{:S(2)}, u32[]{:S(2)}) collective-permute-start(bf16[576,256]{1,0:T(8,128)(2,1)S(1)} %collective-permute-done.1.rest_0_), channel_id=1, source_target_pairs={{0,1},{1,0},{2,3},{3,2},{4,5},{5,4},{6,7},{7,6},{8,9},{9,8},{10,11... | collective-permute-start | bytes 884744 | tf_op jit(solution)/shard_map/ppermute | solution.py:408
  26.0 0.9 %copy-start.7 = (bf16[256,256]{1,0:T(8,128)(2,1)S(1)}, bf16[256,256]{1,0:T(8,128)(2,1)}, u32[]{:S(2)}) copy-start(bf16[256,256]{1,0:T(8,128)(2,1)} %copy-done.6) | copy-start | bytes 393220
  28.8 3.9 %collective-permute-start.7 = (bf16[2,128,1152]{2,1,0:T(8,128)(2,1)S(1)}, bf16[2,128,1152]{2,1,0:T(8,128)(2,1)S(1)}, u32[]{:S(2)}, u32[]{:S(2)}) collective-permute-start(bf16[2,128,1152]{2,1,0:T(8,128)(2,1)S(1)} %get-tuple-element.76), channel_id=1, source_target_pairs={{0,1},{1,0},{2,3},{3,2},{4,5},{5,4},{6,7},{7,6},{8,9},{9,8},{10,11... | collective-permute-start | bytes 1769480 | tf_op jit(solution)/shard_map/ppermute | solution.py:408
  31.1 1.6 %collective-permute-start.8 = (bf16[2,128,512]{2,1,0:T(8,128)(2,1)S(1)}, bf16[2,128,512]{2,1,0:T(8,128)(2,1)S(1)}, u32[]{:S(2)}, u32[]{:S(2)}) collective-permute-start(bf16[2,128,512]{2,1,0:T(8,128)(2,1)S(1)} %get-tuple-element.78), channel_id=1, source_target_pairs={{0,1},{1,0},{2,3},{3,2},{4,5},{5,4},{6,7},{7,6},{8,9},{9,8},{10,11... | collective-permute-start | bytes 786440 | tf_op jit(solution)/shard_map/ppermute | solution.py:408
  32.9 7.4 %collective-permute-start.9 = (bf16[4,16,1664]{2,1,0:T(8,128)(2,1)S(1)}, bf16[4,16,1664]{2,1,0:T(8,128)(2,1)S(1)}, u32[]{:S(2)}, u32[]{:S(2)}) collective-permute-start(bf16[4,16,1664]{2,1,0:T(8,128)(2,1)S(1)} %get-tuple-element.80), channel_id=1, source_target_pairs={{0,2},{1,3},{2,0},{3,1},{4,6},{5,7},{6,4},{7,5},{8,10},{9,11},{10,... | collective-permute-start | bytes 638984 | tf_op jit(solution)/shard_map/ppermute | solution.py:408
  33.1 8.1 %collective-permute-start.10 = (bf16[4,16,1664]{2,1,0:T(8,128)(2,1)S(1)}, bf16[4,16,1664]{2,1,0:T(8,128)(2,1)S(1)}, u32[]{:S(2)}, u32[]{:S(2)}) collective-permute-start(bf16[4,16,1664]{2,1,0:T(8,128)(2,1)S(1)} %get-tuple-element.81), channel_id=1, source_target_pairs={{0,16},{1,17},{2,18},{3,19},{4,20},{5,21},{6,22},{7,23},{8,24},{9,... | collective-permute-start | bytes 638984 | tf_op jit(solution)/shard_map/ppermute | solution.py:408
  33.6 12.4 %collective-permute-start.11 = (bf16[4,16,1664]{2,1,0:T(8,128)(2,1)S(1)}, bf16[4,16,1664]{2,1,0:T(8,128)(2,1)S(1)}, u32[]{:S(2)}, u32[]{:S(2)}) collective-permute-start(bf16[4,16,1664]{2,1,0:T(8,128)(2,1)S(1)} %get-tuple-element.82), channel_id=1, source_target_pairs={{0,18},{1,19},{2,16},{3,17},{4,22},{5,23},{6,20},{7,21},{8,26},{9,... | collective-permute-start | bytes 638984 | tf_op jit(solution)/shard_map/ppermute | solution.py:408
  36.4 14.1 %collective-permute-start.6 = (bf16[256,256]{1,0:T(8,128)(2,1)S(1)}, bf16[256,256]{1,0:T(8,128)(2,1)S(1)}, u32[]{:S(2)}, u32[]{:S(2)}) collective-permute-start(bf16[256,256]{1,0:T(8,128)(2,1)S(1)} %get-tuple-element.73.spatial_ref), channel_id=1, source_target_pairs={{0,1},{1,2},{2,3},{3,4},{4,5},{5,6},{6,7},{7,8},{8,9},{9,10},{10,1... | collective-permute-start | bytes 393224 | tf_op jit(solution)/shard_map/ppermute | solution.py:486
  46.1 6.1 %collective-permute-start.12 = (bf16[16,1664]{1,0:T(8,128)(2,1)S(1)}, bf16[16,1664]{1,0:T(8,128)(2,1)S(1)}, u32[]{:S(2)}, u32[]{:S(2)}) collective-permute-start(bf16[16,1664]{1,0:T(8,128)(2,1)S(1)} %get-tuple-element.84), channel_id=1, source_target_pairs={{0,4},{1,5},{2,6},{3,7},{4,8},{5,9},{6,10},{7,11},{8,12},{9,13},{1... | collective-permute-start | bytes 159752 | tf_op jit(solution)/shard_map/ppermute | solution.py:408
  47.5 6.0 %collective-permute-start.13 = (bf16[16,1664]{1,0:T(8,128)(2,1)S(1)}, bf16[16,1664]{1,0:T(8,128)(2,1)S(1)}, u32[]{:S(2)}, u32[]{:S(2)}) collective-permute-start(bf16[16,1664]{1,0:T(8,128)(2,1)S(1)} %get-tuple-element.85), channel_id=1, source_target_pairs={{0,8},{1,9},{2,10},{3,11},{4,12},{5,13},{6,14},{7,15},{8,0},{9,1},... | collective-permute-start | bytes 159752 | tf_op jit(solution)/shard_map/ppermute | solution.py:408
  48.7 4.9 %collective-permute-start.14 = (bf16[16,1664]{1,0:T(8,128)(2,1)S(1)}, bf16[16,1664]{1,0:T(8,128)(2,1)S(1)}, u32[]{:S(2)}, u32[]{:S(2)}) collective-permute-start(bf16[16,1664]{1,0:T(8,128)(2,1)S(1)} %get-tuple-element.86), channel_id=1, source_target_pairs={{0,12},{1,13},{2,14},{3,15},{4,0},{5,1},{6,2},{7,3},{8,4},{9,5},{1... | collective-permute-start | bytes 159752 | tf_op jit(solution)/shard_map/ppermute | solution.py:408

commit v10 on v6

--- a/solution.py
+++ b/solution.py
@@ -76,9 +76,13 @@
     both = jnp.concatenate(
         [jnp.sum(x, axis=0, keepdims=True), jnp.sum(x * x, axis=0, keepdims=True)], axis=0
     )
-    out_ref[...] = jnp.broadcast_to(both[None], out_ref.shape)
+    out_ref[...] = both
     for copy in copies[3:]:
         copy.wait()
+
+
+def add_body(left_ref, right_ref, out_ref):
+    out_ref[...] = left_ref[...] + right_ref[...]
 
 
 def transpose_body(cot_ref, out_ref):
@@ -100,7 +104,7 @@
 
 
 def whiten(lat, stats, count, per_group):
-    total = group_total(jnp.sum(stats, axis=0), per_group) / count
+    total = group_total(stats, per_group) / count
     mean = total[0:1]
     inv_std = 1.0 / jnp.sqrt(total[1:2] - mean * mean + EPSILON)
     return (lat.astype(F32) - mean) * inv_std, inv_std
@@ -167,18 +171,21 @@
         send_ref[owner, :, place : place + 128] = low[half:, at : at + 128]
 
 
-def normalise(lat_ref, stats_ref, affine_ref, count, per_group):
-    white, inv_std = whiten(lat_ref[...], stats_ref[...], count, per_group)
+def normalise(lat_ref, stats, affine_ref, count, per_group):
+    white, inv_std = whiten(lat_ref[...], stats, count, per_group)
     normed = white * affine_ref[0:1] + affine_ref[1:2]
     return white, normed, jax.nn.sigmoid(normed)
 
 
-def first_body(sizes, lat_ref, cot_ref, halo_ref, stats_ref, affine_ref, wt_ref, *rest):
+def first_body(sizes, lat_ref, cot_ref, halo_ref, affine_ref, wt_ref, *rest):
     D, W, frames, cells, cols, count, per_group, aligned = sizes
     pieces, rest = rest[: 2 * (D - 1)], rest[2 * (D - 1) :]
     full_wt, act_pad, gsa_t = rest[-3:]
-    gsa_ref, keep_ref = rest[:2]
-    send_ref = rest[2] if aligned else None
+    outs = rest[-7:-3] if aligned else rest[-6:-3]
+    stats = add([ref[...] for ref in rest[: -3 - len(outs)]])
+    gsa_ref, total_ref, keep_ref = outs[:3]
+    send_ref = outs[3] if aligned else None
+    total_ref[...] = stats
     channels = lat_ref.shape[1]
     core = lax.rem(lax.axis_index("wide"), 2)
     fill_weights(full_wt, wt_ref, pieces, pieces[0].shape[0] - wt_ref.shape[0] // 2, D)
@@ -193,7 +200,7 @@
         )
     gsa_ref[...] = gsa.astype(BF16)
     gsa_t[...] = gsa.astype(BF16).astype(F32).T.astype(BF16)
-    _, normed, sig = normalise(lat_ref, stats_ref, affine_ref, count, per_group)
+    _, normed, sig = normalise(lat_ref, stats, affine_ref, count, per_group)
     act = (normed * sig).astype(BF16).astype(F32)
     store_shifted(act_pad, act, frames, cells, cols)
     left = core_order(gsa_t, W, core) if aligned else gsa_t[...]
@@ -216,7 +223,7 @@
     core = lax.rem(lax.axis_index("wide"), 2)
     fill_weights(full_ws, ws_ref, pieces, 0, D)
     rows = frames * cells
-    white, normed, sig = normalise(lat_ref, stats_ref, affine_ref, count, per_group)
+    white, normed, sig = normalise(lat_ref, stats_ref[...], affine_ref, count, per_group)
     act = (normed * sig).astype(BF16).astype(F32)
     store_shifted(act_pad, act, frames, cells, cols)
     store_shifted(gsa_pad, gsa_ref[...].astype(F32), frames, cells, cols)
@@ -395,7 +402,7 @@
     stats, affine, half = call(
         stats_body,
         [
-            shape((W, 2, channels), F32),
+            shape((2, channels), F32),
             shape((2, channels), F32),
             shape((R // 2, channels), BF16),
         ],
@@ -412,7 +419,14 @@
     firsts = [send(half, lambda d, w: ((d + s) % D, w)) for s in range(1, D)]
 
     halo = lax.ppermute(cot, "wide", [(w + 1, w) for w in range(W - 1)])
-    stats = lax.all_to_all(stats, "wide", split_axis=0, concat_axis=0, tiled=True)
+    steps = [1, 2] if W % 4 == 0 else [1]
+    for step in steps:
+        other = send(stats, lambda d, w: (d, w ^ step))
+        stats = call(add_body, shape((2, channels), F32))(stats, other)
+    block = 2 * steps[-1]
+    stats = [stats] + [
+        send(stats, lambda d, w: (d, (w + block * s) % W)) for s in range(1, W // block)
+    ]
     firsts, stats, halo, cot_t = lax.optimization_barrier((firsts, stats, halo, cot_t))
     pieces = []
     for first in firsts:
@@ -426,13 +440,13 @@
         terms_s = [shape((channels, D * shard_s), BF16)]
         terms_t = [shape((channels, D * shard_t), BF16), shape((D * W, 2, channels), F32)]
     pad = pltpu.VMEM((3, frames, cells + 2 * cols, channels), BF16)
-    gsa, *grads_s = call(
+    gsa, stats, *grads_s = call(
         functools.partial(first_body, sizes),
-        [shape((rows, channels), BF16)] + terms_s,
+        [shape((rows, channels), BF16), shape((2, channels), F32)] + terms_s,
         [pltpu.VMEM((D * shard_t, channels), BF16), pad, pltpu.VMEM((channels, rows), BF16)],
         flops=2 * 12 * rows * channels * channels,
         moved=3_000_000,
-    )(lat, cot, halo, stats, affine, w_temporal, *pieces)
+    )(lat, cot, halo, affine, w_temporal, *pieces, *stats)
     spatial, grad, *grads_t = call(
         functools.partial(second_body, sizes),
         [shape((rows, channels), BF16), shape((rows, channels), F32)] + terms_t,

time: 49.5 us -> 51.1 us (1.032)
  starting transfers between devices: 21.2 us -> 23 us
    ppermute x10 -> x15, starting transfers between devices: 11.8 us -> 20.3 us  [send(): return lax.ppermute(value, ('dp', 'wide'), over_all(moves))]
    all_to_all x1 -> x0, starting transfers between devices: 6.68 us -> none  [local(): lax.all_to_all(stats, 'wide', split_axis=0, concat_axis=0, tiled=True)]
    all_to_all x1 -> x0, waiting for transfers between devices: 6.5 us -> none  [local(): lax.all_to_all(stats, 'wide', split_axis=0, concat_axis=0, tiled=True)]
    ppermute x10 -> x15, waiting for transfers between devices: 13.3 us -> 19.7 us  [send(): return lax.ppermute(value, ('dp', 'wide'), over_all(moves))]
    pallas_call x8 -> x10, Pallas kernels: 7.42 us -> 7.38 us  [run(): pl.pallas_call(body, out_shape=out_shapes, in_specs=in_specs or [VMEM] *...]
  transfers between devices with their start and end apart: 13 -> 17, of which waited for: 8 -> 12; matrix products, arithmetic and copies ran while one was open for 0% -> 0% of each run, Pallas kernels for 6% -> 6%
where the time goes in v10:
time: 51.1 us; the launch traced here: 50.9 us
  starting transfers between devices  23 us (45%)
  waiting for transfers between devices  19.7 us (39%)
  Pallas kernels  7.38 us (14%)
  between operations  0.75 us (1%)
    ppermute x15, starting transfers between devices, send(): return lax.ppermute(value, ('dp', 'wide'), over_all(moves))  20.3 us
    ppermute x15, waiting for transfers between devices, send(): return lax.ppermute(value, ('dp', 'wide'), over_all(moves))  19.7 us
    pallas_call x10, Pallas kernels, run(): pl.pallas_call(body, out_shape=out_shapes, in_specs=in_specs or [VMEM] *...  7.38 us
    ppermute x1, starting transfers between devices, local(): before = lax.ppermute(spatial, 'wide', [(w, w + 1) for w in range(W - 1)])  1.42 us
    ppermute x1, starting transfers between devices, local(): halo = lax.ppermute(cot, 'wide', [(w + 1, w) for w in range(W - 1)])  1.28 us
  transfers between devices with their start and end apart: 17, of which 12 were waited for; matrix products, arithmetic and copies ran while one was open for 0% of the time, Pallas kernels for 6%

profile of v10, /device:TPU:0, one launch (start us, length us, event | category | flops | bytes accessed | tf_op | source)
XLA Modules:
  0.0 50.9 jit_solution(984147745233250624)
XLA Ops:
  0.7 1.9 %shard_map.101 = (f32[2,256]{1,0:T(2,128)}, f32[2,256]{1,0:T(2,128)}, bf16[768,256]{1,0:T(8,128)(2,1)}) custom-call(bf16[256,256]{1,0:T(8,128)(2,1)} %bitcast.12, f32[1,256]{1,0:T(1,128)} %bitcast.26, f32[1,256]{1,0:T(1,128)} %bitcast.27, bf16[1152,256]{1,0:T(8,128)(2,1)} %ws_ref.3, bf16[384,256]{1,0:T(8,128)(2,1)} %wt_ref.5), custom_call_target="tpu_custom_call" | custom-call | tf_op jit(solution)/shard_map/pallas_call | solution.py:26
  2.6 3.0 %collective-permute-start = (bf16[768,256]{1,0:T(8,128)(2,1)}, bf16[768,256]{1,0:T(8,128)(2,1)S(1)}, u32[]{:S(2)}, u32[]{:S(2)}) collective-permute-start(bf16[768,256]{1,0:T(8,128)(2,1)} %get-tuple-element.35), channel_id=1, source_target_pairs={{0,16},{1,17},{2,18},{3,19},{4,20},{5,21},{6,22},{7,23},{8,24},{9,... | collective-permute-start | bytes 1179656 | tf_op jit(solution)/shard_map/ppermute | solution.py:399
  5.6 1.3 %collective-permute-start.6 = (bf16[256,256]{1,0:T(8,128)(2,1)S(1)}, bf16[256,256]{1,0:T(8,128)(2,1)S(1)}, u32[]{:S(2)}, u32[]{:S(2)}) collective-permute-start(bf16[256,256]{1,0:T(8,128)(2,1)S(1)} %bitcast.19), channel_id=1, source_target_pairs={{1,0},{2,1},{3,2},{4,3},{5,4},{6,5},{7,6},{8,7},{9,8},{10,9},{11,1... | collective-permute-start | bytes 393224 | tf_op jit(solution)/shard_map/ppermute | solution.py:421
  6.9 1.2 %collective-permute-start.1 = (f32[2,256]{1,0:T(2,128)S(1)}, f32[2,256]{1,0:T(2,128)S(1)}, u32[]{:S(2)}, u32[]{:S(2)}) collective-permute-start(f32[2,256]{1,0:T(2,128)S(1)} %copy-done.5), channel_id=1, source_target_pairs={{0,1},{1,0},{2,3},{3,2},{4,5},{5,4},{6,7},{7,6},{8,9},{9,8},{10,11... | collective-permute-start | bytes 6152 | tf_op jit(solution)/shard_map/ppermute | solution.py:399
  8.1 0.8 %collective-permute-done.1.right_ref = f32[2,256]{1,0:T(2,128)S(1)} collective-permute-done((f32[2,256]{1,0:T(2,128)S(1)}, f32[2,256]{1,0:T(2,128)S(1)}, u32[]{:S(2)}, u32[]{:S(2)}) %collective-permute-start.1) | collective-permute-done | bytes 2080 | tf_op jit(solution)/shard_map/ppermute | solution.py:399
  8.9 1.5 %collective-permute-start.2 = (f32[2,256]{1,0:T(2,128)S(1)}, f32[2,256]{1,0:T(2,128)S(1)}, u32[]{:S(2)}, u32[]{:S(2)}) collective-permute-start(f32[2,256]{1,0:T(2,128)S(1)} %shard_map.102.left_ref), channel_id=1, source_target_pairs={{0,2},{1,3},{2,0},{3,1},{4,6},{5,7},{6,4},{7,5},{8,10},{9,11},{10,... | collective-permute-start | bytes 6152 | tf_op jit(solution)/shard_map/ppermute | solution.py:399
  10.4 2.1 %collective-permute-done.2.right_ref = f32[2,256]{1,0:T(2,128)S(1)} collective-permute-done((f32[2,256]{1,0:T(2,128)S(1)}, f32[2,256]{1,0:T(2,128)S(1)}, u32[]{:S(2)}, u32[]{:S(2)}) %collective-permute-start.2) | collective-permute-done | bytes 2080 | tf_op jit(solution)/shard_map/ppermute | solution.py:399
  12.5 4.0 %collective-permute-start.5 = (f32[2,256]{1,0:T(2,128)S(1)}, f32[2,256]{1,0:T(2,128)S(1)}, u32[]{:S(2)}, u32[]{:S(2)}) collective-permute-start(f32[2,256]{1,0:T(2,128)S(1)} %shard_map.103.rest_2_), channel_id=1, source_target_pairs={{0,12},{1,13},{2,14},{3,15},{4,0},{5,1},{6,2},{7,3},{8,4},{9,5},{1... | collective-permute-start | bytes 6152 | tf_op jit(solution)/shard_map/ppermute | solution.py:399
  16.6 1.0 %collective-permute-start.3 = (f32[2,256]{1,0:T(2,128)S(1)}, f32[2,256]{1,0:T(2,128)S(1)}, u32[]{:S(2)}, u32[]{:S(2)}) collective-permute-start(f32[2,256]{1,0:T(2,128)S(1)} %shard_map.103.rest_2_), channel_id=1, source_target_pairs={{0,4},{1,5},{2,6},{3,7},{4,8},{5,9},{6,10},{7,11},{8,12},{9,13},{1... | collective-permute-start | bytes 6152 | tf_op jit(solution)/shard_map/ppermute | solution.py:399
  17.9 3.2 %collective-permute-done.4.rest_4_ = f32[2,256]{1,0:T(2,128)S(1)} collective-permute-done((f32[2,256]{1,0:T(2,128)S(1)}, f32[2,256]{1,0:T(2,128)S(1)}, u32[]{:S(2)}, u32[]{:S(2)}) %collective-permute-start.4) | collective-permute-done | bytes 2080 | tf_op jit(solution)/shard_map/ppermute | solution.py:399
  21.0 0.9 %collective-permute-done.3.rest_3_ = f32[2,256]{1,0:T(2,128)S(1)} collective-permute-done((f32[2,256]{1,0:T(2,128)S(1)}, f32[2,256]{1,0:T(2,128)S(1)}, u32[]{:S(2)}, u32[]{:S(2)}) %collective-permute-start.3) | collective-permute-done | bytes 2080 | tf_op jit(solution)/shard_map/ppermute | solution.py:399
  22.0 1.7 %collective-permute-done.7.rest_1_ = bf16[768,256]{1,0:T(8,128)(2,1)S(1)} collective-permute-done((bf16[768,256]{1,0:T(8,128)(2,1)S(1)}, bf16[768,256]{1,0:T(8,128)(2,1)S(1)}, u32[]{:S(2)}, u32[]{:S(2)}) %collective-permute-start.7) | collective-permute-done | bytes 393248 | tf_op jit(solution)/shard_map/ppermute | solution.py:399
  23.7 1.0 %shard_map.105 = (bf16[256,256]{1,0:T(8,128)(2,1)S(1)}, f32[2,256]{1,0:T(2,128)S(1)}, bf16[2,128,1152]{2,1,0:T(8,128)(2,1)S(1)}, bf16[2,128,1152]{2,1,0:T(8,128)(2,1)S(1)}) custom-call(bf16[256,256]{1,0:T(8,128)(2,1)S(1)} %bitcast.13, bf16[256,256]{1,0:T(8,128)(2,1)S(1)} %bitcast.21, bf16[256,256]{1,0:T(8,128)(2,1)S(1)} %collective-permute-done.6.halo_ref, ...), custom_call_target="tpu_custom_call" | custom-call | flops 402653184 | bytes 3000000 | tf_op jit(solution)/shard_map/pallas_call | solution.py:26
  24.7 0.2 collective-permute-start.9
  24.9 1.9 %shard_map.106 = (bf16[256,256]{1,0:T(8,128)(2,1)S(1)}, f32[256,256]{1,0:T(8,128)S(1)}, bf16[2,128,512]{2,1,0:T(8,128)(2,1)S(1)}, bf16[2,128,512]{2,1,0:T(8,128)(2,1)S(1)}) custom-call(bf16[256,256]{1,0:T(8,128)(2,1)S(1)} %bitcast.14, bf16[256,256]{1,0:T(8,128)(2,1)S(1)} %shard_map.104.cot_t_ref, bf16[256,256]{1,0:T(8,128)(2,1)S(1)} %collective-permute-done.6.halo_ref, ...), custom_call_target="tpu_custom_call" | custom-call | flops 704643072 | bytes 3000000 | tf_op jit(solution)/shard_map/pallas_call | solution.py:26
  26.8 0.5 collective-permute-start.10
  27.3 1.2 %collective-permute-done.10 = bf16[2,128,512]{2,1,0:T(8,128)(2,1)S(1)} collective-permute-done((bf16[2,128,512]{2,1,0:T(8,128)(2,1)S(1)}, bf16[2,128,512]{2,1,0:T(8,128)(2,1)S(1)}, u32[]{:S(2)}, u32[]{:S(2)}) %collective-permute-start.10) | collective-permute-done | bytes 262176 | tf_op jit(solution)/shard_map/ppermute | solution.py:399
  28.5 0.2 shard_map.108
  28.7 1.2 %collective-permute-start.11 = (bf16[4,16,1664]{2,1,0:T(8,128)(2,1)S(1)}, bf16[4,16,1664]{2,1,0:T(8,128)(2,1)S(1)}, u32[]{:S(2)}, u32[]{:S(2)}) collective-permute-start(bf16[4,16,1664]{2,1,0:T(8,128)(2,1)S(1)} %get-tuple-element.53), channel_id=1, source_target_pairs={{0,2},{1,3},{2,0},{3,1},{4,6},{5,7},{6,4},{7,5},{8,10},{9,11},{10,... | collective-permute-start | bytes 638984 | tf_op jit(solution)/shard_map/ppermute | solution.py:399
  29.9 0.5 %collective-permute-start.12 = (bf16[4,16,1664]{2,1,0:T(8,128)(2,1)S(1)}, bf16[4,16,1664]{2,1,0:T(8,128)(2,1)S(1)}, u32[]{:S(2)}, u32[]{:S(2)}) collective-permute-start(bf16[4,16,1664]{2,1,0:T(8,128)(2,1)S(1)} %get-tuple-element.54), channel_id=1, source_target_pairs={{0,16},{1,17},{2,18},{3,19},{4,20},{5,21},{6,22},{7,23},{8,24},{9,... | collective-permute-start | bytes 638984 | tf_op jit(solution)/shard_map/ppermute | solution.py:399
  30.4 1.8 %collective-permute-start.13 = (bf16[4,16,1664]{2,1,0:T(8,128)(2,1)S(1)}, bf16[4,16,1664]{2,1,0:T(8,128)(2,1)S(1)}, u32[]{:S(2)}, u32[]{:S(2)}) collective-permute-start(bf16[4,16,1664]{2,1,0:T(8,128)(2,1)S(1)} %get-tuple-element.55), channel_id=1, source_target_pairs={{0,18},{1,19},{2,16},{3,17},{4,22},{5,23},{6,20},{7,21},{8,26},{9,... | collective-permute-start | bytes 638984 | tf_op jit(solution)/shard_map/ppermute | solution.py:399
  32.3 1.4 %collective-permute-start.8 = (bf16[256,256]{1,0:T(8,128)(2,1)S(1)}, bf16[256,256]{1,0:T(8,128)(2,1)S(1)}, u32[]{:S(2)}, u32[]{:S(2)}) collective-permute-start(bf16[256,256]{1,0:T(8,128)(2,1)S(1)} %get-tuple-element.47.spatial_ref), channel_id=1, source_target_pairs={{0,1},{1,2},{2,3},{3,4},{4,5},{5,6},{6,7},{7,8},{8,9},{9,10},{10,1... | collective-permute-start | bytes 393224 | tf_op jit(solution)/shard_map/ppermute | solution.py:462
  33.7 2.6 %collective-permute-done.11.refs_1_ = bf16[4,16,1664]{2,1,0:T(8,128)(2,1)S(1)} collective-permute-done((bf16[4,16,1664]{2,1,0:T(8,128)(2,1)S(1)}, bf16[4,16,1664]{2,1,0:T(8,128)(2,1)S(1)}, u32[]{:S(2)}, u32[]{:S(2)}) %collective-permute-start.11) | collective-permute-done | bytes 213024 | tf_op jit(solution)/shard_map/ppermute | solution.py:399
  36.3 1.7 %collective-permute-done.12.refs_2_ = bf16[4,16,1664]{2,1,0:T(8,128)(2,1)S(1)} collective-permute-done((bf16[4,16,1664]{2,1,0:T(8,128)(2,1)S(1)}, bf16[4,16,1664]{2,1,0:T(8,128)(2,1)S(1)}, u32[]{:S(2)}, u32[]{:S(2)}) %collective-permute-start.12) | collective-permute-done | bytes 213024 | tf_op jit(solution)/shard_map/ppermute | solution.py:399
  38.0 4.0 %collective-permute-done.13.refs_3_ = bf16[4,16,1664]{2,1,0:T(8,128)(2,1)S(1)} collective-permute-done((bf16[4,16,1664]{2,1,0:T(8,128)(2,1)S(1)}, bf16[4,16,1664]{2,1,0:T(8,128)(2,1)S(1)}, u32[]{:S(2)}, u32[]{:S(2)}) %collective-permute-start.13) | collective-permute-done | bytes 213024 | tf_op jit(solution)/shard_map/ppermute | solution.py:399
  42.1 0.7 %collective-permute-start.14 = (bf16[16,1664]{1,0:T(8,128)(2,1)S(1)}, bf16[16,1664]{1,0:T(8,128)(2,1)S(1)}, u32[]{:S(2)}, u32[]{:S(2)}) collective-permute-start(bf16[16,1664]{1,0:T(8,128)(2,1)S(1)} %get-tuple-element.57), channel_id=1, source_target_pairs={{0,4},{1,5},{2,6},{3,7},{4,8},{5,9},{6,10},{7,11},{8,12},{9,13},{1... | collective-permute-start | bytes 159752 | tf_op jit(solution)/shard_map/ppermute | solution.py:399
  42.8 1.8 %collective-permute-start.15 = (bf16[16,1664]{1,0:T(8,128)(2,1)S(1)}, bf16[16,1664]{1,0:T(8,128)(2,1)S(1)}, u32[]{:S(2)}, u32[]{:S(2)}) collective-permute-start(bf16[16,1664]{1,0:T(8,128)(2,1)S(1)} %get-tuple-element.58), channel_id=1, source_target_pairs={{0,8},{1,9},{2,10},{3,11},{4,12},{5,13},{6,14},{7,15},{8,0},{9,1},... | collective-permute-start | bytes 159752 | tf_op jit(solution)/shard_map/ppermute | solution.py:399
  44.6 2.8 %collective-permute-start.16 = (bf16[16,1664]{1,0:T(8,128)(2,1)S(1)}, bf16[16,1664]{1,0:T(8,128)(2,1)S(1)}, u32[]{:S(2)}, u32[]{:S(2)}) collective-permute-start(bf16[16,1664]{1,0:T(8,128)(2,1)S(1)} %get-tuple-element.59), channel_id=1, source_target_pairs={{0,12},{1,13},{2,14},{3,15},{4,0},{5,1},{6,2},{7,3},{8,4},{9,5},{1... | collective-permute-start | bytes 159752 | tf_op jit(solution)/shard_map/ppermute | solution.py:399
  47.5 1.0 %shard_map.107 = bf16[256,256]{1,0:T(8,128)(2,1)} custom-call(bf16[256,256]{1,0:T(8,128)(2,1)S(1)} %bitcast.15, bf16[256,256]{1,0:T(8,128)(2,1)S(1)} %get-tuple-element.47.spatial_ref, bf16[256,256]{1,0:T(8,128)(2,1)S(1)} %collective-permute-done.8.before_ref, bf16[384,256]{1,0:T(8,128)(2,1)S(1)} %copy-done.1, ...), custom_call_target="tpu_custom_call" | custom-call | flops 100663296 | bytes 1000000 | tf_op jit(solution)/shard_map/pallas_call | solution.py:26
  48.5 0.2 collective-permute-done.14.refs_1_
  48.6 1.2 %collective-permute-done.15.refs_2_ = bf16[16,1664]{1,0:T(8,128)(2,1)S(1)} collective-permute-done((bf16[16,1664]{1,0:T(8,128)(2,1)S(1)}, bf16[16,1664]{1,0:T(8,128)(2,1)S(1)}, u32[]{:S(2)}, u32[]{:S(2)}) %collective-permute-start.15) | collective-permute-done | bytes 53280 | tf_op jit(solution)/shard_map/ppermute | solution.py:399
  49.8 1.1 %shard_map.110 = (f32[16,1152]{1,0:T(8,128)}, f32[16,384]{1,0:T(8,128)}, f32[2,16]{1,0:T(2,128)}, bf16[256,256]{1,0:T(8,128)(2,1)}) custom-call(bf16[16,1664]{1,0:T(8,128)(2,1)S(1)} %get-tuple-element.56.refs_0_, bf16[16,1664]{1,0:T(8,128)(2,1)S(1)} %collective-permute-done.14.refs_1_, bf16[16,1664]{1,0:T(8,128)(2,1)S(1)} %collective-permute-done.15.refs_2_, ...), custom_call_target="tpu_custom_call" | custom-call | bytes 1000000 | tf_op jit(solution)/shard_map/pallas_call | solution.py:26
  (24 shorter events, 0.5 us)
Async XLA Ops:
  0.6 5.0 %copy-start.3 = (bf16[1,2,8,16,256]{4,3,2,1,0:T(8,128)(2,1)S(1)}, bf16[1,2,8,16,256]{4,3,2,1,0:T(8,128)(2,1)}, u32[]{:S(2)}) copy-start(bf16[1,2,8,16,256]{4,3,2,1,0:T(8,128)(2,1)} %param.7) | copy-start | bytes 393220
  0.6 23.0 %copy-start.1 = (bf16[384,256]{1,0:T(8,128)(2,1)S(1)}, bf16[384,256]{1,0:T(8,128)(2,1)}, u32[]{:S(2)}) copy-start(bf16[384,256]{1,0:T(8,128)(2,1)} %wt_ref.5) | copy-start | bytes 589828
  2.6 4.3 %copy-start.5 = (f32[2,256]{1,0:T(2,128)S(1)}, f32[2,256]{1,0:T(2,128)}, u32[]{:S(2)}) copy-start(f32[2,256]{1,0:T(2,128)} %get-tuple-element.36.left_ref) | copy-start | bytes 6148
  2.6 19.3 %collective-permute-start = (bf16[768,256]{1,0:T(8,128)(2,1)}, bf16[768,256]{1,0:T(8,128)(2,1)S(1)}, u32[]{:S(2)}, u32[]{:S(2)}) collective-permute-start(bf16[768,256]{1,0:T(8,128)(2,1)} %get-tuple-element.35), channel_id=1, source_target_pairs={{0,16},{1,17},{2,18},{3,19},{4,20},{5,21},{6,22},{7,23},{8,24},{9,... | collective-permute-start | bytes 1179656 | tf_op jit(solution)/shard_map/ppermute | solution.py:399
  5.6 16.3 %collective-permute-start.6 = (bf16[256,256]{1,0:T(8,128)(2,1)S(1)}, bf16[256,256]{1,0:T(8,128)(2,1)S(1)}, u32[]{:S(2)}, u32[]{:S(2)}) collective-permute-start(bf16[256,256]{1,0:T(8,128)(2,1)S(1)} %bitcast.19), channel_id=1, source_target_pairs={{1,0},{2,1},{3,2},{4,3},{5,4},{6,5},{7,6},{8,7},{9,8},{10,9},{11,1... | collective-permute-start | bytes 393224 | tf_op jit(solution)/shard_map/ppermute | solution.py:421
  6.9 2.0 %collective-permute-start.1 = (f32[2,256]{1,0:T(2,128)S(1)}, f32[2,256]{1,0:T(2,128)S(1)}, u32[]{:S(2)}, u32[]{:S(2)}) collective-permute-start(f32[2,256]{1,0:T(2,128)S(1)} %copy-done.5), channel_id=1, source_target_pairs={{0,1},{1,0},{2,3},{3,2},{4,5},{5,4},{6,7},{7,6},{8,9},{9,8},{10,11... | collective-permute-start | bytes 6152 | tf_op jit(solution)/shard_map/ppermute | solution.py:399
  8.9 3.6 %collective-permute-start.2 = (f32[2,256]{1,0:T(2,128)S(1)}, f32[2,256]{1,0:T(2,128)S(1)}, u32[]{:S(2)}, u32[]{:S(2)}) collective-permute-start(f32[2,256]{1,0:T(2,128)S(1)} %shard_map.102.left_ref), channel_id=1, source_target_pairs={{0,2},{1,3},{2,0},{3,1},{4,6},{5,7},{6,4},{7,5},{8,10},{9,11},{10,... | collective-permute-start | bytes 6152 | tf_op jit(solution)/shard_map/ppermute | solution.py:399
  12.5 11.2 %copy-start = (bf16[1,2,8,16,256]{4,3,2,1,0:T(8,128)(2,1)S(1)}, bf16[1,2,8,16,256]{4,3,2,1,0:T(8,128)(2,1)}, u32[]{:S(2)}) copy-start(bf16[1,2,8,16,256]{4,3,2,1,0:T(8,128)(2,1)} %param.6) | copy-start | bytes 393220
  12.5 11.2 %copy-start.4 = (f32[2,256]{1,0:T(2,128)S(1)}, f32[2,256]{1,0:T(2,128)}, u32[]{:S(2)}) copy-start(f32[2,256]{1,0:T(2,128)} %get-tuple-element.39.affine_ref.refs_7_) | copy-start | bytes 6148
  12.5 5.3 %collective-permute-start.5 = (f32[2,256]{1,0:T(2,128)S(1)}, f32[2,256]{1,0:T(2,128)S(1)}, u32[]{:S(2)}, u32[]{:S(2)}) collective-permute-start(f32[2,256]{1,0:T(2,128)S(1)} %shard_map.103.rest_2_), channel_id=1, source_target_pairs={{0,12},{1,13},{2,14},{3,15},{4,0},{5,1},{6,2},{7,3},{8,4},{9,5},{1... | collective-permute-start | bytes 6152 | tf_op jit(solution)/shard_map/ppermute | solution.py:399
  16.6 4.5 %collective-permute-start.4 = (f32[2,256]{1,0:T(2,128)S(1)}, f32[2,256]{1,0:T(2,128)S(1)}, u32[]{:S(2)}, u32[]{:S(2)}) collective-permute-start(f32[2,256]{1,0:T(2,128)S(1)} %shard_map.103.rest_2_), channel_id=1, source_target_pairs={{0,8},{1,9},{2,10},{3,11},{4,12},{5,13},{6,14},{7,15},{8,0},{9,1},... | collective-permute-start | bytes 6152 | tf_op jit(solution)/shard_map/ppermute | solution.py:399
  16.6 5.4 %collective-permute-start.3 = (f32[2,256]{1,0:T(2,128)S(1)}, f32[2,256]{1,0:T(2,128)S(1)}, u32[]{:S(2)}, u32[]{:S(2)}) collective-permute-start(f32[2,256]{1,0:T(2,128)S(1)} %shard_map.103.rest_2_), channel_id=1, source_target_pairs={{0,4},{1,5},{2,6},{3,7},{4,8},{5,9},{6,10},{7,11},{8,12},{9,13},{1... | collective-permute-start | bytes 6152 | tf_op jit(solution)/shard_map/ppermute | solution.py:399
  22.0 1.7 %collective-permute-start.7 = (bf16[768,256]{1,0:T(8,128)(2,1)S(1)}, bf16[768,256]{1,0:T(8,128)(2,1)S(1)}, u32[]{:S(2)}, u32[]{:S(2)}) collective-permute-start(bf16[768,256]{1,0:T(8,128)(2,1)S(1)} %collective-permute-done.rest_0_), channel_id=1, source_target_pairs={{0,1},{1,0},{2,3},{3,2},{4,5},{5,4},{6,7},{7,6},{8,9},{9,8},{10,11... | collective-permute-start | bytes 1179656 | tf_op jit(solution)/shard_map/ppermute | solution.py:399
  23.7 1.2 %copy-start.2 = (bf16[1152,256]{1,0:T(8,128)(2,1)S(1)}, bf16[1152,256]{1,0:T(8,128)(2,1)}, u32[]{:S(2)}) copy-start(bf16[1152,256]{1,0:T(8,128)(2,1)} %ws_ref.3) | copy-start | bytes 1769476
  24.7 3.7 %collective-permute-start.9 = (bf16[2,128,1152]{2,1,0:T(8,128)(2,1)S(1)}, bf16[2,128,1152]{2,1,0:T(8,128)(2,1)S(1)}, u32[]{:S(2)}, u32[]{:S(2)}) collective-permute-start(bf16[2,128,1152]{2,1,0:T(8,128)(2,1)S(1)} %get-tuple-element.49), channel_id=1, source_target_pairs={{0,1},{1,0},{2,3},{3,2},{4,5},{5,4},{6,7},{7,6},{8,9},{9,8},{10,11... | collective-permute-start | bytes 1769480 | tf_op jit(solution)/shard_map/ppermute | solution.py:399
  26.8 1.6 %collective-permute-start.10 = (bf16[2,128,512]{2,1,0:T(8,128)(2,1)S(1)}, bf16[2,128,512]{2,1,0:T(8,128)(2,1)S(1)}, u32[]{:S(2)}, u32[]{:S(2)}) collective-permute-start(bf16[2,128,512]{2,1,0:T(8,128)(2,1)S(1)} %get-tuple-element.51), channel_id=1, source_target_pairs={{0,1},{1,0},{2,3},{3,2},{4,5},{5,4},{6,7},{7,6},{8,9},{9,8},{10,11... | collective-permute-start | bytes 786440 | tf_op jit(solution)/shard_map/ppermute | solution.py:399
  28.7 7.6 %collective-permute-start.11 = (bf16[4,16,1664]{2,1,0:T(8,128)(2,1)S(1)}, bf16[4,16,1664]{2,1,0:T(8,128)(2,1)S(1)}, u32[]{:S(2)}, u32[]{:S(2)}) collective-permute-start(bf16[4,16,1664]{2,1,0:T(8,128)(2,1)S(1)} %get-tuple-element.53), channel_id=1, source_target_pairs={{0,2},{1,3},{2,0},{3,1},{4,6},{5,7},{6,4},{7,5},{8,10},{9,11},{10,... | collective-permute-start | bytes 638984 | tf_op jit(solution)/shard_map/ppermute | solution.py:399
  29.9 8.1 %collective-permute-start.12 = (bf16[4,16,1664]{2,1,0:T(8,128)(2,1)S(1)}, bf16[4,16,1664]{2,1,0:T(8,128)(2,1)S(1)}, u32[]{:S(2)}, u32[]{:S(2)}) collective-permute-start(bf16[4,16,1664]{2,1,0:T(8,128)(2,1)S(1)} %get-tuple-element.54), channel_id=1, source_target_pairs={{0,16},{1,17},{2,18},{3,19},{4,20},{5,21},{6,22},{7,23},{8,24},{9,... | collective-permute-start | bytes 638984 | tf_op jit(solution)/shard_map/ppermute | solution.py:399
  30.4 11.6 %collective-permute-start.13 = (bf16[4,16,1664]{2,1,0:T(8,128)(2,1)S(1)}, bf16[4,16,1664]{2,1,0:T(8,128)(2,1)S(1)}, u32[]{:S(2)}, u32[]{:S(2)}) collective-permute-start(bf16[4,16,1664]{2,1,0:T(8,128)(2,1)S(1)} %get-tuple-element.55), channel_id=1, source_target_pairs={{0,18},{1,19},{2,16},{3,17},{4,22},{5,23},{6,20},{7,21},{8,26},{9,... | collective-permute-start | bytes 638984 | tf_op jit(solution)/shard_map/ppermute | solution.py:399
  32.3 15.2 %collective-permute-start.8 = (bf16[256,256]{1,0:T(8,128)(2,1)S(1)}, bf16[256,256]{1,0:T(8,128)(2,1)S(1)}, u32[]{:S(2)}, u32[]{:S(2)}) collective-permute-start(bf16[256,256]{1,0:T(8,128)(2,1)S(1)} %get-tuple-element.47.spatial_ref), channel_id=1, source_target_pairs={{0,1},{1,2},{2,3},{3,4},{4,5},{5,6},{6,7},{7,8},{8,9},{9,10},{10,1... | collective-permute-start | bytes 393224 | tf_op jit(solution)/shard_map/ppermute | solution.py:462
  42.1 6.5 %collective-permute-start.14 = (bf16[16,1664]{1,0:T(8,128)(2,1)S(1)}, bf16[16,1664]{1,0:T(8,128)(2,1)S(1)}, u32[]{:S(2)}, u32[]{:S(2)}) collective-permute-start(bf16[16,1664]{1,0:T(8,128)(2,1)S(1)} %get-tuple-element.57), channel_id=1, source_target_pairs={{0,4},{1,5},{2,6},{3,7},{4,8},{5,9},{6,10},{7,11},{8,12},{9,13},{1... | collective-permute-start | bytes 159752 | tf_op jit(solution)/shard_map/ppermute | solution.py:399
  42.8 7.0 %collective-permute-start.15 = (bf16[16,1664]{1,0:T(8,128)(2,1)S(1)}, bf16[16,1664]{1,0:T(8,128)(2,1)S(1)}, u32[]{:S(2)}, u32[]{:S(2)}) collective-permute-start(bf16[16,1664]{1,0:T(8,128)(2,1)S(1)} %get-tuple-element.58), channel_id=1, source_target_pairs={{0,8},{1,9},{2,10},{3,11},{4,12},{5,13},{6,14},{7,15},{8,0},{9,1},... | collective-permute-start | bytes 159752 | tf_op jit(solution)/shard_map/ppermute | solution.py:399
  44.6 5.2 %collective-permute-start.16 = (bf16[16,1664]{1,0:T(8,128)(2,1)S(1)}, bf16[16,1664]{1,0:T(8,128)(2,1)S(1)}, u32[]{:S(2)}, u32[]{:S(2)}) collective-permute-start(bf16[16,1664]{1,0:T(8,128)(2,1)S(1)} %get-tuple-element.59), channel_id=1, source_target_pairs={{0,12},{1,13},{2,14},{3,15},{4,0},{5,1},{6,2},{7,3},{8,4},{9,5},{1... | collective-permute-start | bytes 159752 | tf_op jit(solution)/shard_map/ppermute | solution.py:399

commit v11 on v6

--- a/solution.py
+++ b/solution.py
@@ -56,25 +56,27 @@
     )
 
 
-def stats_body(lat_ref, gain_ref, bias_ref, ws_ref, wt_ref, out_ref, affine_ref, half_ref, *scratch):
+def stats_body(lat_ref, gain_ref, bias_ref, ws_ref, wt_ref, out_ref, half_ref, *scratch):
     lat_here, gain_here, bias_here, sems = scratch
     core = lax.rem(lax.axis_index("wide"), 2)
-    moves, place = [(lat_ref, lat_here), (gain_ref, gain_here), (bias_ref, bias_here)], 0
-    for source in (ws_ref, wt_ref):
-        half = source.shape[0] // 2
-        start = pl.multiple_of(core * half, 16)
-        moves.append((source.at[pl.ds(start, half)], half_ref.at[pl.ds(place, half)]))
-        place += half
+    moves = [(lat_ref, lat_here), (gain_ref, gain_here), (bias_ref, bias_here)]
+    half = ws_ref.shape[0] // 2
+    start = pl.multiple_of(core * half, 16)
+    moves.append((ws_ref.at[pl.ds(start, half)], half_ref.at[pl.ds(0, half)]))
+    moves.append((wt_ref, half_ref.at[pl.ds(half, wt_ref.shape[0])]))
     copies = [pltpu.make_async_copy(*move, sems.at[at]) for at, move in enumerate(moves)]
     for copy in copies:
         copy.start()
     for copy in copies[:3]:
         copy.wait()
-    affine_ref[0:1] = gain_here[...]
-    affine_ref[1:2] = bias_here[...]
     x = lat_here[...].astype(F32)
+    sums = [jnp.sum(x, axis=0, keepdims=True), jnp.sum(x * x, axis=0, keepdims=True)]
     both = jnp.concatenate(
-        [jnp.sum(x, axis=0, keepdims=True), jnp.sum(x * x, axis=0, keepdims=True)], axis=0
+        [
+            jnp.concatenate([sums[0], gain_here[...]], axis=1),
+            jnp.concatenate([sums[1], bias_here[...]], axis=1),
+        ],
+        axis=0,
     )
     out_ref[...] = jnp.broadcast_to(both[None], out_ref.shape)
     for copy in copies[3:]:
@@ -85,7 +87,7 @@
     out_ref[...] = cot_ref[...].astype(F32).T.astype(BF16)
 
 
-def fill_weights(full, shard_ref, pieces, offset, D):
+def fill_spatial(full, shard_ref, pieces, D):
     d = lax.axis_index("dp")
     core = lax.rem(lax.axis_index("wide"), 2)
     n = shard_ref.shape[0]
@@ -96,11 +98,20 @@
         for which in range(2):
             holder = core if which == 0 else 1 - core
             start = pl.multiple_of(source * n + holder * half, 16)
-            full[pl.ds(start, half)] = pieces[2 * (s - 1) + which][offset : offset + half]
+            full[pl.ds(start, half)] = pieces[2 * (s - 1) + which][0:half]
+
+
+def fill_temporal(full, shard_ref, firsts, D):
+    d = lax.axis_index("dp")
+    n = shard_ref.shape[0]
+    full[pl.ds(pl.multiple_of(d * n, 16), n)] = shard_ref[...]
+    for s in range(1, D):
+        start = pl.multiple_of(lax.rem(d + D - s, D) * n, 16)
+        full[pl.ds(start, n)] = firsts[s - 1][firsts[s - 1].shape[0] - n :]
 
 
 def whiten(lat, stats, count, per_group):
-    total = group_total(jnp.sum(stats, axis=0), per_group) / count
+    total = group_total(jnp.sum(stats[:, :, : lat.shape[1]], axis=0), per_group) / count
     mean = total[0:1]
     inv_std = 1.0 / jnp.sqrt(total[1:2] - mean * mean + EPSILON)
     return (lat.astype(F32) - mean) * inv_std, inv_std
@@ -167,21 +178,26 @@
         send_ref[owner, :, place : place + 128] = low[half:, at : at + 128]
 
 
-def normalise(lat_ref, stats_ref, affine_ref, count, per_group):
+def affine_of(stats_ref):
+    return stats_ref[0, :, stats_ref.shape[2] // 2 :]
+
+
+def normalise(lat_ref, stats_ref, count, per_group):
     white, inv_std = whiten(lat_ref[...], stats_ref[...], count, per_group)
-    normed = white * affine_ref[0:1] + affine_ref[1:2]
+    affine = affine_of(stats_ref)
+    normed = white * affine[0:1] + affine[1:2]
     return white, normed, jax.nn.sigmoid(normed)
 
 
-def first_body(sizes, lat_ref, cot_ref, halo_ref, stats_ref, affine_ref, wt_ref, *rest):
+def first_body(sizes, lat_ref, cot_ref, halo_ref, stats_ref, wt_ref, *rest):
     D, W, frames, cells, cols, count, per_group, aligned = sizes
-    pieces, rest = rest[: 2 * (D - 1)], rest[2 * (D - 1) :]
+    firsts, rest = rest[: D - 1], rest[D - 1 :]
     full_wt, act_pad, gsa_t = rest[-3:]
-    gsa_ref, keep_ref = rest[:2]
-    send_ref = rest[2] if aligned else None
+    gsa_ref, seen_ref, keep_ref = rest[:3]
+    send_ref = rest[3] if aligned else None
     channels = lat_ref.shape[1]
     core = lax.rem(lax.axis_index("wide"), 2)
-    fill_weights(full_wt, wt_ref, pieces, pieces[0].shape[0] - wt_ref.shape[0] // 2, D)
+    fill_temporal(full_wt, wt_ref, firsts, D)
     rows = frames * cells
     extended = jnp.concatenate([cot_ref[...], halo_ref[...]], axis=0)
     gsa = jnp.zeros((rows, channels), F32)
@@ -193,32 +209,32 @@
         )
     gsa_ref[...] = gsa.astype(BF16)
     gsa_t[...] = gsa.astype(BF16).astype(F32).T.astype(BF16)
-    _, normed, sig = normalise(lat_ref, stats_ref, affine_ref, count, per_group)
+    _, normed, sig = normalise(lat_ref, stats_ref, count, per_group)
     act = (normed * sig).astype(BF16).astype(F32)
     store_shifted(act_pad, act, frames, cells, cols)
     left = core_order(gsa_t, W, core) if aligned else gsa_t[...]
     shard = wt_ref.shape[0] * 3
     for dy in range(3):
         for dx in range(3):
+            at = (3 * dy + dx) * channels
             seen = window(act_pad, dy, dx, frames, cells, cols)
-            put(mm(left, seen), (3 * dy + dx) * channels, shard, keep_ref, send_ref)
+            seen_ref[:, at : at + channels] = seen
+            put(mm(left, seen), at, shard, keep_ref, send_ref)
 
 
 def second_body(
-    sizes, lat_ref, cot_t_ref, halo_ref, stats_ref, affine_ref, gsa_ref, ws_ref, *rest
+    sizes, lat_ref, cot_t_ref, halo_ref, stats_ref, gsa_ref, seen_ref, ws_ref, *rest
 ):
     D, W, frames, cells, cols, count, per_group, aligned = sizes
     pieces, rest = rest[: 2 * (D - 1)], rest[2 * (D - 1) :]
-    full_ws, act_pad, gsa_pad, cot_t = rest[-4:]
+    full_ws, side_ws, gsa_pad, gsa_seen, cot_t = rest[-5:]
     spatial_ref, grad_ref, keep_ref, other_ref = rest[:4]
     send_ref = other_ref if aligned else None
     channels = lat_ref.shape[1]
     core = lax.rem(lax.axis_index("wide"), 2)
-    fill_weights(full_ws, ws_ref, pieces, 0, D)
+    fill_spatial(full_ws, ws_ref, pieces, D)
     rows = frames * cells
-    white, normed, sig = normalise(lat_ref, stats_ref, affine_ref, count, per_group)
-    act = (normed * sig).astype(BF16).astype(F32)
-    store_shifted(act_pad, act, frames, cells, cols)
+    white, normed, sig = normalise(lat_ref, stats_ref, count, per_group)
     store_shifted(gsa_pad, gsa_ref[...].astype(F32), frames, cells, cols)
     cot_t[:, :rows] = cot_t_ref[...]
     for f in range(2):
@@ -226,25 +242,21 @@
             halo_ref[f * cells : (f + 1) * cells].astype(F32).T.astype(BF16)
         )
     left = core_order(cot_t, W, core) if aligned else cot_t[...]
-    out = jnp.zeros((rows, channels), F32)
-    for dy in range(3):
-        for dx in range(3):
-            tap = 3 * dy + dx
-            seen = window(act_pad, dy, dx, frames, cells, cols)
-            out += mm(seen, full_ws[tap * channels : (tap + 1) * channels])
-    spatial = out.astype(BF16)
+    spatial = mm(seen_ref[...], full_ws[...]).astype(BF16)
     spatial_ref[...] = spatial
     shard = ws_ref.shape[0] // 3
     for k in range(3):
         block = mm(left[:, k * cells : k * cells + rows], spatial)
         put(block, k * channels, shard, keep_ref, send_ref)
 
-    grad = jnp.zeros((rows, channels), F32)
     for dy in range(3):
         for dx in range(3):
-            tap = 3 * dy + dx
-            seen = window(gsa_pad, 2 - dy, 2 - dx, frames, cells, cols)
-            grad += mm(seen, full_ws[tap * channels : (tap + 1) * channels], NT)
+            at = (3 * dy + dx) * channels
+            gsa_seen[:, at : at + channels] = window(
+                gsa_pad, 2 - dy, 2 - dx, frames, cells, cols
+            )
+            side_ws[:, at : at + channels] = full_ws[at : at + channels]
+    grad = mm(gsa_seen[...], side_ws[...], NT)
     grad = grad * (sig * (1.0 + normed * (1.0 - sig)))
     grad_ref[...] = grad
     gain_term = jnp.sum(grad * white, axis=0, keepdims=True)
@@ -268,10 +280,10 @@
 
 def block_body(sizes, lat_ref, spatial_ref, before_ref, wt_ref, *rest):
     D, W, frames, cells, cols, count, per_group, aligned = sizes
-    pieces = rest[: 2 * (D - 1)]
-    block_ref, full_wt = rest[2 * (D - 1) :]
+    firsts = rest[: D - 1]
+    block_ref, full_wt = rest[D - 1 :]
     channels = lat_ref.shape[1]
-    fill_weights(full_wt, wt_ref, pieces, pieces[0].shape[0] - wt_ref.shape[0] // 2, D)
+    fill_temporal(full_wt, wt_ref, firsts, D)
     extended = jnp.concatenate([before_ref[...], spatial_ref[...]], axis=0)
     rows = frames * cells
     temporal = jnp.zeros((rows, channels), F32)
@@ -283,10 +295,10 @@
     block_ref[...] = (lat_ref[...].astype(F32) + temporal).astype(BF16)
 
 
-def latent_gradient(sizes, total, lat_ref, cot_ref, stats_ref, affine_ref, grad_ref):
+def latent_gradient(sizes, total, lat_ref, cot_ref, stats_ref, grad_ref):
     D, W, frames, cells, cols, count, per_group, aligned = sizes
     white, inv_std = whiten(lat_ref[...], stats_ref[...], count, per_group)
-    gain = affine_ref[0:1]
+    gain = affine_of(stats_ref)[0:1]
     means = group_total(total * gain, per_group) / count
     inner = inv_std * (grad_ref[...] * gain - means[1:2] - white * means[0:1])
     return (cot_ref[...].astype(F32) + inner).astype(BF16)
@@ -392,12 +404,11 @@
         return lax.ppermute(value, ("dp", "wide"), over_all(moves))
 
     R = shard_s + shard_t
-    stats, affine, half = call(
+    stats, half = call(
         stats_body,
         [
-            shape((W, 2, channels), F32),
-            shape((2, channels), F32),
-            shape((R // 2, channels), BF16),
+            shape((W, 2, 2 * channels), F32),
+            shape((shard_s // 2 + shard_t, channels), BF16),
         ],
         [
             pltpu.VMEM((rows, channels), BF16),
@@ -426,25 +437,27 @@
         terms_s = [shape((channels, D * shard_s), BF16)]
         terms_t = [shape((channels, D * shard_t), BF16), shape((D * W, 2, channels), F32)]
     pad = pltpu.VMEM((3, frames, cells + 2 * cols, channels), BF16)
-    gsa, *grads_s = call(
+    taps = D * shard_s
+    gsa, seen, *grads_s = call(
         functools.partial(first_body, sizes),
-        [shape((rows, channels), BF16)] + terms_s,
+        [shape((rows, channels), BF16), shape((rows, taps), BF16)] + terms_s,
         [pltpu.VMEM((D * shard_t, channels), BF16), pad, pltpu.VMEM((channels, rows), BF16)],
         flops=2 * 12 * rows * channels * channels,
         moved=3_000_000,
-    )(lat, cot, halo, stats, affine, w_temporal, *pieces)
+    )(lat, cot, halo, stats, w_temporal, *firsts)
     spatial, grad, *grads_t = call(
         functools.partial(second_body, sizes),
         [shape((rows, channels), BF16), shape((rows, channels), F32)] + terms_t,
         [
-            pltpu.VMEM((D * shard_s, channels), BF16),
+            pltpu.VMEM((taps, channels), BF16),
+            pltpu.VMEM((channels, taps), BF16),
             pad,
-            pad,
+            pltpu.VMEM((rows, taps), BF16),
             pltpu.VMEM((channels, rows + 2 * cells), BF16),
         ],
         flops=2 * 21 * rows * channels * channels,
         moved=3_000_000,
-    )(lat, cot_t, halo, stats, affine, gsa, w_spatial, *pieces)
+    )(lat, cot_t, halo, stats, gsa, seen, w_spatial, *pieces)
     before = lax.ppermute(spatial, "wide", [(w, w + 1) for w in range(W - 1)])
     block_out = call(
         functools.partial(block_body, sizes),
@@ -452,10 +465,10 @@
         [pltpu.VMEM((D * shard_t, channels), BF16)],
         flops=2 * 3 * rows * channels * channels,
         moved=1_000_000,
-    )(lat, spatial, before, w_temporal, *pieces)
+    )(lat, spatial, before, w_temporal, *firsts)
 
     width = channels // W
-    operands = (lat, cot, stats, affine, grad)
+    operands = (lat, cot, stats, grad)
     if aligned:
         Z = W // 4
 
@@ -469,7 +482,7 @@
         plane = call(
             plane_body, [shape((Z, width, R + ride), BF16)] * (2 * D), moved=3_000_000
         )(*pairs)
-        seen = [plane[0]] + [
+        parts = [plane[0]] + [
             send(plane[2 * a + b], lambda d, w: ((d + a) % D, w ^ (2 * b)))
             for a, b in ((0, 1), (1, 0), (1, 1))
         ]
@@ -477,7 +490,7 @@
             functools.partial(line_body, Z),
             [shape((width, R + ride), BF16)] * Z,
             moved=1_000_000,
-        )(*seen)
+        )(*parts)
         terms = [line[0]]
         for s in range(1, Z):
             terms.append(send(line[s], lambda d, w: (d, (w + 4 * s) % W)))

time: 49.5 us -> 48 us (0.970)
  waiting for transfers between devices: 19.8 us -> 17.8 us
  local copies, waits for them, and re-layouts: 0.03 us -> 0.92 us
    ppermute x10, waiting for transfers between devices: 13.3 us -> 11.9 us  [send(): return lax.ppermute(value, ('dp', 'wide'), over_all(moves))]
    unnamed x10, local copies, waits for them, and re-layouts: 0.03 us -> 0.92 us
    all_to_all x1, waiting for transfers between devices: 6.5 us -> 5.88 us  [local(): lax.all_to_all(stats, 'wide', split_axis=0, concat_axis=0, tiled=True)]
  transfers between devices with their start and end apart: 13 -> 13, of which waited for: 8 -> 8; matrix products, arithmetic and copies ran while one was open for 0% -> 0% of each run, Pallas kernels for 6% -> 8%
where the time goes in v11:
time: 48 us; the launch traced here: 47.7 us
  starting transfers between devices  21 us (44%)
  waiting for transfers between devices  17.8 us (37%)
  Pallas kernels  7.25 us (15%)
  local copies, waits for them, and re-layouts  0.92 us (2%)
  between operations  0.77 us (2%)
    ppermute x10, waiting for transfers between devices, send(): return lax.ppermute(value, ('dp', 'wide'), over_all(moves))  11.9 us
    ppermute x10, starting transfers between devices, send(): return lax.ppermute(value, ('dp', 'wide'), over_all(moves))  11.7 us
    pallas_call x8, Pallas kernels, run(): pl.pallas_call(body, out_shape=out_shapes, in_specs=in_specs or [VMEM] *...  7.25 us
    all_to_all x1, starting transfers between devices, local(): lax.all_to_all(stats, 'wide', split_axis=0, concat_axis=0, tiled=True)  6.69 us
    all_to_all x1, waiting for transfers between devices, local(): lax.all_to_all(stats, 'wide', split_axis=0, concat_axis=0, tiled=True)  5.88 us
    ppermute x1, starting transfers between devices, local(): before = lax.ppermute(spatial, 'wide', [(w, w + 1) for w in range(W - 1)])  1.29 us
    ppermute x1, starting transfers between devices, local(): halo = lax.ppermute(cot, 'wide', [(w + 1, w) for w in range(W - 1)])  1.28 us
  transfers between devices with their start and end apart: 13, of which 8 were waited for; matrix products, arithmetic and copies ran while one was open for 0% of the time, Pallas kernels for 8%

profile of v11, /device:TPU:0, one launch (start us, length us, event | category | flops | bytes accessed | tf_op | source)
XLA Modules:
  0.0 47.7 jit_solution(432132556546427580)
XLA Ops:
  0.7 0.0 copy-start.4
  0.7 2.1 %shard_map.101 = (f32[16,2,512]{2,1,0:T(2,128)}, bf16[960,256]{1,0:T(8,128)(2,1)}) custom-call(bf16[256,256]{1,0:T(8,128)(2,1)} %bitcast.12, f32[1,256]{1,0:T(1,128)} %bitcast.26, f32[1,256]{1,0:T(1,128)} %bitcast.27, bf16[1152,256]{1,0:T(8,128)(2,1)} %ws_ref.3, bf16[384,256]{1,0:T(8,128)(2,1)} %wt_ref.5), custom_call_target="tpu_custom_call" | custom-call | tf_op jit(solution)/shard_map/pallas_call | solution.py:26
  2.7 3.0 %collective-permute-start = (bf16[960,256]{1,0:T(8,128)(2,1)}, bf16[960,256]{1,0:T(8,128)(2,1)S(1)}, u32[]{:S(2)}, u32[]{:S(2)}) collective-permute-start(bf16[960,256]{1,0:T(8,128)(2,1)} %get-tuple-element.31), channel_id=1, source_target_pairs={{0,16},{1,17},{2,18},{3,19},{4,20},{5,21},{6,22},{7,23},{8,24},{9,... | collective-permute-start | bytes 1474568 | tf_op jit(solution)/shard_map/ppermute | solution.py:404
  5.7 1.3 %collective-permute-start.1 = (bf16[256,256]{1,0:T(8,128)(2,1)}, bf16[256,256]{1,0:T(8,128)(2,1)S(1)}, u32[]{:S(2)}, u32[]{:S(2)}) collective-permute-start(bf16[256,256]{1,0:T(8,128)(2,1)} %bitcast.19), channel_id=1, source_target_pairs={{1,0},{2,1},{3,2},{4,3},{5,4},{6,5},{7,6},{8,7},{9,8},{10,9},{11,1... | collective-permute-start | bytes 393224 | tf_op jit(solution)/shard_map/ppermute | solution.py:425
  7.0 6.7 %all-to-all-start = ((f32[16,2,512]{2,1,0:T(2,128)}), f32[16,2,512]{2,1,0:T(2,128)S(1)}, u32[]{:S(2)}, u32[]{:S(2)}) async-start(f32[16,2,512]{2,1,0:T(2,128)} %get-tuple-element.32), calls=%async_computation | async-start | bytes 131072 | tf_op jit(solution)/shard_map/all_to_all | solution.py:426
  13.7 0.0 copy-start.3
  13.7 0.9 %copy-done.3 = bf16[1,2,8,16,256]{4,3,2,1,0:T(8,128)(2,1)S(1)} copy-done((bf16[1,2,8,16,256]{4,3,2,1,0:T(8,128)(2,1)S(1)}, bf16[1,2,8,16,256]{4,3,2,1,0:T(8,128)(2,1)}, u32[]{:S(2)}) %copy-start.3) | copy-done | bytes 131096
  14.6 0.1 shard_map.102.cot_t_ref
  14.7 5.9 %all-to-all-done.stats_ref.refs_6_ = f32[16,2,512]{2,1,0:T(2,128)S(1)} async-done(((f32[16,2,512]{2,1,0:T(2,128)}), f32[16,2,512]{2,1,0:T(2,128)S(1)}, u32[]{:S(2)}, u32[]{:S(2)}) %all-to-all-start) | async-done | bytes 65568 | tf_op jit(solution)/shard_map/all_to_all | solution.py:426
  20.7 1.0 %shard_map.103 = (bf16[256,256]{1,0:T(8,128)(2,1)S(1)}, bf16[256,2304]{1,0:T(8,128)(2,1)S(1)}, bf16[2,128,1152]{2,1,0:T(8,128)(2,1)S(1)}, bf16[2,128,1152]{2,1,0:T(8,128)(2,1)S(1)}) custom-call(bf16[256,256]{1,0:T(8,128)(2,1)S(1)} %bitcast.13, bf16[256,256]{1,0:T(8,128)(2,1)S(1)} %bitcast.21, bf16[256,256]{1,0:T(8,128)(2,1)S(1)} %collective-permute-done.1.halo_ref, ...), custom_call_target="tpu_custom_call" | custom-call | flops 402653184 | bytes 3000000 | tf_op jit(solution)/shard_map/pallas_call | solution.py:26
  21.7 0.6 %collective-permute-start.4 = (bf16[2,128,1152]{2,1,0:T(8,128)(2,1)S(1)}, bf16[2,128,1152]{2,1,0:T(8,128)(2,1)S(1)}, u32[]{:S(2)}, u32[]{:S(2)}) collective-permute-start(bf16[2,128,1152]{2,1,0:T(8,128)(2,1)S(1)} %get-tuple-element.41), channel_id=1, source_target_pairs={{0,1},{1,0},{2,3},{3,2},{4,5},{5,4},{6,7},{7,6},{8,9},{9,8},{10,11... | collective-permute-start | bytes 1769480 | tf_op jit(solution)/shard_map/ppermute | solution.py:404
  22.3 0.2 collective-permute-done.2.rest_1_
  22.5 1.6 %shard_map.104 = (bf16[256,256]{1,0:T(8,128)(2,1)S(1)}, f32[256,256]{1,0:T(8,128)S(1)}, bf16[2,128,512]{2,1,0:T(8,128)(2,1)S(1)}, bf16[2,128,512]{2,1,0:T(8,128)(2,1)S(1)}) custom-call(bf16[256,256]{1,0:T(8,128)(2,1)S(1)} %bitcast.14, bf16[256,256]{1,0:T(8,128)(2,1)S(1)} %shard_map.102.cot_t_ref, bf16[256,256]{1,0:T(8,128)(2,1)S(1)} %collective-permute-done.1.halo_ref, ...), custom_call_target="tpu_custom_call" | custom-call | flops 704643072 | bytes 3000000 | tf_op jit(solution)/shard_map/pallas_call | solution.py:26
  24.1 0.2 collective-permute-start.5
  24.3 1.4 %collective-permute-done.5 = bf16[2,128,512]{2,1,0:T(8,128)(2,1)S(1)} collective-permute-done((bf16[2,128,512]{2,1,0:T(8,128)(2,1)S(1)}, bf16[2,128,512]{2,1,0:T(8,128)(2,1)S(1)}, u32[]{:S(2)}, u32[]{:S(2)}) %collective-permute-start.5) | collective-permute-done | bytes 262176 | tf_op jit(solution)/shard_map/ppermute | solution.py:404
  25.7 0.2 shard_map.106
  25.9 0.2 collective-permute-start.6
  26.1 0.5 %collective-permute-start.7 = (bf16[4,16,1664]{2,1,0:T(8,128)(2,1)S(1)}, bf16[4,16,1664]{2,1,0:T(8,128)(2,1)S(1)}, u32[]{:S(2)}, u32[]{:S(2)}) collective-permute-start(bf16[4,16,1664]{2,1,0:T(8,128)(2,1)S(1)} %get-tuple-element.46), channel_id=1, source_target_pairs={{0,16},{1,17},{2,18},{3,19},{4,20},{5,21},{6,22},{7,23},{8,24},{9,... | collective-permute-start | bytes 638984 | tf_op jit(solution)/shard_map/ppermute | solution.py:404
  26.7 2.8 %collective-permute-start.8 = (bf16[4,16,1664]{2,1,0:T(8,128)(2,1)S(1)}, bf16[4,16,1664]{2,1,0:T(8,128)(2,1)S(1)}, u32[]{:S(2)}, u32[]{:S(2)}) collective-permute-start(bf16[4,16,1664]{2,1,0:T(8,128)(2,1)S(1)} %get-tuple-element.47), channel_id=1, source_target_pairs={{0,18},{1,19},{2,16},{3,17},{4,22},{5,23},{6,20},{7,21},{8,26},{9,... | collective-permute-start | bytes 638984 | tf_op jit(solution)/shard_map/ppermute | solution.py:404
  29.5 1.3 %collective-permute-start.3 = (bf16[256,256]{1,0:T(8,128)(2,1)S(1)}, bf16[256,256]{1,0:T(8,128)(2,1)S(1)}, u32[]{:S(2)}, u32[]{:S(2)}) collective-permute-start(bf16[256,256]{1,0:T(8,128)(2,1)S(1)} %get-tuple-element.39.spatial_ref), channel_id=1, source_target_pairs={{0,1},{1,2},{2,3},{3,4},{4,5},{5,6},{6,7},{7,8},{8,9},{9,10},{10,1... | collective-permute-start | bytes 393224 | tf_op jit(solution)/shard_map/ppermute | solution.py:461
  30.8 2.5 %collective-permute-done.6.refs_1_ = bf16[4,16,1664]{2,1,0:T(8,128)(2,1)S(1)} collective-permute-done((bf16[4,16,1664]{2,1,0:T(8,128)(2,1)S(1)}, bf16[4,16,1664]{2,1,0:T(8,128)(2,1)S(1)}, u32[]{:S(2)}, u32[]{:S(2)}) %collective-permute-start.6) | collective-permute-done | bytes 213024 | tf_op jit(solution)/shard_map/ppermute | solution.py:404
  33.3 0.9 %collective-permute-done.7.refs_2_ = bf16[4,16,1664]{2,1,0:T(8,128)(2,1)S(1)} collective-permute-done((bf16[4,16,1664]{2,1,0:T(8,128)(2,1)S(1)}, bf16[4,16,1664]{2,1,0:T(8,128)(2,1)S(1)}, u32[]{:S(2)}, u32[]{:S(2)}) %collective-permute-start.7) | collective-permute-done | bytes 213024 | tf_op jit(solution)/shard_map/ppermute | solution.py:404
  34.2 4.8 %collective-permute-done.8.refs_3_ = bf16[4,16,1664]{2,1,0:T(8,128)(2,1)S(1)} collective-permute-done((bf16[4,16,1664]{2,1,0:T(8,128)(2,1)S(1)}, bf16[4,16,1664]{2,1,0:T(8,128)(2,1)S(1)}, u32[]{:S(2)}, u32[]{:S(2)}) %collective-permute-start.8) | collective-permute-done | bytes 213024 | tf_op jit(solution)/shard_map/ppermute | solution.py:404
  39.1 0.1 shard_map.107
  39.2 1.4 %collective-permute-start.9 = (bf16[16,1664]{1,0:T(8,128)(2,1)S(1)}, bf16[16,1664]{1,0:T(8,128)(2,1)S(1)}, u32[]{:S(2)}, u32[]{:S(2)}) collective-permute-start(bf16[16,1664]{1,0:T(8,128)(2,1)S(1)} %get-tuple-element.49), channel_id=1, source_target_pairs={{0,4},{1,5},{2,6},{3,7},{4,8},{5,9},{6,10},{7,11},{8,12},{9,13},{1... | collective-permute-start | bytes 159752 | tf_op jit(solution)/shard_map/ppermute | solution.py:404
  40.6 1.0 %collective-permute-start.10 = (bf16[16,1664]{1,0:T(8,128)(2,1)S(1)}, bf16[16,1664]{1,0:T(8,128)(2,1)S(1)}, u32[]{:S(2)}, u32[]{:S(2)}) collective-permute-start(bf16[16,1664]{1,0:T(8,128)(2,1)S(1)} %get-tuple-element.50), channel_id=1, source_target_pairs={{0,8},{1,9},{2,10},{3,11},{4,12},{5,13},{6,14},{7,15},{8,0},{9,1},... | collective-permute-start | bytes 159752 | tf_op jit(solution)/shard_map/ppermute | solution.py:404
  41.6 2.0 %collective-permute-start.11 = (bf16[16,1664]{1,0:T(8,128)(2,1)S(1)}, bf16[16,1664]{1,0:T(8,128)(2,1)S(1)}, u32[]{:S(2)}, u32[]{:S(2)}) collective-permute-start(bf16[16,1664]{1,0:T(8,128)(2,1)S(1)} %get-tuple-element.51), channel_id=1, source_target_pairs={{0,12},{1,13},{2,14},{3,15},{4,0},{5,1},{6,2},{7,3},{8,4},{9,5},{1... | collective-permute-start | bytes 159752 | tf_op jit(solution)/shard_map/ppermute | solution.py:404
  43.6 0.0 collective-permute-done.3.before_ref
  43.6 1.0 %shard_map.105 = bf16[256,256]{1,0:T(8,128)(2,1)} custom-call(bf16[256,256]{1,0:T(8,128)(2,1)S(1)} %bitcast.15, bf16[256,256]{1,0:T(8,128)(2,1)S(1)} %get-tuple-element.39.spatial_ref, bf16[256,256]{1,0:T(8,128)(2,1)S(1)} %collective-permute-done.3.before_ref, bf16[384,256]{1,0:T(8,128)(2,1)S(1)} %copy-done.2, bf16[960,256]{1,0:T(8,128)(2,1)S(1)} %collective-permute-done.rest_0_), custom_call_target="tpu_custom_call" | custom-call | flops 100663296 | bytes 1000000 | tf_op jit(solution)/shard_map/pallas_call | solution.py:26
  44.6 0.7 %collective-permute-done.9.refs_1_ = bf16[16,1664]{1,0:T(8,128)(2,1)S(1)} collective-permute-done((bf16[16,1664]{1,0:T(8,128)(2,1)S(1)}, bf16[16,1664]{1,0:T(8,128)(2,1)S(1)}, u32[]{:S(2)}, u32[]{:S(2)}) %collective-permute-start.9) | collective-permute-done | bytes 53280 | tf_op jit(solution)/shard_map/ppermute | solution.py:404
  45.3 1.3 %collective-permute-done.10.refs_2_ = bf16[16,1664]{1,0:T(8,128)(2,1)S(1)} collective-permute-done((bf16[16,1664]{1,0:T(8,128)(2,1)S(1)}, bf16[16,1664]{1,0:T(8,128)(2,1)S(1)}, u32[]{:S(2)}, u32[]{:S(2)}) %collective-permute-start.10) | collective-permute-done | bytes 53280 | tf_op jit(solution)/shard_map/ppermute | solution.py:404
  46.6 1.1 %shard_map.108 = (f32[16,1152]{1,0:T(8,128)}, f32[16,384]{1,0:T(8,128)}, f32[2,16]{1,0:T(2,128)}, bf16[256,256]{1,0:T(8,128)(2,1)}) custom-call(bf16[16,1664]{1,0:T(8,128)(2,1)S(1)} %get-tuple-element.48.refs_0_, bf16[16,1664]{1,0:T(8,128)(2,1)S(1)} %collective-permute-done.9.refs_1_, bf16[16,1664]{1,0:T(8,128)(2,1)S(1)} %collective-permute-done.10.refs_2_, ...), custom_call_target="tpu_custom_call" | custom-call | bytes 1000000 | tf_op jit(solution)/shard_map/pallas_call | solution.py:26
  (12 shorter events, 0.0 us)
Async XLA Ops:
  0.6 20.0 %copy-start.2 = (bf16[384,256]{1,0:T(8,128)(2,1)S(1)}, bf16[384,256]{1,0:T(8,128)(2,1)}, u32[]{:S(2)}) copy-start(bf16[384,256]{1,0:T(8,128)(2,1)} %wt_ref.5) | copy-start | bytes 589828
  0.6 20.0 %copy-start.1 = (bf16[1,2,8,16,256]{4,3,2,1,0:T(8,128)(2,1)S(1)}, bf16[1,2,8,16,256]{4,3,2,1,0:T(8,128)(2,1)}, u32[]{:S(2)}) copy-start(bf16[1,2,8,16,256]{4,3,2,1,0:T(8,128)(2,1)} %param.6) | copy-start | bytes 393220
  0.7 20.0 %copy-start.4 = (bf16[1,2,8,16,256]{4,3,2,1,0:T(8,128)(2,1)S(1)}, bf16[1,2,8,16,256]{4,3,2,1,0:T(8,128)(2,1)}, u32[]{:S(2)}) copy-start(bf16[1,2,8,16,256]{4,3,2,1,0:T(8,128)(2,1)} %param.7) | copy-start | bytes 393220
  0.7 21.8 %copy-start = (bf16[1152,256]{1,0:T(8,128)(2,1)S(1)}, bf16[1152,256]{1,0:T(8,128)(2,1)}, u32[]{:S(2)}) copy-start(bf16[1152,256]{1,0:T(8,128)(2,1)} %ws_ref.3) | copy-start | bytes 1769476
  2.7 17.9 %collective-permute-start = (bf16[960,256]{1,0:T(8,128)(2,1)}, bf16[960,256]{1,0:T(8,128)(2,1)S(1)}, u32[]{:S(2)}, u32[]{:S(2)}) collective-permute-start(bf16[960,256]{1,0:T(8,128)(2,1)} %get-tuple-element.31), channel_id=1, source_target_pairs={{0,16},{1,17},{2,18},{3,19},{4,20},{5,21},{6,22},{7,23},{8,24},{9,... | collective-permute-start | bytes 1474568 | tf_op jit(solution)/shard_map/ppermute | solution.py:404
  5.7 14.9 %collective-permute-start.1 = (bf16[256,256]{1,0:T(8,128)(2,1)}, bf16[256,256]{1,0:T(8,128)(2,1)S(1)}, u32[]{:S(2)}, u32[]{:S(2)}) collective-permute-start(bf16[256,256]{1,0:T(8,128)(2,1)} %bitcast.19), channel_id=1, source_target_pairs={{1,0},{2,1},{3,2},{4,3},{5,4},{6,5},{7,6},{8,7},{9,8},{10,9},{11,1... | collective-permute-start | bytes 393224 | tf_op jit(solution)/shard_map/ppermute | solution.py:425
  7.0 13.6 %all-to-all-start = ((f32[16,2,512]{2,1,0:T(2,128)}), f32[16,2,512]{2,1,0:T(2,128)S(1)}, u32[]{:S(2)}, u32[]{:S(2)}) async-start(f32[16,2,512]{2,1,0:T(2,128)} %get-tuple-element.32), calls=%async_computation | async-start | bytes 131072 | tf_op jit(solution)/shard_map/all_to_all | solution.py:426
  13.7 0.9 %copy-start.3 = (bf16[1,2,8,16,256]{4,3,2,1,0:T(8,128)(2,1)S(1)}, bf16[1,2,8,16,256]{4,3,2,1,0:T(8,128)(2,1)}, u32[]{:S(2)}) copy-start(bf16[1,2,8,16,256]{4,3,2,1,0:T(8,128)(2,1)} %param.7) | copy-start | bytes 393220
  20.6 1.9 %collective-permute-start.2 = (bf16[960,256]{1,0:T(8,128)(2,1)S(1)}, bf16[960,256]{1,0:T(8,128)(2,1)S(1)}, u32[]{:S(2)}, u32[]{:S(2)}) collective-permute-start(bf16[960,256]{1,0:T(8,128)(2,1)S(1)} %collective-permute-done.rest_0_), channel_id=1, source_target_pairs={{0,1},{1,0},{2,3},{3,2},{4,5},{5,4},{6,7},{7,6},{8,9},{9,8},{10,11... | collective-permute-start | bytes 1474568 | tf_op jit(solution)/shard_map/ppermute | solution.py:404
  21.7 2.6 %collective-permute-start.4 = (bf16[2,128,1152]{2,1,0:T(8,128)(2,1)S(1)}, bf16[2,128,1152]{2,1,0:T(8,128)(2,1)S(1)}, u32[]{:S(2)}, u32[]{:S(2)}) collective-permute-start(bf16[2,128,1152]{2,1,0:T(8,128)(2,1)S(1)} %get-tuple-element.41), channel_id=1, source_target_pairs={{0,1},{1,0},{2,3},{3,2},{4,5},{5,4},{6,7},{7,6},{8,9},{9,8},{10,11... | collective-permute-start | bytes 1769480 | tf_op jit(solution)/shard_map/ppermute | solution.py:404
  24.1 1.6 %collective-permute-start.5 = (bf16[2,128,512]{2,1,0:T(8,128)(2,1)S(1)}, bf16[2,128,512]{2,1,0:T(8,128)(2,1)S(1)}, u32[]{:S(2)}, u32[]{:S(2)}) collective-permute-start(bf16[2,128,512]{2,1,0:T(8,128)(2,1)S(1)} %get-tuple-element.43), channel_id=1, source_target_pairs={{0,1},{1,0},{2,3},{3,2},{4,5},{5,4},{6,7},{7,6},{8,9},{9,8},{10,11... | collective-permute-start | bytes 786440 | tf_op jit(solution)/shard_map/ppermute | solution.py:404
  25.9 7.4 %collective-permute-start.6 = (bf16[4,16,1664]{2,1,0:T(8,128)(2,1)S(1)}, bf16[4,16,1664]{2,1,0:T(8,128)(2,1)S(1)}, u32[]{:S(2)}, u32[]{:S(2)}) collective-permute-start(bf16[4,16,1664]{2,1,0:T(8,128)(2,1)S(1)} %get-tuple-element.45), channel_id=1, source_target_pairs={{0,2},{1,3},{2,0},{3,1},{4,6},{5,7},{6,4},{7,5},{8,10},{9,11},{10,... | collective-permute-start | bytes 638984 | tf_op jit(solution)/shard_map/ppermute | solution.py:404
  26.1 8.1 %collective-permute-start.7 = (bf16[4,16,1664]{2,1,0:T(8,128)(2,1)S(1)}, bf16[4,16,1664]{2,1,0:T(8,128)(2,1)S(1)}, u32[]{:S(2)}, u32[]{:S(2)}) collective-permute-start(bf16[4,16,1664]{2,1,0:T(8,128)(2,1)S(1)} %get-tuple-element.46), channel_id=1, source_target_pairs={{0,16},{1,17},{2,18},{3,19},{4,20},{5,21},{6,22},{7,23},{8,24},{9,... | collective-permute-start | bytes 638984 | tf_op jit(solution)/shard_map/ppermute | solution.py:404
  26.7 12.4 %collective-permute-start.8 = (bf16[4,16,1664]{2,1,0:T(8,128)(2,1)S(1)}, bf16[4,16,1664]{2,1,0:T(8,128)(2,1)S(1)}, u32[]{:S(2)}, u32[]{:S(2)}) collective-permute-start(bf16[4,16,1664]{2,1,0:T(8,128)(2,1)S(1)} %get-tuple-element.47), channel_id=1, source_target_pairs={{0,18},{1,19},{2,16},{3,17},{4,22},{5,23},{6,20},{7,21},{8,26},{9,... | collective-permute-start | bytes 638984 | tf_op jit(solution)/shard_map/ppermute | solution.py:404
  29.5 14.1 %collective-permute-start.3 = (bf16[256,256]{1,0:T(8,128)(2,1)S(1)}, bf16[256,256]{1,0:T(8,128)(2,1)S(1)}, u32[]{:S(2)}, u32[]{:S(2)}) collective-permute-start(bf16[256,256]{1,0:T(8,128)(2,1)S(1)} %get-tuple-element.39.spatial_ref), channel_id=1, source_target_pairs={{0,1},{1,2},{2,3},{3,4},{4,5},{5,6},{6,7},{7,8},{8,9},{9,10},{10,1... | collective-permute-start | bytes 393224 | tf_op jit(solution)/shard_map/ppermute | solution.py:461
  39.2 6.1 %collective-permute-start.9 = (bf16[16,1664]{1,0:T(8,128)(2,1)S(1)}, bf16[16,1664]{1,0:T(8,128)(2,1)S(1)}, u32[]{:S(2)}, u32[]{:S(2)}) collective-permute-start(bf16[16,1664]{1,0:T(8,128)(2,1)S(1)} %get-tuple-element.49), channel_id=1, source_target_pairs={{0,4},{1,5},{2,6},{3,7},{4,8},{5,9},{6,10},{7,11},{8,12},{9,13},{1... | collective-permute-start | bytes 159752 | tf_op jit(solution)/shard_map/ppermute | solution.py:404
  40.6 6.0 %collective-permute-start.10 = (bf16[16,1664]{1,0:T(8,128)(2,1)S(1)}, bf16[16,1664]{1,0:T(8,128)(2,1)S(1)}, u32[]{:S(2)}, u32[]{:S(2)}) collective-permute-start(bf16[16,1664]{1,0:T(8,128)(2,1)S(1)} %get-tuple-element.50), channel_id=1, source_target_pairs={{0,8},{1,9},{2,10},{3,11},{4,12},{5,13},{6,14},{7,15},{8,0},{9,1},... | collective-permute-start | bytes 159752 | tf_op jit(solution)/shard_map/ppermute | solution.py:404
  41.6 5.0 %collective-permute-start.11 = (bf16[16,1664]{1,0:T(8,128)(2,1)S(1)}, bf16[16,1664]{1,0:T(8,128)(2,1)S(1)}, u32[]{:S(2)}, u32[]{:S(2)}) collective-permute-start(bf16[16,1664]{1,0:T(8,128)(2,1)S(1)} %get-tuple-element.51), channel_id=1, source_target_pairs={{0,12},{1,13},{2,14},{3,15},{4,0},{5,1},{6,2},{7,3},{8,4},{9,5},{1... | collective-permute-start | bytes 159752 | tf_op jit(solution)/shard_map/ppermute | solution.py:404

commit v12 on v11

--- a/solution.py
+++ b/solution.py
@@ -56,31 +56,32 @@
     )
 
 
-def stats_body(lat_ref, gain_ref, bias_ref, ws_ref, wt_ref, out_ref, half_ref, *scratch):
-    lat_here, gain_here, bias_here, sems = scratch
+def cut_body(ws_ref, wt_ref, half_ref, sems):
     core = lax.rem(lax.axis_index("wide"), 2)
-    moves = [(lat_ref, lat_here), (gain_ref, gain_here), (bias_ref, bias_here)]
     half = ws_ref.shape[0] // 2
     start = pl.multiple_of(core * half, 16)
-    moves.append((ws_ref.at[pl.ds(start, half)], half_ref.at[pl.ds(0, half)]))
-    moves.append((wt_ref, half_ref.at[pl.ds(half, wt_ref.shape[0])]))
+    moves = (
+        (ws_ref.at[pl.ds(start, half)], half_ref.at[pl.ds(0, half)]),
+        (wt_ref, half_ref.at[pl.ds(half, wt_ref.shape[0])]),
+    )
     copies = [pltpu.make_async_copy(*move, sems.at[at]) for at, move in enumerate(moves)]
     for copy in copies:
         copy.start()
-    for copy in copies[:3]:
+    for copy in copies:
         copy.wait()
-    x = lat_here[...].astype(F32)
+
+
+def stats_body(lat_ref, gain_ref, bias_ref, out_ref):
+    x = lat_ref[...].astype(F32)
     sums = [jnp.sum(x, axis=0, keepdims=True), jnp.sum(x * x, axis=0, keepdims=True)]
     both = jnp.concatenate(
         [
-            jnp.concatenate([sums[0], gain_here[...]], axis=1),
-            jnp.concatenate([sums[1], bias_here[...]], axis=1),
+            jnp.concatenate([sums[0], gain_ref[...]], axis=1),
+            jnp.concatenate([sums[1], bias_ref[...]], axis=1),
         ],
         axis=0,
     )
     out_ref[...] = jnp.broadcast_to(both[None], out_ref.shape)
-    for copy in copies[3:]:
-        copy.wait()
 
 
 def transpose_body(cot_ref, out_ref):
@@ -404,21 +405,14 @@
         return lax.ppermute(value, ("dp", "wide"), over_all(moves))
 
     R = shard_s + shard_t
-    stats, half = call(
-        stats_body,
-        [
-            shape((W, 2, 2 * channels), F32),
-            shape((shard_s // 2 + shard_t, channels), BF16),
-        ],
-        [
-            pltpu.VMEM((rows, channels), BF16),
-            pltpu.VMEM((1, channels), F32),
-            pltpu.VMEM((1, channels), F32),
-            pltpu.SemaphoreType.DMA((5,)),
-        ],
-        in_specs=[HBM] * 5,
+    half = call(
+        cut_body,
+        shape((shard_s // 2 + shard_t, channels), BF16),
+        [pltpu.SemaphoreType.DMA((2,))],
+        in_specs=[HBM] * 2,
         vmem=FIRST_VMEM,
-    )(lat, gain, bias, w_spatial, w_temporal)
+    )(w_spatial, w_temporal)
+    stats = call(stats_body, shape((W, 2, 2 * channels), F32))(lat, gain, bias)
     cot_t = call(transpose_body, shape((channels, rows), BF16), moved=300_000)(cot)
     firsts = [send(half, lambda d, w: ((d + s) % D, w)) for s in range(1, D)]
 

time: 48 us -> 48.6 us (1.012)
  waiting for transfers between devices: 17.8 us -> 18.7 us
  local copies, waits for them, and re-layouts: 0.92 us -> 0.03 us
  Pallas kernels: 7.25 us -> 7.83 us
    all_to_all x1, waiting for transfers between devices: 5.88 us -> 6.79 us  [local(): lax.all_to_all(stats, 'wide', split_axis=0, concat_axis=0, tiled=True)]
    unnamed x10 -> x12, local copies, waits for them, and re-layouts: 0.92 us -> 0.03 us
    pallas_call x8 -> x9, Pallas kernels: 7.25 us -> 7.83 us  [run(): pl.pallas_call(body, out_shape=out_shapes, in_specs=in_specs or [VMEM] *...]
  transfers between devices with their start and end apart: 13 -> 13, of which waited for: 8 -> 8; matrix products, arithmetic and copies ran while one was open for 0% -> 0% of each run, Pallas kernels for 8% -> 9%
where the time goes in v12:
time: 48.6 us; the launch traced here: 48.4 us
  starting transfers between devices  21 us (43%)
  waiting for transfers between devices  18.7 us (38%)
  Pallas kernels  7.83 us (16%)
  between operations  0.79 us (2%)
    ppermute x10, waiting for transfers between devices, send(): return lax.ppermute(value, ('dp', 'wide'), over_all(moves))  11.9 us
    ppermute x10, starting transfers between devices, send(): return lax.ppermute(value, ('dp', 'wide'), over_all(moves))  11.7 us
    pallas_call x9, Pallas kernels, run(): pl.pallas_call(body, out_shape=out_shapes, in_specs=in_specs or [VMEM] *...  7.83 us
    all_to_all x1, waiting for transfers between devices, local(): lax.all_to_all(stats, 'wide', split_axis=0, concat_axis=0, tiled=True)  6.79 us
    all_to_all x1, starting transfers between devices, local(): lax.all_to_all(stats, 'wide', split_axis=0, concat_axis=0, tiled=True)  6.67 us
    ppermute x1, starting transfers between devices, local(): before = lax.ppermute(spatial, 'wide', [(w, w + 1) for w in range(W - 1)])  1.29 us
    ppermute x1, starting transfers between devices, local(): halo = lax.ppermute(cot, 'wide', [(w + 1, w) for w in range(W - 1)])  1.28 us
  transfers between devices with their start and end apart: 13, of which 8 were waited for; matrix products, arithmetic and copies ran while one was open for 0% of the time, Pallas kernels for 9%

profile of v12, /device:TPU:0, one launch (start us, length us, event | category | flops | bytes accessed | tf_op | source)
XLA Modules:
  0.0 48.4 jit_solution(13449704790381685926)
XLA Ops:
  0.7 2.0 %shard_map.101 = bf16[960,256]{1,0:T(8,128)(2,1)} custom-call(bf16[1152,256]{1,0:T(8,128)(2,1)} %ws_ref.3, bf16[384,256]{1,0:T(8,128)(2,1)} %wt_ref.5), custom_call_target="tpu_custom_call" | custom-call | tf_op jit(solution)/shard_map/pallas_call | solution.py:26
  2.6 0.0 copy-start
  2.7 3.0 %collective-permute-start = (bf16[960,256]{1,0:T(8,128)(2,1)}, bf16[960,256]{1,0:T(8,128)(2,1)S(1)}, u32[]{:S(2)}, u32[]{:S(2)}) collective-permute-start(bf16[960,256]{1,0:T(8,128)(2,1)} %shard_map.101), channel_id=1, source_target_pairs={{0,16},{1,17},{2,18},{3,19},{4,20},{5,21},{6,22},{7,23},{8,24},{9,... | collective-permute-start | bytes 1474568 | tf_op jit(solution)/shard_map/ppermute | solution.py:405
  5.7 1.3 %collective-permute-start.1 = (bf16[256,256]{1,0:T(8,128)(2,1)S(1)}, bf16[256,256]{1,0:T(8,128)(2,1)S(1)}, u32[]{:S(2)}, u32[]{:S(2)}) collective-permute-start(bf16[256,256]{1,0:T(8,128)(2,1)S(1)} %bitcast.19), channel_id=1, source_target_pairs={{1,0},{2,1},{3,2},{4,3},{5,4},{6,5},{7,6},{8,7},{9,8},{10,9},{11,1... | collective-permute-start | bytes 393224 | tf_op jit(solution)/shard_map/ppermute | solution.py:419
  7.0 0.7 %shard_map.102 = f32[16,2,512]{2,1,0:T(2,128)} custom-call(bf16[256,256]{1,0:T(8,128)(2,1)S(1)} %bitcast.12, f32[1,256]{1,0:T(1,128)S(1)} %bitcast.25, f32[1,256]{1,0:T(1,128)S(1)} %bitcast.26), custom_call_target="tpu_custom_call" | custom-call | tf_op jit(solution)/shard_map/pallas_call | solution.py:26
  7.7 6.7 %all-to-all-start = ((f32[16,2,512]{2,1,0:T(2,128)}), f32[16,2,512]{2,1,0:T(2,128)S(1)}, u32[]{:S(2)}, u32[]{:S(2)}) async-start(f32[16,2,512]{2,1,0:T(2,128)} %shard_map.102), calls=%async_computation | async-start | bytes 131072 | tf_op jit(solution)/shard_map/all_to_all | solution.py:420
  14.3 0.1 shard_map.103.cot_t_ref
  14.4 6.8 %all-to-all-done.stats_ref.refs_6_ = f32[16,2,512]{2,1,0:T(2,128)S(1)} async-done(((f32[16,2,512]{2,1,0:T(2,128)}), f32[16,2,512]{2,1,0:T(2,128)S(1)}, u32[]{:S(2)}, u32[]{:S(2)}) %all-to-all-start) | async-done | bytes 65568 | tf_op jit(solution)/shard_map/all_to_all | solution.py:420
  21.2 0.0 collective-permute-done.1.halo_ref
  21.2 0.0 collective-permute-done.rest_0_
  21.3 1.0 %shard_map.104 = (bf16[256,256]{1,0:T(8,128)(2,1)S(1)}, bf16[256,2304]{1,0:T(8,128)(2,1)S(1)}, bf16[2,128,1152]{2,1,0:T(8,128)(2,1)S(1)}, bf16[2,128,1152]{2,1,0:T(8,128)(2,1)S(1)}) custom-call(bf16[256,256]{1,0:T(8,128)(2,1)S(1)} %bitcast.13, bf16[256,256]{1,0:T(8,128)(2,1)S(1)} %bitcast.21, bf16[256,256]{1,0:T(8,128)(2,1)S(1)} %collective-permute-done.1.halo_ref, ...), custom_call_target="tpu_custom_call" | custom-call | flops 402653184 | bytes 3000000 | tf_op jit(solution)/shard_map/pallas_call | solution.py:26
  22.3 0.6 %collective-permute-start.4 = (bf16[2,128,1152]{2,1,0:T(8,128)(2,1)S(1)}, bf16[2,128,1152]{2,1,0:T(8,128)(2,1)S(1)}, u32[]{:S(2)}, u32[]{:S(2)}) collective-permute-start(bf16[2,128,1152]{2,1,0:T(8,128)(2,1)S(1)} %get-tuple-element.37), channel_id=1, source_target_pairs={{0,1},{1,0},{2,3},{3,2},{4,5},{5,4},{6,7},{7,6},{8,9},{9,8},{10,11... | collective-permute-start | bytes 1769480 | tf_op jit(solution)/shard_map/ppermute | solution.py:405
  22.9 0.2 collective-permute-done.2.rest_1_
  23.1 1.6 %shard_map.105 = (bf16[256,256]{1,0:T(8,128)(2,1)S(1)}, f32[256,256]{1,0:T(8,128)S(1)}, bf16[2,128,512]{2,1,0:T(8,128)(2,1)S(1)}, bf16[2,128,512]{2,1,0:T(8,128)(2,1)S(1)}) custom-call(bf16[256,256]{1,0:T(8,128)(2,1)S(1)} %bitcast.14, bf16[256,256]{1,0:T(8,128)(2,1)S(1)} %shard_map.103.cot_t_ref, bf16[256,256]{1,0:T(8,128)(2,1)S(1)} %collective-permute-done.1.halo_ref, ...), custom_call_target="tpu_custom_call" | custom-call | flops 704643072 | bytes 3000000 | tf_op jit(solution)/shard_map/pallas_call | solution.py:26
  24.7 0.2 collective-permute-start.5
  24.9 1.4 %collective-permute-done.5 = bf16[2,128,512]{2,1,0:T(8,128)(2,1)S(1)} collective-permute-done((bf16[2,128,512]{2,1,0:T(8,128)(2,1)S(1)}, bf16[2,128,512]{2,1,0:T(8,128)(2,1)S(1)}, u32[]{:S(2)}, u32[]{:S(2)}) %collective-permute-start.5) | collective-permute-done | bytes 262176 | tf_op jit(solution)/shard_map/ppermute | solution.py:405
  26.3 0.2 shard_map.107
  26.6 0.2 collective-permute-start.6
  26.7 0.5 %collective-permute-start.7 = (bf16[4,16,1664]{2,1,0:T(8,128)(2,1)S(1)}, bf16[4,16,1664]{2,1,0:T(8,128)(2,1)S(1)}, u32[]{:S(2)}, u32[]{:S(2)}) collective-permute-start(bf16[4,16,1664]{2,1,0:T(8,128)(2,1)S(1)} %get-tuple-element.42), channel_id=1, source_target_pairs={{0,16},{1,17},{2,18},{3,19},{4,20},{5,21},{6,22},{7,23},{8,24},{9,... | collective-permute-start | bytes 638984 | tf_op jit(solution)/shard_map/ppermute | solution.py:405
  27.3 2.8 %collective-permute-start.8 = (bf16[4,16,1664]{2,1,0:T(8,128)(2,1)S(1)}, bf16[4,16,1664]{2,1,0:T(8,128)(2,1)S(1)}, u32[]{:S(2)}, u32[]{:S(2)}) collective-permute-start(bf16[4,16,1664]{2,1,0:T(8,128)(2,1)S(1)} %get-tuple-element.43), channel_id=1, source_target_pairs={{0,18},{1,19},{2,16},{3,17},{4,22},{5,23},{6,20},{7,21},{8,26},{9,... | collective-permute-start | bytes 638984 | tf_op jit(solution)/shard_map/ppermute | solution.py:405
  30.1 1.3 %collective-permute-start.3 = (bf16[256,256]{1,0:T(8,128)(2,1)S(1)}, bf16[256,256]{1,0:T(8,128)(2,1)S(1)}, u32[]{:S(2)}, u32[]{:S(2)}) collective-permute-start(bf16[256,256]{1,0:T(8,128)(2,1)S(1)} %get-tuple-element.35.spatial_ref), channel_id=1, source_target_pairs={{0,1},{1,2},{2,3},{3,4},{4,5},{5,6},{6,7},{7,8},{8,9},{9,10},{10,1... | collective-permute-start | bytes 393224 | tf_op jit(solution)/shard_map/ppermute | solution.py:455
  31.4 2.5 %collective-permute-done.6.refs_1_ = bf16[4,16,1664]{2,1,0:T(8,128)(2,1)S(1)} collective-permute-done((bf16[4,16,1664]{2,1,0:T(8,128)(2,1)S(1)}, bf16[4,16,1664]{2,1,0:T(8,128)(2,1)S(1)}, u32[]{:S(2)}, u32[]{:S(2)}) %collective-permute-start.6) | collective-permute-done | bytes 213024 | tf_op jit(solution)/shard_map/ppermute | solution.py:405
  33.9 0.9 %collective-permute-done.7.refs_2_ = bf16[4,16,1664]{2,1,0:T(8,128)(2,1)S(1)} collective-permute-done((bf16[4,16,1664]{2,1,0:T(8,128)(2,1)S(1)}, bf16[4,16,1664]{2,1,0:T(8,128)(2,1)S(1)}, u32[]{:S(2)}, u32[]{:S(2)}) %collective-permute-start.7) | collective-permute-done | bytes 213024 | tf_op jit(solution)/shard_map/ppermute | solution.py:405
  34.9 4.8 %collective-permute-done.8.refs_3_ = bf16[4,16,1664]{2,1,0:T(8,128)(2,1)S(1)} collective-permute-done((bf16[4,16,1664]{2,1,0:T(8,128)(2,1)S(1)}, bf16[4,16,1664]{2,1,0:T(8,128)(2,1)S(1)}, u32[]{:S(2)}, u32[]{:S(2)}) %collective-permute-start.8) | collective-permute-done | bytes 213024 | tf_op jit(solution)/shard_map/ppermute | solution.py:405
  39.7 0.1 shard_map.108
  39.8 1.4 %collective-permute-start.9 = (bf16[16,1664]{1,0:T(8,128)(2,1)S(1)}, bf16[16,1664]{1,0:T(8,128)(2,1)S(1)}, u32[]{:S(2)}, u32[]{:S(2)}) collective-permute-start(bf16[16,1664]{1,0:T(8,128)(2,1)S(1)} %get-tuple-element.45), channel_id=1, source_target_pairs={{0,4},{1,5},{2,6},{3,7},{4,8},{5,9},{6,10},{7,11},{8,12},{9,13},{1... | collective-permute-start | bytes 159752 | tf_op jit(solution)/shard_map/ppermute | solution.py:405
  41.2 1.0 %collective-permute-start.10 = (bf16[16,1664]{1,0:T(8,128)(2,1)S(1)}, bf16[16,1664]{1,0:T(8,128)(2,1)S(1)}, u32[]{:S(2)}, u32[]{:S(2)}) collective-permute-start(bf16[16,1664]{1,0:T(8,128)(2,1)S(1)} %get-tuple-element.46), channel_id=1, source_target_pairs={{0,8},{1,9},{2,10},{3,11},{4,12},{5,13},{6,14},{7,15},{8,0},{9,1},... | collective-permute-start | bytes 159752 | tf_op jit(solution)/shard_map/ppermute | solution.py:405
  42.2 2.0 %collective-permute-start.11 = (bf16[16,1664]{1,0:T(8,128)(2,1)S(1)}, bf16[16,1664]{1,0:T(8,128)(2,1)S(1)}, u32[]{:S(2)}, u32[]{:S(2)}) collective-permute-start(bf16[16,1664]{1,0:T(8,128)(2,1)S(1)} %get-tuple-element.47), channel_id=1, source_target_pairs={{0,12},{1,13},{2,14},{3,15},{4,0},{5,1},{6,2},{7,3},{8,4},{9,5},{1... | collective-permute-start | bytes 159752 | tf_op jit(solution)/shard_map/ppermute | solution.py:405
  44.2 1.0 %shard_map.106 = bf16[256,256]{1,0:T(8,128)(2,1)} custom-call(bf16[256,256]{1,0:T(8,128)(2,1)S(1)} %bitcast.15, bf16[256,256]{1,0:T(8,128)(2,1)S(1)} %get-tuple-element.35.spatial_ref, bf16[256,256]{1,0:T(8,128)(2,1)S(1)} %collective-permute-done.3.before_ref, bf16[384,256]{1,0:T(8,128)(2,1)S(1)} %copy-done.2, bf16[960,256]{1,0:T(8,128)(2,1)S(1)} %collective-permute-done.rest_0_), custom_call_target="tpu_custom_call" | custom-call | flops 100663296 | bytes 1000000 | tf_op jit(solution)/shard_map/pallas_call | solution.py:26
  45.2 0.7 %collective-permute-done.9.refs_1_ = bf16[16,1664]{1,0:T(8,128)(2,1)S(1)} collective-permute-done((bf16[16,1664]{1,0:T(8,128)(2,1)S(1)}, bf16[16,1664]{1,0:T(8,128)(2,1)S(1)}, u32[]{:S(2)}, u32[]{:S(2)}) %collective-permute-start.9) | collective-permute-done | bytes 53280 | tf_op jit(solution)/shard_map/ppermute | solution.py:405
  45.9 1.3 %collective-permute-done.10.refs_2_ = bf16[16,1664]{1,0:T(8,128)(2,1)S(1)} collective-permute-done((bf16[16,1664]{1,0:T(8,128)(2,1)S(1)}, bf16[16,1664]{1,0:T(8,128)(2,1)S(1)}, u32[]{:S(2)}, u32[]{:S(2)}) %collective-permute-start.10) | collective-permute-done | bytes 53280 | tf_op jit(solution)/shard_map/ppermute | solution.py:405
  47.2 1.1 %shard_map.109 = (f32[16,1152]{1,0:T(8,128)}, f32[16,384]{1,0:T(8,128)}, f32[2,16]{1,0:T(2,128)}, bf16[256,256]{1,0:T(8,128)(2,1)}) custom-call(bf16[16,1664]{1,0:T(8,128)(2,1)S(1)} %get-tuple-element.44.refs_0_, bf16[16,1664]{1,0:T(8,128)(2,1)S(1)} %collective-permute-done.9.refs_1_, bf16[16,1664]{1,0:T(8,128)(2,1)S(1)} %collective-permute-done.10.refs_2_, ...), custom_call_target="tpu_custom_call" | custom-call | bytes 1000000 | tf_op jit(solution)/shard_map/pallas_call | solution.py:26
  (15 shorter events, 0.0 us)
Async XLA Ops:
  0.6 20.6 %copy-start.2 = (bf16[384,256]{1,0:T(8,128)(2,1)S(1)}, bf16[384,256]{1,0:T(8,128)(2,1)}, u32[]{:S(2)}) copy-start(bf16[384,256]{1,0:T(8,128)(2,1)} %wt_ref.5) | copy-start | bytes 589828
  0.6 5.0 %copy-start.3 = (bf16[1,2,8,16,256]{4,3,2,1,0:T(8,128)(2,1)S(1)}, bf16[1,2,8,16,256]{4,3,2,1,0:T(8,128)(2,1)}, u32[]{:S(2)}) copy-start(bf16[1,2,8,16,256]{4,3,2,1,0:T(8,128)(2,1)} %param.7) | copy-start | bytes 393220
  0.7 6.3 %copy-start.5 = (f32[256]{0:T(256)S(1)}, f32[256]{0:T(256)}, u32[]{:S(2)}) copy-start(f32[256]{0:T(256)} %param.9) | copy-start | bytes 3076
  0.7 6.3 %copy-start.4 = (f32[256]{0:T(256)S(1)}, f32[256]{0:T(256)}, u32[]{:S(2)}) copy-start(f32[256]{0:T(256)} %param.8) | copy-start | bytes 3076
  0.7 6.3 %copy-start.1 = (bf16[1,2,8,16,256]{4,3,2,1,0:T(8,128)(2,1)S(1)}, bf16[1,2,8,16,256]{4,3,2,1,0:T(8,128)(2,1)}, u32[]{:S(2)}) copy-start(bf16[1,2,8,16,256]{4,3,2,1,0:T(8,128)(2,1)} %param.6) | copy-start | bytes 393220
  2.6 20.5 %copy-start = (bf16[1152,256]{1,0:T(8,128)(2,1)S(1)}, bf16[1152,256]{1,0:T(8,128)(2,1)}, u32[]{:S(2)}) copy-start(bf16[1152,256]{1,0:T(8,128)(2,1)} %ws_ref.3) | copy-start | bytes 1769476
  2.7 18.6 %collective-permute-start = (bf16[960,256]{1,0:T(8,128)(2,1)}, bf16[960,256]{1,0:T(8,128)(2,1)S(1)}, u32[]{:S(2)}, u32[]{:S(2)}) collective-permute-start(bf16[960,256]{1,0:T(8,128)(2,1)} %shard_map.101), channel_id=1, source_target_pairs={{0,16},{1,17},{2,18},{3,19},{4,20},{5,21},{6,22},{7,23},{8,24},{9,... | collective-permute-start | bytes 1474568 | tf_op jit(solution)/shard_map/ppermute | solution.py:405
  5.7 15.6 %collective-permute-start.1 = (bf16[256,256]{1,0:T(8,128)(2,1)S(1)}, bf16[256,256]{1,0:T(8,128)(2,1)S(1)}, u32[]{:S(2)}, u32[]{:S(2)}) collective-permute-start(bf16[256,256]{1,0:T(8,128)(2,1)S(1)} %bitcast.19), channel_id=1, source_target_pairs={{1,0},{2,1},{3,2},{4,3},{5,4},{6,5},{7,6},{8,7},{9,8},{10,9},{11,1... | collective-permute-start | bytes 393224 | tf_op jit(solution)/shard_map/ppermute | solution.py:419
  7.7 13.6 %all-to-all-start = ((f32[16,2,512]{2,1,0:T(2,128)}), f32[16,2,512]{2,1,0:T(2,128)S(1)}, u32[]{:S(2)}, u32[]{:S(2)}) async-start(f32[16,2,512]{2,1,0:T(2,128)} %shard_map.102), calls=%async_computation | async-start | bytes 131072 | tf_op jit(solution)/shard_map/all_to_all | solution.py:420
  21.2 1.9 %collective-permute-start.2 = (bf16[960,256]{1,0:T(8,128)(2,1)S(1)}, bf16[960,256]{1,0:T(8,128)(2,1)S(1)}, u32[]{:S(2)}, u32[]{:S(2)}) collective-permute-start(bf16[960,256]{1,0:T(8,128)(2,1)S(1)} %collective-permute-done.rest_0_), channel_id=1, source_target_pairs={{0,1},{1,0},{2,3},{3,2},{4,5},{5,4},{6,7},{7,6},{8,9},{9,8},{10,11... | collective-permute-start | bytes 1474568 | tf_op jit(solution)/shard_map/ppermute | solution.py:405
  22.3 2.6 %collective-permute-start.4 = (bf16[2,128,1152]{2,1,0:T(8,128)(2,1)S(1)}, bf16[2,128,1152]{2,1,0:T(8,128)(2,1)S(1)}, u32[]{:S(2)}, u32[]{:S(2)}) collective-permute-start(bf16[2,128,1152]{2,1,0:T(8,128)(2,1)S(1)} %get-tuple-element.37), channel_id=1, source_target_pairs={{0,1},{1,0},{2,3},{3,2},{4,5},{5,4},{6,7},{7,6},{8,9},{9,8},{10,11... | collective-permute-start | bytes 1769480 | tf_op jit(solution)/shard_map/ppermute | solution.py:405
  24.7 1.6 %collective-permute-start.5 = (bf16[2,128,512]{2,1,0:T(8,128)(2,1)S(1)}, bf16[2,128,512]{2,1,0:T(8,128)(2,1)S(1)}, u32[]{:S(2)}, u32[]{:S(2)}) collective-permute-start(bf16[2,128,512]{2,1,0:T(8,128)(2,1)S(1)} %get-tuple-element.39), channel_id=1, source_target_pairs={{0,1},{1,0},{2,3},{3,2},{4,5},{5,4},{6,7},{7,6},{8,9},{9,8},{10,11... | collective-permute-start | bytes 786440 | tf_op jit(solution)/shard_map/ppermute | solution.py:405
  26.6 7.4 %collective-permute-start.6 = (bf16[4,16,1664]{2,1,0:T(8,128)(2,1)S(1)}, bf16[4,16,1664]{2,1,0:T(8,128)(2,1)S(1)}, u32[]{:S(2)}, u32[]{:S(2)}) collective-permute-start(bf16[4,16,1664]{2,1,0:T(8,128)(2,1)S(1)} %get-tuple-element.41), channel_id=1, source_target_pairs={{0,2},{1,3},{2,0},{3,1},{4,6},{5,7},{6,4},{7,5},{8,10},{9,11},{10,... | collective-permute-start | bytes 638984 | tf_op jit(solution)/shard_map/ppermute | solution.py:405
  26.7 8.1 %collective-permute-start.7 = (bf16[4,16,1664]{2,1,0:T(8,128)(2,1)S(1)}, bf16[4,16,1664]{2,1,0:T(8,128)(2,1)S(1)}, u32[]{:S(2)}, u32[]{:S(2)}) collective-permute-start(bf16[4,16,1664]{2,1,0:T(8,128)(2,1)S(1)} %get-tuple-element.42), channel_id=1, source_target_pairs={{0,16},{1,17},{2,18},{3,19},{4,20},{5,21},{6,22},{7,23},{8,24},{9,... | collective-permute-start | bytes 638984 | tf_op jit(solution)/shard_map/ppermute | solution.py:405
  27.3 12.4 %collective-permute-start.8 = (bf16[4,16,1664]{2,1,0:T(8,128)(2,1)S(1)}, bf16[4,16,1664]{2,1,0:T(8,128)(2,1)S(1)}, u32[]{:S(2)}, u32[]{:S(2)}) collective-permute-start(bf16[4,16,1664]{2,1,0:T(8,128)(2,1)S(1)} %get-tuple-element.43), channel_id=1, source_target_pairs={{0,18},{1,19},{2,16},{3,17},{4,22},{5,23},{6,20},{7,21},{8,26},{9,... | collective-permute-start | bytes 638984 | tf_op jit(solution)/shard_map/ppermute | solution.py:405
  30.1 14.1 %collective-permute-start.3 = (bf16[256,256]{1,0:T(8,128)(2,1)S(1)}, bf16[256,256]{1,0:T(8,128)(2,1)S(1)}, u32[]{:S(2)}, u32[]{:S(2)}) collective-permute-start(bf16[256,256]{1,0:T(8,128)(2,1)S(1)} %get-tuple-element.35.spatial_ref), channel_id=1, source_target_pairs={{0,1},{1,2},{2,3},{3,4},{4,5},{5,6},{6,7},{7,8},{8,9},{9,10},{10,1... | collective-permute-start | bytes 393224 | tf_op jit(solution)/shard_map/ppermute | solution.py:455
  39.8 6.1 %collective-permute-start.9 = (bf16[16,1664]{1,0:T(8,128)(2,1)S(1)}, bf16[16,1664]{1,0:T(8,128)(2,1)S(1)}, u32[]{:S(2)}, u32[]{:S(2)}) collective-permute-start(bf16[16,1664]{1,0:T(8,128)(2,1)S(1)} %get-tuple-element.45), channel_id=1, source_target_pairs={{0,4},{1,5},{2,6},{3,7},{4,8},{5,9},{6,10},{7,11},{8,12},{9,13},{1... | collective-permute-start | bytes 159752 | tf_op jit(solution)/shard_map/ppermute | solution.py:405
  41.2 6.0 %collective-permute-start.10 = (bf16[16,1664]{1,0:T(8,128)(2,1)S(1)}, bf16[16,1664]{1,0:T(8,128)(2,1)S(1)}, u32[]{:S(2)}, u32[]{:S(2)}) collective-permute-start(bf16[16,1664]{1,0:T(8,128)(2,1)S(1)} %get-tuple-element.46), channel_id=1, source_target_pairs={{0,8},{1,9},{2,10},{3,11},{4,12},{5,13},{6,14},{7,15},{8,0},{9,1},... | collective-permute-start | bytes 159752 | tf_op jit(solution)/shard_map/ppermute | solution.py:405
  42.2 5.0 %collective-permute-start.11 = (bf16[16,1664]{1,0:T(8,128)(2,1)S(1)}, bf16[16,1664]{1,0:T(8,128)(2,1)S(1)}, u32[]{:S(2)}, u32[]{:S(2)}) collective-permute-start(bf16[16,1664]{1,0:T(8,128)(2,1)S(1)} %get-tuple-element.47), channel_id=1, source_target_pairs={{0,12},{1,13},{2,14},{3,15},{4,0},{5,1},{6,2},{7,3},{8,4},{9,5},{1... | collective-permute-start | bytes 159752 | tf_op jit(solution)/shard_map/ppermute | solution.py:405

commit v13 on v11

--- a/solution.py
+++ b/solution.py
@@ -56,18 +56,12 @@
     )
 
 
-def stats_body(lat_ref, gain_ref, bias_ref, ws_ref, wt_ref, out_ref, half_ref, *scratch):
-    lat_here, gain_here, bias_here, sems = scratch
-    core = lax.rem(lax.axis_index("wide"), 2)
-    moves = [(lat_ref, lat_here), (gain_ref, gain_here), (bias_ref, bias_here)]
-    half = ws_ref.shape[0] // 2
-    start = pl.multiple_of(core * half, 16)
-    moves.append((ws_ref.at[pl.ds(start, half)], half_ref.at[pl.ds(0, half)]))
-    moves.append((wt_ref, half_ref.at[pl.ds(half, wt_ref.shape[0])]))
+def stats_body(lat_ref, gain_ref, bias_ref, out_ref, lat_here, gain_here, bias_here, sems):
+    moves = ((lat_ref, lat_here), (gain_ref, gain_here), (bias_ref, bias_here))
     copies = [pltpu.make_async_copy(*move, sems.at[at]) for at, move in enumerate(moves)]
     for copy in copies:
         copy.start()
-    for copy in copies[:3]:
+    for copy in copies:
         copy.wait()
     x = lat_here[...].astype(F32)
     sums = [jnp.sum(x, axis=0, keepdims=True), jnp.sum(x * x, axis=0, keepdims=True)]
@@ -79,35 +73,30 @@
         axis=0,
     )
     out_ref[...] = jnp.broadcast_to(both[None], out_ref.shape)
-    for copy in copies[3:]:
-        copy.wait()
-
-
-def transpose_body(cot_ref, out_ref):
-    out_ref[...] = cot_ref[...].astype(F32).T.astype(BF16)
-
-
-def fill_spatial(full, shard_ref, pieces, D):
+
+
+def ready_body(cot_ref, lat_ref, wt_ref, cot_t_ref, *copies):
+    for source, target in zip((cot_ref, lat_ref, wt_ref), copies):
+        target[...] = source[...]
+    cot_t_ref[...] = cot_ref[...].astype(F32).T.astype(BF16)
+
+
+def fill_weights(full, shard_ref, pieces, fetcher, D):
     d = lax.axis_index("dp")
     core = lax.rem(lax.axis_index("wide"), 2)
-    n = shard_ref.shape[0]
-    half = n // 2
-    full[pl.ds(pl.multiple_of(d * n, 16), n)] = shard_ref[...]
-    for s in range(1, D):
-        source = lax.rem(d + D - s, D)
-        for which in range(2):
-            holder = core if which == 0 else 1 - core
-            start = pl.multiple_of(source * n + holder * half, 16)
-            full[pl.ds(start, half)] = pieces[2 * (s - 1) + which][0:half]
-
-
-def fill_temporal(full, shard_ref, firsts, D):
-    d = lax.axis_index("dp")
     n = shard_ref.shape[0]
     full[pl.ds(pl.multiple_of(d * n, 16), n)] = shard_ref[...]
     for s in range(1, D):
         start = pl.multiple_of(lax.rem(d + D - s, D) * n, 16)
-        full[pl.ds(start, n)] = firsts[s - 1][firsts[s - 1].shape[0] - n :]
+        fetched, passed_on = pieces[2 * (s - 1) : 2 * s]
+
+        @pl.when(core == fetcher)
+        def _(start=start, fetched=fetched):
+            full[pl.ds(start, n)] = fetched[...]
+
+        @pl.when(core != fetcher)
+        def _(start=start, passed_on=passed_on):
+            full[pl.ds(start, n)] = passed_on[...]
 
 
 def whiten(lat, stats, count, per_group):
@@ -191,13 +180,13 @@
 
 def first_body(sizes, lat_ref, cot_ref, halo_ref, stats_ref, wt_ref, *rest):
     D, W, frames, cells, cols, count, per_group, aligned = sizes
-    firsts, rest = rest[: D - 1], rest[D - 1 :]
+    pieces, rest = rest[: 2 * (D - 1)], rest[2 * (D - 1) :]
     full_wt, act_pad, gsa_t = rest[-3:]
     gsa_ref, seen_ref, keep_ref = rest[:3]
     send_ref = rest[3] if aligned else None
     channels = lat_ref.shape[1]
     core = lax.rem(lax.axis_index("wide"), 2)
-    fill_temporal(full_wt, wt_ref, firsts, D)
+    fill_weights(full_wt, wt_ref, pieces, 0, D)
     rows = frames * cells
     extended = jnp.concatenate([cot_ref[...], halo_ref[...]], axis=0)
     gsa = jnp.zeros((rows, channels), F32)
@@ -232,7 +221,7 @@
     send_ref = other_ref if aligned else None
     channels = lat_ref.shape[1]
     core = lax.rem(lax.axis_index("wide"), 2)
-    fill_spatial(full_ws, ws_ref, pieces, D)
+    fill_weights(full_ws, ws_ref, pieces, 1, D)
     rows = frames * cells
     white, normed, sig = normalise(lat_ref, stats_ref, count, per_group)
     store_shifted(gsa_pad, gsa_ref[...].astype(F32), frames, cells, cols)
@@ -280,10 +269,10 @@
 
 def block_body(sizes, lat_ref, spatial_ref, before_ref, wt_ref, *rest):
     D, W, frames, cells, cols, count, per_group, aligned = sizes
-    firsts = rest[: D - 1]
-    block_ref, full_wt = rest[D - 1 :]
+    pieces = rest[: 2 * (D - 1)]
+    block_ref, full_wt = rest[2 * (D - 1) :]
     channels = lat_ref.shape[1]
-    fill_temporal(full_wt, wt_ref, firsts, D)
+    fill_weights(full_wt, wt_ref, pieces, 0, D)
     extended = jnp.concatenate([before_ref[...], spatial_ref[...]], axis=0)
     rows = frames * cells
     temporal = jnp.zeros((rows, channels), F32)
@@ -404,30 +393,56 @@
         return lax.ppermute(value, ("dp", "wide"), over_all(moves))
 
     R = shard_s + shard_t
-    stats, half = call(
+    def fetch(value, core):
+        return [
+            lax.ppermute(
+                value,
+                ("dp", "wide"),
+                [
+                    (d * W + w, (d + s) % D * W + w)
+                    for d in range(D)
+                    for w in range(core, W, 2)
+                ],
+            )
+            for s in range(1, D)
+        ]
+
+    def pass_on(values, core):
+        pairs = [(w, w ^ 1) for w in range(core, W, 2)]
+        return [lax.ppermute(value, "wide", pairs) for value in values]
+
+    firsts = (fetch(w_temporal, 0), fetch(w_spatial, 1))
+    stats = call(
         stats_body,
-        [
-            shape((W, 2, 2 * channels), F32),
-            shape((shard_s // 2 + shard_t, channels), BF16),
-        ],
+        shape((W, 2, 2 * channels), F32),
         [
             pltpu.VMEM((rows, channels), BF16),
             pltpu.VMEM((1, channels), F32),
             pltpu.VMEM((1, channels), F32),
-            pltpu.SemaphoreType.DMA((5,)),
+            pltpu.SemaphoreType.DMA((3,)),
         ],
-        in_specs=[HBM] * 5,
+        in_specs=[HBM] * 3,
         vmem=FIRST_VMEM,
-    )(lat, gain, bias, w_spatial, w_temporal)
-    cot_t = call(transpose_body, shape((channels, rows), BF16), moved=300_000)(cot)
-    firsts = [send(half, lambda d, w: ((d + s) % D, w)) for s in range(1, D)]
+    )(lat, gain, bias)
+    ready = call(
+        ready_body,
+        [
+            shape((channels, rows), BF16),
+            shape((rows, channels), BF16),
+            shape((rows, channels), BF16),
+            shape((shard_t, channels), BF16),
+        ],
+        moved=1_000_000,
+    )(cot, lat, w_temporal)
 
     halo = lax.ppermute(cot, "wide", [(w + 1, w) for w in range(W - 1)])
     stats = lax.all_to_all(stats, "wide", split_axis=0, concat_axis=0, tiled=True)
-    firsts, stats, halo, cot_t = lax.optimization_barrier((firsts, stats, halo, cot_t))
-    pieces = []
-    for first in firsts:
-        pieces += [first, send(first, lambda d, w: (d, w ^ 1))]
+    firsts, stats, halo, ready = lax.optimization_barrier((firsts, stats, halo, ready))
+    cot_t, cot, lat, w_temporal = ready
+    pieces_t, pieces_s = (
+        [piece for pair in zip(values, pass_on(values, core)) for piece in pair]
+        for core, values in enumerate(firsts)
+    )
 
     ride = 128 if aligned else 0
     if aligned:
@@ -444,7 +459,7 @@
         [pltpu.VMEM((D * shard_t, channels), BF16), pad, pltpu.VMEM((channels, rows), BF16)],
         flops=2 * 12 * rows * channels * channels,
         moved=3_000_000,
-    )(lat, cot, halo, stats, w_temporal, *firsts)
+    )(lat, cot, halo, stats, w_temporal, *pieces_t)
     spatial, grad, *grads_t = call(
         functools.partial(second_body, sizes),
         [shape((rows, channels), BF16), shape((rows, channels), F32)] + terms_t,
@@ -457,7 +472,7 @@
         ],
         flops=2 * 21 * rows * channels * channels,
         moved=3_000_000,
-    )(lat, cot_t, halo, stats, gsa, seen, w_spatial, *pieces)
+    )(lat, cot_t, halo, stats, gsa, seen, w_spatial, *pieces_s)
     before = lax.ppermute(spatial, "wide", [(w, w + 1) for w in range(W - 1)])
     block_out = call(
         functools.partial(block_body, sizes),
@@ -465,7 +480,7 @@
         [pltpu.VMEM((D * shard_t, channels), BF16)],
         flops=2 * 3 * rows * channels * channels,
         moved=1_000_000,
-    )(lat, spatial, before, w_temporal, *firsts)
+    )(lat, spatial, before, w_temporal, *pieces_t)
 
     width = channels // W
     operands = (lat, cot, stats, grad)

time: 48 us -> 55.4 us (1.15)
  starting transfers between devices: 21 us -> 27.9 us
  local copies, waits for them, and re-layouts: 0.92 us -> 2.73 us
  waiting for transfers between devices: 17.8 us -> 16.8 us
    ppermute x0 -> x4, starting transfers between devices: none -> 10 us  [the longest x2 5.68 us: fetch(): lax.ppermute(value, ('dp', 'wide'), [(d * W + w, (d + s) % D * W + w) for...]
    ppermute x10 -> x8, starting transfers between devices: 11.7 us -> 8.62 us  [send(): return lax.ppermute(value, ('dp', 'wide'), over_all(moves))]
    all_to_all x1, waiting for transfers between devices: 5.88 us -> 4.05 us  [local(): lax.all_to_all(stats, 'wide', split_axis=0, concat_axis=0, tiled=True)]
    unnamed x10 -> x8, local copies, waits for them, and re-layouts: 0.92 us -> 2.73 us
    ppermute x0 -> x4, waiting for transfers between devices: none -> 1.05 us  [the longest x2 1.04 us: pass_on(): return [lax.ppermute(value, 'wide', pairs) for value in values]]
    ppermute x10 -> x8, waiting for transfers between devices: 11.9 us -> 11.7 us  [send(): return lax.ppermute(value, ('dp', 'wide'), over_all(moves))]
  transfers between devices with their start and end apart: 13 -> 15, of which waited for: 8 -> 8; matrix products, arithmetic and copies ran while one was open for 0% -> 0% of each run, Pallas kernels for 8% -> 10%
where the time goes in v13:
time: 55.4 us; the launch traced here: 55 us
  starting transfers between devices  27.9 us (50%)
  waiting for transfers between devices  16.8 us (30%)
  Pallas kernels  6.84 us (12%)
  local copies, waits for them, and re-layouts  2.73 us (5%)
  between operations  0.75 us (1%)
    ppermute x8, waiting for transfers between devices, send(): return lax.ppermute(value, ('dp', 'wide'), over_all(moves))  11.7 us
    ppermute x8, starting transfers between devices, send(): return lax.ppermute(value, ('dp', 'wide'), over_all(moves))  8.62 us
    pallas_call x8, Pallas kernels, run(): pl.pallas_call(body, out_shape=out_shapes, in_specs=in_specs or [VMEM] *...  6.84 us
    all_to_all x1, starting transfers between devices, local(): lax.all_to_all(stats, 'wide', split_axis=0, concat_axis=0, tiled=True)  6.69 us
    ppermute x2, starting transfers between devices, fetch(): lax.ppermute(value, ('dp', 'wide'), [(d * W + w, (d + s) % D * W + w) for...  5.68 us
    ppermute x2, starting transfers between devices, pass_on(): return [lax.ppermute(value, 'wide', pairs) for value in values]  4.37 us
    all_to_all x1, waiting for transfers between devices, local(): lax.all_to_all(stats, 'wide', split_axis=0, concat_axis=0, tiled=True)  4.05 us
    unnamed x8, local copies, waits for them, and re-layouts  2.73 us
  transfers between devices with their start and end apart: 15, of which 8 were waited for; matrix products, arithmetic and copies ran while one was open for 0% of the time, Pallas kernels for 10%

profile of v13, /device:TPU:0, one launch (start us, length us, event | category | flops | bytes accessed | tf_op | source)
XLA Modules:
  0.0 55.0 jit_solution(17434900575431450456)
XLA Ops:
  0.6 0.8 %collective-permute-start.1 = (bf16[1152,256]{1,0:T(8,128)(2,1)}, bf16[1152,256]{1,0:T(8,128)(2,1)S(1)}, u32[]{:S(2)}, u32[]{:S(2)}) collective-permute-start(bf16[1152,256]{1,0:T(8,128)(2,1)} %ws_ref.1), channel_id=1, source_target_pairs={{1,17},{3,19},{5,21},{7,23},{9,25},{11,27},{13,29},{15,31},{17,1},... | collective-permute-start | bytes 1769480 | tf_op jit(solution)/shard_map/ppermute | solution.py:398
  1.5 4.8 %collective-permute-start = (bf16[384,256]{1,0:T(8,128)(2,1)}, bf16[384,256]{1,0:T(8,128)(2,1)S(1)}, u32[]{:S(2)}, u32[]{:S(2)}) collective-permute-start(bf16[384,256]{1,0:T(8,128)(2,1)} %wt_ref.1), channel_id=1, source_target_pairs={{0,16},{2,18},{4,20},{6,22},{8,24},{10,26},{12,28},{14,30},{16,0},... | collective-permute-start | bytes 589832 | tf_op jit(solution)/shard_map/ppermute | solution.py:398
  6.3 1.3 %collective-permute-start.2 = (bf16[256,256]{1,0:T(8,128)(2,1)}, bf16[256,256]{1,0:T(8,128)(2,1)S(1)}, u32[]{:S(2)}, u32[]{:S(2)}) collective-permute-start(bf16[256,256]{1,0:T(8,128)(2,1)} %bitcast.18), channel_id=1, source_target_pairs={{1,0},{2,1},{3,2},{4,3},{5,4},{6,5},{7,6},{8,7},{9,8},{10,9},{11,1... | collective-permute-start | bytes 393224 | tf_op jit(solution)/shard_map/ppermute | solution.py:438
  7.6 1.6 %shard_map.101 = f32[16,2,512]{2,1,0:T(2,128)} custom-call(bf16[256,256]{1,0:T(8,128)(2,1)} %bitcast.14, f32[1,256]{1,0:T(1,128)} %bitcast.21, f32[1,256]{1,0:T(1,128)} %bitcast.22), custom_call_target="tpu_custom_call" | custom-call | tf_op jit(solution)/shard_map/pallas_call | solution.py:26
  9.3 6.7 %all-to-all-start = ((f32[16,2,512]{2,1,0:T(2,128)}), f32[16,2,512]{2,1,0:T(2,128)S(1)}, u32[]{:S(2)}, u32[]{:S(2)}) async-start(f32[16,2,512]{2,1,0:T(2,128)} %shard_map.101), calls=%async_computation | async-start | bytes 131072 | tf_op jit(solution)/shard_map/all_to_all | solution.py:439
  16.0 0.9 %copy-done.1 = bf16[1,2,8,16,256]{4,3,2,1,0:T(8,128)(2,1)S(1)} copy-done((bf16[1,2,8,16,256]{4,3,2,1,0:T(8,128)(2,1)S(1)}, bf16[1,2,8,16,256]{4,3,2,1,0:T(8,128)(2,1)}, u32[]{:S(2)}) %copy-start.1) | copy-done | bytes 131096
  16.9 0.9 %copy-done.2 = bf16[384,256]{1,0:T(8,128)(2,1)S(1)} copy-done((bf16[384,256]{1,0:T(8,128)(2,1)S(1)}, bf16[384,256]{1,0:T(8,128)(2,1)}, u32[]{:S(2)}) %copy-start.2) | copy-done | bytes 196632
  17.8 0.9 %copy-done.3 = bf16[1,2,8,16,256]{4,3,2,1,0:T(8,128)(2,1)S(1)} copy-done((bf16[1,2,8,16,256]{4,3,2,1,0:T(8,128)(2,1)S(1)}, bf16[1,2,8,16,256]{4,3,2,1,0:T(8,128)(2,1)}, u32[]{:S(2)}) %copy-start.3) | copy-done | bytes 131096
  18.8 4.1 %all-to-all-done.stats_ref.refs_6_ = f32[16,2,512]{2,1,0:T(2,128)S(1)} async-done(((f32[16,2,512]{2,1,0:T(2,128)}), f32[16,2,512]{2,1,0:T(2,128)S(1)}, u32[]{:S(2)}, u32[]{:S(2)}) %all-to-all-start) | async-done | bytes 65568 | tf_op jit(solution)/shard_map/all_to_all | solution.py:439
  22.9 1.3 %collective-permute-start.4 = (bf16[1152,256]{1,0:T(8,128)(2,1)S(1)}, bf16[1152,256]{1,0:T(8,128)(2,1)S(1)}, u32[]{:S(2)}, u32[]{:S(2)}) collective-permute-start(bf16[1152,256]{1,0:T(8,128)(2,1)S(1)} %collective-permute-done.1.rest_0_), channel_id=1, source_target_pairs={{1,0},{3,2},{5,4},{7,6},{9,8},{11,10},{13,12},{15,14},{17,16},{19,... | collective-permute-start | bytes 1769480 | tf_op jit(solution)/shard_map/ppermute | solution.py:412
  24.2 3.1 %collective-permute-start.3 = (bf16[384,256]{1,0:T(8,128)(2,1)S(1)}, bf16[384,256]{1,0:T(8,128)(2,1)S(1)}, u32[]{:S(2)}, u32[]{:S(2)}) collective-permute-start(bf16[384,256]{1,0:T(8,128)(2,1)S(1)} %collective-permute-done.rest_0_), channel_id=1, source_target_pairs={{0,1},{2,3},{4,5},{6,7},{8,9},{10,11},{12,13},{14,15},{16,17},{18,... | collective-permute-start | bytes 589832 | tf_op jit(solution)/shard_map/ppermute | solution.py:412
  27.2 1.0 %collective-permute-done.3.rest_1_ = bf16[384,256]{1,0:T(8,128)(2,1)S(1)} collective-permute-done((bf16[384,256]{1,0:T(8,128)(2,1)S(1)}, bf16[384,256]{1,0:T(8,128)(2,1)S(1)}, u32[]{:S(2)}, u32[]{:S(2)}) %collective-permute-start.3) | collective-permute-done | bytes 196640 | tf_op jit(solution)/shard_map/ppermute | solution.py:412
  28.3 1.0 %shard_map.103 = (bf16[256,256]{1,0:T(8,128)(2,1)S(1)}, bf16[256,2304]{1,0:T(8,128)(2,1)S(1)}, bf16[2,128,1152]{2,1,0:T(8,128)(2,1)S(1)}, bf16[2,128,1152]{2,1,0:T(8,128)(2,1)S(1)}) custom-call(bf16[256,256]{1,0:T(8,128)(2,1)S(1)} %get-tuple-element.41.lat_ref.refs_4_, bf16[256,256]{1,0:T(8,128)(2,1)S(1)} %get-tuple-element.45.cot_ref.refs_5_, ...), custom_call_target="tpu_custom_call" | custom-call | flops 402653184 | bytes 3000000 | tf_op jit(solution)/shard_map/pallas_call | solution.py:26
  29.3 0.4 collective-permute-start.6
  29.8 1.6 %shard_map.104 = (bf16[256,256]{1,0:T(8,128)(2,1)S(1)}, f32[256,256]{1,0:T(8,128)S(1)}, bf16[2,128,512]{2,1,0:T(8,128)(2,1)S(1)}, bf16[2,128,512]{2,1,0:T(8,128)(2,1)S(1)}) custom-call(bf16[256,256]{1,0:T(8,128)(2,1)S(1)} %get-tuple-element.41.lat_ref.refs_4_, bf16[256,256]{1,0:T(8,128)(2,1)S(1)} %get-tuple-element.42.cot_t_ref, ...), custom_call_target="tpu_custom_call" | custom-call | flops 704643072 | bytes 3000000 | tf_op jit(solution)/shard_map/pallas_call | solution.py:26
  31.4 0.2 collective-permute-start.7
  31.6 1.4 %collective-permute-done.7 = bf16[2,128,512]{2,1,0:T(8,128)(2,1)S(1)} collective-permute-done((bf16[2,128,512]{2,1,0:T(8,128)(2,1)S(1)}, bf16[2,128,512]{2,1,0:T(8,128)(2,1)S(1)}, u32[]{:S(2)}, u32[]{:S(2)}) %collective-permute-start.7) | collective-permute-done | bytes 262176 | tf_op jit(solution)/shard_map/ppermute | solution.py:393
  33.0 0.2 shard_map.106
  33.3 0.2 collective-permute-start.8
  33.4 0.5 collective-permute-start.9
  34.0 2.8 %collective-permute-start.10 = (bf16[4,16,1664]{2,1,0:T(8,128)(2,1)S(1)}, bf16[4,16,1664]{2,1,0:T(8,128)(2,1)S(1)}, u32[]{:S(2)}, u32[]{:S(2)}) collective-permute-start(bf16[4,16,1664]{2,1,0:T(8,128)(2,1)S(1)} %get-tuple-element.59), channel_id=1, source_target_pairs={{0,18},{1,19},{2,16},{3,17},{4,22},{5,23},{6,20},{7,21},{8,26},{9,... | collective-permute-start | bytes 638984 | tf_op jit(solution)/shard_map/ppermute | solution.py:393
  36.8 1.3 %collective-permute-start.5 = (bf16[256,256]{1,0:T(8,128)(2,1)S(1)}, bf16[256,256]{1,0:T(8,128)(2,1)S(1)}, u32[]{:S(2)}, u32[]{:S(2)}) collective-permute-start(bf16[256,256]{1,0:T(8,128)(2,1)S(1)} %get-tuple-element.51.spatial_ref), channel_id=1, source_target_pairs={{0,1},{1,2},{2,3},{3,4},{4,5},{5,6},{6,7},{7,8},{8,9},{9,10},{10,1... | collective-permute-start | bytes 393224 | tf_op jit(solution)/shard_map/ppermute | solution.py:476
  38.1 2.5 %collective-permute-done.8.refs_1_ = bf16[4,16,1664]{2,1,0:T(8,128)(2,1)S(1)} collective-permute-done((bf16[4,16,1664]{2,1,0:T(8,128)(2,1)S(1)}, bf16[4,16,1664]{2,1,0:T(8,128)(2,1)S(1)}, u32[]{:S(2)}, u32[]{:S(2)}) %collective-permute-start.8) | collective-permute-done | bytes 213024 | tf_op jit(solution)/shard_map/ppermute | solution.py:393
  40.6 0.9 %collective-permute-done.9.refs_2_ = bf16[4,16,1664]{2,1,0:T(8,128)(2,1)S(1)} collective-permute-done((bf16[4,16,1664]{2,1,0:T(8,128)(2,1)S(1)}, bf16[4,16,1664]{2,1,0:T(8,128)(2,1)S(1)}, u32[]{:S(2)}, u32[]{:S(2)}) %collective-permute-start.9) | collective-permute-done | bytes 213024 | tf_op jit(solution)/shard_map/ppermute | solution.py:393
  41.5 4.8 %collective-permute-done.10.refs_3_ = bf16[4,16,1664]{2,1,0:T(8,128)(2,1)S(1)} collective-permute-done((bf16[4,16,1664]{2,1,0:T(8,128)(2,1)S(1)}, bf16[4,16,1664]{2,1,0:T(8,128)(2,1)S(1)}, u32[]{:S(2)}, u32[]{:S(2)}) %collective-permute-start.10) | collective-permute-done | bytes 213024 | tf_op jit(solution)/shard_map/ppermute | solution.py:393
  46.5 1.4 %collective-permute-start.11 = (bf16[16,1664]{1,0:T(8,128)(2,1)S(1)}, bf16[16,1664]{1,0:T(8,128)(2,1)S(1)}, u32[]{:S(2)}, u32[]{:S(2)}) collective-permute-start(bf16[16,1664]{1,0:T(8,128)(2,1)S(1)} %get-tuple-element.61), channel_id=1, source_target_pairs={{0,4},{1,5},{2,6},{3,7},{4,8},{5,9},{6,10},{7,11},{8,12},{9,13},{1... | collective-permute-start | bytes 159752 | tf_op jit(solution)/shard_map/ppermute | solution.py:393
  47.9 1.0 %collective-permute-start.12 = (bf16[16,1664]{1,0:T(8,128)(2,1)S(1)}, bf16[16,1664]{1,0:T(8,128)(2,1)S(1)}, u32[]{:S(2)}, u32[]{:S(2)}) collective-permute-start(bf16[16,1664]{1,0:T(8,128)(2,1)S(1)} %get-tuple-element.62), channel_id=1, source_target_pairs={{0,8},{1,9},{2,10},{3,11},{4,12},{5,13},{6,14},{7,15},{8,0},{9,1},... | collective-permute-start | bytes 159752 | tf_op jit(solution)/shard_map/ppermute | solution.py:393
  48.9 2.0 %collective-permute-start.13 = (bf16[16,1664]{1,0:T(8,128)(2,1)S(1)}, bf16[16,1664]{1,0:T(8,128)(2,1)S(1)}, u32[]{:S(2)}, u32[]{:S(2)}) collective-permute-start(bf16[16,1664]{1,0:T(8,128)(2,1)S(1)} %get-tuple-element.63), channel_id=1, source_target_pairs={{0,12},{1,13},{2,14},{3,15},{4,0},{5,1},{6,2},{7,3},{8,4},{9,5},{1... | collective-permute-start | bytes 159752 | tf_op jit(solution)/shard_map/ppermute | solution.py:393
  50.9 1.0 %shard_map.105 = bf16[256,256]{1,0:T(8,128)(2,1)} custom-call(bf16[256,256]{1,0:T(8,128)(2,1)S(1)} %get-tuple-element.41.lat_ref.refs_4_, bf16[256,256]{1,0:T(8,128)(2,1)S(1)} %get-tuple-element.51.spatial_ref, bf16[256,256]{1,0:T(8,128)(2,1)S(1)} %collective-permute-done.5.before_ref, bf16[384,256]{1,0:T(8,128)(2,1)S(1)} %get-tuple-element.46.wt_ref, ...), custom_call_target="tpu_custom_call" | custom-call | flops 100663296 | bytes 1000000 | tf_op jit(solution)/shard_map/pallas_call | solution.py:26
  51.9 0.7 %collective-permute-done.11.refs_1_ = bf16[16,1664]{1,0:T(8,128)(2,1)S(1)} collective-permute-done((bf16[16,1664]{1,0:T(8,128)(2,1)S(1)}, bf16[16,1664]{1,0:T(8,128)(2,1)S(1)}, u32[]{:S(2)}, u32[]{:S(2)}) %collective-permute-start.11) | collective-permute-done | bytes 53280 | tf_op jit(solution)/shard_map/ppermute | solution.py:393
  52.6 1.3 %collective-permute-done.12.refs_2_ = bf16[16,1664]{1,0:T(8,128)(2,1)S(1)} collective-permute-done((bf16[16,1664]{1,0:T(8,128)(2,1)S(1)}, bf16[16,1664]{1,0:T(8,128)(2,1)S(1)}, u32[]{:S(2)}, u32[]{:S(2)}) %collective-permute-start.12) | collective-permute-done | bytes 53280 | tf_op jit(solution)/shard_map/ppermute | solution.py:393
  53.9 1.1 %shard_map.108 = (f32[16,1152]{1,0:T(8,128)}, f32[16,384]{1,0:T(8,128)}, f32[2,16]{1,0:T(2,128)}, bf16[256,256]{1,0:T(8,128)(2,1)}) custom-call(bf16[16,1664]{1,0:T(8,128)(2,1)S(1)} %get-tuple-element.60.refs_0_, bf16[16,1664]{1,0:T(8,128)(2,1)S(1)} %collective-permute-done.11.refs_1_, bf16[16,1664]{1,0:T(8,128)(2,1)S(1)} %collective-permute-done.12.refs_2_, ...), custom_call_target="tpu_custom_call" | custom-call | bytes 1000000 | tf_op jit(solution)/shard_map/pallas_call | solution.py:26
  (14 shorter events, 0.2 us)
Async XLA Ops:
  0.6 29.2 %copy-start = (bf16[1152,256]{1,0:T(8,128)(2,1)S(1)}, bf16[1152,256]{1,0:T(8,128)(2,1)}, u32[]{:S(2)}) copy-start(bf16[1152,256]{1,0:T(8,128)(2,1)} %ws_ref.1) | copy-start | bytes 1769476
  0.6 22.2 %collective-permute-start.1 = (bf16[1152,256]{1,0:T(8,128)(2,1)}, bf16[1152,256]{1,0:T(8,128)(2,1)S(1)}, u32[]{:S(2)}, u32[]{:S(2)}) collective-permute-start(bf16[1152,256]{1,0:T(8,128)(2,1)} %ws_ref.1), channel_id=1, source_target_pairs={{1,17},{3,19},{5,21},{7,23},{9,25},{11,27},{13,29},{15,31},{17,1},... | collective-permute-start | bytes 1769480 | tf_op jit(solution)/shard_map/ppermute | solution.py:398
  1.5 21.4 %collective-permute-start = (bf16[384,256]{1,0:T(8,128)(2,1)}, bf16[384,256]{1,0:T(8,128)(2,1)S(1)}, u32[]{:S(2)}, u32[]{:S(2)}) collective-permute-start(bf16[384,256]{1,0:T(8,128)(2,1)} %wt_ref.1), channel_id=1, source_target_pairs={{0,16},{2,18},{4,20},{6,22},{8,24},{10,26},{12,28},{14,30},{16,0},... | collective-permute-start | bytes 589832 | tf_op jit(solution)/shard_map/ppermute | solution.py:398
  6.3 16.5 %collective-permute-start.2 = (bf16[256,256]{1,0:T(8,128)(2,1)}, bf16[256,256]{1,0:T(8,128)(2,1)S(1)}, u32[]{:S(2)}, u32[]{:S(2)}) collective-permute-start(bf16[256,256]{1,0:T(8,128)(2,1)} %bitcast.18), channel_id=1, source_target_pairs={{1,0},{2,1},{3,2},{4,3},{5,4},{6,5},{7,6},{8,7},{9,8},{10,9},{11,1... | collective-permute-start | bytes 393224 | tf_op jit(solution)/shard_map/ppermute | solution.py:438
  9.3 13.6 %all-to-all-start = ((f32[16,2,512]{2,1,0:T(2,128)}), f32[16,2,512]{2,1,0:T(2,128)S(1)}, u32[]{:S(2)}, u32[]{:S(2)}) async-start(f32[16,2,512]{2,1,0:T(2,128)} %shard_map.101), calls=%async_computation | async-start | bytes 131072 | tf_op jit(solution)/shard_map/all_to_all | solution.py:439
  16.0 0.9 %copy-start.1 = (bf16[1,2,8,16,256]{4,3,2,1,0:T(8,128)(2,1)S(1)}, bf16[1,2,8,16,256]{4,3,2,1,0:T(8,128)(2,1)}, u32[]{:S(2)}) copy-start(bf16[1,2,8,16,256]{4,3,2,1,0:T(8,128)(2,1)} %param.6) | copy-start | bytes 393220
  16.9 0.9 %copy-start.2 = (bf16[384,256]{1,0:T(8,128)(2,1)S(1)}, bf16[384,256]{1,0:T(8,128)(2,1)}, u32[]{:S(2)}) copy-start(bf16[384,256]{1,0:T(8,128)(2,1)} %wt_ref.1) | copy-start | bytes 589828
  17.8 0.9 %copy-start.3 = (bf16[1,2,8,16,256]{4,3,2,1,0:T(8,128)(2,1)S(1)}, bf16[1,2,8,16,256]{4,3,2,1,0:T(8,128)(2,1)}, u32[]{:S(2)}) copy-start(bf16[1,2,8,16,256]{4,3,2,1,0:T(8,128)(2,1)} %param.7) | copy-start | bytes 393220
  22.9 6.9 %collective-permute-start.4 = (bf16[1152,256]{1,0:T(8,128)(2,1)S(1)}, bf16[1152,256]{1,0:T(8,128)(2,1)S(1)}, u32[]{:S(2)}, u32[]{:S(2)}) collective-permute-start(bf16[1152,256]{1,0:T(8,128)(2,1)S(1)} %collective-permute-done.1.rest_0_), channel_id=1, source_target_pairs={{1,0},{3,2},{5,4},{7,6},{9,8},{11,10},{13,12},{15,14},{17,16},{19,... | collective-permute-start | bytes 1769480 | tf_op jit(solution)/shard_map/ppermute | solution.py:412
  24.2 4.1 %collective-permute-start.3 = (bf16[384,256]{1,0:T(8,128)(2,1)S(1)}, bf16[384,256]{1,0:T(8,128)(2,1)S(1)}, u32[]{:S(2)}, u32[]{:S(2)}) collective-permute-start(bf16[384,256]{1,0:T(8,128)(2,1)S(1)} %collective-permute-done.rest_0_), channel_id=1, source_target_pairs={{0,1},{2,3},{4,5},{6,7},{8,9},{10,11},{12,13},{14,15},{16,17},{18,... | collective-permute-start | bytes 589832 | tf_op jit(solution)/shard_map/ppermute | solution.py:412
  29.3 2.3 %collective-permute-start.6 = (bf16[2,128,1152]{2,1,0:T(8,128)(2,1)S(1)}, bf16[2,128,1152]{2,1,0:T(8,128)(2,1)S(1)}, u32[]{:S(2)}, u32[]{:S(2)}) collective-permute-start(bf16[2,128,1152]{2,1,0:T(8,128)(2,1)S(1)} %get-tuple-element.53), channel_id=1, source_target_pairs={{0,1},{1,0},{2,3},{3,2},{4,5},{5,4},{6,7},{7,6},{8,9},{9,8},{10,11... | collective-permute-start | bytes 1769480 | tf_op jit(solution)/shard_map/ppermute | solution.py:393
  31.4 1.6 %collective-permute-start.7 = (bf16[2,128,512]{2,1,0:T(8,128)(2,1)S(1)}, bf16[2,128,512]{2,1,0:T(8,128)(2,1)S(1)}, u32[]{:S(2)}, u32[]{:S(2)}) collective-permute-start(bf16[2,128,512]{2,1,0:T(8,128)(2,1)S(1)} %get-tuple-element.55), channel_id=1, source_target_pairs={{0,1},{1,0},{2,3},{3,2},{4,5},{5,4},{6,7},{7,6},{8,9},{9,8},{10,11... | collective-permute-start | bytes 786440 | tf_op jit(solution)/shard_map/ppermute | solution.py:393
  33.3 7.4 %collective-permute-start.8 = (bf16[4,16,1664]{2,1,0:T(8,128)(2,1)S(1)}, bf16[4,16,1664]{2,1,0:T(8,128)(2,1)S(1)}, u32[]{:S(2)}, u32[]{:S(2)}) collective-permute-start(bf16[4,16,1664]{2,1,0:T(8,128)(2,1)S(1)} %get-tuple-element.57), channel_id=1, source_target_pairs={{0,2},{1,3},{2,0},{3,1},{4,6},{5,7},{6,4},{7,5},{8,10},{9,11},{10,... | collective-permute-start | bytes 638984 | tf_op jit(solution)/shard_map/ppermute | solution.py:393
  33.4 8.1 %collective-permute-start.9 = (bf16[4,16,1664]{2,1,0:T(8,128)(2,1)S(1)}, bf16[4,16,1664]{2,1,0:T(8,128)(2,1)S(1)}, u32[]{:S(2)}, u32[]{:S(2)}) collective-permute-start(bf16[4,16,1664]{2,1,0:T(8,128)(2,1)S(1)} %get-tuple-element.58), channel_id=1, source_target_pairs={{0,16},{1,17},{2,18},{3,19},{4,20},{5,21},{6,22},{7,23},{8,24},{9,... | collective-permute-start | bytes 638984 | tf_op jit(solution)/shard_map/ppermute | solution.py:393
  34.0 12.4 %collective-permute-start.10 = (bf16[4,16,1664]{2,1,0:T(8,128)(2,1)S(1)}, bf16[4,16,1664]{2,1,0:T(8,128)(2,1)S(1)}, u32[]{:S(2)}, u32[]{:S(2)}) collective-permute-start(bf16[4,16,1664]{2,1,0:T(8,128)(2,1)S(1)} %get-tuple-element.59), channel_id=1, source_target_pairs={{0,18},{1,19},{2,16},{3,17},{4,22},{5,23},{6,20},{7,21},{8,26},{9,... | collective-permute-start | bytes 638984 | tf_op jit(solution)/shard_map/ppermute | solution.py:393
  36.8 14.1 %collective-permute-start.5 = (bf16[256,256]{1,0:T(8,128)(2,1)S(1)}, bf16[256,256]{1,0:T(8,128)(2,1)S(1)}, u32[]{:S(2)}, u32[]{:S(2)}) collective-permute-start(bf16[256,256]{1,0:T(8,128)(2,1)S(1)} %get-tuple-element.51.spatial_ref), channel_id=1, source_target_pairs={{0,1},{1,2},{2,3},{3,4},{4,5},{5,6},{6,7},{7,8},{8,9},{9,10},{10,1... | collective-permute-start | bytes 393224 | tf_op jit(solution)/shard_map/ppermute | solution.py:476
  46.5 6.1 %collective-permute-start.11 = (bf16[16,1664]{1,0:T(8,128)(2,1)S(1)}, bf16[16,1664]{1,0:T(8,128)(2,1)S(1)}, u32[]{:S(2)}, u32[]{:S(2)}) collective-permute-start(bf16[16,1664]{1,0:T(8,128)(2,1)S(1)} %get-tuple-element.61), channel_id=1, source_target_pairs={{0,4},{1,5},{2,6},{3,7},{4,8},{5,9},{6,10},{7,11},{8,12},{9,13},{1... | collective-permute-start | bytes 159752 | tf_op jit(solution)/shard_map/ppermute | solution.py:393
  47.9 6.0 %collective-permute-start.12 = (bf16[16,1664]{1,0:T(8,128)(2,1)S(1)}, bf16[16,1664]{1,0:T(8,128)(2,1)S(1)}, u32[]{:S(2)}, u32[]{:S(2)}) collective-permute-start(bf16[16,1664]{1,0:T(8,128)(2,1)S(1)} %get-tuple-element.62), channel_id=1, source_target_pairs={{0,8},{1,9},{2,10},{3,11},{4,12},{5,13},{6,14},{7,15},{8,0},{9,1},... | collective-permute-start | bytes 159752 | tf_op jit(solution)/shard_map/ppermute | solution.py:393
  48.9 5.0 %collective-permute-start.13 = (bf16[16,1664]{1,0:T(8,128)(2,1)S(1)}, bf16[16,1664]{1,0:T(8,128)(2,1)S(1)}, u32[]{:S(2)}, u32[]{:S(2)}) collective-permute-start(bf16[16,1664]{1,0:T(8,128)(2,1)S(1)} %get-tuple-element.63), channel_id=1, source_target_pairs={{0,12},{1,13},{2,14},{3,15},{4,0},{5,1},{6,2},{7,3},{8,4},{9,5},{1... | collective-permute-start | bytes 159752 | tf_op jit(solution)/shard_map/ppermute | solution.py:393

commit v14 on v11

--- a/solution.py
+++ b/solution.py
@@ -19,7 +19,7 @@
 NN = (((1,), (0,)), ((), ()))
 
 
-def call(body, out_shapes, scratch=(), flops=0, moved=0, in_specs=None, vmem=40 << 20):
+def call(body, out_shapes, scratch=(), flops=0, moved=0, in_specs=None, out_specs=None, vmem=40 << 20):
     many = isinstance(out_shapes, (tuple, list))
 
     def run(*operands):
@@ -27,7 +27,7 @@
             body,
             out_shape=out_shapes,
             in_specs=in_specs or [VMEM] * len(operands),
-            out_specs=[VMEM] * len(out_shapes) if many else VMEM,
+            out_specs=out_specs or ([VMEM] * len(out_shapes) if many else VMEM),
             scratch_shapes=list(scratch),
             compiler_params=pltpu.CompilerParams(vmem_limit_bytes=vmem),
             cost_estimate=pl.CostEstimate(
@@ -57,16 +57,24 @@
 
 
 def stats_body(lat_ref, gain_ref, bias_ref, ws_ref, wt_ref, out_ref, half_ref, *scratch):
-    lat_here, gain_here, bias_here, sems = scratch
+    lat_here, gain_here, bias_here, half_here, sems = scratch
     core = lax.rem(lax.axis_index("wide"), 2)
     moves = [(lat_ref, lat_here), (gain_ref, gain_here), (bias_ref, bias_here)]
     half = ws_ref.shape[0] // 2
     start = pl.multiple_of(core * half, 16)
-    moves.append((ws_ref.at[pl.ds(start, half)], half_ref.at[pl.ds(0, half)]))
-    moves.append((wt_ref, half_ref.at[pl.ds(half, wt_ref.shape[0])]))
+    moves.append((ws_ref.at[pl.ds(start, half)], half_here.at[pl.ds(0, half)]))
+    moves.append((wt_ref, half_here.at[pl.ds(half, wt_ref.shape[0])]))
     copies = [pltpu.make_async_copy(*move, sems.at[at]) for at, move in enumerate(moves)]
     for copy in copies:
         copy.start()
+    parts = (pl.ds(0, half), pl.ds(half, wt_ref.shape[0]))
+    leaving = [
+        pltpu.make_async_copy(half_here.at[part], half_ref.at[part], sems.at[5 + at])
+        for at, part in enumerate(parts)
+    ]
+    for copy, leave in zip(copies[3:], leaving):
+        copy.wait()
+        leave.start()
     for copy in copies[:3]:
         copy.wait()
     x = lat_here[...].astype(F32)
@@ -79,7 +87,7 @@
         axis=0,
     )
     out_ref[...] = jnp.broadcast_to(both[None], out_ref.shape)
-    for copy in copies[3:]:
+    for copy in leaving:
         copy.wait()
 
 
@@ -414,9 +422,11 @@
             pltpu.VMEM((rows, channels), BF16),
             pltpu.VMEM((1, channels), F32),
             pltpu.VMEM((1, channels), F32),
-            pltpu.SemaphoreType.DMA((5,)),
+            pltpu.VMEM((shard_s // 2 + shard_t, channels), BF16),
+            pltpu.SemaphoreType.DMA((7,)),
         ],
         in_specs=[HBM] * 5,
+        out_specs=[VMEM, HBM],
         vmem=FIRST_VMEM,
     )(lat, gain, bias, w_spatial, w_temporal)
     cot_t = call(transpose_body, shape((channels, rows), BF16), moved=300_000)(cot)

time: 48 us -> 48.6 us (1.012)
  Pallas kernels: 7.25 us -> 7.83 us
    pallas_call x8, Pallas kernels: 7.25 us -> 7.83 us  [run(): pl.pallas_call(body, out_shape=out_shapes, in_specs=in_specs or [VMEM] *...]
where the time goes in v14:
time: 48.6 us; the launch traced here: 48.3 us
  starting transfers between devices  21 us (43%)
  waiting for transfers between devices  17.8 us (37%)
  Pallas kernels  7.83 us (16%)
  local copies, waits for them, and re-layouts  0.92 us (2%)
  between operations  0.77 us (2%)
    ppermute x10, waiting for transfers between devices, send(): return lax.ppermute(value, ('dp', 'wide'), over_all(moves))  11.9 us
    ppermute x10, starting transfers between devices, send(): return lax.ppermute(value, ('dp', 'wide'), over_all(moves))  11.7 us
    pallas_call x8, Pallas kernels, run(): pl.pallas_call(body, out_shape=out_shapes, in_specs=in_specs or [VMEM] *...  7.83 us
    all_to_all x1, starting transfers between devices, local(): lax.all_to_all(stats, 'wide', split_axis=0, concat_axis=0, tiled=True)  6.69 us
    all_to_all x1, waiting for transfers between devices, local(): lax.all_to_all(stats, 'wide', split_axis=0, concat_axis=0, tiled=True)  5.88 us
    ppermute x1, starting transfers between devices, local(): before = lax.ppermute(spatial, 'wide', [(w, w + 1) for w in range(W - 1)])  1.29 us
    ppermute x1, starting transfers between devices, local(): halo = lax.ppermute(cot, 'wide', [(w + 1, w) for w in range(W - 1)])  1.28 us
  transfers between devices with their start and end apart: 13, of which 8 were waited for; matrix products, arithmetic and copies ran while one was open for 0% of the time, Pallas kernels for 8%

profile of v14, /device:TPU:0, one launch (start us, length us, event | category | flops | bytes accessed | tf_op | source)
XLA Modules:
  0.0 48.3 jit_solution(3675474354691767018)
XLA Ops:
  0.7 0.0 copy-start.4
  0.7 2.6 %shard_map.101 = (f32[16,2,512]{2,1,0:T(2,128)}, bf16[960,256]{1,0:T(8,128)(2,1)}) custom-call(bf16[256,256]{1,0:T(8,128)(2,1)} %bitcast.12, f32[1,256]{1,0:T(1,128)} %bitcast.26, f32[1,256]{1,0:T(1,128)} %bitcast.27, bf16[1152,256]{1,0:T(8,128)(2,1)} %ws_ref.3, bf16[384,256]{1,0:T(8,128)(2,1)} %wt_ref.5), custom_call_target="tpu_custom_call" | custom-call | tf_op jit(solution)/shard_map/pallas_call | solution.py:26
  3.3 3.0 %collective-permute-start = (bf16[960,256]{1,0:T(8,128)(2,1)}, bf16[960,256]{1,0:T(8,128)(2,1)S(1)}, u32[]{:S(2)}, u32[]{:S(2)}) collective-permute-start(bf16[960,256]{1,0:T(8,128)(2,1)} %get-tuple-element.31), channel_id=1, source_target_pairs={{0,16},{1,17},{2,18},{3,19},{4,20},{5,21},{6,22},{7,23},{8,24},{9,... | collective-permute-start | bytes 1474568 | tf_op jit(solution)/shard_map/ppermute | solution.py:412
  6.3 1.3 %collective-permute-start.1 = (bf16[256,256]{1,0:T(8,128)(2,1)}, bf16[256,256]{1,0:T(8,128)(2,1)S(1)}, u32[]{:S(2)}, u32[]{:S(2)}) collective-permute-start(bf16[256,256]{1,0:T(8,128)(2,1)} %bitcast.19), channel_id=1, source_target_pairs={{1,0},{2,1},{3,2},{4,3},{5,4},{6,5},{7,6},{8,7},{9,8},{10,9},{11,1... | collective-permute-start | bytes 393224 | tf_op jit(solution)/shard_map/ppermute | solution.py:435
  7.6 6.7 %all-to-all-start = ((f32[16,2,512]{2,1,0:T(2,128)}), f32[16,2,512]{2,1,0:T(2,128)S(1)}, u32[]{:S(2)}, u32[]{:S(2)}) async-start(f32[16,2,512]{2,1,0:T(2,128)} %get-tuple-element.32), calls=%async_computation | async-start | bytes 131072 | tf_op jit(solution)/shard_map/all_to_all | solution.py:436
  14.3 0.0 copy-start.3
  14.3 0.9 %copy-done.3 = bf16[1,2,8,16,256]{4,3,2,1,0:T(8,128)(2,1)S(1)} copy-done((bf16[1,2,8,16,256]{4,3,2,1,0:T(8,128)(2,1)S(1)}, bf16[1,2,8,16,256]{4,3,2,1,0:T(8,128)(2,1)}, u32[]{:S(2)}) %copy-start.3) | copy-done | bytes 131096
  15.2 0.1 shard_map.102.cot_t_ref
  15.3 5.9 %all-to-all-done.stats_ref.refs_6_ = f32[16,2,512]{2,1,0:T(2,128)S(1)} async-done(((f32[16,2,512]{2,1,0:T(2,128)}), f32[16,2,512]{2,1,0:T(2,128)S(1)}, u32[]{:S(2)}, u32[]{:S(2)}) %all-to-all-start) | async-done | bytes 65568 | tf_op jit(solution)/shard_map/all_to_all | solution.py:436
  21.2 1.1 %shard_map.103 = (bf16[256,256]{1,0:T(8,128)(2,1)S(1)}, bf16[256,2304]{1,0:T(8,128)(2,1)S(1)}, bf16[2,128,1152]{2,1,0:T(8,128)(2,1)S(1)}, bf16[2,128,1152]{2,1,0:T(8,128)(2,1)S(1)}) custom-call(bf16[256,256]{1,0:T(8,128)(2,1)S(1)} %bitcast.13, bf16[256,256]{1,0:T(8,128)(2,1)S(1)} %bitcast.21, bf16[256,256]{1,0:T(8,128)(2,1)S(1)} %collective-permute-done.1.halo_ref, ...), custom_call_target="tpu_custom_call" | custom-call | flops 402653184 | bytes 3000000 | tf_op jit(solution)/shard_map/pallas_call | solution.py:26
  22.3 0.5 %collective-permute-start.4 = (bf16[2,128,1152]{2,1,0:T(8,128)(2,1)S(1)}, bf16[2,128,1152]{2,1,0:T(8,128)(2,1)S(1)}, u32[]{:S(2)}, u32[]{:S(2)}) collective-permute-start(bf16[2,128,1152]{2,1,0:T(8,128)(2,1)S(1)} %get-tuple-element.41), channel_id=1, source_target_pairs={{0,1},{1,0},{2,3},{3,2},{4,5},{5,4},{6,7},{7,6},{8,9},{9,8},{10,11... | collective-permute-start | bytes 1769480 | tf_op jit(solution)/shard_map/ppermute | solution.py:412
  22.8 0.2 collective-permute-done.2.rest_1_
  23.1 1.6 %shard_map.104 = (bf16[256,256]{1,0:T(8,128)(2,1)S(1)}, f32[256,256]{1,0:T(8,128)S(1)}, bf16[2,128,512]{2,1,0:T(8,128)(2,1)S(1)}, bf16[2,128,512]{2,1,0:T(8,128)(2,1)S(1)}) custom-call(bf16[256,256]{1,0:T(8,128)(2,1)S(1)} %bitcast.14, bf16[256,256]{1,0:T(8,128)(2,1)S(1)} %shard_map.102.cot_t_ref, bf16[256,256]{1,0:T(8,128)(2,1)S(1)} %collective-permute-done.1.halo_ref, ...), custom_call_target="tpu_custom_call" | custom-call | flops 704643072 | bytes 3000000 | tf_op jit(solution)/shard_map/pallas_call | solution.py:26
  24.7 0.2 collective-permute-start.5
  24.9 0.0 collective-permute-done.4
  24.9 1.4 %collective-permute-done.5 = bf16[2,128,512]{2,1,0:T(8,128)(2,1)S(1)} collective-permute-done((bf16[2,128,512]{2,1,0:T(8,128)(2,1)S(1)}, bf16[2,128,512]{2,1,0:T(8,128)(2,1)S(1)}, u32[]{:S(2)}, u32[]{:S(2)}) %collective-permute-start.5) | collective-permute-done | bytes 262176 | tf_op jit(solution)/shard_map/ppermute | solution.py:412
  26.3 0.2 shard_map.106
  26.5 0.2 collective-permute-start.6
  26.7 0.5 %collective-permute-start.7 = (bf16[4,16,1664]{2,1,0:T(8,128)(2,1)S(1)}, bf16[4,16,1664]{2,1,0:T(8,128)(2,1)S(1)}, u32[]{:S(2)}, u32[]{:S(2)}) collective-permute-start(bf16[4,16,1664]{2,1,0:T(8,128)(2,1)S(1)} %get-tuple-element.46), channel_id=1, source_target_pairs={{0,16},{1,17},{2,18},{3,19},{4,20},{5,21},{6,22},{7,23},{8,24},{9,... | collective-permute-start | bytes 638984 | tf_op jit(solution)/shard_map/ppermute | solution.py:412
  27.2 2.8 %collective-permute-start.8 = (bf16[4,16,1664]{2,1,0:T(8,128)(2,1)S(1)}, bf16[4,16,1664]{2,1,0:T(8,128)(2,1)S(1)}, u32[]{:S(2)}, u32[]{:S(2)}) collective-permute-start(bf16[4,16,1664]{2,1,0:T(8,128)(2,1)S(1)} %get-tuple-element.47), channel_id=1, source_target_pairs={{0,18},{1,19},{2,16},{3,17},{4,22},{5,23},{6,20},{7,21},{8,26},{9,... | collective-permute-start | bytes 638984 | tf_op jit(solution)/shard_map/ppermute | solution.py:412
  30.1 1.3 %collective-permute-start.3 = (bf16[256,256]{1,0:T(8,128)(2,1)S(1)}, bf16[256,256]{1,0:T(8,128)(2,1)S(1)}, u32[]{:S(2)}, u32[]{:S(2)}) collective-permute-start(bf16[256,256]{1,0:T(8,128)(2,1)S(1)} %get-tuple-element.39.spatial_ref), channel_id=1, source_target_pairs={{0,1},{1,2},{2,3},{3,4},{4,5},{5,6},{6,7},{7,8},{8,9},{9,10},{10,1... | collective-permute-start | bytes 393224 | tf_op jit(solution)/shard_map/ppermute | solution.py:471
  31.4 2.5 %collective-permute-done.6.refs_1_ = bf16[4,16,1664]{2,1,0:T(8,128)(2,1)S(1)} collective-permute-done((bf16[4,16,1664]{2,1,0:T(8,128)(2,1)S(1)}, bf16[4,16,1664]{2,1,0:T(8,128)(2,1)S(1)}, u32[]{:S(2)}, u32[]{:S(2)}) %collective-permute-start.6) | collective-permute-done | bytes 213024 | tf_op jit(solution)/shard_map/ppermute | solution.py:412
  33.9 0.9 %collective-permute-done.7.refs_2_ = bf16[4,16,1664]{2,1,0:T(8,128)(2,1)S(1)} collective-permute-done((bf16[4,16,1664]{2,1,0:T(8,128)(2,1)S(1)}, bf16[4,16,1664]{2,1,0:T(8,128)(2,1)S(1)}, u32[]{:S(2)}, u32[]{:S(2)}) %collective-permute-start.7) | collective-permute-done | bytes 213024 | tf_op jit(solution)/shard_map/ppermute | solution.py:412
  34.8 4.8 %collective-permute-done.8.refs_3_ = bf16[4,16,1664]{2,1,0:T(8,128)(2,1)S(1)} collective-permute-done((bf16[4,16,1664]{2,1,0:T(8,128)(2,1)S(1)}, bf16[4,16,1664]{2,1,0:T(8,128)(2,1)S(1)}, u32[]{:S(2)}, u32[]{:S(2)}) %collective-permute-start.8) | collective-permute-done | bytes 213024 | tf_op jit(solution)/shard_map/ppermute | solution.py:412
  39.6 0.1 shard_map.107
  39.7 1.4 %collective-permute-start.9 = (bf16[16,1664]{1,0:T(8,128)(2,1)S(1)}, bf16[16,1664]{1,0:T(8,128)(2,1)S(1)}, u32[]{:S(2)}, u32[]{:S(2)}) collective-permute-start(bf16[16,1664]{1,0:T(8,128)(2,1)S(1)} %get-tuple-element.49), channel_id=1, source_target_pairs={{0,4},{1,5},{2,6},{3,7},{4,8},{5,9},{6,10},{7,11},{8,12},{9,13},{1... | collective-permute-start | bytes 159752 | tf_op jit(solution)/shard_map/ppermute | solution.py:412
  41.1 1.0 %collective-permute-start.10 = (bf16[16,1664]{1,0:T(8,128)(2,1)S(1)}, bf16[16,1664]{1,0:T(8,128)(2,1)S(1)}, u32[]{:S(2)}, u32[]{:S(2)}) collective-permute-start(bf16[16,1664]{1,0:T(8,128)(2,1)S(1)} %get-tuple-element.50), channel_id=1, source_target_pairs={{0,8},{1,9},{2,10},{3,11},{4,12},{5,13},{6,14},{7,15},{8,0},{9,1},... | collective-permute-start | bytes 159752 | tf_op jit(solution)/shard_map/ppermute | solution.py:412
  42.1 2.0 %collective-permute-start.11 = (bf16[16,1664]{1,0:T(8,128)(2,1)S(1)}, bf16[16,1664]{1,0:T(8,128)(2,1)S(1)}, u32[]{:S(2)}, u32[]{:S(2)}) collective-permute-start(bf16[16,1664]{1,0:T(8,128)(2,1)S(1)} %get-tuple-element.51), channel_id=1, source_target_pairs={{0,12},{1,13},{2,14},{3,15},{4,0},{5,1},{6,2},{7,3},{8,4},{9,5},{1... | collective-permute-start | bytes 159752 | tf_op jit(solution)/shard_map/ppermute | solution.py:412
  44.2 1.0 %shard_map.105 = bf16[256,256]{1,0:T(8,128)(2,1)} custom-call(bf16[256,256]{1,0:T(8,128)(2,1)S(1)} %bitcast.15, bf16[256,256]{1,0:T(8,128)(2,1)S(1)} %get-tuple-element.39.spatial_ref, bf16[256,256]{1,0:T(8,128)(2,1)S(1)} %collective-permute-done.3.before_ref, bf16[384,256]{1,0:T(8,128)(2,1)S(1)} %copy-done.2, bf16[960,256]{1,0:T(8,128)(2,1)S(1)} %collective-permute-done.rest_0_), custom_call_target="tpu_custom_call" | custom-call | flops 100663296 | bytes 1000000 | tf_op jit(solution)/shard_map/pallas_call | solution.py:26
  45.1 0.7 %collective-permute-done.9.refs_1_ = bf16[16,1664]{1,0:T(8,128)(2,1)S(1)} collective-permute-done((bf16[16,1664]{1,0:T(8,128)(2,1)S(1)}, bf16[16,1664]{1,0:T(8,128)(2,1)S(1)}, u32[]{:S(2)}, u32[]{:S(2)}) %collective-permute-start.9) | collective-permute-done | bytes 53280 | tf_op jit(solution)/shard_map/ppermute | solution.py:412
  45.8 1.3 %collective-permute-done.10.refs_2_ = bf16[16,1664]{1,0:T(8,128)(2,1)S(1)} collective-permute-done((bf16[16,1664]{1,0:T(8,128)(2,1)S(1)}, bf16[16,1664]{1,0:T(8,128)(2,1)S(1)}, u32[]{:S(2)}, u32[]{:S(2)}) %collective-permute-start.10) | collective-permute-done | bytes 53280 | tf_op jit(solution)/shard_map/ppermute | solution.py:412
  47.2 1.1 %shard_map.108 = (f32[16,1152]{1,0:T(8,128)}, f32[16,384]{1,0:T(8,128)}, f32[2,16]{1,0:T(2,128)}, bf16[256,256]{1,0:T(8,128)(2,1)}) custom-call(bf16[16,1664]{1,0:T(8,128)(2,1)S(1)} %get-tuple-element.48.refs_0_, bf16[16,1664]{1,0:T(8,128)(2,1)S(1)} %collective-permute-done.9.refs_1_, bf16[16,1664]{1,0:T(8,128)(2,1)S(1)} %collective-permute-done.10.refs_2_, ...), custom_call_target="tpu_custom_call" | custom-call | bytes 1000000 | tf_op jit(solution)/shard_map/pallas_call | solution.py:26
  (12 shorter events, 0.0 us)
Async XLA Ops:
  0.6 20.6 %copy-start.2 = (bf16[384,256]{1,0:T(8,128)(2,1)S(1)}, bf16[384,256]{1,0:T(8,128)(2,1)}, u32[]{:S(2)}) copy-start(bf16[384,256]{1,0:T(8,128)(2,1)} %wt_ref.5) | copy-start | bytes 589828
  0.6 20.6 %copy-start.1 = (bf16[1,2,8,16,256]{4,3,2,1,0:T(8,128)(2,1)S(1)}, bf16[1,2,8,16,256]{4,3,2,1,0:T(8,128)(2,1)}, u32[]{:S(2)}) copy-start(bf16[1,2,8,16,256]{4,3,2,1,0:T(8,128)(2,1)} %param.6) | copy-start | bytes 393220
  0.7 20.6 %copy-start.4 = (bf16[1,2,8,16,256]{4,3,2,1,0:T(8,128)(2,1)S(1)}, bf16[1,2,8,16,256]{4,3,2,1,0:T(8,128)(2,1)}, u32[]{:S(2)}) copy-start(bf16[1,2,8,16,256]{4,3,2,1,0:T(8,128)(2,1)} %param.7) | copy-start | bytes 393220
  0.7 22.4 %copy-start = (bf16[1152,256]{1,0:T(8,128)(2,1)S(1)}, bf16[1152,256]{1,0:T(8,128)(2,1)}, u32[]{:S(2)}) copy-start(bf16[1152,256]{1,0:T(8,128)(2,1)} %ws_ref.3) | copy-start | bytes 1769476
  3.3 17.9 %collective-permute-start = (bf16[960,256]{1,0:T(8,128)(2,1)}, bf16[960,256]{1,0:T(8,128)(2,1)S(1)}, u32[]{:S(2)}, u32[]{:S(2)}) collective-permute-start(bf16[960,256]{1,0:T(8,128)(2,1)} %get-tuple-element.31), channel_id=1, source_target_pairs={{0,16},{1,17},{2,18},{3,19},{4,20},{5,21},{6,22},{7,23},{8,24},{9,... | collective-permute-start | bytes 1474568 | tf_op jit(solution)/shard_map/ppermute | solution.py:412
  6.3 14.9 %collective-permute-start.1 = (bf16[256,256]{1,0:T(8,128)(2,1)}, bf16[256,256]{1,0:T(8,128)(2,1)S(1)}, u32[]{:S(2)}, u32[]{:S(2)}) collective-permute-start(bf16[256,256]{1,0:T(8,128)(2,1)} %bitcast.19), channel_id=1, source_target_pairs={{1,0},{2,1},{3,2},{4,3},{5,4},{6,5},{7,6},{8,7},{9,8},{10,9},{11,1... | collective-permute-start | bytes 393224 | tf_op jit(solution)/shard_map/ppermute | solution.py:435
  7.6 13.6 %all-to-all-start = ((f32[16,2,512]{2,1,0:T(2,128)}), f32[16,2,512]{2,1,0:T(2,128)S(1)}, u32[]{:S(2)}, u32[]{:S(2)}) async-start(f32[16,2,512]{2,1,0:T(2,128)} %get-tuple-element.32), calls=%async_computation | async-start | bytes 131072 | tf_op jit(solution)/shard_map/all_to_all | solution.py:436
  14.3 0.9 %copy-start.3 = (bf16[1,2,8,16,256]{4,3,2,1,0:T(8,128)(2,1)S(1)}, bf16[1,2,8,16,256]{4,3,2,1,0:T(8,128)(2,1)}, u32[]{:S(2)}) copy-start(bf16[1,2,8,16,256]{4,3,2,1,0:T(8,128)(2,1)} %param.7) | copy-start | bytes 393220
  21.2 1.9 %collective-permute-start.2 = (bf16[960,256]{1,0:T(8,128)(2,1)S(1)}, bf16[960,256]{1,0:T(8,128)(2,1)S(1)}, u32[]{:S(2)}, u32[]{:S(2)}) collective-permute-start(bf16[960,256]{1,0:T(8,128)(2,1)S(1)} %collective-permute-done.rest_0_), channel_id=1, source_target_pairs={{0,1},{1,0},{2,3},{3,2},{4,5},{5,4},{6,7},{7,6},{8,9},{9,8},{10,11... | collective-permute-start | bytes 1474568 | tf_op jit(solution)/shard_map/ppermute | solution.py:412
  22.3 2.6 %collective-permute-start.4 = (bf16[2,128,1152]{2,1,0:T(8,128)(2,1)S(1)}, bf16[2,128,1152]{2,1,0:T(8,128)(2,1)S(1)}, u32[]{:S(2)}, u32[]{:S(2)}) collective-permute-start(bf16[2,128,1152]{2,1,0:T(8,128)(2,1)S(1)} %get-tuple-element.41), channel_id=1, source_target_pairs={{0,1},{1,0},{2,3},{3,2},{4,5},{5,4},{6,7},{7,6},{8,9},{9,8},{10,11... | collective-permute-start | bytes 1769480 | tf_op jit(solution)/shard_map/ppermute | solution.py:412
  24.7 1.6 %collective-permute-start.5 = (bf16[2,128,512]{2,1,0:T(8,128)(2,1)S(1)}, bf16[2,128,512]{2,1,0:T(8,128)(2,1)S(1)}, u32[]{:S(2)}, u32[]{:S(2)}) collective-permute-start(bf16[2,128,512]{2,1,0:T(8,128)(2,1)S(1)} %get-tuple-element.43), channel_id=1, source_target_pairs={{0,1},{1,0},{2,3},{3,2},{4,5},{5,4},{6,7},{7,6},{8,9},{9,8},{10,11... | collective-permute-start | bytes 786440 | tf_op jit(solution)/shard_map/ppermute | solution.py:412
  26.5 7.4 %collective-permute-start.6 = (bf16[4,16,1664]{2,1,0:T(8,128)(2,1)S(1)}, bf16[4,16,1664]{2,1,0:T(8,128)(2,1)S(1)}, u32[]{:S(2)}, u32[]{:S(2)}) collective-permute-start(bf16[4,16,1664]{2,1,0:T(8,128)(2,1)S(1)} %get-tuple-element.45), channel_id=1, source_target_pairs={{0,2},{1,3},{2,0},{3,1},{4,6},{5,7},{6,4},{7,5},{8,10},{9,11},{10,... | collective-permute-start | bytes 638984 | tf_op jit(solution)/shard_map/ppermute | solution.py:412
  26.7 8.1 %collective-permute-start.7 = (bf16[4,16,1664]{2,1,0:T(8,128)(2,1)S(1)}, bf16[4,16,1664]{2,1,0:T(8,128)(2,1)S(1)}, u32[]{:S(2)}, u32[]{:S(2)}) collective-permute-start(bf16[4,16,1664]{2,1,0:T(8,128)(2,1)S(1)} %get-tuple-element.46), channel_id=1, source_target_pairs={{0,16},{1,17},{2,18},{3,19},{4,20},{5,21},{6,22},{7,23},{8,24},{9,... | collective-permute-start | bytes 638984 | tf_op jit(solution)/shard_map/ppermute | solution.py:412
  27.2 12.4 %collective-permute-start.8 = (bf16[4,16,1664]{2,1,0:T(8,128)(2,1)S(1)}, bf16[4,16,1664]{2,1,0:T(8,128)(2,1)S(1)}, u32[]{:S(2)}, u32[]{:S(2)}) collective-permute-start(bf16[4,16,1664]{2,1,0:T(8,128)(2,1)S(1)} %get-tuple-element.47), channel_id=1, source_target_pairs={{0,18},{1,19},{2,16},{3,17},{4,22},{5,23},{6,20},{7,21},{8,26},{9,... | collective-permute-start | bytes 638984 | tf_op jit(solution)/shard_map/ppermute | solution.py:412
  30.1 14.1 %collective-permute-start.3 = (bf16[256,256]{1,0:T(8,128)(2,1)S(1)}, bf16[256,256]{1,0:T(8,128)(2,1)S(1)}, u32[]{:S(2)}, u32[]{:S(2)}) collective-permute-start(bf16[256,256]{1,0:T(8,128)(2,1)S(1)} %get-tuple-element.39.spatial_ref), channel_id=1, source_target_pairs={{0,1},{1,2},{2,3},{3,4},{4,5},{5,6},{6,7},{7,8},{8,9},{9,10},{10,1... | collective-permute-start | bytes 393224 | tf_op jit(solution)/shard_map/ppermute | solution.py:471
  39.7 6.1 %collective-permute-start.9 = (bf16[16,1664]{1,0:T(8,128)(2,1)S(1)}, bf16[16,1664]{1,0:T(8,128)(2,1)S(1)}, u32[]{:S(2)}, u32[]{:S(2)}) collective-permute-start(bf16[16,1664]{1,0:T(8,128)(2,1)S(1)} %get-tuple-element.49), channel_id=1, source_target_pairs={{0,4},{1,5},{2,6},{3,7},{4,8},{5,9},{6,10},{7,11},{8,12},{9,13},{1... | collective-permute-start | bytes 159752 | tf_op jit(solution)/shard_map/ppermute | solution.py:412
  41.1 6.0 %collective-permute-start.10 = (bf16[16,1664]{1,0:T(8,128)(2,1)S(1)}, bf16[16,1664]{1,0:T(8,128)(2,1)S(1)}, u32[]{:S(2)}, u32[]{:S(2)}) collective-permute-start(bf16[16,1664]{1,0:T(8,128)(2,1)S(1)} %get-tuple-element.50), channel_id=1, source_target_pairs={{0,8},{1,9},{2,10},{3,11},{4,12},{5,13},{6,14},{7,15},{8,0},{9,1},... | collective-permute-start | bytes 159752 | tf_op jit(solution)/shard_map/ppermute | solution.py:412
  42.1 5.0 %collective-permute-start.11 = (bf16[16,1664]{1,0:T(8,128)(2,1)S(1)}, bf16[16,1664]{1,0:T(8,128)(2,1)S(1)}, u32[]{:S(2)}, u32[]{:S(2)}) collective-permute-start(bf16[16,1664]{1,0:T(8,128)(2,1)S(1)} %get-tuple-element.51), channel_id=1, source_target_pairs={{0,12},{1,13},{2,14},{3,15},{4,0},{5,1},{6,2},{7,3},{8,4},{9,5},{1... | collective-permute-start | bytes 159752 | tf_op jit(solution)/shard_map/ppermute | solution.py:412

commit v15 on v11

--- a/solution.py
+++ b/solution.py
@@ -484,7 +484,7 @@
         )(*pairs)
         parts = [plane[0]] + [
             send(plane[2 * a + b], lambda d, w: ((d + a) % D, w ^ (2 * b)))
-            for a, b in ((0, 1), (1, 0), (1, 1))
+            for a, b in ((1, 1), (1, 0), (0, 1))
         ]
         line = call(
             functools.partial(line_body, Z),

time: 48 us -> 48.3 us (level)
  no operation moved by 1% of the time
where the time goes in v15:
time: 48.3 us; the launch traced here: 48 us
  starting transfers between devices  21.2 us (44%)
  waiting for transfers between devices  17.9 us (37%)
  Pallas kernels  7.25 us (15%)
  local copies, waits for them, and re-layouts  0.92 us (2%)
  between operations  0.77 us (2%)
    ppermute x10, waiting for transfers between devices, send(): return lax.ppermute(value, ('dp', 'wide'), over_all(moves))  12 us
    ppermute x10, starting transfers between devices, send(): return lax.ppermute(value, ('dp', 'wide'), over_all(moves))  11.9 us
    pallas_call x8, Pallas kernels, run(): pl.pallas_call(body, out_shape=out_shapes, in_specs=in_specs or [VMEM] *...  7.25 us
    all_to_all x1, starting transfers between devices, local(): lax.all_to_all(stats, 'wide', split_axis=0, concat_axis=0, tiled=True)  6.69 us
    all_to_all x1, waiting for transfers between devices, local(): lax.all_to_all(stats, 'wide', split_axis=0, concat_axis=0, tiled=True)  5.88 us
    ppermute x1, starting transfers between devices, local(): before = lax.ppermute(spatial, 'wide', [(w, w + 1) for w in range(W - 1)])  1.29 us
    ppermute x1, starting transfers between devices, local(): halo = lax.ppermute(cot, 'wide', [(w + 1, w) for w in range(W - 1)])  1.28 us
  transfers between devices with their start and end apart: 13, of which 8 were waited for; matrix products, arithmetic and copies ran while one was open for 0% of the time, Pallas kernels for 8%

profile of v15, /device:TPU:0, one launch (start us, length us, event | category | flops | bytes accessed | tf_op | source)
XLA Modules:
  0.0 48.0 jit_solution(12235362133241474614)
XLA Ops:
  0.7 0.0 copy-start.4
  0.7 2.1 %shard_map.101 = (f32[16,2,512]{2,1,0:T(2,128)}, bf16[960,256]{1,0:T(8,128)(2,1)}) custom-call(bf16[256,256]{1,0:T(8,128)(2,1)} %bitcast.12, f32[1,256]{1,0:T(1,128)} %bitcast.26, f32[1,256]{1,0:T(1,128)} %bitcast.27, bf16[1152,256]{1,0:T(8,128)(2,1)} %ws_ref.3, bf16[384,256]{1,0:T(8,128)(2,1)} %wt_ref.5), custom_call_target="tpu_custom_call" | custom-call | tf_op jit(solution)/shard_map/pallas_call | solution.py:26
  2.7 3.0 %collective-permute-start = (bf16[960,256]{1,0:T(8,128)(2,1)}, bf16[960,256]{1,0:T(8,128)(2,1)S(1)}, u32[]{:S(2)}, u32[]{:S(2)}) collective-permute-start(bf16[960,256]{1,0:T(8,128)(2,1)} %get-tuple-element.31), channel_id=1, source_target_pairs={{0,16},{1,17},{2,18},{3,19},{4,20},{5,21},{6,22},{7,23},{8,24},{9,... | collective-permute-start | bytes 1474568 | tf_op jit(solution)/shard_map/ppermute | solution.py:404
  5.7 1.3 %collective-permute-start.1 = (bf16[256,256]{1,0:T(8,128)(2,1)}, bf16[256,256]{1,0:T(8,128)(2,1)S(1)}, u32[]{:S(2)}, u32[]{:S(2)}) collective-permute-start(bf16[256,256]{1,0:T(8,128)(2,1)} %bitcast.19), channel_id=1, source_target_pairs={{1,0},{2,1},{3,2},{4,3},{5,4},{6,5},{7,6},{8,7},{9,8},{10,9},{11,1... | collective-permute-start | bytes 393224 | tf_op jit(solution)/shard_map/ppermute | solution.py:425
  7.0 6.7 %all-to-all-start = ((f32[16,2,512]{2,1,0:T(2,128)}), f32[16,2,512]{2,1,0:T(2,128)S(1)}, u32[]{:S(2)}, u32[]{:S(2)}) async-start(f32[16,2,512]{2,1,0:T(2,128)} %get-tuple-element.32), calls=%async_computation | async-start | bytes 131072 | tf_op jit(solution)/shard_map/all_to_all | solution.py:426
  13.7 0.0 copy-start.3
  13.7 0.9 %copy-done.3 = bf16[1,2,8,16,256]{4,3,2,1,0:T(8,128)(2,1)S(1)} copy-done((bf16[1,2,8,16,256]{4,3,2,1,0:T(8,128)(2,1)S(1)}, bf16[1,2,8,16,256]{4,3,2,1,0:T(8,128)(2,1)}, u32[]{:S(2)}) %copy-start.3) | copy-done | bytes 131096
  14.6 0.1 shard_map.102.cot_t_ref
  14.7 5.9 %all-to-all-done.stats_ref.refs_6_ = f32[16,2,512]{2,1,0:T(2,128)S(1)} async-done(((f32[16,2,512]{2,1,0:T(2,128)}), f32[16,2,512]{2,1,0:T(2,128)S(1)}, u32[]{:S(2)}, u32[]{:S(2)}) %all-to-all-start) | async-done | bytes 65568 | tf_op jit(solution)/shard_map/all_to_all | solution.py:426
  20.6 0.0 collective-permute-start.2
  20.7 1.0 %shard_map.103 = (bf16[256,256]{1,0:T(8,128)(2,1)S(1)}, bf16[256,2304]{1,0:T(8,128)(2,1)S(1)}, bf16[2,128,1152]{2,1,0:T(8,128)(2,1)S(1)}, bf16[2,128,1152]{2,1,0:T(8,128)(2,1)S(1)}) custom-call(bf16[256,256]{1,0:T(8,128)(2,1)S(1)} %bitcast.13, bf16[256,256]{1,0:T(8,128)(2,1)S(1)} %bitcast.21, bf16[256,256]{1,0:T(8,128)(2,1)S(1)} %collective-permute-done.1.halo_ref, ...), custom_call_target="tpu_custom_call" | custom-call | flops 402653184 | bytes 3000000 | tf_op jit(solution)/shard_map/pallas_call | solution.py:26
  21.7 0.6 %collective-permute-start.4 = (bf16[2,128,1152]{2,1,0:T(8,128)(2,1)S(1)}, bf16[2,128,1152]{2,1,0:T(8,128)(2,1)S(1)}, u32[]{:S(2)}, u32[]{:S(2)}) collective-permute-start(bf16[2,128,1152]{2,1,0:T(8,128)(2,1)S(1)} %get-tuple-element.41), channel_id=1, source_target_pairs={{0,1},{1,0},{2,3},{3,2},{4,5},{5,4},{6,7},{7,6},{8,9},{9,8},{10,11... | collective-permute-start | bytes 1769480 | tf_op jit(solution)/shard_map/ppermute | solution.py:404
  22.3 0.2 collective-permute-done.2.rest_1_
  22.5 1.6 %shard_map.104 = (bf16[256,256]{1,0:T(8,128)(2,1)S(1)}, f32[256,256]{1,0:T(8,128)S(1)}, bf16[2,128,512]{2,1,0:T(8,128)(2,1)S(1)}, bf16[2,128,512]{2,1,0:T(8,128)(2,1)S(1)}) custom-call(bf16[256,256]{1,0:T(8,128)(2,1)S(1)} %bitcast.14, bf16[256,256]{1,0:T(8,128)(2,1)S(1)} %shard_map.102.cot_t_ref, bf16[256,256]{1,0:T(8,128)(2,1)S(1)} %collective-permute-done.1.halo_ref, ...), custom_call_target="tpu_custom_call" | custom-call | flops 704643072 | bytes 3000000 | tf_op jit(solution)/shard_map/pallas_call | solution.py:26
  24.1 0.2 collective-permute-start.5
  24.3 1.4 %collective-permute-done.5 = bf16[2,128,512]{2,1,0:T(8,128)(2,1)S(1)} collective-permute-done((bf16[2,128,512]{2,1,0:T(8,128)(2,1)S(1)}, bf16[2,128,512]{2,1,0:T(8,128)(2,1)S(1)}, u32[]{:S(2)}, u32[]{:S(2)}) %collective-permute-start.5) | collective-permute-done | bytes 262176 | tf_op jit(solution)/shard_map/ppermute | solution.py:404
  25.7 0.2 shard_map.106
  25.9 0.2 collective-permute-start.6
  26.1 1.5 %collective-permute-start.7 = (bf16[4,16,1664]{2,1,0:T(8,128)(2,1)S(1)}, bf16[4,16,1664]{2,1,0:T(8,128)(2,1)S(1)}, u32[]{:S(2)}, u32[]{:S(2)}) collective-permute-start(bf16[4,16,1664]{2,1,0:T(8,128)(2,1)S(1)} %get-tuple-element.46), channel_id=1, source_target_pairs={{0,16},{1,17},{2,18},{3,19},{4,20},{5,21},{6,22},{7,23},{8,24},{9,... | collective-permute-start | bytes 638984 | tf_op jit(solution)/shard_map/ppermute | solution.py:404
  27.6 1.9 %collective-permute-start.8 = (bf16[4,16,1664]{2,1,0:T(8,128)(2,1)S(1)}, bf16[4,16,1664]{2,1,0:T(8,128)(2,1)S(1)}, u32[]{:S(2)}, u32[]{:S(2)}) collective-permute-start(bf16[4,16,1664]{2,1,0:T(8,128)(2,1)S(1)} %get-tuple-element.47), channel_id=1, source_target_pairs={{0,2},{1,3},{2,0},{3,1},{4,6},{5,7},{6,4},{7,5},{8,10},{9,11},{10,... | collective-permute-start | bytes 638984 | tf_op jit(solution)/shard_map/ppermute | solution.py:404
  29.5 1.3 %collective-permute-start.3 = (bf16[256,256]{1,0:T(8,128)(2,1)S(1)}, bf16[256,256]{1,0:T(8,128)(2,1)S(1)}, u32[]{:S(2)}, u32[]{:S(2)}) collective-permute-start(bf16[256,256]{1,0:T(8,128)(2,1)S(1)} %get-tuple-element.39.spatial_ref), channel_id=1, source_target_pairs={{0,1},{1,2},{2,3},{3,4},{4,5},{5,6},{6,7},{7,8},{8,9},{9,10},{10,1... | collective-permute-start | bytes 393224 | tf_op jit(solution)/shard_map/ppermute | solution.py:461
  30.8 4.3 %collective-permute-done.6.refs_1_ = bf16[4,16,1664]{2,1,0:T(8,128)(2,1)S(1)} collective-permute-done((bf16[4,16,1664]{2,1,0:T(8,128)(2,1)S(1)}, bf16[4,16,1664]{2,1,0:T(8,128)(2,1)S(1)}, u32[]{:S(2)}, u32[]{:S(2)}) %collective-permute-start.6) | collective-permute-done | bytes 213024 | tf_op jit(solution)/shard_map/ppermute | solution.py:404
  35.0 2.4 %collective-permute-done.7.refs_2_ = bf16[4,16,1664]{2,1,0:T(8,128)(2,1)S(1)} collective-permute-done((bf16[4,16,1664]{2,1,0:T(8,128)(2,1)S(1)}, bf16[4,16,1664]{2,1,0:T(8,128)(2,1)S(1)}, u32[]{:S(2)}, u32[]{:S(2)}) %collective-permute-start.7) | collective-permute-done | bytes 213024 | tf_op jit(solution)/shard_map/ppermute | solution.py:404
  37.5 1.3 %collective-permute-done.8.refs_3_ = bf16[4,16,1664]{2,1,0:T(8,128)(2,1)S(1)} collective-permute-done((bf16[4,16,1664]{2,1,0:T(8,128)(2,1)S(1)}, bf16[4,16,1664]{2,1,0:T(8,128)(2,1)S(1)}, u32[]{:S(2)}, u32[]{:S(2)}) %collective-permute-start.8) | collective-permute-done | bytes 213024 | tf_op jit(solution)/shard_map/ppermute | solution.py:404
  38.8 0.1 shard_map.107
  38.9 1.6 %collective-permute-start.9 = (bf16[16,1664]{1,0:T(8,128)(2,1)S(1)}, bf16[16,1664]{1,0:T(8,128)(2,1)S(1)}, u32[]{:S(2)}, u32[]{:S(2)}) collective-permute-start(bf16[16,1664]{1,0:T(8,128)(2,1)S(1)} %get-tuple-element.49), channel_id=1, source_target_pairs={{0,4},{1,5},{2,6},{3,7},{4,8},{5,9},{6,10},{7,11},{8,12},{9,13},{1... | collective-permute-start | bytes 159752 | tf_op jit(solution)/shard_map/ppermute | solution.py:404
  40.5 1.0 %collective-permute-start.10 = (bf16[16,1664]{1,0:T(8,128)(2,1)S(1)}, bf16[16,1664]{1,0:T(8,128)(2,1)S(1)}, u32[]{:S(2)}, u32[]{:S(2)}) collective-permute-start(bf16[16,1664]{1,0:T(8,128)(2,1)S(1)} %get-tuple-element.50), channel_id=1, source_target_pairs={{0,8},{1,9},{2,10},{3,11},{4,12},{5,13},{6,14},{7,15},{8,0},{9,1},... | collective-permute-start | bytes 159752 | tf_op jit(solution)/shard_map/ppermute | solution.py:404
  41.5 2.0 %collective-permute-start.11 = (bf16[16,1664]{1,0:T(8,128)(2,1)S(1)}, bf16[16,1664]{1,0:T(8,128)(2,1)S(1)}, u32[]{:S(2)}, u32[]{:S(2)}) collective-permute-start(bf16[16,1664]{1,0:T(8,128)(2,1)S(1)} %get-tuple-element.51), channel_id=1, source_target_pairs={{0,12},{1,13},{2,14},{3,15},{4,0},{5,1},{6,2},{7,3},{8,4},{9,5},{1... | collective-permute-start | bytes 159752 | tf_op jit(solution)/shard_map/ppermute | solution.py:404
  43.5 1.0 %shard_map.105 = bf16[256,256]{1,0:T(8,128)(2,1)} custom-call(bf16[256,256]{1,0:T(8,128)(2,1)S(1)} %bitcast.15, bf16[256,256]{1,0:T(8,128)(2,1)S(1)} %get-tuple-element.39.spatial_ref, bf16[256,256]{1,0:T(8,128)(2,1)S(1)} %collective-permute-done.3.before_ref, bf16[384,256]{1,0:T(8,128)(2,1)S(1)} %copy-done.2, bf16[960,256]{1,0:T(8,128)(2,1)S(1)} %collective-permute-done.rest_0_), custom_call_target="tpu_custom_call" | custom-call | flops 100663296 | bytes 1000000 | tf_op jit(solution)/shard_map/pallas_call | solution.py:26
  44.4 0.9 %collective-permute-done.9.refs_1_ = bf16[16,1664]{1,0:T(8,128)(2,1)S(1)} collective-permute-done((bf16[16,1664]{1,0:T(8,128)(2,1)S(1)}, bf16[16,1664]{1,0:T(8,128)(2,1)S(1)}, u32[]{:S(2)}, u32[]{:S(2)}) %collective-permute-start.9) | collective-permute-done | bytes 53280 | tf_op jit(solution)/shard_map/ppermute | solution.py:404
  45.3 1.5 %collective-permute-done.10.refs_2_ = bf16[16,1664]{1,0:T(8,128)(2,1)S(1)} collective-permute-done((bf16[16,1664]{1,0:T(8,128)(2,1)S(1)}, bf16[16,1664]{1,0:T(8,128)(2,1)S(1)}, u32[]{:S(2)}, u32[]{:S(2)}) %collective-permute-start.10) | collective-permute-done | bytes 53280 | tf_op jit(solution)/shard_map/ppermute | solution.py:404
  46.9 1.1 %shard_map.108 = (f32[16,1152]{1,0:T(8,128)}, f32[16,384]{1,0:T(8,128)}, f32[2,16]{1,0:T(2,128)}, bf16[256,256]{1,0:T(8,128)(2,1)}) custom-call(bf16[16,1664]{1,0:T(8,128)(2,1)S(1)} %get-tuple-element.48.refs_0_, bf16[16,1664]{1,0:T(8,128)(2,1)S(1)} %collective-permute-done.9.refs_1_, bf16[16,1664]{1,0:T(8,128)(2,1)S(1)} %collective-permute-done.10.refs_2_, ...), custom_call_target="tpu_custom_call" | custom-call | bytes 1000000 | tf_op jit(solution)/shard_map/pallas_call | solution.py:26
  (12 shorter events, 0.0 us)
Async XLA Ops:
  0.6 20.0 %copy-start.2 = (bf16[384,256]{1,0:T(8,128)(2,1)S(1)}, bf16[384,256]{1,0:T(8,128)(2,1)}, u32[]{:S(2)}) copy-start(bf16[384,256]{1,0:T(8,128)(2,1)} %wt_ref.5) | copy-start | bytes 589828
  0.6 20.0 %copy-start.1 = (bf16[1,2,8,16,256]{4,3,2,1,0:T(8,128)(2,1)S(1)}, bf16[1,2,8,16,256]{4,3,2,1,0:T(8,128)(2,1)}, u32[]{:S(2)}) copy-start(bf16[1,2,8,16,256]{4,3,2,1,0:T(8,128)(2,1)} %param.6) | copy-start | bytes 393220
  0.7 20.0 %copy-start.4 = (bf16[1,2,8,16,256]{4,3,2,1,0:T(8,128)(2,1)S(1)}, bf16[1,2,8,16,256]{4,3,2,1,0:T(8,128)(2,1)}, u32[]{:S(2)}) copy-start(bf16[1,2,8,16,256]{4,3,2,1,0:T(8,128)(2,1)} %param.7) | copy-start | bytes 393220
  0.7 21.8 %copy-start = (bf16[1152,256]{1,0:T(8,128)(2,1)S(1)}, bf16[1152,256]{1,0:T(8,128)(2,1)}, u32[]{:S(2)}) copy-start(bf16[1152,256]{1,0:T(8,128)(2,1)} %ws_ref.3) | copy-start | bytes 1769476
  2.7 17.9 %collective-permute-start = (bf16[960,256]{1,0:T(8,128)(2,1)}, bf16[960,256]{1,0:T(8,128)(2,1)S(1)}, u32[]{:S(2)}, u32[]{:S(2)}) collective-permute-start(bf16[960,256]{1,0:T(8,128)(2,1)} %get-tuple-element.31), channel_id=1, source_target_pairs={{0,16},{1,17},{2,18},{3,19},{4,20},{5,21},{6,22},{7,23},{8,24},{9,... | collective-permute-start | bytes 1474568 | tf_op jit(solution)/shard_map/ppermute | solution.py:404
  5.7 14.9 %collective-permute-start.1 = (bf16[256,256]{1,0:T(8,128)(2,1)}, bf16[256,256]{1,0:T(8,128)(2,1)S(1)}, u32[]{:S(2)}, u32[]{:S(2)}) collective-permute-start(bf16[256,256]{1,0:T(8,128)(2,1)} %bitcast.19), channel_id=1, source_target_pairs={{1,0},{2,1},{3,2},{4,3},{5,4},{6,5},{7,6},{8,7},{9,8},{10,9},{11,1... | collective-permute-start | bytes 393224 | tf_op jit(solution)/shard_map/ppermute | solution.py:425
  7.0 13.6 %all-to-all-start = ((f32[16,2,512]{2,1,0:T(2,128)}), f32[16,2,512]{2,1,0:T(2,128)S(1)}, u32[]{:S(2)}, u32[]{:S(2)}) async-start(f32[16,2,512]{2,1,0:T(2,128)} %get-tuple-element.32), calls=%async_computation | async-start | bytes 131072 | tf_op jit(solution)/shard_map/all_to_all | solution.py:426
  13.7 0.9 %copy-start.3 = (bf16[1,2,8,16,256]{4,3,2,1,0:T(8,128)(2,1)S(1)}, bf16[1,2,8,16,256]{4,3,2,1,0:T(8,128)(2,1)}, u32[]{:S(2)}) copy-start(bf16[1,2,8,16,256]{4,3,2,1,0:T(8,128)(2,1)} %param.7) | copy-start | bytes 393220
  20.6 1.9 %collective-permute-start.2 = (bf16[960,256]{1,0:T(8,128)(2,1)S(1)}, bf16[960,256]{1,0:T(8,128)(2,1)S(1)}, u32[]{:S(2)}, u32[]{:S(2)}) collective-permute-start(bf16[960,256]{1,0:T(8,128)(2,1)S(1)} %collective-permute-done.rest_0_), channel_id=1, source_target_pairs={{0,1},{1,0},{2,3},{3,2},{4,5},{5,4},{6,7},{7,6},{8,9},{9,8},{10,11... | collective-permute-start | bytes 1474568 | tf_op jit(solution)/shard_map/ppermute | solution.py:404
  21.7 2.6 %collective-permute-start.4 = (bf16[2,128,1152]{2,1,0:T(8,128)(2,1)S(1)}, bf16[2,128,1152]{2,1,0:T(8,128)(2,1)S(1)}, u32[]{:S(2)}, u32[]{:S(2)}) collective-permute-start(bf16[2,128,1152]{2,1,0:T(8,128)(2,1)S(1)} %get-tuple-element.41), channel_id=1, source_target_pairs={{0,1},{1,0},{2,3},{3,2},{4,5},{5,4},{6,7},{7,6},{8,9},{9,8},{10,11... | collective-permute-start | bytes 1769480 | tf_op jit(solution)/shard_map/ppermute | solution.py:404
  24.1 1.6 %collective-permute-start.5 = (bf16[2,128,512]{2,1,0:T(8,128)(2,1)S(1)}, bf16[2,128,512]{2,1,0:T(8,128)(2,1)S(1)}, u32[]{:S(2)}, u32[]{:S(2)}) collective-permute-start(bf16[2,128,512]{2,1,0:T(8,128)(2,1)S(1)} %get-tuple-element.43), channel_id=1, source_target_pairs={{0,1},{1,0},{2,3},{3,2},{4,5},{5,4},{6,7},{7,6},{8,9},{9,8},{10,11... | collective-permute-start | bytes 786440 | tf_op jit(solution)/shard_map/ppermute | solution.py:404
  25.9 9.1 %collective-permute-start.6 = (bf16[4,16,1664]{2,1,0:T(8,128)(2,1)S(1)}, bf16[4,16,1664]{2,1,0:T(8,128)(2,1)S(1)}, u32[]{:S(2)}, u32[]{:S(2)}) collective-permute-start(bf16[4,16,1664]{2,1,0:T(8,128)(2,1)S(1)} %get-tuple-element.45), channel_id=1, source_target_pairs={{0,18},{1,19},{2,16},{3,17},{4,22},{5,23},{6,20},{7,21},{8,26},{9,... | collective-permute-start | bytes 638984 | tf_op jit(solution)/shard_map/ppermute | solution.py:404
  26.1 11.4 %collective-permute-start.7 = (bf16[4,16,1664]{2,1,0:T(8,128)(2,1)S(1)}, bf16[4,16,1664]{2,1,0:T(8,128)(2,1)S(1)}, u32[]{:S(2)}, u32[]{:S(2)}) collective-permute-start(bf16[4,16,1664]{2,1,0:T(8,128)(2,1)S(1)} %get-tuple-element.46), channel_id=1, source_target_pairs={{0,16},{1,17},{2,18},{3,19},{4,20},{5,21},{6,22},{7,23},{8,24},{9,... | collective-permute-start | bytes 638984 | tf_op jit(solution)/shard_map/ppermute | solution.py:404
  27.6 11.2 %collective-permute-start.8 = (bf16[4,16,1664]{2,1,0:T(8,128)(2,1)S(1)}, bf16[4,16,1664]{2,1,0:T(8,128)(2,1)S(1)}, u32[]{:S(2)}, u32[]{:S(2)}) collective-permute-start(bf16[4,16,1664]{2,1,0:T(8,128)(2,1)S(1)} %get-tuple-element.47), channel_id=1, source_target_pairs={{0,2},{1,3},{2,0},{3,1},{4,6},{5,7},{6,4},{7,5},{8,10},{9,11},{10,... | collective-permute-start | bytes 638984 | tf_op jit(solution)/shard_map/ppermute | solution.py:404
  29.5 14.0 %collective-permute-start.3 = (bf16[256,256]{1,0:T(8,128)(2,1)S(1)}, bf16[256,256]{1,0:T(8,128)(2,1)S(1)}, u32[]{:S(2)}, u32[]{:S(2)}) collective-permute-start(bf16[256,256]{1,0:T(8,128)(2,1)S(1)} %get-tuple-element.39.spatial_ref), channel_id=1, source_target_pairs={{0,1},{1,2},{2,3},{3,4},{4,5},{5,6},{6,7},{7,8},{8,9},{9,10},{10,1... | collective-permute-start | bytes 393224 | tf_op jit(solution)/shard_map/ppermute | solution.py:461
  38.9 6.4 %collective-permute-start.9 = (bf16[16,1664]{1,0:T(8,128)(2,1)S(1)}, bf16[16,1664]{1,0:T(8,128)(2,1)S(1)}, u32[]{:S(2)}, u32[]{:S(2)}) collective-permute-start(bf16[16,1664]{1,0:T(8,128)(2,1)S(1)} %get-tuple-element.49), channel_id=1, source_target_pairs={{0,4},{1,5},{2,6},{3,7},{4,8},{5,9},{6,10},{7,11},{8,12},{9,13},{1... | collective-permute-start | bytes 159752 | tf_op jit(solution)/shard_map/ppermute | solution.py:404
  40.5 6.4 %collective-permute-start.10 = (bf16[16,1664]{1,0:T(8,128)(2,1)S(1)}, bf16[16,1664]{1,0:T(8,128)(2,1)S(1)}, u32[]{:S(2)}, u32[]{:S(2)}) collective-permute-start(bf16[16,1664]{1,0:T(8,128)(2,1)S(1)} %get-tuple-element.50), channel_id=1, source_target_pairs={{0,8},{1,9},{2,10},{3,11},{4,12},{5,13},{6,14},{7,15},{8,0},{9,1},... | collective-permute-start | bytes 159752 | tf_op jit(solution)/shard_map/ppermute | solution.py:404
  41.5 5.4 %collective-permute-start.11 = (bf16[16,1664]{1,0:T(8,128)(2,1)S(1)}, bf16[16,1664]{1,0:T(8,128)(2,1)S(1)}, u32[]{:S(2)}, u32[]{:S(2)}) collective-permute-start(bf16[16,1664]{1,0:T(8,128)(2,1)S(1)} %get-tuple-element.51), channel_id=1, source_target_pairs={{0,12},{1,13},{2,14},{3,15},{4,0},{5,1},{6,2},{7,3},{8,4},{9,5},{1... | collective-permute-start | bytes 159752 | tf_op jit(solution)/shard_map/ppermute | solution.py:404

commit v16 on v11

--- a/solution.py
+++ b/solution.py
@@ -458,14 +458,15 @@
         flops=2 * 21 * rows * channels * channels,
         moved=3_000_000,
     )(lat, cot_t, halo, stats, gsa, seen, w_spatial, *pieces)
-    before = lax.ppermute(spatial, "wide", [(w, w + 1) for w in range(W - 1)])
-    block_out = call(
-        functools.partial(block_body, sizes),
-        shape((rows, channels), BF16),
-        [pltpu.VMEM((D * shard_t, channels), BF16)],
-        flops=2 * 3 * rows * channels * channels,
-        moved=1_000_000,
-    )(lat, spatial, before, w_temporal, *firsts)
+    def finish_block(spatial):
+        before = lax.ppermute(spatial, "wide", [(w, w + 1) for w in range(W - 1)])
+        return call(
+            functools.partial(block_body, sizes),
+            shape((rows, channels), BF16),
+            [pltpu.VMEM((D * shard_t, channels), BF16)],
+            flops=2 * 3 * rows * channels * channels,
+            moved=1_000_000,
+        )(lat, spatial, before, w_temporal, *firsts)
 
     width = channels // W
     operands = (lat, cot, stats, grad)
@@ -491,6 +492,8 @@
             [shape((width, R + ride), BF16)] * Z,
             moved=1_000_000,
         )(*parts)
+        line, spatial = lax.optimization_barrier((line, spatial))
+        block_out = finish_block(spatial)
         terms = [line[0]]
         for s in range(1, Z):
             terms.append(send(line[s], lambda d, w: (d, (w + 4 * s) % W)))
@@ -506,6 +509,7 @@
         )(*terms, *operands)
         grad_s, grad_t = grad_s.T, grad_t.T
     else:
+        block_out = finish_block(spatial)
         sums = lax.all_to_all(
             grads_t[1], ("dp", "wide"), split_axis=0, concat_axis=0, tiled=True
         )

time: 48 us -> 51.4 us (1.071)
  waiting for transfers between devices: 17.8 us -> 21.8 us
    ppermute x10, waiting for transfers between devices: 11.9 us -> 15.9 us  [send(): return lax.ppermute(value, ('dp', 'wide'), over_all(moves))]
    ppermute x10, starting transfers between devices: 11.7 us -> 11.2 us  [send(): return lax.ppermute(value, ('dp', 'wide'), over_all(moves))]
where the time goes in v16:
time: 51.4 us; the launch traced here: 51.2 us
  waiting for transfers between devices  21.8 us (42%)
  starting transfers between devices  20.5 us (40%)
  Pallas kernels  7.26 us (14%)
  local copies, waits for them, and re-layouts  0.92 us (2%)
  between operations  0.77 us (1%)
    ppermute x10, waiting for transfers between devices, send(): return lax.ppermute(value, ('dp', 'wide'), over_all(moves))  15.9 us
    ppermute x10, starting transfers between devices, send(): return lax.ppermute(value, ('dp', 'wide'), over_all(moves))  11.2 us
    pallas_call x8, Pallas kernels, run(): pl.pallas_call(body, out_shape=out_shapes, in_specs=in_specs or [VMEM] *...  7.26 us
    all_to_all x1, starting transfers between devices, local(): lax.all_to_all(stats, 'wide', split_axis=0, concat_axis=0, tiled=True)  6.69 us
    all_to_all x1, waiting for transfers between devices, local(): lax.all_to_all(stats, 'wide', split_axis=0, concat_axis=0, tiled=True)  5.88 us
    ppermute x1, starting transfers between devices, finish_block(): before = lax.ppermute(spatial, 'wide', [(w, w + 1) for w in range(W - 1)])  1.3 us
    ppermute x1, starting transfers between devices, local(): halo = lax.ppermute(cot, 'wide', [(w + 1, w) for w in range(W - 1)])  1.28 us
  transfers between devices with their start and end apart: 13, of which 8 were waited for; matrix products, arithmetic and copies ran while one was open for 0% of the time, Pallas kernels for 8%

profile of v16, /device:TPU:0, one launch (start us, length us, event | category | flops | bytes accessed | tf_op | source)
XLA Modules:
  0.0 51.2 jit_solution(14353658751133562850)
XLA Ops:
  0.7 0.0 copy-start.4
  0.7 2.1 %shard_map.101 = (f32[16,2,512]{2,1,0:T(2,128)}, bf16[960,256]{1,0:T(8,128)(2,1)}) custom-call(bf16[256,256]{1,0:T(8,128)(2,1)} %bitcast.12, f32[1,256]{1,0:T(1,128)} %bitcast.26, f32[1,256]{1,0:T(1,128)} %bitcast.27, bf16[1152,256]{1,0:T(8,128)(2,1)} %ws_ref.3, bf16[384,256]{1,0:T(8,128)(2,1)} %wt_ref.5), custom_call_target="tpu_custom_call" | custom-call | tf_op jit(solution)/shard_map/pallas_call | solution.py:26
  2.7 3.0 %collective-permute-start = (bf16[960,256]{1,0:T(8,128)(2,1)}, bf16[960,256]{1,0:T(8,128)(2,1)S(1)}, u32[]{:S(2)}, u32[]{:S(2)}) collective-permute-start(bf16[960,256]{1,0:T(8,128)(2,1)} %get-tuple-element.36), channel_id=1, source_target_pairs={{0,16},{1,17},{2,18},{3,19},{4,20},{5,21},{6,22},{7,23},{8,24},{9,... | collective-permute-start | bytes 1474568 | tf_op jit(solution)/shard_map/ppermute | solution.py:404
  5.7 1.3 %collective-permute-start.1 = (bf16[256,256]{1,0:T(8,128)(2,1)}, bf16[256,256]{1,0:T(8,128)(2,1)S(1)}, u32[]{:S(2)}, u32[]{:S(2)}) collective-permute-start(bf16[256,256]{1,0:T(8,128)(2,1)} %bitcast.19), channel_id=1, source_target_pairs={{1,0},{2,1},{3,2},{4,3},{5,4},{6,5},{7,6},{8,7},{9,8},{10,9},{11,1... | collective-permute-start | bytes 393224 | tf_op jit(solution)/shard_map/ppermute | solution.py:425
  7.0 6.7 %all-to-all-start = ((f32[16,2,512]{2,1,0:T(2,128)}), f32[16,2,512]{2,1,0:T(2,128)S(1)}, u32[]{:S(2)}, u32[]{:S(2)}) async-start(f32[16,2,512]{2,1,0:T(2,128)} %get-tuple-element.37), calls=%async_computation | async-start | bytes 131072 | tf_op jit(solution)/shard_map/all_to_all | solution.py:426
  13.7 0.0 copy-start.3
  13.7 0.9 %copy-done.3 = bf16[1,2,8,16,256]{4,3,2,1,0:T(8,128)(2,1)S(1)} copy-done((bf16[1,2,8,16,256]{4,3,2,1,0:T(8,128)(2,1)S(1)}, bf16[1,2,8,16,256]{4,3,2,1,0:T(8,128)(2,1)}, u32[]{:S(2)}) %copy-start.3) | copy-done | bytes 131096
  14.6 0.1 shard_map.102.cot_t_ref
  14.7 5.9 %all-to-all-done.stats_ref.refs_6_ = f32[16,2,512]{2,1,0:T(2,128)S(1)} async-done(((f32[16,2,512]{2,1,0:T(2,128)}), f32[16,2,512]{2,1,0:T(2,128)S(1)}, u32[]{:S(2)}, u32[]{:S(2)}) %all-to-all-start) | async-done | bytes 65568 | tf_op jit(solution)/shard_map/all_to_all | solution.py:426
  20.6 0.0 collective-permute-done.1.halo_ref
  20.7 1.0 %shard_map.103 = (bf16[256,256]{1,0:T(8,128)(2,1)S(1)}, bf16[256,2304]{1,0:T(8,128)(2,1)S(1)}, bf16[2,128,1152]{2,1,0:T(8,128)(2,1)S(1)}, bf16[2,128,1152]{2,1,0:T(8,128)(2,1)S(1)}) custom-call(bf16[256,256]{1,0:T(8,128)(2,1)S(1)} %bitcast.13, bf16[256,256]{1,0:T(8,128)(2,1)S(1)} %bitcast.21, bf16[256,256]{1,0:T(8,128)(2,1)S(1)} %collective-permute-done.1.halo_ref, ...), custom_call_target="tpu_custom_call" | custom-call | flops 402653184 | bytes 3000000 | tf_op jit(solution)/shard_map/pallas_call | solution.py:26
  21.7 0.6 %collective-permute-start.2 = (bf16[2,128,1152]{2,1,0:T(8,128)(2,1)S(1)}, bf16[2,128,1152]{2,1,0:T(8,128)(2,1)S(1)}, u32[]{:S(2)}, u32[]{:S(2)}) collective-permute-start(bf16[2,128,1152]{2,1,0:T(8,128)(2,1)S(1)} %get-tuple-element.42), channel_id=1, source_target_pairs={{0,1},{1,0},{2,3},{3,2},{4,5},{5,4},{6,7},{7,6},{8,9},{9,8},{10,11... | collective-permute-start | bytes 1769480 | tf_op jit(solution)/shard_map/ppermute | solution.py:404
  22.3 0.2 collective-permute-done.3.rest_1_
  22.5 1.6 %shard_map.104 = (bf16[256,256]{1,0:T(8,128)(2,1)S(1)}, f32[256,256]{1,0:T(8,128)S(1)}, bf16[2,128,512]{2,1,0:T(8,128)(2,1)S(1)}, bf16[2,128,512]{2,1,0:T(8,128)(2,1)S(1)}) custom-call(bf16[256,256]{1,0:T(8,128)(2,1)S(1)} %bitcast.14, bf16[256,256]{1,0:T(8,128)(2,1)S(1)} %shard_map.102.cot_t_ref, bf16[256,256]{1,0:T(8,128)(2,1)S(1)} %collective-permute-done.1.halo_ref, ...), custom_call_target="tpu_custom_call" | custom-call | flops 704643072 | bytes 3000000 | tf_op jit(solution)/shard_map/pallas_call | solution.py:26
  24.1 0.2 collective-permute-start.4
  24.3 1.4 %collective-permute-done.4 = bf16[2,128,512]{2,1,0:T(8,128)(2,1)S(1)} collective-permute-done((bf16[2,128,512]{2,1,0:T(8,128)(2,1)S(1)}, bf16[2,128,512]{2,1,0:T(8,128)(2,1)S(1)}, u32[]{:S(2)}, u32[]{:S(2)}) %collective-permute-start.4) | collective-permute-done | bytes 262176 | tf_op jit(solution)/shard_map/ppermute | solution.py:404
  25.7 0.2 shard_map.105
  25.9 0.2 collective-permute-start.5
  26.1 0.5 %collective-permute-start.6 = (bf16[4,16,1664]{2,1,0:T(8,128)(2,1)S(1)}, bf16[4,16,1664]{2,1,0:T(8,128)(2,1)S(1)}, u32[]{:S(2)}, u32[]{:S(2)}) collective-permute-start(bf16[4,16,1664]{2,1,0:T(8,128)(2,1)S(1)} %get-tuple-element.50), channel_id=1, source_target_pairs={{0,16},{1,17},{2,18},{3,19},{4,20},{5,21},{6,22},{7,23},{8,24},{9,... | collective-permute-start | bytes 638984 | tf_op jit(solution)/shard_map/ppermute | solution.py:404
  26.7 2.8 %collective-permute-start.7 = (bf16[4,16,1664]{2,1,0:T(8,128)(2,1)S(1)}, bf16[4,16,1664]{2,1,0:T(8,128)(2,1)S(1)}, u32[]{:S(2)}, u32[]{:S(2)}) collective-permute-start(bf16[4,16,1664]{2,1,0:T(8,128)(2,1)S(1)} %get-tuple-element.51), channel_id=1, source_target_pairs={{0,18},{1,19},{2,16},{3,17},{4,22},{5,23},{6,20},{7,21},{8,26},{9,... | collective-permute-start | bytes 638984 | tf_op jit(solution)/shard_map/ppermute | solution.py:404
  29.5 3.8 %collective-permute-done.5.refs_1_ = bf16[4,16,1664]{2,1,0:T(8,128)(2,1)S(1)} collective-permute-done((bf16[4,16,1664]{2,1,0:T(8,128)(2,1)S(1)}, bf16[4,16,1664]{2,1,0:T(8,128)(2,1)S(1)}, u32[]{:S(2)}, u32[]{:S(2)}) %collective-permute-start.5) | collective-permute-done | bytes 213024 | tf_op jit(solution)/shard_map/ppermute | solution.py:404
  33.3 0.9 %collective-permute-done.6.refs_2_ = bf16[4,16,1664]{2,1,0:T(8,128)(2,1)S(1)} collective-permute-done((bf16[4,16,1664]{2,1,0:T(8,128)(2,1)S(1)}, bf16[4,16,1664]{2,1,0:T(8,128)(2,1)S(1)}, u32[]{:S(2)}, u32[]{:S(2)}) %collective-permute-start.6) | collective-permute-done | bytes 213024 | tf_op jit(solution)/shard_map/ppermute | solution.py:404
  34.2 4.8 %collective-permute-done.7.refs_3_ = bf16[4,16,1664]{2,1,0:T(8,128)(2,1)S(1)} collective-permute-done((bf16[4,16,1664]{2,1,0:T(8,128)(2,1)S(1)}, bf16[4,16,1664]{2,1,0:T(8,128)(2,1)S(1)}, u32[]{:S(2)}, u32[]{:S(2)}) %collective-permute-start.7) | collective-permute-done | bytes 213024 | tf_op jit(solution)/shard_map/ppermute | solution.py:404
  39.1 0.1 shard_map.106
  39.2 1.3 %collective-permute-start.8 = (bf16[256,256]{1,0:T(8,128)(2,1)S(1)}, bf16[256,256]{1,0:T(8,128)(2,1)S(1)}, u32[]{:S(2)}, u32[]{:S(2)}) collective-permute-start(bf16[256,256]{1,0:T(8,128)(2,1)S(1)} %get-tuple-element.57.spatial_ref), channel_id=1, source_target_pairs={{0,1},{1,2},{2,3},{3,4},{4,5},{5,6},{6,7},{7,8},{8,9},{9,10},{10,1... | collective-permute-start | bytes 393224 | tf_op jit(solution)/shard_map/ppermute | solution.py:462
  40.5 0.8 %collective-permute-start.9 = (bf16[16,1664]{1,0:T(8,128)(2,1)S(1)}, bf16[16,1664]{1,0:T(8,128)(2,1)S(1)}, u32[]{:S(2)}, u32[]{:S(2)}) collective-permute-start(bf16[16,1664]{1,0:T(8,128)(2,1)S(1)} %get-tuple-element.59), channel_id=1, source_target_pairs={{0,4},{1,5},{2,6},{3,7},{4,8},{5,9},{6,10},{7,11},{8,12},{9,13},{1... | collective-permute-start | bytes 159752 | tf_op jit(solution)/shard_map/ppermute | solution.py:404
  41.3 1.0 %collective-permute-start.10 = (bf16[16,1664]{1,0:T(8,128)(2,1)S(1)}, bf16[16,1664]{1,0:T(8,128)(2,1)S(1)}, u32[]{:S(2)}, u32[]{:S(2)}) collective-permute-start(bf16[16,1664]{1,0:T(8,128)(2,1)S(1)} %get-tuple-element.60), channel_id=1, source_target_pairs={{0,8},{1,9},{2,10},{3,11},{4,12},{5,13},{6,14},{7,15},{8,0},{9,1},... | collective-permute-start | bytes 159752 | tf_op jit(solution)/shard_map/ppermute | solution.py:404
  42.3 2.1 %collective-permute-start.11 = (bf16[16,1664]{1,0:T(8,128)(2,1)S(1)}, bf16[16,1664]{1,0:T(8,128)(2,1)S(1)}, u32[]{:S(2)}, u32[]{:S(2)}) collective-permute-start(bf16[16,1664]{1,0:T(8,128)(2,1)S(1)} %get-tuple-element.61), channel_id=1, source_target_pairs={{0,12},{1,13},{2,14},{3,15},{4,0},{5,1},{6,2},{7,3},{8,4},{9,5},{1... | collective-permute-start | bytes 159752 | tf_op jit(solution)/shard_map/ppermute | solution.py:404
  44.4 2.7 %collective-permute-done.9.refs_1_ = bf16[16,1664]{1,0:T(8,128)(2,1)S(1)} collective-permute-done((bf16[16,1664]{1,0:T(8,128)(2,1)S(1)}, bf16[16,1664]{1,0:T(8,128)(2,1)S(1)}, u32[]{:S(2)}, u32[]{:S(2)}) %collective-permute-start.9) | collective-permute-done | bytes 53280 | tf_op jit(solution)/shard_map/ppermute | solution.py:404
  47.1 2.0 %collective-permute-done.10.refs_2_ = bf16[16,1664]{1,0:T(8,128)(2,1)S(1)} collective-permute-done((bf16[16,1664]{1,0:T(8,128)(2,1)S(1)}, bf16[16,1664]{1,0:T(8,128)(2,1)S(1)}, u32[]{:S(2)}, u32[]{:S(2)}) %collective-permute-start.10) | collective-permute-done | bytes 53280 | tf_op jit(solution)/shard_map/ppermute | solution.py:404
  49.1 1.1 %shard_map.108 = (f32[16,1152]{1,0:T(8,128)}, f32[16,384]{1,0:T(8,128)}, f32[2,16]{1,0:T(2,128)}, bf16[256,256]{1,0:T(8,128)(2,1)}) custom-call(bf16[16,1664]{1,0:T(8,128)(2,1)S(1)} %get-tuple-element.58.refs_0_, bf16[16,1664]{1,0:T(8,128)(2,1)S(1)} %collective-permute-done.9.refs_1_, bf16[16,1664]{1,0:T(8,128)(2,1)S(1)} %collective-permute-done.10.refs_2_, ...), custom_call_target="tpu_custom_call" | custom-call | bytes 1000000 | tf_op jit(solution)/shard_map/pallas_call | solution.py:26
  50.2 1.0 %shard_map.107 = bf16[256,256]{1,0:T(8,128)(2,1)} custom-call(bf16[256,256]{1,0:T(8,128)(2,1)S(1)} %bitcast.16, bf16[256,256]{1,0:T(8,128)(2,1)S(1)} %get-tuple-element.57.spatial_ref, bf16[256,256]{1,0:T(8,128)(2,1)S(1)} %collective-permute-done.8.before_ref, bf16[384,256]{1,0:T(8,128)(2,1)S(1)} %copy-done.2, bf16[960,256]{1,0:T(8,128)(2,1)S(1)} %collective-permute-done.rest_0_), custom_call_target="tpu_custom_call" | custom-call | flops 100663296 | bytes 1000000 | tf_op jit(solution)/shard_map/pallas_call | solution.py:26
  (12 shorter events, 0.0 us)
Async XLA Ops:
  0.6 20.0 %copy-start.2 = (bf16[384,256]{1,0:T(8,128)(2,1)S(1)}, bf16[384,256]{1,0:T(8,128)(2,1)}, u32[]{:S(2)}) copy-start(bf16[384,256]{1,0:T(8,128)(2,1)} %wt_ref.5) | copy-start | bytes 589828
  0.6 20.0 %copy-start.1 = (bf16[1,2,8,16,256]{4,3,2,1,0:T(8,128)(2,1)S(1)}, bf16[1,2,8,16,256]{4,3,2,1,0:T(8,128)(2,1)}, u32[]{:S(2)}) copy-start(bf16[1,2,8,16,256]{4,3,2,1,0:T(8,128)(2,1)} %param.6) | copy-start | bytes 393220
  0.7 20.0 %copy-start.4 = (bf16[1,2,8,16,256]{4,3,2,1,0:T(8,128)(2,1)S(1)}, bf16[1,2,8,16,256]{4,3,2,1,0:T(8,128)(2,1)}, u32[]{:S(2)}) copy-start(bf16[1,2,8,16,256]{4,3,2,1,0:T(8,128)(2,1)} %param.7) | copy-start | bytes 393220
  0.7 21.8 %copy-start = (bf16[1152,256]{1,0:T(8,128)(2,1)S(1)}, bf16[1152,256]{1,0:T(8,128)(2,1)}, u32[]{:S(2)}) copy-start(bf16[1152,256]{1,0:T(8,128)(2,1)} %ws_ref.3) | copy-start | bytes 1769476
  2.7 17.9 %collective-permute-start = (bf16[960,256]{1,0:T(8,128)(2,1)}, bf16[960,256]{1,0:T(8,128)(2,1)S(1)}, u32[]{:S(2)}, u32[]{:S(2)}) collective-permute-start(bf16[960,256]{1,0:T(8,128)(2,1)} %get-tuple-element.36), channel_id=1, source_target_pairs={{0,16},{1,17},{2,18},{3,19},{4,20},{5,21},{6,22},{7,23},{8,24},{9,... | collective-permute-start | bytes 1474568 | tf_op jit(solution)/shard_map/ppermute | solution.py:404
  5.7 14.9 %collective-permute-start.1 = (bf16[256,256]{1,0:T(8,128)(2,1)}, bf16[256,256]{1,0:T(8,128)(2,1)S(1)}, u32[]{:S(2)}, u32[]{:S(2)}) collective-permute-start(bf16[256,256]{1,0:T(8,128)(2,1)} %bitcast.19), channel_id=1, source_target_pairs={{1,0},{2,1},{3,2},{4,3},{5,4},{6,5},{7,6},{8,7},{9,8},{10,9},{11,1... | collective-permute-start | bytes 393224 | tf_op jit(solution)/shard_map/ppermute | solution.py:425
  7.0 13.6 %all-to-all-start = ((f32[16,2,512]{2,1,0:T(2,128)}), f32[16,2,512]{2,1,0:T(2,128)S(1)}, u32[]{:S(2)}, u32[]{:S(2)}) async-start(f32[16,2,512]{2,1,0:T(2,128)} %get-tuple-element.37), calls=%async_computation | async-start | bytes 131072 | tf_op jit(solution)/shard_map/all_to_all | solution.py:426
  13.7 0.9 %copy-start.3 = (bf16[1,2,8,16,256]{4,3,2,1,0:T(8,128)(2,1)S(1)}, bf16[1,2,8,16,256]{4,3,2,1,0:T(8,128)(2,1)}, u32[]{:S(2)}) copy-start(bf16[1,2,8,16,256]{4,3,2,1,0:T(8,128)(2,1)} %param.7) | copy-start | bytes 393220
  20.6 1.9 %collective-permute-start.3 = (bf16[960,256]{1,0:T(8,128)(2,1)S(1)}, bf16[960,256]{1,0:T(8,128)(2,1)S(1)}, u32[]{:S(2)}, u32[]{:S(2)}) collective-permute-start(bf16[960,256]{1,0:T(8,128)(2,1)S(1)} %collective-permute-done.rest_0_), channel_id=1, source_target_pairs={{0,1},{1,0},{2,3},{3,2},{4,5},{5,4},{6,7},{7,6},{8,9},{9,8},{10,11... | collective-permute-start | bytes 1474568 | tf_op jit(solution)/shard_map/ppermute | solution.py:404
  21.7 2.6 %collective-permute-start.2 = (bf16[2,128,1152]{2,1,0:T(8,128)(2,1)S(1)}, bf16[2,128,1152]{2,1,0:T(8,128)(2,1)S(1)}, u32[]{:S(2)}, u32[]{:S(2)}) collective-permute-start(bf16[2,128,1152]{2,1,0:T(8,128)(2,1)S(1)} %get-tuple-element.42), channel_id=1, source_target_pairs={{0,1},{1,0},{2,3},{3,2},{4,5},{5,4},{6,7},{7,6},{8,9},{9,8},{10,11... | collective-permute-start | bytes 1769480 | tf_op jit(solution)/shard_map/ppermute | solution.py:404
  24.1 1.6 %collective-permute-start.4 = (bf16[2,128,512]{2,1,0:T(8,128)(2,1)S(1)}, bf16[2,128,512]{2,1,0:T(8,128)(2,1)S(1)}, u32[]{:S(2)}, u32[]{:S(2)}) collective-permute-start(bf16[2,128,512]{2,1,0:T(8,128)(2,1)S(1)} %get-tuple-element.47), channel_id=1, source_target_pairs={{0,1},{1,0},{2,3},{3,2},{4,5},{5,4},{6,7},{7,6},{8,9},{9,8},{10,11... | collective-permute-start | bytes 786440 | tf_op jit(solution)/shard_map/ppermute | solution.py:404
  25.9 7.4 %collective-permute-start.5 = (bf16[4,16,1664]{2,1,0:T(8,128)(2,1)S(1)}, bf16[4,16,1664]{2,1,0:T(8,128)(2,1)S(1)}, u32[]{:S(2)}, u32[]{:S(2)}) collective-permute-start(bf16[4,16,1664]{2,1,0:T(8,128)(2,1)S(1)} %get-tuple-element.49), channel_id=1, source_target_pairs={{0,2},{1,3},{2,0},{3,1},{4,6},{5,7},{6,4},{7,5},{8,10},{9,11},{10,... | collective-permute-start | bytes 638984 | tf_op jit(solution)/shard_map/ppermute | solution.py:404
  26.1 8.1 %collective-permute-start.6 = (bf16[4,16,1664]{2,1,0:T(8,128)(2,1)S(1)}, bf16[4,16,1664]{2,1,0:T(8,128)(2,1)S(1)}, u32[]{:S(2)}, u32[]{:S(2)}) collective-permute-start(bf16[4,16,1664]{2,1,0:T(8,128)(2,1)S(1)} %get-tuple-element.50), channel_id=1, source_target_pairs={{0,16},{1,17},{2,18},{3,19},{4,20},{5,21},{6,22},{7,23},{8,24},{9,... | collective-permute-start | bytes 638984 | tf_op jit(solution)/shard_map/ppermute | solution.py:404
  26.7 12.4 %collective-permute-start.7 = (bf16[4,16,1664]{2,1,0:T(8,128)(2,1)S(1)}, bf16[4,16,1664]{2,1,0:T(8,128)(2,1)S(1)}, u32[]{:S(2)}, u32[]{:S(2)}) collective-permute-start(bf16[4,16,1664]{2,1,0:T(8,128)(2,1)S(1)} %get-tuple-element.51), channel_id=1, source_target_pairs={{0,18},{1,19},{2,16},{3,17},{4,22},{5,23},{6,20},{7,21},{8,26},{9,... | collective-permute-start | bytes 638984 | tf_op jit(solution)/shard_map/ppermute | solution.py:404
  39.2 11.0 %collective-permute-start.8 = (bf16[256,256]{1,0:T(8,128)(2,1)S(1)}, bf16[256,256]{1,0:T(8,128)(2,1)S(1)}, u32[]{:S(2)}, u32[]{:S(2)}) collective-permute-start(bf16[256,256]{1,0:T(8,128)(2,1)S(1)} %get-tuple-element.57.spatial_ref), channel_id=1, source_target_pairs={{0,1},{1,2},{2,3},{3,4},{4,5},{5,6},{6,7},{7,8},{8,9},{9,10},{10,1... | collective-permute-start | bytes 393224 | tf_op jit(solution)/shard_map/ppermute | solution.py:462
  40.5 6.6 %collective-permute-start.9 = (bf16[16,1664]{1,0:T(8,128)(2,1)S(1)}, bf16[16,1664]{1,0:T(8,128)(2,1)S(1)}, u32[]{:S(2)}, u32[]{:S(2)}) collective-permute-start(bf16[16,1664]{1,0:T(8,128)(2,1)S(1)} %get-tuple-element.59), channel_id=1, source_target_pairs={{0,4},{1,5},{2,6},{3,7},{4,8},{5,9},{6,10},{7,11},{8,12},{9,13},{1... | collective-permute-start | bytes 159752 | tf_op jit(solution)/shard_map/ppermute | solution.py:404
  41.3 7.8 %collective-permute-start.10 = (bf16[16,1664]{1,0:T(8,128)(2,1)S(1)}, bf16[16,1664]{1,0:T(8,128)(2,1)S(1)}, u32[]{:S(2)}, u32[]{:S(2)}) collective-permute-start(bf16[16,1664]{1,0:T(8,128)(2,1)S(1)} %get-tuple-element.60), channel_id=1, source_target_pairs={{0,8},{1,9},{2,10},{3,11},{4,12},{5,13},{6,14},{7,15},{8,0},{9,1},... | collective-permute-start | bytes 159752 | tf_op jit(solution)/shard_map/ppermute | solution.py:404
  42.3 6.8 %collective-permute-start.11 = (bf16[16,1664]{1,0:T(8,128)(2,1)S(1)}, bf16[16,1664]{1,0:T(8,128)(2,1)S(1)}, u32[]{:S(2)}, u32[]{:S(2)}) collective-permute-start(bf16[16,1664]{1,0:T(8,128)(2,1)S(1)} %get-tuple-element.61), channel_id=1, source_target_pairs={{0,12},{1,13},{2,14},{3,15},{4,0},{5,1},{6,2},{7,3},{8,4},{9,5},{1... | collective-permute-start | bytes 159752 | tf_op jit(solution)/shard_map/ppermute | solution.py:404

commit v17 on v15

--- a/solution.py
+++ b/solution.py
@@ -484,7 +484,7 @@
         )(*pairs)
         parts = [plane[0]] + [
             send(plane[2 * a + b], lambda d, w: ((d + a) % D, w ^ (2 * b)))
-            for a, b in ((1, 1), (1, 0), (0, 1))
+            for a, b in ((1, 0), (0, 1), (1, 1))
         ]
         line = call(
             functools.partial(line_body, Z),

time: 48.3 us -> 47.4 us (0.981)
  waiting for transfers between devices: 17.9 us -> 16.9 us
    ppermute x10, waiting for transfers between devices: 12 us -> 11 us  [send(): return lax.ppermute(value, ('dp', 'wide'), over_all(moves))]
where the time goes in v17:
time: 47.4 us; the launch traced here: 47.2 us
  starting transfers between devices  21.3 us (45%)
  waiting for transfers between devices  16.9 us (36%)
  Pallas kernels  7.25 us (15%)
  local copies, waits for them, and re-layouts  0.92 us (2%)
  between operations  0.77 us (2%)
    ppermute x10, starting transfers between devices, send(): return lax.ppermute(value, ('dp', 'wide'), over_all(moves))  12 us
    ppermute x10, waiting for transfers between devices, send(): return lax.ppermute(value, ('dp', 'wide'), over_all(moves))  11 us
    pallas_call x8, Pallas kernels, run(): pl.pallas_call(body, out_shape=out_shapes, in_specs=in_specs or [VMEM] *...  7.25 us
    all_to_all x1, starting transfers between devices, local(): lax.all_to_all(stats, 'wide', split_axis=0, concat_axis=0, tiled=True)  6.69 us
    all_to_all x1, waiting for transfers between devices, local(): lax.all_to_all(stats, 'wide', split_axis=0, concat_axis=0, tiled=True)  5.88 us
    ppermute x1, starting transfers between devices, local(): before = lax.ppermute(spatial, 'wide', [(w, w + 1) for w in range(W - 1)])  1.29 us
    ppermute x1, starting transfers between devices, local(): halo = lax.ppermute(cot, 'wide', [(w + 1, w) for w in range(W - 1)])  1.28 us
  transfers between devices with their start and end apart: 13, of which 8 were waited for; matrix products, arithmetic and copies ran while one was open for 0% of the time, Pallas kernels for 8%

profile of v17, /device:TPU:0, one launch (start us, length us, event | category | flops | bytes accessed | tf_op | source)
XLA Modules:
  0.0 47.2 jit_solution(8490381984627790188)
XLA Ops:
  0.7 0.0 copy-start.4
  0.7 2.1 %shard_map.101 = (f32[16,2,512]{2,1,0:T(2,128)}, bf16[960,256]{1,0:T(8,128)(2,1)}) custom-call(bf16[256,256]{1,0:T(8,128)(2,1)} %bitcast.12, f32[1,256]{1,0:T(1,128)} %bitcast.26, f32[1,256]{1,0:T(1,128)} %bitcast.27, bf16[1152,256]{1,0:T(8,128)(2,1)} %ws_ref.3, bf16[384,256]{1,0:T(8,128)(2,1)} %wt_ref.5), custom_call_target="tpu_custom_call" | custom-call | tf_op jit(solution)/shard_map/pallas_call | solution.py:26
  2.7 3.0 %collective-permute-start = (bf16[960,256]{1,0:T(8,128)(2,1)}, bf16[960,256]{1,0:T(8,128)(2,1)S(1)}, u32[]{:S(2)}, u32[]{:S(2)}) collective-permute-start(bf16[960,256]{1,0:T(8,128)(2,1)} %get-tuple-element.31), channel_id=1, source_target_pairs={{0,16},{1,17},{2,18},{3,19},{4,20},{5,21},{6,22},{7,23},{8,24},{9,... | collective-permute-start | bytes 1474568 | tf_op jit(solution)/shard_map/ppermute | solution.py:404
  5.7 1.3 %collective-permute-start.1 = (bf16[256,256]{1,0:T(8,128)(2,1)}, bf16[256,256]{1,0:T(8,128)(2,1)S(1)}, u32[]{:S(2)}, u32[]{:S(2)}) collective-permute-start(bf16[256,256]{1,0:T(8,128)(2,1)} %bitcast.19), channel_id=1, source_target_pairs={{1,0},{2,1},{3,2},{4,3},{5,4},{6,5},{7,6},{8,7},{9,8},{10,9},{11,1... | collective-permute-start | bytes 393224 | tf_op jit(solution)/shard_map/ppermute | solution.py:425
  7.0 6.7 %all-to-all-start = ((f32[16,2,512]{2,1,0:T(2,128)}), f32[16,2,512]{2,1,0:T(2,128)S(1)}, u32[]{:S(2)}, u32[]{:S(2)}) async-start(f32[16,2,512]{2,1,0:T(2,128)} %get-tuple-element.32), calls=%async_computation | async-start | bytes 131072 | tf_op jit(solution)/shard_map/all_to_all | solution.py:426
  13.7 0.0 copy-start.3
  13.7 0.9 %copy-done.3 = bf16[1,2,8,16,256]{4,3,2,1,0:T(8,128)(2,1)S(1)} copy-done((bf16[1,2,8,16,256]{4,3,2,1,0:T(8,128)(2,1)S(1)}, bf16[1,2,8,16,256]{4,3,2,1,0:T(8,128)(2,1)}, u32[]{:S(2)}) %copy-start.3) | copy-done | bytes 131096
  14.6 0.1 shard_map.102.cot_t_ref
  14.7 5.9 %all-to-all-done.stats_ref.refs_6_ = f32[16,2,512]{2,1,0:T(2,128)S(1)} async-done(((f32[16,2,512]{2,1,0:T(2,128)}), f32[16,2,512]{2,1,0:T(2,128)S(1)}, u32[]{:S(2)}, u32[]{:S(2)}) %all-to-all-start) | async-done | bytes 65568 | tf_op jit(solution)/shard_map/all_to_all | solution.py:426
  20.6 0.0 collective-permute-done.1.halo_ref
  20.7 1.0 %shard_map.103 = (bf16[256,256]{1,0:T(8,128)(2,1)S(1)}, bf16[256,2304]{1,0:T(8,128)(2,1)S(1)}, bf16[2,128,1152]{2,1,0:T(8,128)(2,1)S(1)}, bf16[2,128,1152]{2,1,0:T(8,128)(2,1)S(1)}) custom-call(bf16[256,256]{1,0:T(8,128)(2,1)S(1)} %bitcast.13, bf16[256,256]{1,0:T(8,128)(2,1)S(1)} %bitcast.21, bf16[256,256]{1,0:T(8,128)(2,1)S(1)} %collective-permute-done.1.halo_ref, ...), custom_call_target="tpu_custom_call" | custom-call | flops 402653184 | bytes 3000000 | tf_op jit(solution)/shard_map/pallas_call | solution.py:26
  21.7 0.6 %collective-permute-start.4 = (bf16[2,128,1152]{2,1,0:T(8,128)(2,1)S(1)}, bf16[2,128,1152]{2,1,0:T(8,128)(2,1)S(1)}, u32[]{:S(2)}, u32[]{:S(2)}) collective-permute-start(bf16[2,128,1152]{2,1,0:T(8,128)(2,1)S(1)} %get-tuple-element.41), channel_id=1, source_target_pairs={{0,1},{1,0},{2,3},{3,2},{4,5},{5,4},{6,7},{7,6},{8,9},{9,8},{10,11... | collective-permute-start | bytes 1769480 | tf_op jit(solution)/shard_map/ppermute | solution.py:404
  22.3 0.2 collective-permute-done.2.rest_1_
  22.5 1.6 %shard_map.104 = (bf16[256,256]{1,0:T(8,128)(2,1)S(1)}, f32[256,256]{1,0:T(8,128)S(1)}, bf16[2,128,512]{2,1,0:T(8,128)(2,1)S(1)}, bf16[2,128,512]{2,1,0:T(8,128)(2,1)S(1)}) custom-call(bf16[256,256]{1,0:T(8,128)(2,1)S(1)} %bitcast.14, bf16[256,256]{1,0:T(8,128)(2,1)S(1)} %shard_map.102.cot_t_ref, bf16[256,256]{1,0:T(8,128)(2,1)S(1)} %collective-permute-done.1.halo_ref, ...), custom_call_target="tpu_custom_call" | custom-call | flops 704643072 | bytes 3000000 | tf_op jit(solution)/shard_map/pallas_call | solution.py:26
  24.1 0.2 collective-permute-start.5
  24.3 1.4 %collective-permute-done.5 = bf16[2,128,512]{2,1,0:T(8,128)(2,1)S(1)} collective-permute-done((bf16[2,128,512]{2,1,0:T(8,128)(2,1)S(1)}, bf16[2,128,512]{2,1,0:T(8,128)(2,1)S(1)}, u32[]{:S(2)}, u32[]{:S(2)}) %collective-permute-start.5) | collective-permute-done | bytes 262176 | tf_op jit(solution)/shard_map/ppermute | solution.py:404
  25.7 0.2 shard_map.106
  25.9 0.6 %collective-permute-start.6 = (bf16[4,16,1664]{2,1,0:T(8,128)(2,1)S(1)}, bf16[4,16,1664]{2,1,0:T(8,128)(2,1)S(1)}, u32[]{:S(2)}, u32[]{:S(2)}) collective-permute-start(bf16[4,16,1664]{2,1,0:T(8,128)(2,1)S(1)} %get-tuple-element.45), channel_id=1, source_target_pairs={{0,16},{1,17},{2,18},{3,19},{4,20},{5,21},{6,22},{7,23},{8,24},{9,... | collective-permute-start | bytes 638984 | tf_op jit(solution)/shard_map/ppermute | solution.py:404
  26.5 0.1 collective-permute-start.7
  26.7 2.8 %collective-permute-start.8 = (bf16[4,16,1664]{2,1,0:T(8,128)(2,1)S(1)}, bf16[4,16,1664]{2,1,0:T(8,128)(2,1)S(1)}, u32[]{:S(2)}, u32[]{:S(2)}) collective-permute-start(bf16[4,16,1664]{2,1,0:T(8,128)(2,1)S(1)} %get-tuple-element.47), channel_id=1, source_target_pairs={{0,18},{1,19},{2,16},{3,17},{4,22},{5,23},{6,20},{7,21},{8,26},{9,... | collective-permute-start | bytes 638984 | tf_op jit(solution)/shard_map/ppermute | solution.py:404
  29.5 1.3 %collective-permute-start.3 = (bf16[256,256]{1,0:T(8,128)(2,1)S(1)}, bf16[256,256]{1,0:T(8,128)(2,1)S(1)}, u32[]{:S(2)}, u32[]{:S(2)}) collective-permute-start(bf16[256,256]{1,0:T(8,128)(2,1)S(1)} %get-tuple-element.39.spatial_ref), channel_id=1, source_target_pairs={{0,1},{1,2},{2,3},{3,4},{4,5},{5,6},{6,7},{7,8},{8,9},{9,10},{10,1... | collective-permute-start | bytes 393224 | tf_op jit(solution)/shard_map/ppermute | solution.py:461
  30.8 3.3 %collective-permute-done.6.refs_1_ = bf16[4,16,1664]{2,1,0:T(8,128)(2,1)S(1)} collective-permute-done((bf16[4,16,1664]{2,1,0:T(8,128)(2,1)S(1)}, bf16[4,16,1664]{2,1,0:T(8,128)(2,1)S(1)}, u32[]{:S(2)}, u32[]{:S(2)}) %collective-permute-start.6) | collective-permute-done | bytes 213024 | tf_op jit(solution)/shard_map/ppermute | solution.py:404
  34.1 4.0 %collective-permute-done.7.refs_2_ = bf16[4,16,1664]{2,1,0:T(8,128)(2,1)S(1)} collective-permute-done((bf16[4,16,1664]{2,1,0:T(8,128)(2,1)S(1)}, bf16[4,16,1664]{2,1,0:T(8,128)(2,1)S(1)}, u32[]{:S(2)}, u32[]{:S(2)}) %collective-permute-start.7) | collective-permute-done | bytes 213024 | tf_op jit(solution)/shard_map/ppermute | solution.py:404
  38.1 0.1 shard_map.107
  38.2 1.6 %collective-permute-start.9 = (bf16[16,1664]{1,0:T(8,128)(2,1)S(1)}, bf16[16,1664]{1,0:T(8,128)(2,1)S(1)}, u32[]{:S(2)}, u32[]{:S(2)}) collective-permute-start(bf16[16,1664]{1,0:T(8,128)(2,1)S(1)} %get-tuple-element.49), channel_id=1, source_target_pairs={{0,4},{1,5},{2,6},{3,7},{4,8},{5,9},{6,10},{7,11},{8,12},{9,13},{1... | collective-permute-start | bytes 159752 | tf_op jit(solution)/shard_map/ppermute | solution.py:404
  39.8 1.8 %collective-permute-start.10 = (bf16[16,1664]{1,0:T(8,128)(2,1)S(1)}, bf16[16,1664]{1,0:T(8,128)(2,1)S(1)}, u32[]{:S(2)}, u32[]{:S(2)}) collective-permute-start(bf16[16,1664]{1,0:T(8,128)(2,1)S(1)} %get-tuple-element.50), channel_id=1, source_target_pairs={{0,8},{1,9},{2,10},{3,11},{4,12},{5,13},{6,14},{7,15},{8,0},{9,1},... | collective-permute-start | bytes 159752 | tf_op jit(solution)/shard_map/ppermute | solution.py:404
  41.6 1.3 %collective-permute-start.11 = (bf16[16,1664]{1,0:T(8,128)(2,1)S(1)}, bf16[16,1664]{1,0:T(8,128)(2,1)S(1)}, u32[]{:S(2)}, u32[]{:S(2)}) collective-permute-start(bf16[16,1664]{1,0:T(8,128)(2,1)S(1)} %get-tuple-element.51), channel_id=1, source_target_pairs={{0,12},{1,13},{2,14},{3,15},{4,0},{5,1},{6,2},{7,3},{8,4},{9,5},{1... | collective-permute-start | bytes 159752 | tf_op jit(solution)/shard_map/ppermute | solution.py:404
  43.0 1.0 %shard_map.105 = bf16[256,256]{1,0:T(8,128)(2,1)} custom-call(bf16[256,256]{1,0:T(8,128)(2,1)S(1)} %bitcast.15, bf16[256,256]{1,0:T(8,128)(2,1)S(1)} %get-tuple-element.39.spatial_ref, bf16[256,256]{1,0:T(8,128)(2,1)S(1)} %collective-permute-done.3.before_ref, bf16[384,256]{1,0:T(8,128)(2,1)S(1)} %copy-done.2, bf16[960,256]{1,0:T(8,128)(2,1)S(1)} %collective-permute-done.rest_0_), custom_call_target="tpu_custom_call" | custom-call | flops 100663296 | bytes 1000000 | tf_op jit(solution)/shard_map/pallas_call | solution.py:26
  43.9 0.4 collective-permute-done.9.refs_1_
  44.3 1.2 %collective-permute-done.10.refs_2_ = bf16[16,1664]{1,0:T(8,128)(2,1)S(1)} collective-permute-done((bf16[16,1664]{1,0:T(8,128)(2,1)S(1)}, bf16[16,1664]{1,0:T(8,128)(2,1)S(1)}, u32[]{:S(2)}, u32[]{:S(2)}) %collective-permute-start.10) | collective-permute-done | bytes 53280 | tf_op jit(solution)/shard_map/ppermute | solution.py:404
  45.5 0.5 %collective-permute-done.11.refs_3_ = bf16[16,1664]{1,0:T(8,128)(2,1)S(1)} collective-permute-done((bf16[16,1664]{1,0:T(8,128)(2,1)S(1)}, bf16[16,1664]{1,0:T(8,128)(2,1)S(1)}, u32[]{:S(2)}, u32[]{:S(2)}) %collective-permute-start.11) | collective-permute-done | bytes 53280 | tf_op jit(solution)/shard_map/ppermute | solution.py:404
  46.0 1.1 %shard_map.108 = (f32[16,1152]{1,0:T(8,128)}, f32[16,384]{1,0:T(8,128)}, f32[2,16]{1,0:T(2,128)}, bf16[256,256]{1,0:T(8,128)(2,1)}) custom-call(bf16[16,1664]{1,0:T(8,128)(2,1)S(1)} %get-tuple-element.48.refs_0_, bf16[16,1664]{1,0:T(8,128)(2,1)S(1)} %collective-permute-done.9.refs_1_, bf16[16,1664]{1,0:T(8,128)(2,1)S(1)} %collective-permute-done.10.refs_2_, ...), custom_call_target="tpu_custom_call" | custom-call | bytes 1000000 | tf_op jit(solution)/shard_map/pallas_call | solution.py:26
  (12 shorter events, 0.0 us)
Async XLA Ops:
  0.6 20.0 %copy-start.2 = (bf16[384,256]{1,0:T(8,128)(2,1)S(1)}, bf16[384,256]{1,0:T(8,128)(2,1)}, u32[]{:S(2)}) copy-start(bf16[384,256]{1,0:T(8,128)(2,1)} %wt_ref.5) | copy-start | bytes 589828
  0.6 20.0 %copy-start.1 = (bf16[1,2,8,16,256]{4,3,2,1,0:T(8,128)(2,1)S(1)}, bf16[1,2,8,16,256]{4,3,2,1,0:T(8,128)(2,1)}, u32[]{:S(2)}) copy-start(bf16[1,2,8,16,256]{4,3,2,1,0:T(8,128)(2,1)} %param.6) | copy-start | bytes 393220
  0.7 20.0 %copy-start.4 = (bf16[1,2,8,16,256]{4,3,2,1,0:T(8,128)(2,1)S(1)}, bf16[1,2,8,16,256]{4,3,2,1,0:T(8,128)(2,1)}, u32[]{:S(2)}) copy-start(bf16[1,2,8,16,256]{4,3,2,1,0:T(8,128)(2,1)} %param.7) | copy-start | bytes 393220
  0.7 21.8 %copy-start = (bf16[1152,256]{1,0:T(8,128)(2,1)S(1)}, bf16[1152,256]{1,0:T(8,128)(2,1)}, u32[]{:S(2)}) copy-start(bf16[1152,256]{1,0:T(8,128)(2,1)} %ws_ref.3) | copy-start | bytes 1769476
  2.7 17.9 %collective-permute-start = (bf16[960,256]{1,0:T(8,128)(2,1)}, bf16[960,256]{1,0:T(8,128)(2,1)S(1)}, u32[]{:S(2)}, u32[]{:S(2)}) collective-permute-start(bf16[960,256]{1,0:T(8,128)(2,1)} %get-tuple-element.31), channel_id=1, source_target_pairs={{0,16},{1,17},{2,18},{3,19},{4,20},{5,21},{6,22},{7,23},{8,24},{9,... | collective-permute-start | bytes 1474568 | tf_op jit(solution)/shard_map/ppermute | solution.py:404
  5.7 14.9 %collective-permute-start.1 = (bf16[256,256]{1,0:T(8,128)(2,1)}, bf16[256,256]{1,0:T(8,128)(2,1)S(1)}, u32[]{:S(2)}, u32[]{:S(2)}) collective-permute-start(bf16[256,256]{1,0:T(8,128)(2,1)} %bitcast.19), channel_id=1, source_target_pairs={{1,0},{2,1},{3,2},{4,3},{5,4},{6,5},{7,6},{8,7},{9,8},{10,9},{11,1... | collective-permute-start | bytes 393224 | tf_op jit(solution)/shard_map/ppermute | solution.py:425
  7.0 13.6 %all-to-all-start = ((f32[16,2,512]{2,1,0:T(2,128)}), f32[16,2,512]{2,1,0:T(2,128)S(1)}, u32[]{:S(2)}, u32[]{:S(2)}) async-start(f32[16,2,512]{2,1,0:T(2,128)} %get-tuple-element.32), calls=%async_computation | async-start | bytes 131072 | tf_op jit(solution)/shard_map/all_to_all | solution.py:426
  13.7 0.9 %copy-start.3 = (bf16[1,2,8,16,256]{4,3,2,1,0:T(8,128)(2,1)S(1)}, bf16[1,2,8,16,256]{4,3,2,1,0:T(8,128)(2,1)}, u32[]{:S(2)}) copy-start(bf16[1,2,8,16,256]{4,3,2,1,0:T(8,128)(2,1)} %param.7) | copy-start | bytes 393220
  20.6 1.9 %collective-permute-start.2 = (bf16[960,256]{1,0:T(8,128)(2,1)S(1)}, bf16[960,256]{1,0:T(8,128)(2,1)S(1)}, u32[]{:S(2)}, u32[]{:S(2)}) collective-permute-start(bf16[960,256]{1,0:T(8,128)(2,1)S(1)} %collective-permute-done.rest_0_), channel_id=1, source_target_pairs={{0,1},{1,0},{2,3},{3,2},{4,5},{5,4},{6,7},{7,6},{8,9},{9,8},{10,11... | collective-permute-start | bytes 1474568 | tf_op jit(solution)/shard_map/ppermute | solution.py:404
  21.7 2.6 %collective-permute-start.4 = (bf16[2,128,1152]{2,1,0:T(8,128)(2,1)S(1)}, bf16[2,128,1152]{2,1,0:T(8,128)(2,1)S(1)}, u32[]{:S(2)}, u32[]{:S(2)}) collective-permute-start(bf16[2,128,1152]{2,1,0:T(8,128)(2,1)S(1)} %get-tuple-element.41), channel_id=1, source_target_pairs={{0,1},{1,0},{2,3},{3,2},{4,5},{5,4},{6,7},{7,6},{8,9},{9,8},{10,11... | collective-permute-start | bytes 1769480 | tf_op jit(solution)/shard_map/ppermute | solution.py:404
  24.1 1.6 %collective-permute-start.5 = (bf16[2,128,512]{2,1,0:T(8,128)(2,1)S(1)}, bf16[2,128,512]{2,1,0:T(8,128)(2,1)S(1)}, u32[]{:S(2)}, u32[]{:S(2)}) collective-permute-start(bf16[2,128,512]{2,1,0:T(8,128)(2,1)S(1)} %get-tuple-element.43), channel_id=1, source_target_pairs={{0,1},{1,0},{2,3},{3,2},{4,5},{5,4},{6,7},{7,6},{8,9},{9,8},{10,11... | collective-permute-start | bytes 786440 | tf_op jit(solution)/shard_map/ppermute | solution.py:404
  25.9 8.2 %collective-permute-start.6 = (bf16[4,16,1664]{2,1,0:T(8,128)(2,1)S(1)}, bf16[4,16,1664]{2,1,0:T(8,128)(2,1)S(1)}, u32[]{:S(2)}, u32[]{:S(2)}) collective-permute-start(bf16[4,16,1664]{2,1,0:T(8,128)(2,1)S(1)} %get-tuple-element.45), channel_id=1, source_target_pairs={{0,16},{1,17},{2,18},{3,19},{4,20},{5,21},{6,22},{7,23},{8,24},{9,... | collective-permute-start | bytes 638984 | tf_op jit(solution)/shard_map/ppermute | solution.py:404
  26.5 11.6 %collective-permute-start.7 = (bf16[4,16,1664]{2,1,0:T(8,128)(2,1)S(1)}, bf16[4,16,1664]{2,1,0:T(8,128)(2,1)S(1)}, u32[]{:S(2)}, u32[]{:S(2)}) collective-permute-start(bf16[4,16,1664]{2,1,0:T(8,128)(2,1)S(1)} %get-tuple-element.46), channel_id=1, source_target_pairs={{0,2},{1,3},{2,0},{3,1},{4,6},{5,7},{6,4},{7,5},{8,10},{9,11},{10,... | collective-permute-start | bytes 638984 | tf_op jit(solution)/shard_map/ppermute | solution.py:404
  26.7 11.5 %collective-permute-start.8 = (bf16[4,16,1664]{2,1,0:T(8,128)(2,1)S(1)}, bf16[4,16,1664]{2,1,0:T(8,128)(2,1)S(1)}, u32[]{:S(2)}, u32[]{:S(2)}) collective-permute-start(bf16[4,16,1664]{2,1,0:T(8,128)(2,1)S(1)} %get-tuple-element.47), channel_id=1, source_target_pairs={{0,18},{1,19},{2,16},{3,17},{4,22},{5,23},{6,20},{7,21},{8,26},{9,... | collective-permute-start | bytes 638984 | tf_op jit(solution)/shard_map/ppermute | solution.py:404
  29.5 13.5 %collective-permute-start.3 = (bf16[256,256]{1,0:T(8,128)(2,1)S(1)}, bf16[256,256]{1,0:T(8,128)(2,1)S(1)}, u32[]{:S(2)}, u32[]{:S(2)}) collective-permute-start(bf16[256,256]{1,0:T(8,128)(2,1)S(1)} %get-tuple-element.39.spatial_ref), channel_id=1, source_target_pairs={{0,1},{1,2},{2,3},{3,4},{4,5},{5,6},{6,7},{7,8},{8,9},{9,10},{10,1... | collective-permute-start | bytes 393224 | tf_op jit(solution)/shard_map/ppermute | solution.py:461
  38.2 6.1 %collective-permute-start.9 = (bf16[16,1664]{1,0:T(8,128)(2,1)S(1)}, bf16[16,1664]{1,0:T(8,128)(2,1)S(1)}, u32[]{:S(2)}, u32[]{:S(2)}) collective-permute-start(bf16[16,1664]{1,0:T(8,128)(2,1)S(1)} %get-tuple-element.49), channel_id=1, source_target_pairs={{0,4},{1,5},{2,6},{3,7},{4,8},{5,9},{6,10},{7,11},{8,12},{9,13},{1... | collective-permute-start | bytes 159752 | tf_op jit(solution)/shard_map/ppermute | solution.py:404
  39.8 5.6 %collective-permute-start.10 = (bf16[16,1664]{1,0:T(8,128)(2,1)S(1)}, bf16[16,1664]{1,0:T(8,128)(2,1)S(1)}, u32[]{:S(2)}, u32[]{:S(2)}) collective-permute-start(bf16[16,1664]{1,0:T(8,128)(2,1)S(1)} %get-tuple-element.50), channel_id=1, source_target_pairs={{0,8},{1,9},{2,10},{3,11},{4,12},{5,13},{6,14},{7,15},{8,0},{9,1},... | collective-permute-start | bytes 159752 | tf_op jit(solution)/shard_map/ppermute | solution.py:404
  41.6 4.4 %collective-permute-start.11 = (bf16[16,1664]{1,0:T(8,128)(2,1)S(1)}, bf16[16,1664]{1,0:T(8,128)(2,1)S(1)}, u32[]{:S(2)}, u32[]{:S(2)}) collective-permute-start(bf16[16,1664]{1,0:T(8,128)(2,1)S(1)} %get-tuple-element.51), channel_id=1, source_target_pairs={{0,12},{1,13},{2,14},{3,15},{4,0},{5,1},{6,2},{7,3},{8,4},{9,5},{1... | collective-permute-start | bytes 159752 | tf_op jit(solution)/shard_map/ppermute | solution.py:404
